TPU v7x, 512 devices: a whole 4x8x8 slice. The times are simulated.
512 devices in a mesh: store: 32 (over x, z), tp: 16 (over y, core).
Axes of the slice: x: 4, y: 8, z: 8, core: 2. Of those that a mesh axis runs over, the one named last changes fastest.
Arguments:
- hidden: bfloat16 [32, 64, 8192], P('store', None, 'tp'), may hold values from -6 to 6
- norm_gain: bfloat16 [8192], replicated, may hold values from 0.25 to 1.75
- q_weight: bfloat16 [8192, 16, 512], P('store', 'tp'), may hold values from -1 to 1
- kv_weight: bfloat16 [8192, 16, 128], P('store', 'tp'), may hold values from -0.0625 to 0.0625
- cache_store: bfloat16 [256, 16, 128, 256], P('store', 'tp'), may hold values from -6 to 6
- location: int32 [256], replicated, may hold values from 0 to 255, as said below
- stretch_ids: int32 [32, 32], P('store'), may hold values from -1 to 255, as said below
- rec_pos: int32 [32, 64], P('store'), may hold values from 0 to 8191, as said below
Outputs:
- attended: bfloat16 [32, 64, 16, 512], P('store', None, 'tp')
Inputs may be any that keep to these rules, and one draw needn't show every extreme that they name: A permutation: stretch c is row location[c] of cache_store, on store shard location[c] // 8. `stretch_ids`: each row holds 8 to 32 distinct stretch ids followed by -1s, and some row holds 32; at most 1 of one request's stretches lie on one store shard, and every request reaches that many on some shard. `rec_pos`: each row: 64 distinct increasing positions below 256 times the request's number of stretches; the request's last position is always among them.
All inputs are finite; a program needn't handle non-finite values.
Results may differ from a plain program's by a relative error of at most 0.014.
Values may be sent and summed in bfloat16 or wider, within the bound.
No kernel may reach another device: no remote copies, remote signals or barrier semaphores. Data moves between devices by JAX's collectives and lax.ppermute only.
A program may use at most 64 MiB of HBM per device.

v0:
```python
import math

import jax
import jax.numpy as jnp
from jax import lax
from jax.sharding import PartitionSpec as P

KVH = 8
HD = 128
STRETCH = 256
MAXC = 32
CH_DEV = 8
QS = 4
HALF = 128


theta_base = 500000.0
neg_large = -1e30


def from_partner(block, axis, stride):
    count = lax.axis_size(axis)
    route = []
    for low in range(count):
        high = low | 1 << stride
        if high != low and high < count:
            route += [(low, high), (high, low)]
    return lax.ppermute(block, axis, route)


def rotary(values_in, positions):
    half_width = values_in.shape[-1] // 2
    frequency = jnp.exp(
        -math.log(theta_base) * jnp.arange(half_width, dtype=jnp.float32) / half_width
    )
    angles = positions.astype(jnp.float32)[:, None] * frequency[None, :]
    angle_shape = (angles.shape[0],) + (1,) * (values_in.ndim - 2) + (half_width,)
    cosine = jnp.cos(angles).reshape(angle_shape)
    sine_part = jnp.sin(angles).reshape(angle_shape)
    first_part = values_in[..., :half_width]
    second = values_in[..., half_width:]
    return jnp.concatenate(
        [first_part * cosine - second * sine_part, second * cosine + first_part * sine_part],
        axis=-1,
    )


def rms_normed(states, norm_gain):
    widened = states.astype(jnp.float32)
    variance = jnp.mean(widened * widened, axis=-1, keepdims=True)
    return (widened * lax.rsqrt(variance + 1e-05) * norm_gain.astype(jnp.float32)).astype(
        jnp.bfloat16
    )


def update_softmax(carried, scores, allowed, combine_values):
    row_peak, weight_sum, accum_out = carried
    axes = tuple(range(4, scores.ndim))
    block_peak = jnp.max(jnp.where(allowed, scores, neg_large), axis=axes)
    new_peak = jnp.maximum(row_peak, block_peak)
    expanded = new_peak.reshape(new_peak.shape + (1,) * len(axes))
    weights = jnp.where(allowed, jnp.exp(scores - expanded), 0.0)
    factor = jnp.exp(row_peak - new_peak)
    weight_sum = weight_sum * factor + jnp.sum(weights, axis=axes)
    accum_out = accum_out * factor[..., None] + combine_values(weights.astype(jnp.bfloat16))
    return (new_peak, weight_sum, accum_out)


def body(hidden, norm_gain, q_weight, kv_weight, cache_store, location, stretch_ids, rec_pos):
    store_count = lax.axis_size("store")
    tp_count = lax.axis_size("tp")
    my_store = lax.axis_index("store")
    my_tp = lax.axis_index("tp")
    heads_here = cache_store.shape[1]
    which_half = my_tp * heads_here // KVH
    is_first = which_half == 0
    slot_count = max(1, MAXC // store_count)
    slot_total = store_count * slot_count
    partner_bit = tp_count.bit_length() - 2
    score_scale = 1.0 / math.sqrt(HD)
    positions = rec_pos[0]
    row_total = positions.shape[0]
    every_list = lax.all_gather(stretch_ids, "store", axis=0, tiled=True)
    states = lax.all_gather(hidden, "tp", axis=2, tiled=True)[0]
    normed = rms_normed(states, norm_gain)

    def add_rows(weight_piece):
        flat_piece = weight_piece.reshape(weight_piece.shape[0], -1)
        return jnp.dot(normed, flat_piece, preferred_element_type=jnp.float32)

    query_sum = add_rows(lax.all_gather(q_weight, "store", axis=0, tiled=True))
    fresh_sum = add_rows(lax.all_gather(kv_weight, "store", axis=0, tiled=True))
    own_queries = rotary(query_sum.reshape(row_total, heads_here, QS, HD), positions).astype(
        jnp.bfloat16
    )
    fresh_piece = fresh_sum.reshape(row_total, heads_here, HD)
    fresh_piece = jnp.where(is_first, rotary(fresh_piece, positions), fresh_piece).astype(
        jnp.bfloat16
    )
    other_queries, other_piece = from_partner((own_queries, fresh_piece), "tp", partner_bit)
    first_queries = jnp.where(is_first, own_queries, other_queries)
    second_queries = jnp.where(is_first, other_queries, own_queries)
    queries = jnp.stack([first_queries, second_queries], axis=2)
    fresh_keys = jnp.where(is_first, fresh_piece, other_piece)
    fresh_values = jnp.where(is_first, other_piece, fresh_piece)
    valid_all = every_list >= 0
    rows_all = location[jnp.maximum(every_list, 0)]
    shard_all = rows_all // CH_DEV
    local_all = rows_all % CH_DEV
    slot_ids = jnp.arange(slot_count, dtype=jnp.int32)
    sending = valid_all & (shard_all == my_store)
    sent_rank = jnp.cumsum(sending.astype(jnp.int32), axis=1) - 1
    picked = sending[:, None, :] & (sent_rank[:, None, :] == slot_ids[None, :, None])
    send_rows = jnp.sum(jnp.where(picked, local_all[:, None, :], 0), axis=2)
    send_live = jnp.any(picked, axis=2)
    outgoing = cache_store[send_rows]
    outgoing = jnp.where(send_live[:, :, None, None, None], outgoing, jnp.zeros((), jnp.bfloat16))
    arrived = lax.all_to_all(outgoing, "store", split_axis=0, concat_axis=0, tiled=True)
    arrived = arrived.reshape(slot_total, heads_here, HALF, 2 * HD)
    own_list = lax.dynamic_index_in_dim(every_list, my_store, 0, keepdims=False)
    own_shard = lax.dynamic_index_in_dim(shard_all, my_store, 0, keepdims=False)
    own_valid = own_list >= 0
    list_order = jnp.arange(MAXC, dtype=jnp.int32)
    earlier = (
        (list_order[None, :] < list_order[:, None])
        & (own_shard[None, :] == own_shard[:, None])
        & own_valid[None, :]
    )
    own_rank = jnp.sum(earlier.astype(jnp.int32), axis=1)
    own_slot = own_shard * slot_count + own_rank
    offsets = which_half * HALF + jnp.arange(HALF, dtype=jnp.int32)

    def attend(carried, key_block, key_pos, key_live):
        replaced = jnp.any(key_pos[:, :, None] == positions[None, None, :], axis=2)
        allowed = (key_live & jnp.logical_not(replaced))[None] & (
            key_pos[None] <= positions[:, None, None]
        )
        scores = (
            jnp.einsum(
                "rgsqc,bgic->rgsqbi",
                queries,
                key_block[..., :HD],
                preferred_element_type=jnp.float32,
            )
            * score_scale
        )
        value_block = key_block[..., HD:]

        def combine_values(rounded):
            return jnp.einsum(
                "rgsqbi,bgic->rgsqc", rounded, value_block, preferred_element_type=jnp.float32
            )

        return update_softmax(carried, scores, allowed[:, None, None, None], combine_values)

    stat_shape = (row_total, heads_here, 2, QS)
    carried = (
        jnp.full(stat_shape, neg_large, jnp.float32),
        jnp.zeros(stat_shape, jnp.float32),
        jnp.zeros(stat_shape + (HD,), jnp.float32),
    )
    block_width = max(1, 512 // HALF)
    slot_match = (
        own_slot[None, :] == jnp.arange(slot_total, dtype=jnp.int32)[:, None]
    ) & own_valid[None, :]
    slot_stretch = jnp.sum(jnp.where(slot_match, list_order[None, :], 0), axis=1)
    slot_live = jnp.broadcast_to(jnp.any(slot_match, axis=1)[:, None], (slot_total, HALF))
    slot_pos = slot_stretch[:, None] * STRETCH + offsets[None, :]
    per_block = math.gcd(slot_total, block_width)

    def all_step(block_index, running):
        begin = block_index * per_block
        return attend(
            running,
            lax.dynamic_slice_in_dim(arrived, begin, per_block, 0),
            lax.dynamic_slice_in_dim(slot_pos, begin, per_block, 0),
            lax.dynamic_slice_in_dim(slot_live, begin, per_block, 0),
        )

    carried = lax.fori_loop(0, slot_total // per_block, all_step, carried)
    fresh_here = positions % STRETCH // HALF == which_half
    fresh_allowed = fresh_here[None, :] & (positions[None, :] <= positions[:, None])
    fresh_scores = (
        jnp.einsum("rgsqc,ngc->rgsqn", queries, fresh_keys, preferred_element_type=jnp.float32)
        * score_scale
    )

    def fresh_combine(rounded):
        return jnp.einsum(
            "rgsqn,ngc->rgsqc", rounded, fresh_values, preferred_element_type=jnp.float32
        )

    carried = update_softmax(
        carried, fresh_scores, fresh_allowed[:, None, None, None, :], fresh_combine
    )
    row_peak, weight_sum, accum_out = carried

    def handed(stat):
        return jnp.where(is_first, stat[:, :, 1], stat[:, :, 0])

    def retained(stat):
        return jnp.where(is_first, stat[:, :, 0], stat[:, :, 1])

    got_peak, got_sum, got_accum = (
        from_partner(handed(row_peak).astype(jnp.bfloat16), "tp", partner_bit).astype(jnp.float32),
        from_partner(handed(weight_sum).astype(jnp.bfloat16), "tp", partner_bit).astype(
            jnp.float32
        ),
        from_partner(handed(accum_out).astype(jnp.bfloat16), "tp", partner_bit).astype(jnp.float32),
    )
    mine_peak = retained(row_peak)
    joint_peak = jnp.maximum(mine_peak, got_peak)
    mine_factor = jnp.exp(mine_peak - joint_peak)
    got_factor = jnp.exp(got_peak - joint_peak)
    joint_sum = retained(weight_sum) * mine_factor + got_sum * got_factor
    joint_accum = retained(accum_out) * mine_factor[..., None] + got_accum * got_factor[..., None]
    attended = (joint_accum / joint_sum[..., None]).astype(jnp.bfloat16)
    return attended.reshape(1, row_total, heads_here, QS * HD)


def solution(mesh):
    in_specs = (
        P("store", None, "tp"),
        P(),
        P("store", "tp", None),
        P("store", "tp", None),
        P("store", "tp", None, None),
        P(),
        P("store", None),
        P("store", None),
    )
    out_specs = P("store", None, "tp", None)
    return jax.shard_map(body, mesh=mesh, in_specs=in_specs, out_specs=out_specs, check_vma=False)
```

profile of v0, /device:TPU:16, one launch (start us, length us, event | category | flops | bytes accessed | tf_op | source)
XLA Modules:
  0.0 320.1 jit_solution(8087013488972030239)
XLA Ops:
  6.5 0.7 all-gather.5.cloned.1.call-update
  7.3 0.7 all-gather.9.cloned.1.call-update
  8.1 0.7 all-gather.7.cloned.1.call-update
  8.8 44.1 %all-gather = s32[32,1,32]{2,1,0:T(1,128)S(1)} all-gather(s32[1,1,32]{2,1,0:T(1,128)} %bitcast.220), channel_id=1, replica_groups=mesh['store'=32,'tp'=16] {'store'}, dimensions={0}, use_global_device_ids=true | all-gather | bytes 4224 | tf_op jit(solution)/shard_map/all_gather | solution.py:83
  53.0 6.8 %gather_fusion = s32[1024]{0:T(1024)S(1)} fusion(s32[256]{0:T(256)S(1)} %copy-done.1, s32[1024]{0:T(1024)S(1)} %broadcast_clamp_fusion), kind=kCustom, calls=%fused_computation | custom fusion | bytes 12288 | tf_op jit(solution)/shard_map/gather | solution.py:107
  60.4 0.7 gather_fusion.1
  61.1 1.6 bitcast_select_fusion
  62.6 6.6 %all-to-all-start = ((bf16[32,1,1,128,256]{4,3,2,1,0:T(8,128)(2,1)}), bf16[32,1,1,128,256]{4,3,2,1,0:T(8,128)(2,1)S(1)}, u32[]{:S(2)}, u32[]{:S(2)}) async-start(bf16[32,1,1,128,256]{4,3,2,1,0:T(8,128)(2,1)} %bitcast_select_fusion), calls=%async_computation | async-start | bytes 4194304 | tf_op jit(solution)/shard_map/all_to_all | solution.py:118
  70.3 1.5 fusion.14
  71.8 74.1 %all-gather.9.cloned.1.call-done = bf16[8192,1,128]{2,0,1:T(8,128)(2,1)} async-done(((bf16[256,1,128]{2,0,1:T(8,128)(2,1)}), bf16[8192,1,128]{2,0,1:T(8,128)(2,1)}) %all-gather.9.cloned.1.call-update) | async-done | bytes 2097168 | tf_op jit(solution)/shard_map/all_gather | solution.py:92
  145.9 2.4 fusion.17
  148.6 101.9 %all-gather.7.cloned.1.call-done = bf16[8192,1,512]{2,0,1:T(8,128)(2,1)} async-done(((bf16[256,1,512]{2,0,1:T(8,128)(2,1)}), bf16[8192,1,512]{2,0,1:T(8,128)(2,1)}) %all-gather.7.cloned.1.call-update) | async-done | bytes 8388624 | tf_op jit(solution)/shard_map/all_gather | solution.py:91
  250.5 11.4 %copy.27 = bf16[512,8192]{1,0:T(8,128)(2,1)} copy(bf16[512,8192]{0,1:T(8,128)(2,1)} %bitcast.208) | data formatting | bytes 16777216 | tf_op jit(solution)/shard_map/dot_general | solution.py:89
  261.9 6.4 %convolution_bitcast_fusion.2 = f32[64,1,4,128]{3,0,2,1:T(8,128)S(1)} fusion(bf16[4,128,8192]{2,1,0:T(8,128)(2,1)} %bitcast.207, bf16[1,64,8192]{2,1,0:T(8,128)(2,1)} %all-gather.5.cloned.1.call-done, f32[8192]{0:T(1024)S(1)} %convert_element_type.112, f32[64]{0:T(128)S(1)} %add_rsqrt_fusion), kind=kOutput, calls=%fused_computation.42 | convolution fusion | flops 538968064 | bytes 9601280 | tf_op jit(solution)/shard_map/dot_general | solution.py:89
  268.5 5.6 %collective-permute-start = (bf16[64,1,4,128]{3,0,2,1:T(8,128)(2,1)S(1)}, bf16[64,1,4,128]{3,0,2,1:T(8,128)(2,1)S(1)}, u32[]{:S(2)}, u32[]{:S(2)}) collective-permute-start(bf16[64,1,4,128]{3,0,2,1:T(8,128)(2,1)S(1)} %pad_maximum_fusion.1), channel_id=1, source_target_pairs={{0,8},{8,0},{1,9},{9,1},{2,10},{10,2},{3,11},{11,3},{4,12},{12,4},... | collective-permute-start | bytes 196616 | tf_op jit(solution)/shard_map/ppermute | solution.py:28
  274.2 4.2 %collective-permute-start.1 = (bf16[64,1,128]{2,0,1:T(8,128)(2,1)S(1)}, bf16[64,1,128]{2,0,1:T(8,128)(2,1)S(1)}, u32[]{:S(2)}, u32[]{:S(2)}) collective-permute-start(bf16[64,1,128]{2,0,1:T(8,128)(2,1)S(1)} %fusion.48), channel_id=1, source_target_pairs={{0,8},{8,0},{1,9},{9,1},{2,10},{10,2},{3,11},{11,3},{4,12},{12,4},... | collective-permute-start | bytes 49160 | tf_op jit(solution)/shard_map/ppermute | solution.py:28
  278.3 0.9 collective-permute-done
  279.4 12.0 %while.18 = (s32[]{:T(128)}, f32[64,1,2,4]{0,3,2,1:T(4,128)S(1)}, f32[64,1,2,4]{0,3,2,1:T(4,128)S(1)}, f32[64,1,2,4,128]{4,0,3,2,1:T(8,128)S(1)}, pred[32,128]{1...) while((s32[]{:T(128)}, f32[64,1,2,4]{0,3,2,1:T(4,128)S(1)}, ...), condition=%wide.region_11.12_spmd.clone, body=%wide.region_7.11_spmd.clone.sunk | while | flops 136908288 | bytes 4242663 | solution.py:180
  280.4 0.4 fusion.87
  281.9 0.4 fusion.87
  282.7 0.4 select_reduce_fusion.4
  283.4 0.4 fusion.87
  284.9 0.4 fusion.87
  286.4 0.4 fusion.87
  288.0 0.4 fusion.87
  289.5 0.4 fusion.87
  291.0 0.4 fusion.87
  291.9 5.6 %collective-permute-start.2 = (bf16[64,1,4]{0,2,1:T(4,128)(2,1)S(1)}, bf16[64,1,4]{0,2,1:T(4,128)(2,1)S(1)}, u32[]{:S(2)}, u32[]{:S(2)}) collective-permute-start(bf16[64,1,4]{0,2,1:T(4,128)(2,1)S(1)} %fusion.67), channel_id=1, source_target_pairs={{0,8},{8,0},{1,9},{9,1},{2,10},{10,2},{3,11},{11,3},{4,12},{12,4},... | collective-permute-start | bytes 1544 | tf_op jit(solution)/shard_map/ppermute | solution.py:28
  297.5 4.1 %collective-permute-start.4 = (bf16[64,1,4]{0,2,1:T(4,128)(2,1)S(1)}, bf16[64,1,4]{0,2,1:T(4,128)(2,1)S(1)}, u32[]{:S(2)}, u32[]{:S(2)}) collective-permute-start(bf16[64,1,4]{0,2,1:T(4,128)(2,1)S(1)} %fusion.68), channel_id=1, source_target_pairs={{0,8},{8,0},{1,9},{9,1},{2,10},{10,2},{3,11},{11,3},{4,12},{12,4},... | collective-permute-start | bytes 1544 | tf_op jit(solution)/shard_map/ppermute | solution.py:28
  301.9 5.6 %collective-permute-start.3 = (bf16[64,1,4,128]{3,0,2,1:T(8,128)(2,1)S(1)}, bf16[64,1,4,128]{3,0,2,1:T(8,128)(2,1)S(1)}, u32[]{:S(2)}, u32[]{:S(2)}) collective-permute-start(bf16[64,1,4,128]{3,0,2,1:T(8,128)(2,1)S(1)} %fusion.36), channel_id=1, source_target_pairs={{0,8},{8,0},{1,9},{9,1},{2,10},{10,2},{3,11},{11,3},{4,12},{12,4},... | collective-permute-start | bytes 196616 | tf_op jit(solution)/shard_map/ppermute | solution.py:28
  307.6 5.1 %collective-permute-done.3 = bf16[64,1,4,128]{3,0,2,1:T(8,128)(2,1)S(1)} collective-permute-done((bf16[64,1,4,128]{3,0,2,1:T(8,128)(2,1)S(1)}, bf16[64,1,4,128]{3,0,2,1:T(8,128)(2,1)S(1)}, u32[]{:S(2)}, u32[]{:S(2)}) %collective-permute-start.3) | collective-permute-done | bytes 65568 | tf_op jit(solution)/shard_map/ppermute | solution.py:28
  312.9 0.7 reshape.581
  (135 shorter events, 10.8 us)
Async XLA Ops:
  6.5 53.8 %copy-start = (bf16[8,1,128,256]{3,2,1,0:T(8,128)(2,1)S(1)}, bf16[8,1,128,256]{3,2,1,0:T(8,128)(2,1)}, u32[]{:S(2)}) copy-start(bf16[8,1,128,256]{3,2,1,0:T(8,128)(2,1)} %param.14) | copy-start | bytes 1572868
  6.5 46.4 %copy-start.1 = (s32[256]{0:T(256)S(1)}, s32[256]{0:T(256)}, u32[]{:S(2)}) copy-start(s32[256]{0:T(256)} %param.15) | copy-start | bytes 3076
  6.5 63.7 %all-gather.5.cloned.1.call-start = ((), (), s32[]{:S(2)}) async-start(), calls=%async_computation.1 | async-start | bytes 1114112 | tf_op jit(solution)/shard_map/all_gather | solution.py:84
  7.3 138.7 %all-gather.9.cloned.1.call-start = ((), (), s32[]{:S(2)}) async-start(), calls=%async_computation.3 | async-start | bytes 2162688 | tf_op jit(solution)/shard_map/all_gather | solution.py:92
  8.0 242.5 %all-gather.7.cloned.1.call-start = ((), (), s32[]{:S(2)}) async-start(), calls=%async_computation.2 | async-start | bytes 8650752 | tf_op jit(solution)/shard_map/all_gather | solution.py:91
  62.6 6.7 %copy-start.3 = (bf16[8192]{0:T(1024)(128)(2,1)S(1)}, bf16[8192]{0:T(1024)(128)(2,1)}, u32[]{:S(2)}) copy-start(bf16[8192]{0:T(1024)(128)(2,1)} %param.11) | copy-start | bytes 49156
  62.6 7.2 %copy-start.2 = (s32[1,64]{1,0:T(1,128)S(1)}, s32[1,64]{1,0:T(1,128)}, u32[]{:S(2)}) copy-start(s32[1,64]{1,0:T(1,128)} %param.17) | copy-start | bytes 772
  62.6 216.7 %all-to-all-start = ((bf16[32,1,1,128,256]{4,3,2,1,0:T(8,128)(2,1)}), bf16[32,1,1,128,256]{4,3,2,1,0:T(8,128)(2,1)S(1)}, u32[]{:S(2)}, u32[]{:S(2)}) async-start(bf16[32,1,1,128,256]{4,3,2,1,0:T(8,128)(2,1)} %bitcast_select_fusion), calls=%async_computation | async-start | bytes 4194304 | tf_op jit(solution)/shard_map/all_to_all | solution.py:118
  268.5 10.7 %collective-permute-start = (bf16[64,1,4,128]{3,0,2,1:T(8,128)(2,1)S(1)}, bf16[64,1,4,128]{3,0,2,1:T(8,128)(2,1)S(1)}, u32[]{:S(2)}, u32[]{:S(2)}) collective-permute-start(bf16[64,1,4,128]{3,0,2,1:T(8,128)(2,1)S(1)} %pad_maximum_fusion.1), channel_id=1, source_target_pairs={{0,8},{8,0},{1,9},{9,1},{2,10},{10,2},{3,11},{11,3},{4,12},{12,4},... | collective-permute-start | bytes 196616 | tf_op jit(solution)/shard_map/ppermute | solution.py:28
  274.2 17.3 %collective-permute-start.1 = (bf16[64,1,128]{2,0,1:T(8,128)(2,1)S(1)}, bf16[64,1,128]{2,0,1:T(8,128)(2,1)S(1)}, u32[]{:S(2)}, u32[]{:S(2)}) collective-permute-start(bf16[64,1,128]{2,0,1:T(8,128)(2,1)S(1)} %fusion.48), channel_id=1, source_target_pairs={{0,8},{8,0},{1,9},{9,1},{2,10},{10,2},{3,11},{11,3},{4,12},{12,4},... | collective-permute-start | bytes 49160 | tf_op jit(solution)/shard_map/ppermute | solution.py:28
  291.9 15.7 %collective-permute-start.2 = (bf16[64,1,4]{0,2,1:T(4,128)(2,1)S(1)}, bf16[64,1,4]{0,2,1:T(4,128)(2,1)S(1)}, u32[]{:S(2)}, u32[]{:S(2)}) collective-permute-start(bf16[64,1,4]{0,2,1:T(4,128)(2,1)S(1)} %fusion.67), channel_id=1, source_target_pairs={{0,8},{8,0},{1,9},{9,1},{2,10},{10,2},{3,11},{11,3},{4,12},{12,4},... | collective-permute-start | bytes 1544 | tf_op jit(solution)/shard_map/ppermute | solution.py:28
  297.5 10.1 %collective-permute-start.4 = (bf16[64,1,4]{0,2,1:T(4,128)(2,1)S(1)}, bf16[64,1,4]{0,2,1:T(4,128)(2,1)S(1)}, u32[]{:S(2)}, u32[]{:S(2)}) collective-permute-start(bf16[64,1,4]{0,2,1:T(4,128)(2,1)S(1)} %fusion.68), channel_id=1, source_target_pairs={{0,8},{8,0},{1,9},{9,1},{2,10},{10,2},{3,11},{11,3},{4,12},{12,4},... | collective-permute-start | bytes 1544 | tf_op jit(solution)/shard_map/ppermute | solution.py:28
  301.9 10.8 %collective-permute-start.3 = (bf16[64,1,4,128]{3,0,2,1:T(8,128)(2,1)S(1)}, bf16[64,1,4,128]{3,0,2,1:T(8,128)(2,1)S(1)}, u32[]{:S(2)}, u32[]{:S(2)}) collective-permute-start(bf16[64,1,4,128]{3,0,2,1:T(8,128)(2,1)S(1)} %fusion.36), channel_id=1, source_target_pairs={{0,8},{8,0},{1,9},{9,1},{2,10},{10,2},{3,11},{11,3},{4,12},{12,4},... | collective-permute-start | bytes 196616 | tf_op jit(solution)/shard_map/ppermute | solution.py:28
Sparse Core Ops, SparseCore 0:
  9.5 44.1 all-gather.4
  56.9 89.0 all-gather.8
  149.1 101.3 all-gather.6
where the time goes:
time: 321 us; the launch traced here: 320 us
  waiting for transfers between devices  184 us (57%)
  blocking collectives  44.1 us (14%)
  starting transfers between devices  31.8 us (10%)
  local copies, waits for them, and re-layouts  19.9 us (6%)
  matrix products  15.9 us (5%)
  between operations  13.5 us (4%)
  other arithmetic  10.1 us (3%)
    all_gather x1, waiting for transfers between devices, body(): query_sum = add_rows(lax.all_gather(q_weight, 'store', axis=0, tiled=True))  102 us
    all_gather x1, waiting for transfers between devices, body(): fresh_sum = add_rows(lax.all_gather(kv_weight, 'store', axis=0, tiled=True))  74.1 us
    all_gather x1, blocking collectives, body(): every_list = lax.all_gather(stretch_ids, 'store', axis=0, tiled=True)  44.1 us
    ppermute x5, starting transfers between devices, from_partner(): return lax.ppermute(block, axis, route)  25.1 us
    dot_general x1, local copies, waits for them, and re-layouts, add_rows(): return jnp.dot(normed, flat_piece, preferred_element_type=jnp.float32)  11.4 us
    dot_general x2, matrix products, add_rows(): return jnp.dot(normed, flat_piece, preferred_element_type=jnp.float32)  8.82 us
    gather x2, local copies, waits for them, and re-layouts, body(): rows_all = location[jnp.maximum(every_list, 0)]  6.9 us
    all_to_all x1, starting transfers between devices, body(): lax.all_to_all(outgoing, 'store', split_axis=0, concat_axis=0, tiled=True)  6.61 us
  transfers between devices with their start and end apart: 9, of which 4 were waited for; matrix products, arithmetic and copies ran while one was open for 14% of the time, Pallas kernels for 0%

commit v1 on v0

v1 whole, which is shorter than its diff:
```python
import math

import jax
import jax.numpy as jnp
from jax import lax
from jax.experimental import pallas as pl
from jax.experimental.pallas import tpu as pltpu
from jax.sharding import Mesh
from jax.sharding import PartitionSpec as P

NX, NZ, NY, NC = 4, 8, 8, 2
KVH = 8
HD = 128
STRETCH = 256
MAXC = 32
CH_DEV = 8
QS = 4
HALF = 128
ROWS = 64
D = 8192
QW = QS * HD
COLS = QW + HD
QROWS = QS * ROWS

theta_base = 500000.0
neg_large = -1e30
far_away = 1 << 29

STORE = ("x", "z")
TP = ("y", "c")


def exchange(block):
    return lax.ppermute(block, "y", [(i, (i + NY // 2) % NY) for i in range(NY)])


def call(kernel, outs, name, flops=0, bytes_accessed=0):
    return pl.pallas_call(
        kernel,
        out_shape=outs,
        name=name,
        compiler_params=pltpu.CompilerParams(vmem_limit_bytes=32 * 1024 * 1024),
        cost_estimate=pl.CostEstimate(
            flops=flops, bytes_accessed=bytes_accessed, transcendentals=0
        ),
    )


def finish_kernel(parts_ref, inv_ref, cos_ref, sin_ref, fcos_ref, fsin_ref, out_ref):
    inv = inv_ref[...]
    for group in range(QS + 1):
        lanes = pl.ds(group * HD, HD)
        total = parts_ref[0, :, lanes].astype(jnp.float32)
        for part in range(1, NZ):
            total += parts_ref[part, :, lanes].astype(jnp.float32)
        total = total * inv
        cos = cos_ref[...] if group < QS else fcos_ref[...]
        sin = sin_ref[...] if group < QS else fsin_ref[...]
        turned = total * cos + pltpu.roll(total, HD // 2, 1) * sin
        out_ref[pl.ds(group * ROWS, ROWS), :] = turned.astype(jnp.bfloat16)


def attend_kernel(
    count_ref,
    shard_ref,
    flag_ref,
    own_ref,
    other_ref,
    kv_ref,
    eff_ref,
    fresh_eff_ref,
    pos_ref,
    own_out_ref,
    stat_ref,
    sent_ref,
    acc_ref,
    run_ref,
):
    is_first = flag_ref[0] == 0
    queries = jnp.concatenate([own_ref[:QROWS, :], other_ref[:QROWS, :]], axis=0)
    own_piece = own_ref[QROWS:, :]
    other_piece = other_ref[QROWS:, :]
    first = jnp.broadcast_to(is_first, own_piece.shape)
    fresh_keys = jnp.where(first, own_piece, other_piece)
    fresh_values = jnp.where(first, other_piece, own_piece)
    pos = pos_ref[...]
    nt = (((1,), (1,)), ((), ()))
    tn = (((0,), (0,)), ((), ()))

    scores = lax.dot_general(fresh_keys, queries, nt, preferred_element_type=jnp.float32)
    scores = jnp.where(fresh_eff_ref[:, 0:1] <= pos, scores, neg_large)
    peak = jnp.max(scores, axis=0, keepdims=True)
    weights = jnp.exp2(scores - peak)
    run_ref[0:1, :] = peak
    run_ref[1:2, :] = jnp.sum(weights, axis=0, keepdims=True)
    acc_ref[...] = lax.dot_general(
        fresh_values, weights.astype(jnp.bfloat16), tn, preferred_element_type=jnp.float32
    )

    per = 4
    for group in range(MAXC // per):

        @pl.when(group * per < count_ref[0])
        def _():
            pieces = []
            for j in range(group * per, group * per + per):
                keys = kv_ref[shard_ref[j], :, :HD]
                piece = lax.dot_general(keys, queries, nt, preferred_element_type=jnp.float32)
                pieces.append(jnp.where(eff_ref[:, j : j + 1] <= pos, piece, neg_large))
            old_peak = run_ref[0:1, :]
            new_peak = old_peak
            for piece in pieces:
                new_peak = jnp.maximum(new_peak, jnp.max(piece, axis=0, keepdims=True))
            factor = jnp.exp2(old_peak - new_peak)
            total = run_ref[1:2, :] * factor
            acc = acc_ref[...] * factor
            for at, piece in enumerate(pieces):
                weights = jnp.exp2(piece - new_peak)
                total += jnp.sum(weights, axis=0, keepdims=True)
                values = kv_ref[shard_ref[group * per + at], :, HD:]
                acc += lax.dot_general(
                    values,
                    weights.astype(jnp.bfloat16),
                    tn,
                    preferred_element_type=jnp.float32,
                )
            run_ref[0:1, :] = new_peak
            run_ref[1:2, :] = total
            acc_ref[...] = acc

    peak = run_ref[0:1, :]
    total = run_ref[1:2, :]
    mixed = acc_ref[...] / total
    own_out_ref[...] = mixed[:, :QROWS]
    stat_ref[0:1, :] = peak[:, :QROWS]
    stat_ref[1:2, :] = total[:, :QROWS]
    stat_ref[2:8, :] = jnp.zeros((6, QROWS), jnp.float32)
    peak = peak[:, QROWS:]
    total = total[:, QROWS:]
    peak_high = peak.astype(jnp.bfloat16).astype(jnp.float32)
    total_high = total.astype(jnp.bfloat16).astype(jnp.float32)
    stats = jnp.concatenate(
        [
            peak_high,
            peak - peak_high,
            total_high,
            total - total_high,
            jnp.zeros((12, QROWS), jnp.float32),
        ],
        axis=0,
    )
    sent_ref[:HD, :] = mixed[:, QROWS:].astype(jnp.bfloat16)
    sent_ref[HD:, :] = stats.astype(jnp.bfloat16)


def merge_kernel(own_ref, stat_ref, got_ref, out_ref):
    stats = got_ref[HD:, :].astype(jnp.float32)
    got_peak = stats[0:1, :] + stats[1:2, :]
    got_total = stats[2:3, :] + stats[3:4, :]
    peak = stat_ref[0:1, :]
    total = stat_ref[1:2, :]
    joint = jnp.maximum(peak, got_peak)
    mine = jnp.exp2(peak - joint) * total
    theirs = jnp.exp2(got_peak - joint) * got_total
    whole = mine + theirs
    mixed = own_ref[...] * (mine / whole) + got_ref[:HD, :].astype(jnp.float32) * (theirs / whole)
    turned = mixed.T.astype(jnp.bfloat16)
    for head in range(QS):
        out_ref[:, pl.ds(head * HD, HD)] = turned[head * ROWS : (head + 1) * ROWS, :]


def body(hidden, norm_gain, q_weight, kv_weight, cache_store, location, stretch_ids, rec_pos):
    x = lax.axis_index("x")
    z = lax.axis_index("z")
    y = lax.axis_index("y")
    c = lax.axis_index("c")
    my_store = x * NZ + z
    my_tp = y * NC + c
    which_half = my_tp // KVH
    is_first = which_half == 0
    positions = rec_pos[0]
    own_list = stretch_ids[0]

    lists = lax.all_to_all(
        jnp.broadcast_to(stretch_ids[None], (NX * NZ, 1, MAXC)), STORE, 0, 0, tiled=True
    )[:, 0]

    weight = jnp.concatenate([q_weight[:, 0], kv_weight[:, 0]], axis=1)
    weight = lax.all_gather(weight, "x", axis=0)

    states = hidden[0]
    squares = lax.psum(jnp.sum(jnp.square(states.astype(jnp.float32)), axis=1), TP)
    gain = lax.dynamic_slice_in_dim(norm_gain, my_tp * 512, 512)
    gained = (states.astype(jnp.float32) * gain.astype(jnp.float32)).astype(jnp.bfloat16)
    blocks = gained.reshape(NY, 8, 2, NC, HD).transpose(2, 0, 3, 1, 4)
    blocks = jnp.broadcast_to(blocks[None], (4, 2, NY, NC, 8, HD)).reshape(NZ * NY * NC, 8, HD)
    blocks = lax.all_to_all(blocks, ("z", "y", "c"), 0, 0, tiled=True)
    blocks = blocks.reshape(NZ, NX, 4, 8, HD)
    blocks = lax.dynamic_index_in_dim(blocks, z // 2, 2, keepdims=False)
    blocks = blocks.transpose(0, 2, 1, 3).reshape(NZ, 8, NX * HD)
    tokens = lax.all_to_all(
        jnp.broadcast_to(blocks[None], (NY * NC, NZ, 8, NX * HD)), TP, 0, 0, tiled=True
    )
    tokens = tokens.reshape(NY, NC, NZ, 8, NX * HD).transpose(2, 0, 3, 1, 4)
    tokens = tokens.reshape(NZ * ROWS, NC * NX * HD)
    weight = weight.reshape(NX, NC, HD, COLS).transpose(1, 0, 2, 3).reshape(NC * NX * HD, COLS)
    partial = jnp.dot(tokens, weight, preferred_element_type=jnp.float32).astype(jnp.bfloat16)
    parts = lax.all_to_all(partial.reshape(NZ, ROWS, COLS), "z", 0, 0, tiled=True)

    row_ids = my_store * CH_DEV + jnp.arange(CH_DEV, dtype=jnp.int32)
    here = location[None, :] == row_ids[:, None]
    held = jnp.sum(jnp.where(here, jnp.arange(location.shape[0], dtype=jnp.int32), 0), axis=1)
    wanted = jnp.any(lists[:, :, None] == held[None, None, :], axis=1)
    send_rows = jnp.sum(jnp.where(wanted, jnp.arange(CH_DEV, dtype=jnp.int32)[None], 0), axis=1)
    outgoing = cache_store[:, 0][send_rows]
    arrived = lax.all_to_all(outgoing, STORE, 0, 0, tiled=True)

    inverse = lax.rsqrt(squares * (1.0 / D) + 1e-05)
    frequency = jnp.exp(
        -math.log(theta_base) * jnp.arange(HD // 2, dtype=jnp.float32) / (HD // 2)
    )
    angles = positions.astype(jnp.float32)[:, None] * frequency[None, :]
    cos = jnp.cos(angles)
    sin = jnp.sin(angles)
    cos = jnp.concatenate([cos, cos], axis=1)
    sin = jnp.concatenate([-sin, sin], axis=1)
    fresh_cos = jnp.where(is_first, cos, 1.0)
    fresh_sin = jnp.where(is_first, sin, 0.0)
    scale = math.log2(math.e) / math.sqrt(HD)
    inverse = jnp.broadcast_to(inverse[:, None], (ROWS, HD))

    own = call(
        finish_kernel, jax.ShapeDtypeStruct((QROWS + ROWS, HD), jnp.bfloat16), "finish"
    )(parts, inverse, cos * scale, sin * scale, fresh_cos, fresh_sin)
    other = exchange(own)

    table = jnp.arange(location.shape[0], dtype=jnp.int32)
    own_row = jnp.sum(jnp.where(own_list[:, None] == table[None, :], location[None, :], 0), axis=1)
    own_shard = own_row // CH_DEV
    count = jnp.sum((own_list >= 0).astype(jnp.int32)).reshape(1)
    order = jnp.arange(MAXC, dtype=jnp.int32)
    key_pos = (
        order[None, :] * STRETCH
        + which_half * HALF
        + jnp.arange(HALF, dtype=jnp.int32)[:, None]
    )
    replaced = jnp.any(key_pos[:, :, None] == positions[None, None, :], axis=2)
    eff = jnp.where(replaced | (order >= count[0])[None, :], far_away, key_pos)
    fresh_eff = jnp.where(positions % STRETCH // HALF == which_half, positions, far_away)
    fresh_eff = jnp.broadcast_to(fresh_eff[:, None], (ROWS, HD))
    pos_row = jnp.tile(positions, 2 * QS).reshape(1, 2 * QROWS)

    smem = pl.BlockSpec(memory_space=pltpu.SMEM)
    vmem = pl.BlockSpec(memory_space=pltpu.VMEM)
    own_part, stats, sent = pl.pallas_call(
        attend_kernel,
        out_shape=[
            jax.ShapeDtypeStruct((HD, QROWS), jnp.float32),
            jax.ShapeDtypeStruct((8, QROWS), jnp.float32),
            jax.ShapeDtypeStruct((HD + 16, QROWS), jnp.bfloat16),
        ],
        in_specs=[smem] * 3 + [vmem] * 6,
        out_specs=[vmem] * 3,
        scratch_shapes=[
            pltpu.VMEM((HD, 2 * QROWS), jnp.float32),
            pltpu.VMEM((8, 2 * QROWS), jnp.float32),
        ],
        name="attend",
        compiler_params=pltpu.CompilerParams(vmem_limit_bytes=32 * 1024 * 1024),
        cost_estimate=pl.CostEstimate(
            flops=4 * 2 * QROWS * MAXC * HALF * HD,
            bytes_accessed=MAXC * HALF * 2 * HD * 2,
            transcendentals=2 * QROWS * MAXC * HALF,
        ),
    )(count, own_shard, which_half.reshape(1), own, other, arrived, eff, fresh_eff, pos_row)
    got = exchange(sent)
    attended = call(merge_kernel, jax.ShapeDtypeStruct((ROWS, QW), jnp.bfloat16), "merge")(
        own_part, stats, got
    )
    return attended.reshape(1, ROWS, 1, QW)


def solution(mesh):
    fine = Mesh(mesh.devices.reshape(NX, NZ, NY, NC), ("x", "z", "y", "c"))
    in_specs = (
        P(STORE, None, TP),
        P(),
        P(STORE, TP, None),
        P(STORE, TP, None),
        P(STORE, TP, None, None),
        P(),
        P(STORE, None),
        P(STORE, None),
    )
    return jax.shard_map(
        body, mesh=fine, in_specs=in_specs, out_specs=P(STORE, None, TP, None), check_vma=False
    )
```

time: 321 us -> 192 us (0.60)
  the two profiles are of different devices: /device:TPU:16 before, /device:TPU:128 now
where the time goes in v1:
time: 192 us
  waiting for transfers between devices  83.4 us (43%)
  starting transfers between devices  45.6 us (24%)
  blocking collectives  24.7 us (13%)
  between operations  13.7 us (7%)
  local copies, waits for them, and re-layouts  8.52 us (4%)
  Pallas kernels  8.26 us (4%)
  other arithmetic  5.7 us (3%)
    psum x1, blocking collectives, body(): lax.psum(jnp.sum(jnp.square(states.astype(jnp.float32)), axis=1), TP)  24.7 us
    all_gather x1, waiting for transfers between devices, body(): weight = lax.all_gather(weight, 'x', axis=0)  16.2 us
    all_to_all x1, starting transfers between devices, body(): blocks = lax.all_to_all(blocks, ('z', 'y', 'c'), 0, 0, tiled=True)  15.8 us
    ppermute x2, waiting for transfers between devices, exchange(): lax.ppermute(block, 'y', [(i, (i + NY // 2) % NY) for i in range(NY)])  14.6 us
    all_to_all x1, waiting for transfers between devices, body(): lax.all_to_all(partial.reshape(NZ, ROWS, COLS), 'z', 0, 0, tiled=True)  14.5 us
    all_to_all x1, waiting for transfers between devices, body(): arrived = lax.all_to_all(outgoing, STORE, 0, 0, tiled=True)  12.9 us
    all_to_all x1, waiting for transfers between devices, body(): blocks = lax.all_to_all(blocks, ('z', 'y', 'c'), 0, 0, tiled=True)  11.7 us
    all_to_all x1, waiting for transfers between devices, body(): lax.all_to_all(jnp.broadcast_to(blocks[None], (NY * NC, NZ, 8, NX * HD)),...  8.95 us
  transfers between devices with their start and end apart: 8, of which 8 were waited for; matrix products, arithmetic and copies ran while one was open for 7% of the time, Pallas kernels for 0%

profile of v1, /device:TPU:128, one launch (start us, length us, event | category | flops | bytes accessed | tf_op | source)
XLA Modules:
  0.0 191.7 jit_solution(6254420134027856400)
XLA Ops:
  6.5 0.8 dynamic_slice.7
  7.4 0.9 fusion
  8.2 0.8 broadcast_in_dim.94
  9.0 15.8 %all-to-all-start = ((bf16[128,8,128]{2,1,0:T(8,128)(2,1)}), bf16[128,8,128]{2,1,0:T(8,128)(2,1)S(1)}, u32[]{:S(2)}, u32[]{:S(2)}) async-start(bf16[128,8,128]{2,1,0:T(8,128)(2,1)} %bitcast.6), calls=%async_computation | async-start | bytes 524288 | tf_op jit(solution)/shard_map/all_to_all | solution.py:197
  24.8 1.6 pad_maximum_fusion
  26.5 11.7 %all-to-all-done = bf16[128,8,128]{2,1,0:T(8,128)(2,1)S(1)} async-done(((bf16[128,8,128]{2,1,0:T(8,128)(2,1)}), bf16[128,8,128]{2,1,0:T(8,128)(2,1)S(1)}, u32[]{:S(2)}, u32[]{:S(2)}) %all-to-all-start) | async-done | bytes 262176 | tf_op jit(solution)/shard_map/all_to_all | solution.py:197
  38.2 1.1 broadcast_in_dim.96
  39.3 3.7 %all-to-all-start.1 = ((bf16[16,8,8,512]{3,2,1,0:T(8,128)(2,1)}), bf16[16,8,8,512]{3,2,1,0:T(8,128)(2,1)S(1)}, u32[]{:S(2)}, u32[]{:S(2)}) async-start(bf16[16,8,8,512]{3,2,1,0:T(8,128)(2,1)} %broadcast_in_dim.96), calls=%async_computation.1 | async-start | bytes 2097152 | tf_op jit(solution)/shard_map/all_to_all | solution.py:201
  42.9 16.2 %all-gather.3.cloned.1.call-done = bf16[1024,640]{1,0:T(8,128)(2,1)} async-done(((bf16[256,640]{1,0:T(8,128)(2,1)}), bf16[1024,640]{1,0:T(8,128)(2,1)}) %all-gather.3.cloned.1.call-update) | async-done | bytes 1310736 | tf_op jit(solution)/shard_map/all_gather | solution.py:189
  59.1 1.4 copy.25
  60.6 8.9 %all-to-all-done.1 = bf16[16,8,8,512]{3,2,1,0:T(8,128)(2,1)S(1)} async-done(((bf16[16,8,8,512]{3,2,1,0:T(8,128)(2,1)}), bf16[16,8,8,512]{3,2,1,0:T(8,128)(2,1)S(1)}, u32[]{:S(2)}, u32[]{:S(2)}) %all-to-all-start.1) | async-done | bytes 1048608 | tf_op jit(solution)/shard_map/all_to_all | solution.py:201
  69.5 0.6 broadcast_in_dim.100
  70.2 7.6 %all-to-all-start.3 = ((s32[32,1,32]{2,1,0:T(1,128)}), s32[32,1,32]{2,1,0:T(1,128)S(1)}, u32[]{:S(2)}, u32[]{:S(2)}) async-start(s32[32,1,32]{2,1,0:T(1,128)} %broadcast_in_dim.100), calls=%async_computation.3 | async-start | bytes 32768 | tf_op jit(solution)/shard_map/all_to_all | solution.py:184
  77.8 1.1 copy.24
  79.1 1.8 convolution_convert_fusion
  81.0 4.5 %all-to-all-done.3 = s32[32,1,32]{2,1,0:T(1,128)S(1)} async-done(((s32[32,1,32]{2,1,0:T(1,128)}), s32[32,1,32]{2,1,0:T(1,128)S(1)}, u32[]{:S(2)}, u32[]{:S(2)}) %all-to-all-start.3) | async-done | bytes 4128 | tf_op jit(solution)/shard_map/all_to_all | solution.py:184
  85.5 5.7 %all-to-all-start.2 = ((bf16[8,64,640]{2,1,0:T(8,128)(2,1)}), bf16[8,64,640]{2,1,0:T(8,128)(2,1)S(1)}, u32[]{:S(2)}, u32[]{:S(2)}) async-start(bf16[8,64,640]{2,1,0:T(8,128)(2,1)} %bitcast.18), calls=%async_computation.2 | async-start | bytes 1310720 | tf_op jit(solution)/shard_map/all_to_all | solution.py:208
  91.4 0.7 compare_reduce_fusion.1
  92.3 2.0 %gather_fusion = bf16[32,128,256]{2,1,0:T(8,128)(2,1)} fusion(bf16[8,128,256]{2,1,0:T(8,128)(2,1)S(1)} %bitcast.43, s32[1024]{0:T(1024)S(1)} %pad_clamp_fusion), kind=kCustom, calls=%fused_computation | custom fusion | bytes 4194432 | tf_op jit(solution)/shard_map/gather | solution.py:215
  94.3 14.5 %all-to-all-done.2.parts_ref = bf16[8,64,640]{2,1,0:T(8,128)(2,1)S(1)} async-done(((bf16[8,64,640]{2,1,0:T(8,128)(2,1)}), bf16[8,64,640]{2,1,0:T(8,128)(2,1)S(1)}, u32[]{:S(2)}, u32[]{:S(2)}) %all-to-all-start.2) | async-done | bytes 655392 | tf_op jit(solution)/shard_map/all_to_all | solution.py:208
  108.8 7.1 %all-to-all-start.4 = ((bf16[32,128,256]{2,1,0:T(8,128)(2,1)}), bf16[32,128,256]{2,1,0:T(8,128)(2,1)S(1)}, u32[]{:S(2)}, u32[]{:S(2)}) async-start(bf16[32,128,256]{2,1,0:T(8,128)(2,1)} %gather_fusion), calls=%async_computation.4 | async-start | bytes 4194304 | tf_op jit(solution)/shard_map/all_to_all | solution.py:216
  116.0 0.3 compare_reduce_fusion
  116.5 24.7 %psum.7 = f32[64]{0:T(128)S(1)} all-reduce(f32[64]{0:T(128)S(1)} %multiply_reduce_fusion), channel_id=1, replica_groups=mesh['x'=4,'z'=8,'y'=8,'c'=2] {'y','c'}, use_global_device_ids=true, to_apply=%region_3.4 | all-reduce | flops 64 | bytes 512 | tf_op jit(solution)/shard_map/psum | solution.py:192
  141.3 0.6 fusion.4
  141.9 0.6 iota_compare_fusion.1
  143.3 3.8 %collective-permute-start = (bf16[320,128]{1,0:T(8,128)(2,1)S(1)}, bf16[320,128]{1,0:T(8,128)(2,1)S(1)}, u32[]{:S(2)}, u32[]{:S(2)}) collective-permute-start(bf16[320,128]{1,0:T(8,128)(2,1)S(1)} %finish.1.own_ref), channel_id=1, source_target_pairs={{0,8},{2,10},{4,12},{6,14},{8,0},{10,2},{12,4},{14,6},{1,9},{3,11}... | collective-permute-start | bytes 245768 | tf_op jit(solution)/shard_map/ppermute | solution.py:34
  147.2 6.4 %collective-permute-done.other_ref = bf16[320,128]{1,0:T(8,128)(2,1)S(1)} collective-permute-done((bf16[320,128]{1,0:T(8,128)(2,1)S(1)}, bf16[320,128]{1,0:T(8,128)(2,1)S(1)}, u32[]{:S(2)}, u32[]{:S(2)}) %collective-permute-start) | collective-permute-done | bytes 81952 | tf_op jit(solution)/shard_map/ppermute | solution.py:34
  153.6 12.9 %all-to-all-done.4.kv_ref = bf16[32,128,256]{2,1,0:T(8,128)(2,1)S(1)} async-done(((bf16[32,128,256]{2,1,0:T(8,128)(2,1)}), bf16[32,128,256]{2,1,0:T(8,128)(2,1)S(1)}, u32[]{:S(2)}, u32[]{:S(2)}) %all-to-all-start.4) | async-done | bytes 2097184 | tf_op jit(solution)/shard_map/all_to_all | solution.py:216
  166.6 7.3 %attend.1 = (f32[128,256]{1,0:T(8,128)S(1)}, f32[8,256]{1,0:T(8,128)S(1)}, bf16[144,256]{1,0:T(8,128)(2,1)S(1)}) custom-call(s32[1]{0:T(128)} %bitcast.1.count_ref, s32[32]{0:T(128)S(1)} %and_select_fusion.2.shard_ref, s32[1]{0:T(128)} %bitcast.2.flag_ref, bf16[320,128]{1,0:T(8,128)(2,1)S(1)} %finish.1.own_ref, ...), custom_call_target="tpu_custom_call" | custom-call | flops 1073741824 | bytes 2097152 | tf_op jit(solution)/shard_map/attend/pallas_call | solution.py:255
  173.9 1.9 %collective-permute-start.1 = (bf16[144,256]{1,0:T(8,128)(2,1)S(1)}, bf16[144,256]{1,0:T(8,128)(2,1)S(1)}, u32[]{:S(2)}, u32[]{:S(2)}) collective-permute-start(bf16[144,256]{1,0:T(8,128)(2,1)S(1)} %get-tuple-element.10), channel_id=1, source_target_pairs={{0,8},{2,10},{4,12},{6,14},{8,0},{10,2},{12,4},{14,6},{1,9},{3,11}... | collective-permute-start | bytes 221192 | tf_op jit(solution)/shard_map/ppermute | solution.py:34
  175.8 8.2 %collective-permute-done.1.got_ref = bf16[144,256]{1,0:T(8,128)(2,1)S(1)} collective-permute-done((bf16[144,256]{1,0:T(8,128)(2,1)S(1)}, bf16[144,256]{1,0:T(8,128)(2,1)S(1)}, u32[]{:S(2)}, u32[]{:S(2)}) %collective-permute-start.1) | collective-permute-done | bytes 73760 | tf_op jit(solution)/shard_map/ppermute | solution.py:34
  184.1 0.8 merge.1
  (42 shorter events, 1.9 us)
Async XLA Ops:
  6.5 85.7 %copy-start = (bf16[8,1,128,256]{3,2,1,0:T(8,128)(2,1)S(1)}, bf16[8,1,128,256]{3,2,1,0:T(8,128)(2,1)}, u32[]{:S(2)}) copy-start(bf16[8,1,128,256]{3,2,1,0:T(8,128)(2,1)} %param.12) | copy-start | bytes 1572868
  6.5 18.3 %copy-start.1 = (bf16[256,1,512]{2,0,1:T(8,128)(2,1)S(1)}, bf16[256,1,512]{2,0,1:T(8,128)(2,1)}, u32[]{:S(2)}) copy-start(bf16[256,1,512]{2,0,1:T(8,128)(2,1)} %param.10) | copy-start | bytes 786436
  9.0 29.2 %all-to-all-start = ((bf16[128,8,128]{2,1,0:T(8,128)(2,1)}), bf16[128,8,128]{2,1,0:T(8,128)(2,1)S(1)}, u32[]{:S(2)}, u32[]{:S(2)}) async-start(bf16[128,8,128]{2,1,0:T(8,128)(2,1)} %bitcast.6), calls=%async_computation | async-start | bytes 524288 | tf_op jit(solution)/shard_map/all_to_all | solution.py:197
  24.8 34.4 %all-gather.3.cloned.1.call-start = ((), (), s32[]{:S(2)}) async-start(), calls=%async_computation.5 | async-start | bytes 1638400 | tf_op jit(solution)/shard_map/all_gather | solution.py:189
  39.3 30.3 %all-to-all-start.1 = ((bf16[16,8,8,512]{3,2,1,0:T(8,128)(2,1)}), bf16[16,8,8,512]{3,2,1,0:T(8,128)(2,1)S(1)}, u32[]{:S(2)}, u32[]{:S(2)}) async-start(bf16[16,8,8,512]{3,2,1,0:T(8,128)(2,1)} %broadcast_in_dim.96), calls=%async_computation.1 | async-start | bytes 2097152 | tf_op jit(solution)/shard_map/all_to_all | solution.py:201
  59.1 10.4 %copy-start.4 = (s32[1,32]{1,0:T(1,128)S(1)}, s32[1,32]{1,0:T(1,128)}, u32[]{:S(2)}) copy-start(s32[1,32]{1,0:T(1,128)} %param.14) | copy-start | bytes 388
  70.2 15.3 %all-to-all-start.3 = ((s32[32,1,32]{2,1,0:T(1,128)}), s32[32,1,32]{2,1,0:T(1,128)S(1)}, u32[]{:S(2)}, u32[]{:S(2)}) async-start(s32[32,1,32]{2,1,0:T(1,128)} %broadcast_in_dim.100), calls=%async_computation.3 | async-start | bytes 32768 | tf_op jit(solution)/shard_map/all_to_all | solution.py:184
  81.0 10.2 %copy-start.3 = (s32[256]{0:T(256)S(1)}, s32[256]{0:T(256)}, u32[]{:S(2)}) copy-start(s32[256]{0:T(256)} %param.13) | copy-start | bytes 3076
  85.5 23.3 %all-to-all-start.2 = ((bf16[8,64,640]{2,1,0:T(8,128)(2,1)}), bf16[8,64,640]{2,1,0:T(8,128)(2,1)S(1)}, u32[]{:S(2)}, u32[]{:S(2)}) async-start(bf16[8,64,640]{2,1,0:T(8,128)(2,1)} %bitcast.18), calls=%async_computation.2 | async-start | bytes 1310720 | tf_op jit(solution)/shard_map/all_to_all | solution.py:208
  94.3 21.7 %copy-start.5 = (s32[1,64]{1,0:T(1,128)S(1)}, s32[1,64]{1,0:T(1,128)}, u32[]{:S(2)}) copy-start(s32[1,64]{1,0:T(1,128)} %param.15) | copy-start | bytes 772
  94.3 22.1 %copy-start.2 = (bf16[1,64,512]{2,1,0:T(8,128)(2,1)S(1)}, bf16[1,64,512]{2,1,0:T(8,128)(2,1)}, u32[]{:S(2)}) copy-start(bf16[1,64,512]{2,1,0:T(8,128)(2,1)} %param.8) | copy-start | bytes 196612
  108.8 57.7 %all-to-all-start.4 = ((bf16[32,128,256]{2,1,0:T(8,128)(2,1)}), bf16[32,128,256]{2,1,0:T(8,128)(2,1)S(1)}, u32[]{:S(2)}, u32[]{:S(2)}) async-start(bf16[32,128,256]{2,1,0:T(8,128)(2,1)} %gather_fusion), calls=%async_computation.4 | async-start | bytes 4194304 | tf_op jit(solution)/shard_map/all_to_all | solution.py:216
  143.3 10.2 %collective-permute-start = (bf16[320,128]{1,0:T(8,128)(2,1)S(1)}, bf16[320,128]{1,0:T(8,128)(2,1)S(1)}, u32[]{:S(2)}, u32[]{:S(2)}) collective-permute-start(bf16[320,128]{1,0:T(8,128)(2,1)S(1)} %finish.1.own_ref), channel_id=1, source_target_pairs={{0,8},{2,10},{4,12},{6,14},{8,0},{10,2},{12,4},{14,6},{1,9},{3,11}... | collective-permute-start | bytes 245768 | tf_op jit(solution)/shard_map/ppermute | solution.py:34
  173.9 10.2 %collective-permute-start.1 = (bf16[144,256]{1,0:T(8,128)(2,1)S(1)}, bf16[144,256]{1,0:T(8,128)(2,1)S(1)}, u32[]{:S(2)}, u32[]{:S(2)}) collective-permute-start(bf16[144,256]{1,0:T(8,128)(2,1)S(1)} %get-tuple-element.10), channel_id=1, source_target_pairs={{0,8},{2,10},{4,12},{6,14},{8,0},{10,2},{12,4},{14,6},{1,9},{3,11}... | collective-permute-start | bytes 221192 | tf_op jit(solution)/shard_map/ppermute | solution.py:34
Sparse Core Ops, SparseCore 0:
  27.7 31.3 all-gather.2

commit v2 on v1

v2 whole, which is shorter than its diff:
```python
import math

import jax
import jax.numpy as jnp
from jax import lax
from jax.experimental import pallas as pl
from jax.experimental.pallas import tpu as pltpu
from jax.sharding import Mesh
from jax.sharding import PartitionSpec as P

NX, NZ, NY, NC = 4, 8, 8, 2
KVH = 8
HD = 128
STRETCH = 256
MAXC = 32
CH_DEV = 8
QS = 4
HALF = 128
ROWS = 64
D = 8192
QW = QS * HD
COLS = QW + HD
QROWS = QS * ROWS

theta_base = 500000.0
neg_large = -1e30
far_away = 1 << 29

STORE = ("x", "z")
TP = ("y", "c")


def exchange(block):
    return lax.ppermute(block, "y", [(i, (i + NY // 2) % NY) for i in range(NY)])


def shifted(block, axis, count, by):
    return lax.ppermute(block, axis, [(i, (i + by) % count) for i in range(count)])


def call(kernel, outs, name, flops=0, bytes_accessed=0):
    return pl.pallas_call(
        kernel,
        out_shape=outs,
        name=name,
        compiler_params=pltpu.CompilerParams(vmem_limit_bytes=32 * 1024 * 1024),
        cost_estimate=pl.CostEstimate(
            flops=flops, bytes_accessed=bytes_accessed, transcendentals=0
        ),
    )


def project_kernel(tokens_ref, weight_ref, out_ref):
    rows = []
    stats = []
    for request in range(NZ):
        wide = jnp.concatenate(
            [
                jnp.concatenate(
                    [tokens_ref[y * NC + c, request].astype(jnp.float32) for c in range(NC)],
                    axis=1,
                )
                for y in range(NY)
            ],
            axis=0,
        )
        rows.append(wide.astype(jnp.bfloat16))
        squares = jnp.zeros((ROWS, HD), jnp.float32)
        for at in range(0, wide.shape[1], HD):
            piece = wide[:, at : at + HD]
            squares += piece * piece
        squares = jnp.concatenate([squares, jnp.zeros_like(squares)], axis=0)
        row = jnp.sum(squares.T, axis=0, keepdims=True)
        high = row.astype(jnp.bfloat16).astype(jnp.float32)
        stat = jnp.concatenate([high, row - high, jnp.zeros((6, HD), jnp.float32)], axis=0)
        stats.append(jnp.concatenate([stat, jnp.zeros((8, QW), jnp.float32)], axis=1))
    total = jnp.dot(
        jnp.concatenate(rows, axis=0), weight_ref[...], preferred_element_type=jnp.float32
    )
    for request in range(NZ):
        block = jnp.concatenate([total[request * ROWS : (request + 1) * ROWS], stats[request]], axis=0)
        out_ref[request] = block.astype(jnp.bfloat16)


def finish_kernel(parts_ref, cos_ref, sin_ref, fcos_ref, fsin_ref, out_ref):
    inverse = None
    for group in range(QS + 1):
        lanes = pl.ds(group * HD, HD)
        total = parts_ref[0, :, lanes].astype(jnp.float32)
        for part in range(1, NZ):
            total += parts_ref[part, :, lanes].astype(jnp.float32)
        if inverse is None:
            squares = total[ROWS : ROWS + 1, :] + total[ROWS + 1 : ROWS + 2, :]
            inverse = lax.rsqrt(squares * (1.0 / D) + 1e-05)
            inverse = jnp.broadcast_to(inverse, (HD, HD)).T[:ROWS]
        total = total[:ROWS] * inverse
        cos = cos_ref[...] if group < QS else fcos_ref[...]
        sin = sin_ref[...] if group < QS else fsin_ref[...]
        turned = total * cos + pltpu.roll(total, HD // 2, 1) * sin
        out_ref[pl.ds(group * ROWS, ROWS), :] = turned.astype(jnp.bfloat16)


def pick_kernel(rows_ref, *refs):
    stores, outs, sem = refs[:NX], refs[NX : NX + NZ], refs[NX + NZ]
    copies = []
    for step in range(NZ):
        for k in range(NX):
            copies.append(
                pltpu.make_async_copy(
                    stores[k].at[rows_ref[step * NX + k]],
                    outs[step].at[k],
                    sem.at[step * NX + k],
                )
            )
            copies[-1].start()
    for copy in copies:
        copy.wait()


def attend_kernel(flag_ref, own_ref, other_ref, eff_ref, fresh_eff_ref, pos_ref, *refs):
    kv_refs, (own_out_ref, stat_ref, sent_ref, acc_ref, run_ref) = refs[:NZ], refs[NZ:]
    is_first = flag_ref[0] == 0
    queries = jnp.concatenate([own_ref[:QROWS, :], other_ref[:QROWS, :]], axis=0)
    own_piece = own_ref[QROWS:, :]
    other_piece = other_ref[QROWS:, :]
    first = jnp.broadcast_to(is_first, own_piece.shape)
    fresh_keys = jnp.where(first, own_piece, other_piece)
    fresh_values = jnp.where(first, other_piece, own_piece)
    pos = pos_ref[...]
    nt = (((1,), (1,)), ((), ()))
    tn = (((0,), (0,)), ((), ()))

    scores = lax.dot_general(fresh_keys, queries, nt, preferred_element_type=jnp.float32)
    scores = jnp.where(fresh_eff_ref[:, 0:1] <= pos, scores, neg_large)
    peak = jnp.max(scores, axis=0, keepdims=True)
    weights = jnp.exp2(scores - peak)
    run_ref[0:1, :] = peak
    run_ref[1:2, :] = jnp.sum(weights, axis=0, keepdims=True)
    acc_ref[...] = lax.dot_general(
        fresh_values, weights.astype(jnp.bfloat16), tn, preferred_element_type=jnp.float32
    )

    for step in range(NZ):
        kv_ref = kv_refs[step]
        pieces = []
        for k in range(NX):
            slot = step * NX + k
            piece = lax.dot_general(
                kv_ref[k, :, :HD], queries, nt, preferred_element_type=jnp.float32
            )
            pieces.append(jnp.where(eff_ref[:, slot : slot + 1] <= pos, piece, neg_large))
        old_peak = run_ref[0:1, :]
        new_peak = old_peak
        for piece in pieces:
            new_peak = jnp.maximum(new_peak, jnp.max(piece, axis=0, keepdims=True))
        factor = jnp.exp2(old_peak - new_peak)
        total = run_ref[1:2, :] * factor
        acc = acc_ref[...] * factor
        for k, piece in enumerate(pieces):
            weights = jnp.exp2(piece - new_peak)
            total += jnp.sum(weights, axis=0, keepdims=True)
            acc += lax.dot_general(
                kv_ref[k, :, HD:],
                weights.astype(jnp.bfloat16),
                tn,
                preferred_element_type=jnp.float32,
            )
        run_ref[0:1, :] = new_peak
        run_ref[1:2, :] = total
        acc_ref[...] = acc

    peak = run_ref[0:1, :]
    total = run_ref[1:2, :]
    mixed = acc_ref[...] / total
    own_out_ref[...] = mixed[:, :QROWS]
    stat_ref[0:1, :] = peak[:, :QROWS]
    stat_ref[1:2, :] = total[:, :QROWS]
    stat_ref[2:8, :] = jnp.zeros((6, QROWS), jnp.float32)
    peak = peak[:, QROWS:]
    total = total[:, QROWS:]
    peak_high = peak.astype(jnp.bfloat16).astype(jnp.float32)
    total_high = total.astype(jnp.bfloat16).astype(jnp.float32)
    stats = jnp.concatenate(
        [
            peak_high,
            peak - peak_high,
            total_high,
            total - total_high,
            jnp.zeros((12, QROWS), jnp.float32),
        ],
        axis=0,
    )
    sent_ref[:HD, :] = mixed[:, QROWS:].astype(jnp.bfloat16)
    sent_ref[HD:, :] = stats.astype(jnp.bfloat16)


def merge_kernel(own_ref, stat_ref, got_ref, out_ref):
    stats = got_ref[HD:, :].astype(jnp.float32)
    got_peak = stats[0:1, :] + stats[1:2, :]
    got_total = stats[2:3, :] + stats[3:4, :]
    peak = stat_ref[0:1, :]
    total = stat_ref[1:2, :]
    joint = jnp.maximum(peak, got_peak)
    mine = jnp.exp2(peak - joint) * total
    theirs = jnp.exp2(got_peak - joint) * got_total
    whole = mine + theirs
    mixed = own_ref[...] * (mine / whole) + got_ref[:HD, :].astype(jnp.float32) * (theirs / whole)
    turned = mixed.T.astype(jnp.bfloat16)
    for head in range(QS):
        out_ref[:, pl.ds(head * HD, HD)] = turned[head * ROWS : (head + 1) * ROWS, :]


def body(hidden, norm_gain, q_weight, kv_weight, cache_store, location, stretch_ids, rec_pos):
    x = lax.axis_index("x")
    z = lax.axis_index("z")
    y = lax.axis_index("y")
    c = lax.axis_index("c")
    my_tp = y * NC + c
    which_half = my_tp // KVH
    is_first = which_half == 0
    positions = rec_pos[0]
    own_list = stretch_ids[0]
    int_rows = jnp.arange(CH_DEV, dtype=jnp.int32)
    table = jnp.arange(location.shape[0], dtype=jnp.int32)

    blocks = hidden[0].reshape(NY, 8, 2, NC, HD).transpose(2, 0, 3, 1, 4)
    listed = jnp.pad(own_list.astype(jnp.bfloat16), (0, HD - MAXC))
    pair = jnp.arange(4, dtype=jnp.int32).reshape(4, 1, 1, 1, 1, 1)
    blocks = jnp.where(pair == my_tp % 4, blocks[None], listed)
    blocks = blocks.reshape(NZ * NY * NC, 8, HD)
    blocks = lax.all_to_all(blocks, ("z", "y", "c"), 0, 0, tiled=True)
    blocks = blocks.reshape(NZ, NX, 4, 8, HD)
    lists = lax.dynamic_index_in_dim(blocks[:, 0, :, 0, :MAXC], (z // 2 + 1) % 4, 1, keepdims=False)
    lists = lists.astype(jnp.int32)
    blocks = lax.dynamic_index_in_dim(blocks, z // 2, 2, keepdims=False)
    blocks = blocks.transpose(0, 2, 1, 3).reshape(NZ, 8, NX * HD)
    tokens = lax.all_to_all(
        jnp.broadcast_to(blocks[None], (NY * NC, NZ, 8, NX * HD)), TP, 0, 0, tiled=True
    )

    weight = jnp.concatenate([q_weight[:, 0], kv_weight[:, 0]], axis=1)
    weight = lax.all_gather(weight, "x", axis=0)
    gain = lax.dynamic_index_in_dim(norm_gain.reshape(NX, NZ, NC, HD), z, 1, keepdims=False)
    weight = weight.reshape(NX, NC, HD, COLS).transpose(1, 0, 2, 3).astype(jnp.float32)
    weight = weight * gain.transpose(1, 0, 2)[..., None].astype(jnp.float32)
    weight = weight.astype(jnp.bfloat16).reshape(NC * NX * HD, COLS)

    store = cache_store[:, 0]
    stores = [store] + [shifted(store, "x", NX, k) for k in range(1, NX)]
    from_x = (x - jnp.arange(NX, dtype=jnp.int32)) % NX
    row_ids = (from_x[:, None] * NZ + z) * CH_DEV + int_rows[None, :]
    here = location[None, None, :] == row_ids[:, :, None]
    held = jnp.sum(jnp.where(here, table, 0), axis=2)
    wanted = jnp.any(lists[:, :, None, None] == held[None, None], axis=1)
    send_rows = jnp.sum(jnp.where(wanted, int_rows, 0), axis=2)
    steps = jnp.arange(NZ, dtype=jnp.int32)
    ahead = (z + steps) % NZ
    turn = ahead[:, None] == steps[None, :]
    send_rows = jnp.sum(jnp.where(turn[:, :, None], send_rows[None], 0), axis=1)
    smem = pl.BlockSpec(memory_space=pltpu.SMEM)
    vmem = pl.BlockSpec(memory_space=pltpu.VMEM)
    hbm = pl.BlockSpec(memory_space=pl.ANY)
    outgoing = pl.pallas_call(
        pick_kernel,
        out_shape=[jax.ShapeDtypeStruct((NX, HALF, 2 * HD), jnp.bfloat16)] * NZ,
        in_specs=[smem] + [hbm] * NX,
        out_specs=[hbm] * NZ,
        scratch_shapes=[pltpu.SemaphoreType.DMA((NZ * NX,))],
        name="pick",
        cost_estimate=pl.CostEstimate(flops=0, bytes_accessed=1 << 22, transcendentals=0),
    )(send_rows.reshape(-1), *stores)
    weight, outgoing = lax.optimization_barrier((weight, outgoing))
    partial = call(
        project_kernel,
        jax.ShapeDtypeStruct((NZ, ROWS + 8, COLS), jnp.bfloat16),
        "project",
        flops=2 * NZ * ROWS * 1024 * COLS,
        bytes_accessed=1 << 22,
    )(tokens, weight)
    late = [1, 2, 3]
    partial, *held_back = lax.optimization_barrier((partial, *[outgoing[k] for k in late]))
    outgoing = list(outgoing)
    for k, block in zip(late, held_back):
        outgoing[k] = block
    parts = lax.all_to_all(partial, "z", 0, 0, tiled=True)

    arrived = [outgoing[0]] + [shifted(outgoing[k], "z", NZ, k) for k in range(1, NZ)]

    frequency = jnp.exp(
        -math.log(theta_base) * jnp.arange(HD // 2, dtype=jnp.float32) / (HD // 2)
    )
    angles = positions.astype(jnp.float32)[:, None] * frequency[None, :]
    cos = jnp.cos(angles)
    sin = jnp.sin(angles)
    cos = jnp.concatenate([cos, cos], axis=1)
    sin = jnp.concatenate([-sin, sin], axis=1)
    fresh_cos = jnp.where(is_first, cos, 1.0)
    fresh_sin = jnp.where(is_first, sin, 0.0)
    scale = math.log2(math.e) / math.sqrt(HD)

    own = call(
        finish_kernel, jax.ShapeDtypeStruct((QROWS + ROWS, HD), jnp.bfloat16), "finish"
    )(parts, cos * scale, sin * scale, fresh_cos, fresh_sin)
    other = exchange(own)

    own_row = jnp.sum(jnp.where(own_list[:, None] == table[None, :], location[None, :], 0), axis=1)
    own_shard = own_row // CH_DEV
    slot_shard = (from_x[None, :] * NZ + ((z - steps) % NZ)[:, None]).reshape(-1)
    match = (own_shard[None, :] == slot_shard[:, None]) & (own_list >= 0)[None, :]
    slot_order = jnp.sum(jnp.where(match, jnp.arange(MAXC, dtype=jnp.int32), 0), axis=1)
    slot_live = jnp.any(match, axis=1)
    key_pos = (
        slot_order[None, :] * STRETCH
        + which_half * HALF
        + jnp.arange(HALF, dtype=jnp.int32)[:, None]
    )
    replaced = jnp.any(key_pos[:, :, None] == positions[None, None, :], axis=2)
    eff = jnp.where(replaced | ~slot_live[None, :], far_away, key_pos)
    fresh_eff = jnp.where(positions % STRETCH // HALF == which_half, positions, far_away)
    fresh_eff = jnp.broadcast_to(fresh_eff[:, None], (ROWS, HD))
    pos_row = jnp.tile(positions, 2 * QS).reshape(1, 2 * QROWS)

    own_part, stats, sent = pl.pallas_call(
        attend_kernel,
        out_shape=[
            jax.ShapeDtypeStruct((HD, QROWS), jnp.float32),
            jax.ShapeDtypeStruct((8, QROWS), jnp.float32),
            jax.ShapeDtypeStruct((HD + 16, QROWS), jnp.bfloat16),
        ],
        in_specs=[smem] + [vmem] * (5 + NZ),
        out_specs=[vmem] * 3,
        scratch_shapes=[
            pltpu.VMEM((HD, 2 * QROWS), jnp.float32),
            pltpu.VMEM((8, 2 * QROWS), jnp.float32),
        ],
        name="attend",
        compiler_params=pltpu.CompilerParams(vmem_limit_bytes=32 * 1024 * 1024),
        cost_estimate=pl.CostEstimate(
            flops=4 * 2 * QROWS * MAXC * HALF * HD,
            bytes_accessed=MAXC * HALF * 2 * HD * 2,
            transcendentals=2 * QROWS * MAXC * HALF,
        ),
    )(which_half.reshape(1), own, other, eff, fresh_eff, pos_row, *arrived)
    got = exchange(sent)
    attended = call(merge_kernel, jax.ShapeDtypeStruct((ROWS, QW), jnp.bfloat16), "merge")(
        own_part, stats, got
    )
    return attended.reshape(1, ROWS, 1, QW)


def solution(mesh):
    fine = Mesh(mesh.devices.reshape(NX, NZ, NY, NC), ("x", "z", "y", "c"))
    in_specs = (
        P(STORE, None, TP),
        P(),
        P(STORE, TP, None),
        P(STORE, TP, None),
        P(STORE, TP, None, None),
        P(),
        P(STORE, None),
        P(STORE, None),
    )
    return jax.shard_map(
        body, mesh=fine, in_specs=in_specs, out_specs=P(STORE, None, TP, None), check_vma=False
    )
```

time: 192 us -> 227 us (1.18)
  the two profiles are of different devices: /device:TPU:128 before, /device:TPU:16 now
where the time goes in v2:
time: 227 us
  starting transfers between devices  87.7 us (39%)
  Pallas kernels  73.4 us (32%)
  waiting for transfers between devices  38.2 us (17%)
  between operations  13.8 us (6%)
  other arithmetic  9.2 us (4%)
  local copies, waits for them, and re-layouts  4.29 us (2%)
    pallas_call x1, Pallas kernels, body(): pl.pallas_call(pick_kernel, out_shape=[jax.ShapeDtypeStruct((NX, HALF, 2...  65.6 us
    ppermute x10, starting transfers between devices, shifted(): lax.ppermute(block, axis, [(i, (i + by) % count) for i in range(count)])  50.3 us
    ppermute x10, waiting for transfers between devices, shifted(): lax.ppermute(block, axis, [(i, (i + by) % count) for i in range(count)])  21.7 us
    all_to_all x1, starting transfers between devices, body(): blocks = lax.all_to_all(blocks, ('z', 'y', 'c'), 0, 0, tiled=True)  17.3 us
    all_to_all x1, waiting for transfers between devices, body(): blocks = lax.all_to_all(blocks, ('z', 'y', 'c'), 0, 0, tiled=True)  11.2 us
    ppermute x2, starting transfers between devices, exchange(): lax.ppermute(block, 'y', [(i, (i + NY // 2) % NY) for i in range(NY)])  11.1 us
    all_to_all x1, starting transfers between devices, body(): lax.all_to_all(jnp.broadcast_to(blocks[None], (NY * NC, NZ, 8, NX * HD)),...  5.29 us
    ppermute x2, waiting for transfers between devices, exchange(): lax.ppermute(block, 'y', [(i, (i + NY // 2) % NY) for i in range(NY)])  5.28 us
  transfers between devices with their start and end apart: 16, of which 7 were waited for; matrix products, arithmetic and copies ran while one was open for 5% of the time, Pallas kernels for 29%

profile of v2, /device:TPU:16, one launch (start us, length us, event | category | flops | bytes accessed | tf_op | source)
XLA Modules:
  0.0 226.6 jit_solution(14051615834054885878)
XLA Ops:
  6.5 3.5 %collective-permute-start = (bf16[8,128,256]{2,1,0:T(8,128)(2,1)}, bf16[8,128,256]{2,1,0:T(8,128)(2,1)S(1)}, u32[]{:S(2)}, u32[]{:S(2)}) collective-permute-start(bf16[8,128,256]{2,1,0:T(8,128)(2,1)} %bitcast.42), channel_id=1, source_target_pairs={{0,128},{128,256},{256,384},{384,0},{1,129},{129,257},{257,385},{3... | collective-permute-start | bytes 1572872 | tf_op jit(solution)/shard_map/ppermute | solution.py:38
  10.1 4.6 %collective-permute-start.1 = (bf16[8,128,256]{2,1,0:T(8,128)(2,1)}, bf16[8,128,256]{2,1,0:T(8,128)(2,1)S(1)}, u32[]{:S(2)}, u32[]{:S(2)}) collective-permute-start(bf16[8,128,256]{2,1,0:T(8,128)(2,1)} %bitcast.43), channel_id=1, source_target_pairs={{0,256},{128,384},{256,0},{384,128},{1,257},{129,385},{257,1},{385... | collective-permute-start | bytes 1572872 | tf_op jit(solution)/shard_map/ppermute | solution.py:38
  14.7 3.3 %collective-permute-start.2 = (bf16[8,128,256]{2,1,0:T(8,128)(2,1)}, bf16[8,128,256]{2,1,0:T(8,128)(2,1)S(1)}, u32[]{:S(2)}, u32[]{:S(2)}) collective-permute-start(bf16[8,128,256]{2,1,0:T(8,128)(2,1)} %bitcast.44), channel_id=1, source_target_pairs={{0,384},{128,0},{256,128},{384,256},{1,385},{129,1},{257,129},{385... | collective-permute-start | bytes 1572872 | tf_op jit(solution)/shard_map/ppermute | solution.py:38
  19.0 1.7 bitcast_select_fusion
  20.7 17.3 %all-to-all-start = ((bf16[128,8,128]{2,1,0:T(8,128)(2,1)}), bf16[128,8,128]{2,1,0:T(8,128)(2,1)S(1)}, u32[]{:S(2)}, u32[]{:S(2)}) async-start(bf16[128,8,128]{2,1,0:T(8,128)(2,1)} %bitcast_select_fusion), calls=%async_computation | async-start | bytes 524288 | tf_op jit(solution)/shard_map/all_to_all | solution.py:231
  38.0 1.7 pad_maximum_fusion
  40.7 11.2 %all-to-all-done = bf16[128,8,128]{2,1,0:T(8,128)(2,1)S(1)} async-done(((bf16[128,8,128]{2,1,0:T(8,128)(2,1)}), bf16[128,8,128]{2,1,0:T(8,128)(2,1)S(1)}, u32[]{:S(2)}, u32[]{:S(2)}) %all-to-all-start) | async-done | bytes 262176 | tf_op jit(solution)/shard_map/all_to_all | solution.py:231
  51.9 1.1 broadcast_in_dim.141
  53.0 5.3 %all-to-all-start.1 = ((bf16[16,8,8,512]{3,2,1,0:T(8,128)(2,1)}), bf16[16,8,8,512]{3,2,1,0:T(8,128)(2,1)S(1)}, u32[]{:S(2)}, u32[]{:S(2)}) async-start(bf16[16,8,8,512]{3,2,1,0:T(8,128)(2,1)} %broadcast_in_dim.141), calls=%async_computation.1 | async-start | bytes 2097152 | tf_op jit(solution)/shard_map/all_to_all | solution.py:237
  61.0 0.8 copy-done.1
  61.9 0.8 copy-done.3
  62.7 65.6 %pick.1 = (bf16[4,128,256]{2,1,0:T(8,128)(2,1)}, bf16[4,128,256]{2,1,0:T(8,128)(2,1)}, bf16[4,128,256]{2,1,0:T(8,128)(2,1)}, bf16[4,128,256]{2,1,0:T(8,128)(2,1)...) custom-call(s32[32]{0:T(128)} %reshape.274.rows_ref, ...), custom_call_target="tpu_custom_call" | custom-call | bytes 4194304 | tf_op jit(solution)/shard_map/pick/pallas_call | solution.py:263
  128.4 1.6 fusion
  130.0 1.9 project.1
  131.9 3.7 %all-to-all-start.2 = ((bf16[8,72,640]{2,1,0:T(8,128)(2,1)}), bf16[8,72,640]{2,1,0:T(8,128)(2,1)S(1)}, u32[]{:S(2)}, u32[]{:S(2)}) async-start(bf16[8,72,640]{2,1,0:T(8,128)(2,1)} %project.1), calls=%async_computation.2 | async-start | bytes 1474560 | tf_op jit(solution)/shard_map/all_to_all | solution.py:285
  136.2 5.1 %collective-permute-start.10 = (bf16[4,128,256]{2,1,0:T(8,128)(2,1)S(1)}, bf16[4,128,256]{2,1,0:T(8,128)(2,1)S(1)}, u32[]{:S(2)}, u32[]{:S(2)}) collective-permute-start(bf16[4,128,256]{2,1,0:T(8,128)(2,1)S(1)} %copy-done.9), channel_id=1, source_target_pairs={{0,112},{16,0},{32,16},{48,32},{64,48},{80,64},{96,80},{112,96},{1... | collective-permute-start | bytes 786440 | tf_op jit(solution)/shard_map/ppermute | solution.py:38
  141.3 5.1 %collective-permute-start.7 = (bf16[4,128,256]{2,1,0:T(8,128)(2,1)S(1)}, bf16[4,128,256]{2,1,0:T(8,128)(2,1)S(1)}, u32[]{:S(2)}, u32[]{:S(2)}) collective-permute-start(bf16[4,128,256]{2,1,0:T(8,128)(2,1)S(1)} %copy-done.8), channel_id=1, source_target_pairs={{0,64},{16,80},{32,96},{48,112},{64,0},{80,16},{96,32},{112,48},{1... | collective-permute-start | bytes 786440 | tf_op jit(solution)/shard_map/ppermute | solution.py:38
  146.8 2.0 collective-permute-start.8
  148.8 6.0 %collective-permute-start.9 = (bf16[4,128,256]{2,1,0:T(8,128)(2,1)}, bf16[4,128,256]{2,1,0:T(8,128)(2,1)S(1)}, u32[]{:S(2)}, u32[]{:S(2)}) collective-permute-start(bf16[4,128,256]{2,1,0:T(8,128)(2,1)} %get-tuple-element.48), channel_id=1, source_target_pairs={{0,96},{16,112},{32,0},{48,16},{64,32},{80,48},{96,64},{112,80},{1... | collective-permute-start | bytes 786440 | tf_op jit(solution)/shard_map/ppermute | solution.py:38
  154.8 2.5 %collective-permute-start.4 = (bf16[4,128,256]{2,1,0:T(8,128)(2,1)}, bf16[4,128,256]{2,1,0:T(8,128)(2,1)S(1)}, u32[]{:S(2)}, u32[]{:S(2)}) collective-permute-start(bf16[4,128,256]{2,1,0:T(8,128)(2,1)} %get-tuple-element.43), channel_id=1, source_target_pairs={{0,16},{16,32},{32,48},{48,64},{64,80},{80,96},{96,112},{112,0},{1... | collective-permute-start | bytes 786440 | tf_op jit(solution)/shard_map/ppermute | solution.py:38
  157.3 4.4 %collective-permute-done.10.refs_7_ = bf16[4,128,256]{2,1,0:T(8,128)(2,1)S(1)} collective-permute-done((bf16[4,128,256]{2,1,0:T(8,128)(2,1)S(1)}, bf16[4,128,256]{2,1,0:T(8,128)(2,1)S(1)}, u32[]{:S(2)}, u32[]{:S(2)}) %collective-permute-start.10) | collective-permute-done | bytes 262176 | tf_op jit(solution)/shard_map/ppermute | solution.py:38
  161.7 3.2 %collective-permute-start.5 = (bf16[4,128,256]{2,1,0:T(8,128)(2,1)}, bf16[4,128,256]{2,1,0:T(8,128)(2,1)S(1)}, u32[]{:S(2)}, u32[]{:S(2)}) collective-permute-start(bf16[4,128,256]{2,1,0:T(8,128)(2,1)} %get-tuple-element.44), channel_id=1, source_target_pairs={{0,32},{16,48},{32,64},{48,80},{64,96},{80,112},{96,0},{112,16},{1... | collective-permute-start | bytes 786440 | tf_op jit(solution)/shard_map/ppermute | solution.py:38
  164.9 4.7 %collective-permute-done.7.refs_4_ = bf16[4,128,256]{2,1,0:T(8,128)(2,1)S(1)} collective-permute-done((bf16[4,128,256]{2,1,0:T(8,128)(2,1)S(1)}, bf16[4,128,256]{2,1,0:T(8,128)(2,1)S(1)}, u32[]{:S(2)}, u32[]{:S(2)}) %collective-permute-start.7) | collective-permute-done | bytes 262176 | tf_op jit(solution)/shard_map/ppermute | solution.py:38
  169.6 14.9 %collective-permute-start.6 = (bf16[4,128,256]{2,1,0:T(8,128)(2,1)S(1)}, bf16[4,128,256]{2,1,0:T(8,128)(2,1)S(1)}, u32[]{:S(2)}, u32[]{:S(2)}) collective-permute-start(bf16[4,128,256]{2,1,0:T(8,128)(2,1)S(1)} %copy-done.7), channel_id=1, source_target_pairs={{0,48},{16,64},{32,80},{48,96},{64,112},{80,0},{96,16},{112,32},{1... | collective-permute-start | bytes 786440 | tf_op jit(solution)/shard_map/ppermute | solution.py:38
  184.9 3.9 %collective-permute-done.8.refs_5_ = bf16[4,128,256]{2,1,0:T(8,128)(2,1)S(1)} collective-permute-done((bf16[4,128,256]{2,1,0:T(8,128)(2,1)}, bf16[4,128,256]{2,1,0:T(8,128)(2,1)S(1)}, u32[]{:S(2)}, u32[]{:S(2)}) %collective-permute-start.8) | collective-permute-done | bytes 262176 | tf_op jit(solution)/shard_map/ppermute | solution.py:38
  188.8 5.5 %collective-permute-start.3 = (bf16[320,128]{1,0:T(8,128)(2,1)S(1)}, bf16[320,128]{1,0:T(8,128)(2,1)S(1)}, u32[]{:S(2)}, u32[]{:S(2)}) collective-permute-start(bf16[320,128]{1,0:T(8,128)(2,1)S(1)} %finish.1.own_ref), channel_id=1, source_target_pairs={{0,8},{2,10},{4,12},{6,14},{8,0},{10,2},{12,4},{14,6},{1,9},{3,11}... | collective-permute-start | bytes 245768 | tf_op jit(solution)/shard_map/ppermute | solution.py:34
  194.4 5.7 %collective-permute-done.9.refs_6_ = bf16[4,128,256]{2,1,0:T(8,128)(2,1)S(1)} collective-permute-done((bf16[4,128,256]{2,1,0:T(8,128)(2,1)}, bf16[4,128,256]{2,1,0:T(8,128)(2,1)S(1)}, u32[]{:S(2)}, u32[]{:S(2)}) %collective-permute-start.9) | collective-permute-done | bytes 262176 | tf_op jit(solution)/shard_map/ppermute | solution.py:38
  200.1 3.0 %collective-permute-done.6.refs_3_ = bf16[4,128,256]{2,1,0:T(8,128)(2,1)S(1)} collective-permute-done((bf16[4,128,256]{2,1,0:T(8,128)(2,1)S(1)}, bf16[4,128,256]{2,1,0:T(8,128)(2,1)S(1)}, u32[]{:S(2)}, u32[]{:S(2)}) %collective-permute-start.6) | collective-permute-done | bytes 262176 | tf_op jit(solution)/shard_map/ppermute | solution.py:38
  203.2 5.0 %attend.1 = (f32[128,256]{1,0:T(8,128)S(1)}, f32[8,256]{1,0:T(8,128)S(1)}, bf16[144,256]{1,0:T(8,128)(2,1)S(1)}) custom-call(s32[1]{0:T(128)} %bitcast.flag_ref, bf16[320,128]{1,0:T(8,128)(2,1)S(1)} %finish.1.own_ref, bf16[320,128]{1,0:T(8,128)(2,1)S(1)} %collective-permute-done.3.other_ref, s32[128,32]{1,0:T(8,128)S(1)} %or_select_fusion.eff_ref, ...), custom_call_target="tpu_custom_call" | custom-call | flops 1073741824 | bytes 2097152 | tf_op jit(solution)/shard_map/attend/pallas_call | solution.py:323
  208.1 5.5 %collective-permute-start.11 = (bf16[144,256]{1,0:T(8,128)(2,1)S(1)}, bf16[144,256]{1,0:T(8,128)(2,1)S(1)}, u32[]{:S(2)}, u32[]{:S(2)}) collective-permute-start(bf16[144,256]{1,0:T(8,128)(2,1)S(1)} %get-tuple-element.52), channel_id=1, source_target_pairs={{0,8},{2,10},{4,12},{6,14},{8,0},{10,2},{12,4},{14,6},{1,9},{3,11}... | collective-permute-start | bytes 221192 | tf_op jit(solution)/shard_map/ppermute | solution.py:34
  213.7 5.3 %collective-permute-done.11.got_ref = bf16[144,256]{1,0:T(8,128)(2,1)S(1)} collective-permute-done((bf16[144,256]{1,0:T(8,128)(2,1)S(1)}, bf16[144,256]{1,0:T(8,128)(2,1)S(1)}, u32[]{:S(2)}, u32[]{:S(2)}) %collective-permute-start.11) | collective-permute-done | bytes 73760 | tf_op jit(solution)/shard_map/ppermute | solution.py:34
  218.9 0.8 merge.1
  (73 shorter events, 6.1 us)
Async XLA Ops:
  6.5 34.2 %copy-start.6 = (s32[1,32]{1,0:T(1,128)S(1)}, s32[1,32]{1,0:T(1,128)}, u32[]{:S(2)}) copy-start(s32[1,32]{1,0:T(1,128)} %param.14) | copy-start | bytes 388
  6.5 54.4 %collective-permute-start = (bf16[8,128,256]{2,1,0:T(8,128)(2,1)}, bf16[8,128,256]{2,1,0:T(8,128)(2,1)S(1)}, u32[]{:S(2)}, u32[]{:S(2)}) collective-permute-start(bf16[8,128,256]{2,1,0:T(8,128)(2,1)} %bitcast.42), channel_id=1, source_target_pairs={{0,128},{128,256},{256,384},{384,0},{1,129},{129,257},{257,385},{3... | collective-permute-start | bytes 1572872 | tf_op jit(solution)/shard_map/ppermute | solution.py:38
  10.1 50.9 %collective-permute-start.1 = (bf16[8,128,256]{2,1,0:T(8,128)(2,1)}, bf16[8,128,256]{2,1,0:T(8,128)(2,1)S(1)}, u32[]{:S(2)}, u32[]{:S(2)}) collective-permute-start(bf16[8,128,256]{2,1,0:T(8,128)(2,1)} %bitcast.43), channel_id=1, source_target_pairs={{0,256},{128,384},{256,0},{384,128},{1,257},{129,385},{257,1},{385... | collective-permute-start | bytes 1572872 | tf_op jit(solution)/shard_map/ppermute | solution.py:38
  14.7 46.3 %collective-permute-start.2 = (bf16[8,128,256]{2,1,0:T(8,128)(2,1)}, bf16[8,128,256]{2,1,0:T(8,128)(2,1)S(1)}, u32[]{:S(2)}, u32[]{:S(2)}) collective-permute-start(bf16[8,128,256]{2,1,0:T(8,128)(2,1)} %bitcast.44), channel_id=1, source_target_pairs={{0,384},{128,0},{256,128},{384,256},{1,385},{129,1},{257,129},{385... | collective-permute-start | bytes 1572872 | tf_op jit(solution)/shard_map/ppermute | solution.py:38
  20.7 31.2 %all-to-all-start = ((bf16[128,8,128]{2,1,0:T(8,128)(2,1)}), bf16[128,8,128]{2,1,0:T(8,128)(2,1)S(1)}, u32[]{:S(2)}, u32[]{:S(2)}) async-start(bf16[128,8,128]{2,1,0:T(8,128)(2,1)} %bitcast_select_fusion), calls=%async_computation | async-start | bytes 524288 | tf_op jit(solution)/shard_map/all_to_all | solution.py:231
  38.0 90.4 %all-gather.3.cloned.1.call-start = ((), (), s32[]{:S(2)}) async-start(), calls=%async_computation.3 | async-start | bytes 1638400 | tf_op jit(solution)/shard_map/all_gather | solution.py:242
  53.0 5.3 %copy-start.4 = (s32[256]{0:T(256)S(1)}, s32[256]{0:T(256)}, u32[]{:S(2)}) copy-start(s32[256]{0:T(256)} %param.13) | copy-start | bytes 3076
  53.0 77.0 %all-to-all-start.1 = ((bf16[16,8,8,512]{3,2,1,0:T(8,128)(2,1)}), bf16[16,8,8,512]{3,2,1,0:T(8,128)(2,1)S(1)}, u32[]{:S(2)}, u32[]{:S(2)}) async-start(bf16[16,8,8,512]{3,2,1,0:T(8,128)(2,1)} %broadcast_in_dim.141), calls=%async_computation.1 | async-start | bytes 2097152 | tf_op jit(solution)/shard_map/all_to_all | solution.py:237
  60.9 0.8 copy-start.1
  61.0 1.0 copy-start.2
  61.9 0.8 copy-start.3
  131.9 3.8 %copy-start.5 = (s32[1,64]{1,0:T(1,128)S(1)}, s32[1,64]{1,0:T(1,128)}, u32[]{:S(2)}) copy-start(s32[1,64]{1,0:T(1,128)} %param.15) | copy-start | bytes 772
  131.9 4.3 %copy-start.9 = (bf16[4,128,256]{2,1,0:T(8,128)(2,1)S(1)}, bf16[4,128,256]{2,1,0:T(8,128)(2,1)}, u32[]{:S(2)}) copy-start(bf16[4,128,256]{2,1,0:T(8,128)(2,1)} %get-tuple-element.49) | copy-start | bytes 786436
  131.9 9.4 %copy-start.8 = (bf16[4,128,256]{2,1,0:T(8,128)(2,1)S(1)}, bf16[4,128,256]{2,1,0:T(8,128)(2,1)}, u32[]{:S(2)}) copy-start(bf16[4,128,256]{2,1,0:T(8,128)(2,1)} %get-tuple-element.46) | copy-start | bytes 786436
  131.9 37.7 %copy-start.7 = (bf16[4,128,256]{2,1,0:T(8,128)(2,1)S(1)}, bf16[4,128,256]{2,1,0:T(8,128)(2,1)}, u32[]{:S(2)}) copy-start(bf16[4,128,256]{2,1,0:T(8,128)(2,1)} %get-tuple-element.45) | copy-start | bytes 786436
  131.9 71.3 %copy-start = (bf16[4,128,256]{2,1,0:T(8,128)(2,1)S(1)}, bf16[4,128,256]{2,1,0:T(8,128)(2,1)}, u32[]{:S(2)}) copy-start(bf16[4,128,256]{2,1,0:T(8,128)(2,1)} %get-tuple-element.42.refs_0_) | copy-start | bytes 786436
  131.9 52.8 %all-to-all-start.2 = ((bf16[8,72,640]{2,1,0:T(8,128)(2,1)}), bf16[8,72,640]{2,1,0:T(8,128)(2,1)S(1)}, u32[]{:S(2)}, u32[]{:S(2)}) async-start(bf16[8,72,640]{2,1,0:T(8,128)(2,1)} %project.1), calls=%async_computation.2 | async-start | bytes 1474560 | tf_op jit(solution)/shard_map/all_to_all | solution.py:285
  136.2 25.5 %collective-permute-start.10 = (bf16[4,128,256]{2,1,0:T(8,128)(2,1)S(1)}, bf16[4,128,256]{2,1,0:T(8,128)(2,1)S(1)}, u32[]{:S(2)}, u32[]{:S(2)}) collective-permute-start(bf16[4,128,256]{2,1,0:T(8,128)(2,1)S(1)} %copy-done.9), channel_id=1, source_target_pairs={{0,112},{16,0},{32,16},{48,32},{64,48},{80,64},{96,80},{112,96},{1... | collective-permute-start | bytes 786440 | tf_op jit(solution)/shard_map/ppermute | solution.py:38
  141.3 28.3 %collective-permute-start.7 = (bf16[4,128,256]{2,1,0:T(8,128)(2,1)S(1)}, bf16[4,128,256]{2,1,0:T(8,128)(2,1)S(1)}, u32[]{:S(2)}, u32[]{:S(2)}) collective-permute-start(bf16[4,128,256]{2,1,0:T(8,128)(2,1)S(1)} %copy-done.8), channel_id=1, source_target_pairs={{0,64},{16,80},{32,96},{48,112},{64,0},{80,16},{96,32},{112,48},{1... | collective-permute-start | bytes 786440 | tf_op jit(solution)/shard_map/ppermute | solution.py:38
  146.8 42.0 %collective-permute-start.8 = (bf16[4,128,256]{2,1,0:T(8,128)(2,1)}, bf16[4,128,256]{2,1,0:T(8,128)(2,1)S(1)}, u32[]{:S(2)}, u32[]{:S(2)}) collective-permute-start(bf16[4,128,256]{2,1,0:T(8,128)(2,1)} %get-tuple-element.47), channel_id=1, source_target_pairs={{0,80},{16,96},{32,112},{48,0},{64,16},{80,32},{96,48},{112,64},{1... | collective-permute-start | bytes 786440 | tf_op jit(solution)/shard_map/ppermute | solution.py:38
  148.8 51.3 %collective-permute-start.9 = (bf16[4,128,256]{2,1,0:T(8,128)(2,1)}, bf16[4,128,256]{2,1,0:T(8,128)(2,1)S(1)}, u32[]{:S(2)}, u32[]{:S(2)}) collective-permute-start(bf16[4,128,256]{2,1,0:T(8,128)(2,1)} %get-tuple-element.48), channel_id=1, source_target_pairs={{0,96},{16,112},{32,0},{48,16},{64,32},{80,48},{96,64},{112,80},{1... | collective-permute-start | bytes 786440 | tf_op jit(solution)/shard_map/ppermute | solution.py:38
  154.8 45.3 %collective-permute-start.4 = (bf16[4,128,256]{2,1,0:T(8,128)(2,1)}, bf16[4,128,256]{2,1,0:T(8,128)(2,1)S(1)}, u32[]{:S(2)}, u32[]{:S(2)}) collective-permute-start(bf16[4,128,256]{2,1,0:T(8,128)(2,1)} %get-tuple-element.43), channel_id=1, source_target_pairs={{0,16},{16,32},{32,48},{48,64},{64,80},{80,96},{96,112},{112,0},{1... | collective-permute-start | bytes 786440 | tf_op jit(solution)/shard_map/ppermute | solution.py:38
  161.7 38.4 %collective-permute-start.5 = (bf16[4,128,256]{2,1,0:T(8,128)(2,1)}, bf16[4,128,256]{2,1,0:T(8,128)(2,1)S(1)}, u32[]{:S(2)}, u32[]{:S(2)}) collective-permute-start(bf16[4,128,256]{2,1,0:T(8,128)(2,1)} %get-tuple-element.44), channel_id=1, source_target_pairs={{0,32},{16,48},{32,64},{48,80},{64,96},{80,112},{96,0},{112,16},{1... | collective-permute-start | bytes 786440 | tf_op jit(solution)/shard_map/ppermute | solution.py:38
  169.6 33.5 %collective-permute-start.6 = (bf16[4,128,256]{2,1,0:T(8,128)(2,1)S(1)}, bf16[4,128,256]{2,1,0:T(8,128)(2,1)S(1)}, u32[]{:S(2)}, u32[]{:S(2)}) collective-permute-start(bf16[4,128,256]{2,1,0:T(8,128)(2,1)S(1)} %copy-done.7), channel_id=1, source_target_pairs={{0,48},{16,64},{32,80},{48,96},{64,112},{80,0},{96,16},{112,32},{1... | collective-permute-start | bytes 786440 | tf_op jit(solution)/shard_map/ppermute | solution.py:38
  188.8 14.3 %collective-permute-start.3 = (bf16[320,128]{1,0:T(8,128)(2,1)S(1)}, bf16[320,128]{1,0:T(8,128)(2,1)S(1)}, u32[]{:S(2)}, u32[]{:S(2)}) collective-permute-start(bf16[320,128]{1,0:T(8,128)(2,1)S(1)} %finish.1.own_ref), channel_id=1, source_target_pairs={{0,8},{2,10},{4,12},{6,14},{8,0},{10,2},{12,4},{14,6},{1,9},{3,11}... | collective-permute-start | bytes 245768 | tf_op jit(solution)/shard_map/ppermute | solution.py:34
  208.1 10.8 %collective-permute-start.11 = (bf16[144,256]{1,0:T(8,128)(2,1)S(1)}, bf16[144,256]{1,0:T(8,128)(2,1)S(1)}, u32[]{:S(2)}, u32[]{:S(2)}) collective-permute-start(bf16[144,256]{1,0:T(8,128)(2,1)S(1)} %get-tuple-element.52), channel_id=1, source_target_pairs={{0,8},{2,10},{4,12},{6,14},{8,0},{10,2},{12,4},{14,6},{1,9},{3,11}... | collective-permute-start | bytes 221192 | tf_op jit(solution)/shard_map/ppermute | solution.py:34
Sparse Core Ops, SparseCore 0:
  40.9 28.9 all-gather.2

commit v3 on v2

v3 whole, which is shorter than its diff:
```python
import functools
import math

import jax
import jax.numpy as jnp
from jax import lax
from jax.experimental import pallas as pl
from jax.experimental.pallas import tpu as pltpu
from jax.sharding import Mesh
from jax.sharding import PartitionSpec as P

NX, NZ, NY, NC = 4, 8, 8, 2
KVH = 8
HD = 128
STRETCH = 256
MAXC = 32
CH_DEV = 8
QS = 4
HALF = 128
ROWS = 64
D = 8192
QW = QS * HD
COLS = QW + HD
QROWS = QS * ROWS

theta_base = 500000.0
neg_large = -1e30
far_away = 1 << 29

STORE = ("x", "z")
TP = ("y", "c")
NT = (((1,), (1,)), ((), ()))
TN = (((0,), (0,)), ((), ()))


def exchange(block):
    return lax.ppermute(block, "y", [(i, (i + NY // 2) % NY) for i in range(NY)])


def shifted(block, axis, count, by):
    return lax.ppermute(block, axis, [(i, (i + by) % count) for i in range(count)])


def call(kernel, outs, name, flops=0, bytes_accessed=0):
    return pl.pallas_call(
        kernel,
        out_shape=outs,
        name=name,
        compiler_params=pltpu.CompilerParams(vmem_limit_bytes=32 * 1024 * 1024),
        cost_estimate=pl.CostEstimate(
            flops=flops, bytes_accessed=bytes_accessed, transcendentals=0
        ),
    )


def project_kernel(tokens_ref, gain_ref, w0_ref, w1_ref, w2_ref, w3_ref, out_ref):
    weights = jnp.concatenate([w[: 2 * HD, :] for w in (w0_ref, w1_ref, w2_ref, w3_ref)], axis=0)
    gain = gain_ref[...]
    rows = []
    stats = []
    for request in range(NZ):
        tall = []
        for y in range(NY):
            halves = [tokens_ref[y * NC + c, request].astype(jnp.float32) for c in range(NC)]
            tall.append(
                jnp.concatenate(
                    [halves[c][:, k * HD : (k + 1) * HD] for k in range(NX) for c in range(NC)],
                    axis=1,
                )
            )
        wide = jnp.concatenate(tall, axis=0)
        rows.append((wide * gain).astype(jnp.bfloat16))
        squares = jnp.zeros((ROWS, HD), jnp.float32)
        for at in range(0, wide.shape[1], HD):
            piece = wide[:, at : at + HD]
            squares += piece * piece
        squares = jnp.concatenate([squares, jnp.zeros_like(squares)], axis=0)
        row = jnp.sum(squares.T, axis=0, keepdims=True)
        high = row.astype(jnp.bfloat16).astype(jnp.float32)
        stat = jnp.concatenate([high, row - high, jnp.zeros((6, HD), jnp.float32)], axis=0)
        stats.append(jnp.concatenate([stat, jnp.zeros((8, QW), jnp.float32)], axis=1))
    total = jnp.dot(jnp.concatenate(rows, axis=0), weights, preferred_element_type=jnp.float32)
    for request in range(NZ):
        block = total[request * ROWS : (request + 1) * ROWS]
        block = jnp.concatenate([block, stats[request]], axis=0)
        out_ref[request] = block.astype(jnp.bfloat16)


def finish_kernel(parts_ref, cos_ref, sin_ref, fcos_ref, fsin_ref, out_ref):
    inverse = None
    for group in range(QS + 1):
        lanes = pl.ds(group * HD, HD)
        total = parts_ref[0, :, lanes].astype(jnp.float32)
        for part in range(1, NZ):
            total += parts_ref[part, :, lanes].astype(jnp.float32)
        if inverse is None:
            squares = total[ROWS : ROWS + 1, :] + total[ROWS + 1 : ROWS + 2, :]
            inverse = lax.rsqrt(squares * (1.0 / D) + 1e-05)
            inverse = jnp.broadcast_to(inverse, (HD, HD)).T[:ROWS]
        total = total[:ROWS] * inverse
        cos = cos_ref[...] if group < QS else fcos_ref[...]
        sin = sin_ref[...] if group < QS else fsin_ref[...]
        turned = total * cos + pltpu.roll(total, HD // 2, 1) * sin
        out_ref[pl.ds(group * ROWS, ROWS), :] = turned.astype(jnp.bfloat16)


def attend_block(kv_ref, slots, queries, eff_ref, pos, run_ref, acc_ref):
    pieces = []
    for at, slot in slots:
        piece = lax.dot_general(
            kv_ref[at, :, :HD], queries, NT, preferred_element_type=jnp.float32
        )
        pieces.append(jnp.where(eff_ref[:, slot : slot + 1] <= pos, piece, neg_large))
    old_peak = run_ref[0:1, :]
    new_peak = old_peak
    for piece in pieces:
        new_peak = jnp.maximum(new_peak, jnp.max(piece, axis=0, keepdims=True))
    factor = jnp.exp2(old_peak - new_peak)
    total = run_ref[1:2, :] * factor
    acc = acc_ref[...] * factor
    for (at, _), piece in zip(slots, pieces):
        weights = jnp.exp2(piece - new_peak)
        total += jnp.sum(weights, axis=0, keepdims=True)
        acc += lax.dot_general(
            kv_ref[at, :, HD:], weights.astype(jnp.bfloat16), TN, preferred_element_type=jnp.float32
        )
    run_ref[0:1, :] = new_peak
    run_ref[1:2, :] = total
    acc_ref[...] = acc


def attend_early_kernel(which, flag_ref, own_ref, other_ref, eff_ref, fresh_eff_ref, pos_ref, *refs):
    kv_refs, (acc_ref, run_ref) = refs[: len(which)], refs[len(which) :]
    is_first = flag_ref[0] == 0
    queries = jnp.concatenate([own_ref[:QROWS, :], other_ref[:QROWS, :]], axis=0)
    own_piece = own_ref[QROWS:, :]
    other_piece = other_ref[QROWS:, :]
    first = jnp.broadcast_to(is_first, own_piece.shape)
    fresh_keys = jnp.where(first, own_piece, other_piece)
    fresh_values = jnp.where(first, other_piece, own_piece)
    pos = pos_ref[...]
    scores = lax.dot_general(fresh_keys, queries, NT, preferred_element_type=jnp.float32)
    scores = jnp.where(fresh_eff_ref[:, 0:1] <= pos, scores, neg_large)
    peak = jnp.max(scores, axis=0, keepdims=True)
    weights = jnp.exp2(scores - peak)
    run_ref[...] = jnp.zeros(run_ref.shape, jnp.float32)
    run_ref[0:1, :] = peak
    run_ref[1:2, :] = jnp.sum(weights, axis=0, keepdims=True)
    acc_ref[...] = lax.dot_general(
        fresh_values, weights.astype(jnp.bfloat16), TN, preferred_element_type=jnp.float32
    )
    for k, kv_ref in zip(which, kv_refs):
        for half in range(0, NZ, 4):
            slots = [(half + i, k * NZ + half + i) for i in range(4)]
            attend_block(kv_ref, slots, queries, eff_ref, pos, run_ref, acc_ref)


def attend_late_kernel(
    which, own_ref, other_ref, eff_ref, pos_ref, acc_in_ref, run_in_ref, *refs
):
    kv_refs, (own_out_ref, stat_ref, sent_ref, acc_ref, run_ref) = (
        refs[: len(which)],
        refs[len(which) :],
    )
    queries = jnp.concatenate([own_ref[:QROWS, :], other_ref[:QROWS, :]], axis=0)
    pos = pos_ref[...]
    acc_ref[...] = acc_in_ref[...]
    run_ref[...] = run_in_ref[...]
    for k, kv_ref in zip(which, kv_refs):
        for half in range(0, NZ, 4):
            slots = [(half + i, k * NZ + half + i) for i in range(4)]
            attend_block(kv_ref, slots, queries, eff_ref, pos, run_ref, acc_ref)
    peak = run_ref[0:1, :]
    total = run_ref[1:2, :]
    mixed = acc_ref[...] / total
    own_out_ref[...] = mixed[:, :QROWS]
    stat_ref[0:1, :] = peak[:, :QROWS]
    stat_ref[1:2, :] = total[:, :QROWS]
    stat_ref[2:8, :] = jnp.zeros((6, QROWS), jnp.float32)
    peak = peak[:, QROWS:]
    total = total[:, QROWS:]
    peak_high = peak.astype(jnp.bfloat16).astype(jnp.float32)
    total_high = total.astype(jnp.bfloat16).astype(jnp.float32)
    stats = jnp.concatenate(
        [
            peak_high,
            peak - peak_high,
            total_high,
            total - total_high,
            jnp.zeros((12, QROWS), jnp.float32),
        ],
        axis=0,
    )
    sent_ref[:HD, :] = mixed[:, QROWS:].astype(jnp.bfloat16)
    sent_ref[HD:, :] = stats.astype(jnp.bfloat16)


def merge_kernel(own_ref, stat_ref, got_ref, out_ref):
    stats = got_ref[HD:, :].astype(jnp.float32)
    got_peak = stats[0:1, :] + stats[1:2, :]
    got_total = stats[2:3, :] + stats[3:4, :]
    peak = stat_ref[0:1, :]
    total = stat_ref[1:2, :]
    joint = jnp.maximum(peak, got_peak)
    mine = jnp.exp2(peak - joint) * total
    theirs = jnp.exp2(got_peak - joint) * got_total
    whole = mine + theirs
    mixed = own_ref[...] * (mine / whole) + got_ref[:HD, :].astype(jnp.float32) * (theirs / whole)
    turned = mixed.T.astype(jnp.bfloat16)
    for head in range(QS):
        out_ref[:, pl.ds(head * HD, HD)] = turned[head * ROWS : (head + 1) * ROWS, :]


def body(hidden, norm_gain, q_weight, kv_weight, cache_store, location, stretch_ids, rec_pos):
    x = lax.axis_index("x")
    z = lax.axis_index("z")
    y = lax.axis_index("y")
    c = lax.axis_index("c")
    my_tp = y * NC + c
    which_half = my_tp // KVH
    is_first = which_half == 0
    positions = rec_pos[0]
    own_list = stretch_ids[0]
    int_rows = jnp.arange(CH_DEV, dtype=jnp.int32)
    table = jnp.arange(location.shape[0], dtype=jnp.int32)

    store = lax.all_gather(cache_store[:, 0], "z", axis=0, tiled=True)

    blocks = hidden[0].reshape(NY, 8, 2, NC, HD).transpose(2, 0, 3, 1, 4)
    blocks = jnp.broadcast_to(blocks[None], (4, 2, NY, NC, 8, HD))
    blocks = blocks.reshape(NZ * NY * NC, 8, HD)
    blocks = lax.all_to_all(blocks, ("z", "y", "c"), 0, 0, tiled=True)
    blocks = blocks.reshape(NZ, NX, 4, 8, HD)
    blocks = lax.dynamic_index_in_dim(blocks, z // 2, 2, keepdims=False)
    blocks = jnp.concatenate([blocks, blocks], axis=1)
    blocks = lax.dynamic_slice_in_dim(blocks, x, NX, 1)
    blocks = blocks.transpose(0, 2, 1, 3).reshape(NZ, 8, NX * HD)
    tokens = lax.all_to_all(
        jnp.broadcast_to(blocks[None], (NY * NC, NZ, 8, NX * HD)), TP, 0, 0, tiled=True
    )

    listed = jnp.pad(own_list.astype(jnp.bfloat16)[None, :], ((0, 15), (0, COLS - MAXC)))
    weight = jnp.concatenate([q_weight[:, 0], kv_weight[:, 0]], axis=1)
    weight = jnp.concatenate([weight, listed], axis=0)
    weights = [weight] + [shifted(weight, "x", NX, -k) for k in range(1, NX)]
    gain = lax.dynamic_index_in_dim(norm_gain.reshape(NX, NZ, NC * HD), z, 1, keepdims=False)
    gain = lax.dynamic_slice_in_dim(jnp.concatenate([gain, gain], axis=0), x, NX, 0)
    gain = gain.astype(jnp.float32).reshape(1, NX * NC * HD)

    partial = call(
        project_kernel,
        jax.ShapeDtypeStruct((NZ, ROWS + 8, COLS), jnp.bfloat16),
        "project",
        flops=2 * NZ * ROWS * 1024 * COLS,
        bytes_accessed=1 << 22,
    )(tokens, gain, *weights)
    parts = lax.all_to_all(partial, "z", 0, 0, tiled=True)

    lists = jnp.stack([w[NC * HD, :MAXC] for w in weights]).astype(jnp.int32)
    steps = jnp.arange(NZ, dtype=jnp.int32)
    row_ids = (x * NZ + steps)[:, None] * CH_DEV + int_rows[None, :]
    here = location[None, None, :] == row_ids[:, :, None]
    held = jnp.sum(jnp.where(here, table, 0), axis=2)
    wanted = jnp.any(lists[:, :, None, None] == held[None, None], axis=1)
    send_rows = jnp.sum(jnp.where(wanted, int_rows, 0), axis=2) + steps[None, :] * CH_DEV
    send_rows, _ = lax.optimization_barrier((send_rows, partial[0, ROWS:, :HD]))
    arrived = [store[send_rows[0]]]
    for k in range(1, NX):
        arrived.append(shifted(store[send_rows[NX - k]], "x", NX, -k))

    frequency = jnp.exp(
        -math.log(theta_base) * jnp.arange(HD // 2, dtype=jnp.float32) / (HD // 2)
    )
    angles = positions.astype(jnp.float32)[:, None] * frequency[None, :]
    cos = jnp.cos(angles)
    sin = jnp.sin(angles)
    cos = jnp.concatenate([cos, cos], axis=1)
    sin = jnp.concatenate([-sin, sin], axis=1)
    fresh_cos = jnp.where(is_first, cos, 1.0)
    fresh_sin = jnp.where(is_first, sin, 0.0)
    scale = math.log2(math.e) / math.sqrt(HD)

    own = call(
        finish_kernel, jax.ShapeDtypeStruct((QROWS + ROWS, HD), jnp.bfloat16), "finish"
    )(parts, cos * scale, sin * scale, fresh_cos, fresh_sin)
    other = exchange(own)

    own_row = jnp.sum(jnp.where(own_list[:, None] == table[None, :], location[None, :], 0), axis=1)
    own_shard = own_row // CH_DEV
    slot_shard = (x * NZ + jnp.arange(MAXC, dtype=jnp.int32)) % (NX * NZ)
    match = (own_shard[None, :] == slot_shard[:, None]) & (own_list >= 0)[None, :]
    slot_order = jnp.sum(jnp.where(match, jnp.arange(MAXC, dtype=jnp.int32), 0), axis=1)
    slot_live = jnp.any(match, axis=1)
    key_pos = (
        slot_order[None, :] * STRETCH
        + which_half * HALF
        + jnp.arange(HALF, dtype=jnp.int32)[:, None]
    )
    replaced = jnp.any(key_pos[:, :, None] == positions[None, None, :], axis=2)
    eff = jnp.where(replaced | ~slot_live[None, :], far_away, key_pos)
    fresh_eff = jnp.where(positions % STRETCH // HALF == which_half, positions, far_away)
    fresh_eff = jnp.broadcast_to(fresh_eff[:, None], (ROWS, HD))
    pos_row = jnp.tile(positions, 2 * QS).reshape(1, 2 * QROWS)

    smem = pl.BlockSpec(memory_space=pltpu.SMEM)
    vmem = pl.BlockSpec(memory_space=pltpu.VMEM)
    early, late = (0, 1, 3), (2,)
    params = pltpu.CompilerParams(vmem_limit_bytes=32 * 1024 * 1024)
    run_shapes = [
        jax.ShapeDtypeStruct((HD, 2 * QROWS), jnp.float32),
        jax.ShapeDtypeStruct((8, 2 * QROWS), jnp.float32),
    ]

    def cost(count):
        pairs = count * NZ * HALF * 2 * QROWS
        return pl.CostEstimate(flops=4 * pairs * HD, bytes_accessed=count << 19, transcendentals=pairs)

    acc, run = pl.pallas_call(
        functools.partial(attend_early_kernel, early),
        out_shape=run_shapes,
        in_specs=[smem] + [vmem] * (5 + len(early)),
        out_specs=[vmem] * 2,
        name="attend_early",
        compiler_params=params,
        cost_estimate=cost(len(early)),
    )(which_half.reshape(1), own, other, eff, fresh_eff, pos_row, *[arrived[k] for k in early])
    own_part, stats, sent = pl.pallas_call(
        functools.partial(attend_late_kernel, late),
        out_shape=[
            jax.ShapeDtypeStruct((HD, QROWS), jnp.float32),
            jax.ShapeDtypeStruct((8, QROWS), jnp.float32),
            jax.ShapeDtypeStruct((HD + 16, QROWS), jnp.bfloat16),
        ],
        in_specs=[vmem] * (6 + len(late)),
        out_specs=[vmem] * 3,
        scratch_shapes=[pltpu.VMEM(r.shape, r.dtype) for r in run_shapes],
        name="attend_late",
        compiler_params=params,
        cost_estimate=cost(len(late)),
    )(own, other, eff, pos_row, acc, run, *[arrived[k] for k in late])
    got = exchange(sent)
    attended = call(merge_kernel, jax.ShapeDtypeStruct((ROWS, QW), jnp.bfloat16), "merge")(
        own_part, stats, got
    )
    return attended.reshape(1, ROWS, 1, QW)


def solution(mesh):
    fine = Mesh(mesh.devices.reshape(NX, NZ, NY, NC), ("x", "z", "y", "c"))
    in_specs = (
        P(STORE, None, TP),
        P(),
        P(STORE, TP, None),
        P(STORE, TP, None),
        P(STORE, TP, None, None),
        P(),
        P(STORE, None),
        P(STORE, None),
    )
    return jax.shard_map(
        body, mesh=fine, in_specs=in_specs, out_specs=P(STORE, None, TP, None), check_vma=False
    )
```

time: 227 us -> 156 us (0.69)
  the two profiles are of different devices: /device:TPU:16 before, /device:TPU:64 now
where the time goes in v3:
time: 156 us; the launch traced here: 155 us
  waiting for transfers between devices  57.4 us (37%)
  starting transfers between devices  53.8 us (34%)
  local copies, waits for them, and re-layouts  16.5 us (11%)
  between operations  13.8 us (9%)
  Pallas kernels  7.94 us (5%)
  other arithmetic  5.58 us (4%)
    all_to_all x1, waiting for transfers between devices, body(): lax.all_to_all(jnp.broadcast_to(blocks[None], (NY * NC, NZ, 8, NX * HD)),...  25.1 us
    ppermute x6, starting transfers between devices, shifted(): lax.ppermute(block, axis, [(i, (i + by) % count) for i in range(count)])  19.8 us
    all_to_all x1, starting transfers between devices, body(): blocks = lax.all_to_all(blocks, ('z', 'y', 'c'), 0, 0, tiled=True)  16.6 us
    all_to_all x1, waiting for transfers between devices, body(): blocks = lax.all_to_all(blocks, ('z', 'y', 'c'), 0, 0, tiled=True)  11.7 us
    ppermute x2, waiting for transfers between devices, exchange(): lax.ppermute(block, 'y', [(i, (i + NY // 2) % NY) for i in range(NY)])  10.3 us
    gather x3, local copies, waits for them, and re-layouts, body(): arrived.append(shifted(store[send_rows[NX - k]], 'x', NX, -k))  9.93 us
    ppermute x2, starting transfers between devices, exchange(): lax.ppermute(block, 'y', [(i, (i + NY // 2) % NY) for i in range(NY)])  9.02 us
    ppermute x6, waiting for transfers between devices, shifted(): lax.ppermute(block, axis, [(i, (i + by) % count) for i in range(count)])  8.79 us
  transfers between devices with their start and end apart: 12, of which 6 were waited for; matrix products, arithmetic and copies ran while one was open for 14% of the time, Pallas kernels for 4%

profile of v3, /device:TPU:64, one launch (start us, length us, event | category | flops | bytes accessed | tf_op | source)
XLA Modules:
  0.0 155.0 jit_solution(2282998682293008503)
XLA Ops:
  6.5 0.7 all-gather.3.cloned.1.call-update
  7.9 1.0 fusion.1.w0_ref
  8.9 4.7 %collective-permute-start = (bf16[272,640]{1,0:T(8,128)(2,1)S(1)}, bf16[272,640]{1,0:T(8,128)(2,1)S(1)}, u32[]{:S(2)}, u32[]{:S(2)}) collective-permute-start(bf16[272,640]{1,0:T(8,128)(2,1)S(1)} %fusion.1.w0_ref), channel_id=1, source_target_pairs={{0,384},{128,0},{256,128},{384,256},{1,385},{129,1},{257,129},{385... | collective-permute-start | bytes 1044488 | tf_op jit(solution)/shard_map/ppermute | solution.py:41
  13.6 2.7 %collective-permute-start.1 = (bf16[272,640]{1,0:T(8,128)(2,1)S(1)}, bf16[272,640]{1,0:T(8,128)(2,1)S(1)}, u32[]{:S(2)}, u32[]{:S(2)}) collective-permute-start(bf16[272,640]{1,0:T(8,128)(2,1)S(1)} %fusion.1.w0_ref), channel_id=1, source_target_pairs={{0,256},{128,384},{256,0},{384,128},{1,257},{129,385},{257,1},{385... | collective-permute-start | bytes 1044488 | tf_op jit(solution)/shard_map/ppermute | solution.py:41
  16.3 2.8 %collective-permute-start.2 = (bf16[272,640]{1,0:T(8,128)(2,1)S(1)}, bf16[272,640]{1,0:T(8,128)(2,1)S(1)}, u32[]{:S(2)}, u32[]{:S(2)}) collective-permute-start(bf16[272,640]{1,0:T(8,128)(2,1)S(1)} %fusion.1.w0_ref), channel_id=1, source_target_pairs={{0,128},{128,256},{256,384},{384,0},{1,129},{129,257},{257,385},{3... | collective-permute-start | bytes 1044488 | tf_op jit(solution)/shard_map/ppermute | solution.py:41
  19.1 0.8 copy.13
  20.0 0.7 broadcast_in_dim.59
  20.7 16.6 %all-to-all-start = ((bf16[128,8,128]{2,1,0:T(8,128)(2,1)}), bf16[128,8,128]{2,1,0:T(8,128)(2,1)S(1)}, u32[]{:S(2)}, u32[]{:S(2)}) async-start(bf16[128,8,128]{2,1,0:T(8,128)(2,1)} %bitcast.2), calls=%async_computation | async-start | bytes 524288 | tf_op jit(solution)/shard_map/all_to_all | solution.py:232
  37.3 0.7 reshape.313
  38.1 0.9 select_reduce_fusion.1
  39.9 11.7 %all-to-all-done = bf16[128,8,128]{2,1,0:T(8,128)(2,1)S(1)} async-done(((bf16[128,8,128]{2,1,0:T(8,128)(2,1)}), bf16[128,8,128]{2,1,0:T(8,128)(2,1)S(1)}, u32[]{:S(2)}, u32[]{:S(2)}) %all-to-all-start) | async-done | bytes 262176 | tf_op jit(solution)/shard_map/all_to_all | solution.py:232
  51.6 1.1 broadcast_in_dim.95
  52.7 3.7 %all-to-all-start.1 = ((bf16[16,8,8,512]{3,2,1,0:T(8,128)(2,1)}), bf16[16,8,8,512]{3,2,1,0:T(8,128)(2,1)S(1)}, u32[]{:S(2)}, u32[]{:S(2)}) async-start(bf16[16,8,8,512]{3,2,1,0:T(8,128)(2,1)} %broadcast_in_dim.95), calls=%async_computation.1 | async-start | bytes 2097152 | tf_op jit(solution)/shard_map/all_to_all | solution.py:238
  57.9 25.1 %all-to-all-done.1.tokens_ref = bf16[16,8,8,512]{3,2,1,0:T(8,128)(2,1)S(1)} async-done(((bf16[16,8,8,512]{3,2,1,0:T(8,128)(2,1)}), bf16[16,8,8,512]{3,2,1,0:T(8,128)(2,1)S(1)}, u32[]{:S(2)}, u32[]{:S(2)}) %all-to-all-start.1) | async-done | bytes 1048608 | tf_op jit(solution)/shard_map/all_to_all | solution.py:238
  83.0 1.9 %project.1 = bf16[8,72,640]{2,1,0:T(8,128)(2,1)} custom-call(bf16[16,8,8,512]{3,2,1,0:T(8,128)(2,1)S(1)} %all-to-all-done.1.tokens_ref, f32[1,1024]{1,0:T(1,128)S(1)} %bitcast.45, bf16[272,640]{1,0:T(8,128)(2,1)S(1)} %fusion.1.w0_ref, bf16[272,640]{1,0:T(8,128)(2,1)S(1)} %collective-permute-done.w1_ref, bf16[272,640]{1,0:T(8,128)(2,1)S(1)} %collective-permute-done.1.w2_ref, ...), custom_call_target="tpu_custom_call" | custom-call | flops 671088640 | bytes 4194304 | tf_op jit(solution)/shard_map/project/pallas_call | solution.py:250
  84.9 4.8 %all-to-all-start.2 = ((bf16[8,72,640]{2,1,0:T(8,128)(2,1)}), bf16[8,72,640]{2,1,0:T(8,128)(2,1)S(1)}, u32[]{:S(2)}, u32[]{:S(2)}) async-start(bf16[8,72,640]{2,1,0:T(8,128)(2,1)} %project.1), calls=%async_computation.2 | async-start | bytes 1474560 | tf_op jit(solution)/shard_map/all_to_all | solution.py:257
  90.6 3.6 %gather_fusion.1 = bf16[8,128,256]{2,1,0:T(8,128)(2,1)} fusion(bf16[64,128,256]{2,1,0:T(8,128)(2,1)} %bitcast.46, s32[1024]{0:T(1024)S(1)} %pad_clamp_fusion.2), kind=kCustom, calls=%fused_computation.1 | custom fusion | bytes 1048608 | tf_op jit(solution)/shard_map/gather | solution.py:269
  94.2 4.3 %collective-permute-start.4 = (bf16[8,128,256]{2,1,0:T(8,128)(2,1)}, bf16[8,128,256]{2,1,0:T(8,128)(2,1)S(1)}, u32[]{:S(2)}, u32[]{:S(2)}) collective-permute-start(bf16[8,128,256]{2,1,0:T(8,128)(2,1)} %gather_fusion.1), channel_id=1, source_target_pairs={{0,384},{128,0},{256,128},{384,256},{1,385},{129,1},{257,129},{385... | collective-permute-start | bytes 1572872 | tf_op jit(solution)/shard_map/ppermute | solution.py:41
  98.4 3.6 %gather_fusion.2 = bf16[8,128,256]{2,1,0:T(8,128)(2,1)} fusion(bf16[64,128,256]{2,1,0:T(8,128)(2,1)} %bitcast.47, s32[1024]{0:T(1024)S(1)} %pad_clamp_fusion.1), kind=kCustom, calls=%fused_computation.2 | custom fusion | bytes 1048608 | tf_op jit(solution)/shard_map/gather | solution.py:269
  102.0 1.9 %collective-permute-start.5 = (bf16[8,128,256]{2,1,0:T(8,128)(2,1)}, bf16[8,128,256]{2,1,0:T(8,128)(2,1)S(1)}, u32[]{:S(2)}, u32[]{:S(2)}) collective-permute-start(bf16[8,128,256]{2,1,0:T(8,128)(2,1)} %gather_fusion.2), channel_id=1, source_target_pairs={{0,128},{128,256},{256,384},{384,0},{1,129},{129,257},{257,385},{3... | collective-permute-start | bytes 1572872 | tf_op jit(solution)/shard_map/ppermute | solution.py:41
  104.0 2.8 %gather_fusion.3 = bf16[8,128,256]{2,1,0:T(8,128)(2,1)S(1)} fusion(bf16[64,128,256]{2,1,0:T(8,128)(2,1)} %bitcast.48, s32[1024]{0:T(1024)S(1)} %pad_clamp_fusion), kind=kCustom, calls=%fused_computation.3 | custom fusion | bytes 1048608 | tf_op jit(solution)/shard_map/gather | solution.py:269
  106.7 3.4 %collective-permute-start.6 = (bf16[8,128,256]{2,1,0:T(8,128)(2,1)S(1)}, bf16[8,128,256]{2,1,0:T(8,128)(2,1)S(1)}, u32[]{:S(2)}, u32[]{:S(2)}) collective-permute-start(bf16[8,128,256]{2,1,0:T(8,128)(2,1)S(1)} %gather_fusion.3), channel_id=1, source_target_pairs={{0,256},{128,384},{256,0},{384,128},{1,257},{129,385},{257,1},{385... | collective-permute-start | bytes 1572872 | tf_op jit(solution)/shard_map/ppermute | solution.py:41
  110.3 0.8 all-to-all-done.2.parts_ref
  111.3 5.0 %collective-permute-start.3 = (bf16[320,128]{1,0:T(8,128)(2,1)S(1)}, bf16[320,128]{1,0:T(8,128)(2,1)S(1)}, u32[]{:S(2)}, u32[]{:S(2)}) collective-permute-start(bf16[320,128]{1,0:T(8,128)(2,1)S(1)} %finish.1.own_ref), channel_id=1, source_target_pairs={{0,8},{2,10},{4,12},{6,14},{8,0},{10,2},{12,4},{14,6},{1,9},{3,11}... | collective-permute-start | bytes 245768 | tf_op jit(solution)/shard_map/ppermute | solution.py:37
  116.4 2.8 %gather_fusion = bf16[8,128,256]{2,1,0:T(8,128)(2,1)S(1)} fusion(bf16[64,128,256]{2,1,0:T(8,128)(2,1)} %bitcast.49, s32[1024]{0:T(1024)S(1)} %pad_clamp_fusion.3), kind=kCustom, calls=%fused_computation | custom fusion | bytes 1048608 | tf_op jit(solution)/shard_map/gather | solution.py:267
  119.2 3.3 %collective-permute-done.3.other_ref = bf16[320,128]{1,0:T(8,128)(2,1)S(1)} collective-permute-done((bf16[320,128]{1,0:T(8,128)(2,1)S(1)}, bf16[320,128]{1,0:T(8,128)(2,1)S(1)}, u32[]{:S(2)}, u32[]{:S(2)}) %collective-permute-start.3) | collective-permute-done | bytes 81952 | tf_op jit(solution)/shard_map/ppermute | solution.py:37
  122.5 8.8 %collective-permute-done.5.refs_2_ = bf16[8,128,256]{2,1,0:T(8,128)(2,1)S(1)} collective-permute-done((bf16[8,128,256]{2,1,0:T(8,128)(2,1)}, bf16[8,128,256]{2,1,0:T(8,128)(2,1)S(1)}, u32[]{:S(2)}, u32[]{:S(2)}) %collective-permute-start.5) | collective-permute-done | bytes 524320 | tf_op jit(solution)/shard_map/ppermute | solution.py:41
  131.3 3.8 %attend_early.1 = (f32[128,512]{1,0:T(8,128)S(1)}, f32[8,512]{1,0:T(8,128)S(1)}) custom-call(s32[1]{0:T(128)} %bitcast.12.flag_ref, bf16[320,128]{1,0:T(8,128)(2,1)S(1)} %finish.1.own_ref, bf16[320,128]{1,0:T(8,128)(2,1)S(1)} %collective-permute-done.3.other_ref, s32[128,32]{1,0:T(8,128)S(1)} %or_select_fusion.eff_ref, ...), custom_call_target="tpu_custom_call" | custom-call | flops 805306368 | bytes 1572864 | tf_op jit(solution)/shard_map/attend_early/pallas_call | solution.py:318
  135.1 1.3 attend_late.1
  136.4 4.0 %collective-permute-start.7 = (bf16[144,256]{1,0:T(8,128)(2,1)S(1)}, bf16[144,256]{1,0:T(8,128)(2,1)S(1)}, u32[]{:S(2)}, u32[]{:S(2)}) collective-permute-start(bf16[144,256]{1,0:T(8,128)(2,1)S(1)} %get-tuple-element.14), channel_id=1, source_target_pairs={{0,8},{2,10},{4,12},{6,14},{8,0},{10,2},{12,4},{14,6},{1,9},{3,11}... | collective-permute-start | bytes 221192 | tf_op jit(solution)/shard_map/ppermute | solution.py:37
  140.4 7.0 %collective-permute-done.7.got_ref = bf16[144,256]{1,0:T(8,128)(2,1)S(1)} collective-permute-done((bf16[144,256]{1,0:T(8,128)(2,1)S(1)}, bf16[144,256]{1,0:T(8,128)(2,1)S(1)}, u32[]{:S(2)}, u32[]{:S(2)}) %collective-permute-start.7) | collective-permute-done | bytes 73760 | tf_op jit(solution)/shard_map/ppermute | solution.py:37
  147.4 0.8 merge.1
  (55 shorter events, 4.3 us)
Async XLA Ops:
  6.5 50.8 %copy-start = (s32[256]{0:T(256)S(1)}, s32[256]{0:T(256)}, u32[]{:S(2)}) copy-start(s32[256]{0:T(256)} %param.13) | copy-start | bytes 3076
  6.5 50.2 %copy-start.1 = (s32[1,64]{1,0:T(1,128)S(1)}, s32[1,64]{1,0:T(1,128)}, u32[]{:S(2)}) copy-start(s32[1,64]{1,0:T(1,128)} %param.15) | copy-start | bytes 772
  6.5 84.1 %all-gather.3.cloned.1.call-start = ((), (), s32[]{:S(2)}) async-start(), calls=%async_computation.3 | async-start | bytes 4718592 | tf_op jit(solution)/shard_map/all_gather | solution.py:227
  8.9 48.9 %collective-permute-start = (bf16[272,640]{1,0:T(8,128)(2,1)S(1)}, bf16[272,640]{1,0:T(8,128)(2,1)S(1)}, u32[]{:S(2)}, u32[]{:S(2)}) collective-permute-start(bf16[272,640]{1,0:T(8,128)(2,1)S(1)} %fusion.1.w0_ref), channel_id=1, source_target_pairs={{0,384},{128,0},{256,128},{384,256},{1,385},{129,1},{257,129},{385... | collective-permute-start | bytes 1044488 | tf_op jit(solution)/shard_map/ppermute | solution.py:41
  13.6 44.2 %collective-permute-start.1 = (bf16[272,640]{1,0:T(8,128)(2,1)S(1)}, bf16[272,640]{1,0:T(8,128)(2,1)S(1)}, u32[]{:S(2)}, u32[]{:S(2)}) collective-permute-start(bf16[272,640]{1,0:T(8,128)(2,1)S(1)} %fusion.1.w0_ref), channel_id=1, source_target_pairs={{0,256},{128,384},{256,0},{384,128},{1,257},{129,385},{257,1},{385... | collective-permute-start | bytes 1044488 | tf_op jit(solution)/shard_map/ppermute | solution.py:41
  16.3 41.5 %collective-permute-start.2 = (bf16[272,640]{1,0:T(8,128)(2,1)S(1)}, bf16[272,640]{1,0:T(8,128)(2,1)S(1)}, u32[]{:S(2)}, u32[]{:S(2)}) collective-permute-start(bf16[272,640]{1,0:T(8,128)(2,1)S(1)} %fusion.1.w0_ref), channel_id=1, source_target_pairs={{0,128},{128,256},{256,384},{384,0},{1,129},{129,257},{257,385},{3... | collective-permute-start | bytes 1044488 | tf_op jit(solution)/shard_map/ppermute | solution.py:41
  20.7 30.9 %all-to-all-start = ((bf16[128,8,128]{2,1,0:T(8,128)(2,1)}), bf16[128,8,128]{2,1,0:T(8,128)(2,1)S(1)}, u32[]{:S(2)}, u32[]{:S(2)}) async-start(bf16[128,8,128]{2,1,0:T(8,128)(2,1)} %bitcast.2), calls=%async_computation | async-start | bytes 524288 | tf_op jit(solution)/shard_map/all_to_all | solution.py:232
  52.7 30.3 %all-to-all-start.1 = ((bf16[16,8,8,512]{3,2,1,0:T(8,128)(2,1)}), bf16[16,8,8,512]{3,2,1,0:T(8,128)(2,1)S(1)}, u32[]{:S(2)}, u32[]{:S(2)}) async-start(bf16[16,8,8,512]{3,2,1,0:T(8,128)(2,1)} %broadcast_in_dim.95), calls=%async_computation.1 | async-start | bytes 2097152 | tf_op jit(solution)/shard_map/all_to_all | solution.py:238
  84.9 26.2 %all-to-all-start.2 = ((bf16[8,72,640]{2,1,0:T(8,128)(2,1)}), bf16[8,72,640]{2,1,0:T(8,128)(2,1)S(1)}, u32[]{:S(2)}, u32[]{:S(2)}) async-start(bf16[8,72,640]{2,1,0:T(8,128)(2,1)} %project.1), calls=%async_computation.2 | async-start | bytes 1474560 | tf_op jit(solution)/shard_map/all_to_all | solution.py:257
  94.2 28.3 %collective-permute-start.4 = (bf16[8,128,256]{2,1,0:T(8,128)(2,1)}, bf16[8,128,256]{2,1,0:T(8,128)(2,1)S(1)}, u32[]{:S(2)}, u32[]{:S(2)}) collective-permute-start(bf16[8,128,256]{2,1,0:T(8,128)(2,1)} %gather_fusion.1), channel_id=1, source_target_pairs={{0,384},{128,0},{256,128},{384,256},{1,385},{129,1},{257,129},{385... | collective-permute-start | bytes 1572872 | tf_op jit(solution)/shard_map/ppermute | solution.py:41
  102.0 29.2 %collective-permute-start.5 = (bf16[8,128,256]{2,1,0:T(8,128)(2,1)}, bf16[8,128,256]{2,1,0:T(8,128)(2,1)S(1)}, u32[]{:S(2)}, u32[]{:S(2)}) collective-permute-start(bf16[8,128,256]{2,1,0:T(8,128)(2,1)} %gather_fusion.2), channel_id=1, source_target_pairs={{0,128},{128,256},{256,384},{384,0},{1,129},{129,257},{257,385},{3... | collective-permute-start | bytes 1572872 | tf_op jit(solution)/shard_map/ppermute | solution.py:41
  106.7 28.3 %collective-permute-start.6 = (bf16[8,128,256]{2,1,0:T(8,128)(2,1)S(1)}, bf16[8,128,256]{2,1,0:T(8,128)(2,1)S(1)}, u32[]{:S(2)}, u32[]{:S(2)}) collective-permute-start(bf16[8,128,256]{2,1,0:T(8,128)(2,1)S(1)} %gather_fusion.3), channel_id=1, source_target_pairs={{0,256},{128,384},{256,0},{384,128},{1,257},{129,385},{257,1},{385... | collective-permute-start | bytes 1572872 | tf_op jit(solution)/shard_map/ppermute | solution.py:41
  111.3 11.2 %collective-permute-start.3 = (bf16[320,128]{1,0:T(8,128)(2,1)S(1)}, bf16[320,128]{1,0:T(8,128)(2,1)S(1)}, u32[]{:S(2)}, u32[]{:S(2)}) collective-permute-start(bf16[320,128]{1,0:T(8,128)(2,1)S(1)} %finish.1.own_ref), channel_id=1, source_target_pairs={{0,8},{2,10},{4,12},{6,14},{8,0},{10,2},{12,4},{14,6},{1,9},{3,11}... | collective-permute-start | bytes 245768 | tf_op jit(solution)/shard_map/ppermute | solution.py:37
  136.4 10.9 %collective-permute-start.7 = (bf16[144,256]{1,0:T(8,128)(2,1)S(1)}, bf16[144,256]{1,0:T(8,128)(2,1)S(1)}, u32[]{:S(2)}, u32[]{:S(2)}) collective-permute-start(bf16[144,256]{1,0:T(8,128)(2,1)S(1)} %get-tuple-element.14), channel_id=1, source_target_pairs={{0,8},{2,10},{4,12},{6,14},{8,0},{10,2},{12,4},{14,6},{1,9},{3,11}... | collective-permute-start | bytes 221192 | tf_op jit(solution)/shard_map/ppermute | solution.py:37
Sparse Core Ops, SparseCore 0:
  9.4 65.4 all-gather.2

commit v4 on v3

--- a/solution.py
+++ b/solution.py
@@ -37,6 +37,10 @@
     return lax.ppermute(block, "y", [(i, (i + NY // 2) % NY) for i in range(NY)])
 
 
+def swap_cores(block):
+    return lax.ppermute(block, "c", [(0, 1), (1, 0)])
+
+
 def shifted(block, axis, count, by):
     return lax.ppermute(block, axis, [(i, (i + by) % count) for i in range(count)])
 
@@ -53,15 +57,19 @@
     )
 
 
-def project_kernel(tokens_ref, gain_ref, w0_ref, w1_ref, w2_ref, w3_ref, out_ref):
+def project_kernel(core_ref, mine_ref, mate_ref, gain_ref, w0_ref, w1_ref, w2_ref, w3_ref, out_ref):
     weights = jnp.concatenate([w[: 2 * HD, :] for w in (w0_ref, w1_ref, w2_ref, w3_ref)], axis=0)
     gain = gain_ref[...]
+    is_zero = core_ref[0] == 0
     rows = []
     stats = []
     for request in range(NZ):
         tall = []
         for y in range(NY):
-            halves = [tokens_ref[y * NC + c, request].astype(jnp.float32) for c in range(NC)]
+            mine = mine_ref[y, request].astype(jnp.float32)
+            mate = mate_ref[y, request].astype(jnp.float32)
+            zero = jnp.broadcast_to(is_zero, mine.shape)
+            halves = [jnp.where(zero, mine, mate), jnp.where(zero, mate, mine)]
             tall.append(
                 jnp.concatenate(
                     [halves[c][:, k * HD : (k + 1) * HD] for k in range(NX) for c in range(NC)],
@@ -102,6 +110,20 @@
         sin = sin_ref[...] if group < QS else fsin_ref[...]
         turned = total * cos + pltpu.roll(total, HD // 2, 1) * sin
         out_ref[pl.ds(group * ROWS, ROWS), :] = turned.astype(jnp.bfloat16)
+
+
+def pick_kernel(rows_ref, store_ref, *refs):
+    outs, sem = refs[:NX], refs[NX]
+    copies = []
+    for k in (2, 1, 3, 0):
+        for i in range(NZ):
+            row = rows_ref[((NX - k) % NX) * NZ + i]
+            copies.append(
+                pltpu.make_async_copy(store_ref.at[row], outs[k].at[i], sem.at[k * NZ + i])
+            )
+            copies[-1].start()
+    for copy in copies:
+        copy.wait()
 
 
 def attend_block(kv_ref, slots, queries, eff_ref, pos, run_ref, acc_ref):
@@ -226,34 +248,45 @@
 
     store = lax.all_gather(cache_store[:, 0], "z", axis=0, tiled=True)
 
-    blocks = hidden[0].reshape(NY, 8, 2, NC, HD).transpose(2, 0, 3, 1, 4)
-    blocks = jnp.broadcast_to(blocks[None], (4, 2, NY, NC, 8, HD))
-    blocks = blocks.reshape(NZ * NY * NC, 8, HD)
-    blocks = lax.all_to_all(blocks, ("z", "y", "c"), 0, 0, tiled=True)
-    blocks = blocks.reshape(NZ, NX, 4, 8, HD)
-    blocks = lax.dynamic_index_in_dim(blocks, z // 2, 2, keepdims=False)
+    states = hidden[0].reshape(ROWS, 2, NC, HD)
+    keep = lax.dynamic_index_in_dim(states, c, 2, keepdims=False)
+    give = lax.dynamic_index_in_dim(states, 1 - c, 2, keepdims=False)
+    taken = swap_cores(give)
+    pairs = jnp.where(c == 0, jnp.stack([keep, taken]), jnp.stack([taken, keep]))
+    blocks = pairs.reshape(2, NY, 8, 2, HD).transpose(0, 3, 1, 2, 4)
+    blocks = jnp.broadcast_to(blocks[None], (2, 2, 2, NY, 8, HD)).reshape(NZ * NY, 8, HD)
+    weight = jnp.concatenate([q_weight[:, 0], kv_weight[:, 0]], axis=1)
+    blocks = lax.all_to_all(blocks, ("z", "y"), 0, 0, tiled=True)
+    blocks = blocks.reshape(NZ, NX, 2, 8, HD)
+    blocks = lax.dynamic_index_in_dim(blocks, z // 4, 2, keepdims=False)
     blocks = jnp.concatenate([blocks, blocks], axis=1)
     blocks = lax.dynamic_slice_in_dim(blocks, x, NX, 1)
     blocks = blocks.transpose(0, 2, 1, 3).reshape(NZ, 8, NX * HD)
     tokens = lax.all_to_all(
-        jnp.broadcast_to(blocks[None], (NY * NC, NZ, 8, NX * HD)), TP, 0, 0, tiled=True
-    )
+        jnp.broadcast_to(blocks[None], (NY, NZ, 8, NX * HD)), "y", 0, 0, tiled=True
+    )
+    mate_tokens = swap_cores(tokens)
 
     listed = jnp.pad(own_list.astype(jnp.bfloat16)[None, :], ((0, 15), (0, COLS - MAXC)))
-    weight = jnp.concatenate([q_weight[:, 0], kv_weight[:, 0]], axis=1)
     weight = jnp.concatenate([weight, listed], axis=0)
     weights = [weight] + [shifted(weight, "x", NX, -k) for k in range(1, NX)]
     gain = lax.dynamic_index_in_dim(norm_gain.reshape(NX, NZ, NC * HD), z, 1, keepdims=False)
     gain = lax.dynamic_slice_in_dim(jnp.concatenate([gain, gain], axis=0), x, NX, 0)
     gain = gain.astype(jnp.float32).reshape(1, NX * NC * HD)
 
-    partial = call(
+    smem = pl.BlockSpec(memory_space=pltpu.SMEM)
+    vmem = pl.BlockSpec(memory_space=pltpu.VMEM)
+    partial = pl.pallas_call(
         project_kernel,
-        jax.ShapeDtypeStruct((NZ, ROWS + 8, COLS), jnp.bfloat16),
-        "project",
-        flops=2 * NZ * ROWS * 1024 * COLS,
-        bytes_accessed=1 << 22,
-    )(tokens, gain, *weights)
+        out_shape=jax.ShapeDtypeStruct((NZ, ROWS + 8, COLS), jnp.bfloat16),
+        in_specs=[smem] + [vmem] * 7,
+        out_specs=vmem,
+        name="project",
+        compiler_params=pltpu.CompilerParams(vmem_limit_bytes=32 * 1024 * 1024),
+        cost_estimate=pl.CostEstimate(
+            flops=2 * NZ * ROWS * 1024 * COLS, bytes_accessed=1 << 22, transcendentals=0
+        ),
+    )(c.reshape(1), tokens, mate_tokens, gain, *weights)
     parts = lax.all_to_all(partial, "z", 0, 0, tiled=True)
 
     lists = jnp.stack([w[NC * HD, :MAXC] for w in weights]).astype(jnp.int32)
@@ -264,9 +297,17 @@
     wanted = jnp.any(lists[:, :, None, None] == held[None, None], axis=1)
     send_rows = jnp.sum(jnp.where(wanted, int_rows, 0), axis=2) + steps[None, :] * CH_DEV
     send_rows, _ = lax.optimization_barrier((send_rows, partial[0, ROWS:, :HD]))
-    arrived = [store[send_rows[0]]]
-    for k in range(1, NX):
-        arrived.append(shifted(store[send_rows[NX - k]], "x", NX, -k))
+    picked = pl.pallas_call(
+        pick_kernel,
+        out_shape=[jax.ShapeDtypeStruct((NZ, HALF, 2 * HD), jnp.bfloat16)] * NX,
+        in_specs=[smem, pl.BlockSpec(memory_space=pl.ANY)],
+        out_specs=[vmem] * NX,
+        scratch_shapes=[pltpu.SemaphoreType.DMA((NX * NZ,))],
+        name="pick",
+        compiler_params=pltpu.CompilerParams(vmem_limit_bytes=32 * 1024 * 1024),
+        cost_estimate=pl.CostEstimate(flops=0, bytes_accessed=1 << 22, transcendentals=0),
+    )(send_rows.reshape(-1), store)
+    arrived = [picked[0]] + [shifted(picked[k], "x", NX, -k) for k in range(1, NX)]
 
     frequency = jnp.exp(
         -math.log(theta_base) * jnp.arange(HD // 2, dtype=jnp.float32) / (HD // 2)
@@ -302,8 +343,6 @@
     fresh_eff = jnp.broadcast_to(fresh_eff[:, None], (ROWS, HD))
     pos_row = jnp.tile(positions, 2 * QS).reshape(1, 2 * QROWS)
 
-    smem = pl.BlockSpec(memory_space=pltpu.SMEM)
-    vmem = pl.BlockSpec(memory_space=pltpu.VMEM)
     early, late = (0, 1, 3), (2,)
     params = pltpu.CompilerParams(vmem_limit_bytes=32 * 1024 * 1024)
     run_shapes = [

time: 156 us -> 151 us (0.968)
  local copies, waits for them, and re-layouts: 16.5 us -> 5.91 us
  Pallas kernels: 7.94 us -> 13.6 us
    gather x4 -> x0, local copies, waits for them, and re-layouts: 12.7 us -> none  [the longest x3 9.93 us: body(): arrived.append(shifted(store[send_rows[NX - k]], 'x', NX, -k))]
    all_to_all x2, waiting for transfers between devices: 36.8 us -> 28.3 us  [the longest x1 16.1 us: body(): lax.all_to_all(jnp.broadcast_to(blocks[None], (NY, NZ, 8, NX * HD)), 'y',...]
    ppermute x2, waiting for transfers between devices: 10.3 us -> 16.2 us  [exchange(): lax.ppermute(block, 'y', [(i, (i + NY // 2) % NY) for i in range(NY)])]
    pallas_call x1 -> x2, Pallas kernels: 1.88 us -> 6.59 us  [the longest x1 4.67 us: body(): pl.pallas_call(pick_kernel, out_shape=[jax.ShapeDtypeStruct((NZ, HALF, 2...]
    ppermute x2, starting transfers between devices: 9.02 us -> 4.94 us  [exchange(): lax.ppermute(block, 'y', [(i, (i + NY // 2) % NY) for i in range(NY)])]
    ppermute x0 -> x2, starting transfers between devices: none -> 3.83 us  [swap_cores(): return lax.ppermute(block, 'c', [(0, 1), (1, 0)])]
    unnamed x6 -> x8, local copies, waits for them, and re-layouts: 0.02 us -> 2.22 us
    all_to_all x1, waiting for transfers between devices: 0.79 us -> 2.96 us  [body(): parts = lax.all_to_all(partial, 'z', 0, 0, tiled=True)]
  transfers between devices with their start and end apart: 12 -> 14, of which waited for: 6 -> 8; matrix products, arithmetic and copies ran while one was open for 14% -> 6% of each run, Pallas kernels for 4% -> 8%
where the time goes in v4:
time: 151 us; the launch traced here: 150 us
  waiting for transfers between devices  58.1 us (38%)
  starting transfers between devices  52.9 us (35%)
  between operations  13.8 us (9%)
  Pallas kernels  13.6 us (9%)
  local copies, waits for them, and re-layouts  5.91 us (4%)
  other arithmetic  5.56 us (4%)
    ppermute x6, starting transfers between devices, shifted(): lax.ppermute(block, axis, [(i, (i + by) % count) for i in range(count)])  19.8 us
    ppermute x2, waiting for transfers between devices, exchange(): lax.ppermute(block, 'y', [(i, (i + NY // 2) % NY) for i in range(NY)])  16.2 us
    all_to_all x1, waiting for transfers between devices, body(): lax.all_to_all(jnp.broadcast_to(blocks[None], (NY, NZ, 8, NX * HD)), 'y',...  16.1 us
    all_to_all x1, starting transfers between devices, body(): blocks = lax.all_to_all(blocks, ('z', 'y'), 0, 0, tiled=True)  15.8 us
    all_to_all x1, waiting for transfers between devices, body(): blocks = lax.all_to_all(blocks, ('z', 'y'), 0, 0, tiled=True)  12.3 us
    ppermute x6, waiting for transfers between devices, shifted(): lax.ppermute(block, axis, [(i, (i + by) % count) for i in range(count)])  8.42 us
    all_to_all x1, starting transfers between devices, body(): parts = lax.all_to_all(partial, 'z', 0, 0, tiled=True)  5.05 us
    ppermute x2, starting transfers between devices, exchange(): lax.ppermute(block, 'y', [(i, (i + NY // 2) % NY) for i in range(NY)])  4.94 us
  transfers between devices with their start and end apart: 14, of which 8 were waited for; matrix products, arithmetic and copies ran while one was open for 6% of the time, Pallas kernels for 8%

profile of v4, /device:TPU:64, one launch (start us, length us, event | category | flops | bytes accessed | tf_op | source)
XLA Modules:
  0.0 149.9 jit_solution(17905513726880394463)
XLA Ops:
  7.9 1.0 fusion.1.w0_ref
  9.0 4.7 %collective-permute-start.2 = (bf16[272,640]{1,0:T(8,128)(2,1)S(1)}, bf16[272,640]{1,0:T(8,128)(2,1)S(1)}, u32[]{:S(2)}, u32[]{:S(2)}) collective-permute-start(bf16[272,640]{1,0:T(8,128)(2,1)S(1)} %fusion.1.w0_ref), channel_id=1, source_target_pairs={{0,384},{128,0},{256,128},{384,256},{1,385},{129,1},{257,129},{385... | collective-permute-start | bytes 1044488 | tf_op jit(solution)/shard_map/ppermute | solution.py:45
  13.6 2.7 %collective-permute-start.3 = (bf16[272,640]{1,0:T(8,128)(2,1)S(1)}, bf16[272,640]{1,0:T(8,128)(2,1)S(1)}, u32[]{:S(2)}, u32[]{:S(2)}) collective-permute-start(bf16[272,640]{1,0:T(8,128)(2,1)S(1)} %fusion.1.w0_ref), channel_id=1, source_target_pairs={{0,256},{128,384},{256,0},{384,128},{1,257},{129,385},{257,1},{385... | collective-permute-start | bytes 1044488 | tf_op jit(solution)/shard_map/ppermute | solution.py:45
  16.3 2.8 %collective-permute-start.4 = (bf16[272,640]{1,0:T(8,128)(2,1)S(1)}, bf16[272,640]{1,0:T(8,128)(2,1)S(1)}, u32[]{:S(2)}, u32[]{:S(2)}) collective-permute-start(bf16[272,640]{1,0:T(8,128)(2,1)S(1)} %fusion.1.w0_ref), channel_id=1, source_target_pairs={{0,128},{128,256},{256,384},{384,0},{1,129},{129,257},{257,385},{3... | collective-permute-start | bytes 1044488 | tf_op jit(solution)/shard_map/ppermute | solution.py:45
  19.2 0.9 reshape_squeeze.3
  20.2 1.9 %collective-permute-start = (bf16[64,2,128]{2,0,1:T(8,128)(2,1)S(1)}, bf16[64,2,128]{2,0,1:T(8,128)(2,1)S(1)}, u32[]{:S(2)}, u32[]{:S(2)}) collective-permute-start(bf16[64,2,128]{2,0,1:T(8,128)(2,1)S(1)} %bitcast.42), channel_id=1, source_target_pairs={{0,1},{1,0},{2,3},{3,2},{4,5},{5,4},{6,7},{7,6},{8,9},{9,8},{10,11... | collective-permute-start | bytes 98312 | tf_op jit(solution)/shard_map/ppermute | solution.py:41
  22.1 0.7 reshape.218
  22.9 0.9 select_reduce_fusion.1
  25.1 15.8 %all-to-all-start = ((bf16[64,8,128]{2,1,0:T(8,128)(2,1)}), bf16[64,8,128]{2,1,0:T(8,128)(2,1)S(1)}, u32[]{:S(2)}, u32[]{:S(2)}) async-start(bf16[64,8,128]{2,1,0:T(8,128)(2,1)} %bitcast.5), calls=%async_computation | async-start | bytes 262144 | tf_op jit(solution)/shard_map/all_to_all | solution.py:259
  41.0 12.3 %all-to-all-done = bf16[64,8,128]{2,1,0:T(8,128)(2,1)S(1)} async-done(((bf16[64,8,128]{2,1,0:T(8,128)(2,1)}), bf16[64,8,128]{2,1,0:T(8,128)(2,1)S(1)}, u32[]{:S(2)}, u32[]{:S(2)}) %all-to-all-start) | async-done | bytes 131104 | tf_op jit(solution)/shard_map/all_to_all | solution.py:259
  53.3 0.8 broadcast_in_dim.91
  54.2 3.5 %all-to-all-start.1 = ((bf16[8,8,8,512]{3,2,1,0:T(8,128)(2,1)}), bf16[8,8,8,512]{3,2,1,0:T(8,128)(2,1)S(1)}, u32[]{:S(2)}, u32[]{:S(2)}) async-start(bf16[8,8,8,512]{3,2,1,0:T(8,128)(2,1)} %broadcast_in_dim.91), calls=%async_computation.1 | async-start | bytes 1048576 | tf_op jit(solution)/shard_map/all_to_all | solution.py:265
  58.2 16.1 %all-to-all-done.1.mine_ref = bf16[8,8,8,512]{3,2,1,0:T(8,128)(2,1)S(1)} async-done(((bf16[8,8,8,512]{3,2,1,0:T(8,128)(2,1)}), bf16[8,8,8,512]{3,2,1,0:T(8,128)(2,1)S(1)}, u32[]{:S(2)}, u32[]{:S(2)}) %all-to-all-start.1) | async-done | bytes 524320 | tf_op jit(solution)/shard_map/all_to_all | solution.py:265
  74.3 1.9 %collective-permute-start.1 = (bf16[8,8,8,512]{3,2,1,0:T(8,128)(2,1)S(1)}, bf16[8,8,8,512]{3,2,1,0:T(8,128)(2,1)S(1)}, u32[]{:S(2)}, u32[]{:S(2)}) collective-permute-start(bf16[8,8,8,512]{3,2,1,0:T(8,128)(2,1)S(1)} %all-to-all-done.1.mine_ref), channel_id=1, source_target_pairs={{0,1},{1,0},{2,3},{3,2},{4,5},{5,4},{6,7},{7,6},{8,9},{9,8},{10,11... | collective-permute-start | bytes 1572872 | tf_op jit(solution)/shard_map/ppermute | solution.py:41
  76.6 1.5 collective-permute-done.1.mate_ref
  78.1 1.9 %project.1 = bf16[8,72,640]{2,1,0:T(8,128)(2,1)} custom-call(s32[1]{0:T(128)} %bitcast.core_ref, bf16[8,8,8,512]{3,2,1,0:T(8,128)(2,1)S(1)} %all-to-all-done.1.mine_ref, bf16[8,8,8,512]{3,2,1,0:T(8,128)(2,1)S(1)} %collective-permute-done.1.mate_ref, f32[1,1024]{1,0:T(1,128)S(1)} %bitcast.37, bf16[272,640]{1,0:T(8,128)(2,1)S(1)} %fusion.1.w0_ref, ...), custom_call_target="tpu_custom_call" | custom-call | flops 671088640 | bytes 4194304 | tf_op jit(solution)/shard_map/project/pallas_call | solution.py:279
  80.0 5.0 %all-to-all-start.2 = ((bf16[8,72,640]{2,1,0:T(8,128)(2,1)}), bf16[8,72,640]{2,1,0:T(8,128)(2,1)S(1)}, u32[]{:S(2)}, u32[]{:S(2)}) async-start(bf16[8,72,640]{2,1,0:T(8,128)(2,1)} %project.1), calls=%async_computation.2 | async-start | bytes 1474560 | tf_op jit(solution)/shard_map/all_to_all | solution.py:290
  86.7 2.2 %copy-done = bf16[64,1,128,256]{3,2,1,0:T(8,128)(2,1)S(1)} copy-done((bf16[64,1,128,256]{3,2,1,0:T(8,128)(2,1)S(1)}, bf16[64,1,128,256]{3,2,1,0:T(8,128)(2,1)}, u32[]{:S(2)}) %copy-start) | copy-done | bytes 4194328
  88.9 4.7 %pick.1 = (bf16[8,128,256]{2,1,0:T(8,128)(2,1)S(1)}, bf16[8,128,256]{2,1,0:T(8,128)(2,1)}, bf16[8,128,256]{2,1,0:T(8,128)(2,1)S(1)}, bf16[8,128,256]{2,1,0:T(8,128)(2,1)}) custom-call(s32[32]{0:T(128)S(1)} %reshape.222.rows_ref, bf16[64,128,256]{2,1,0:T(8,128)(2,1)S(1)} %bitcast.36), custom_call_target="tpu_custom_call" | custom-call | bytes 4194304 | tf_op jit(solution)/shard_map/pick/pallas_call | solution.py:300
  93.5 4.3 %collective-permute-start.6 = (bf16[8,128,256]{2,1,0:T(8,128)(2,1)}, bf16[8,128,256]{2,1,0:T(8,128)(2,1)S(1)}, u32[]{:S(2)}, u32[]{:S(2)}) collective-permute-start(bf16[8,128,256]{2,1,0:T(8,128)(2,1)} %get-tuple-element.15), channel_id=1, source_target_pairs={{0,384},{128,0},{256,128},{384,256},{1,385},{129,1},{257,129},{385... | collective-permute-start | bytes 1572872 | tf_op jit(solution)/shard_map/ppermute | solution.py:45
  97.8 1.9 %collective-permute-start.7 = (bf16[8,128,256]{2,1,0:T(8,128)(2,1)}, bf16[8,128,256]{2,1,0:T(8,128)(2,1)}, u32[]{:S(2)}, u32[]{:S(2)}) collective-permute-start(bf16[8,128,256]{2,1,0:T(8,128)(2,1)} %get-tuple-element.16), channel_id=1, source_target_pairs={{0,128},{128,256},{256,384},{384,0},{1,129},{129,257},{257,385},{3... | collective-permute-start | bytes 1572872 | tf_op jit(solution)/shard_map/ppermute | solution.py:45
  99.8 3.4 %collective-permute-start.8 = (bf16[8,128,256]{2,1,0:T(8,128)(2,1)S(1)}, bf16[8,128,256]{2,1,0:T(8,128)(2,1)S(1)}, u32[]{:S(2)}, u32[]{:S(2)}) collective-permute-start(bf16[8,128,256]{2,1,0:T(8,128)(2,1)S(1)} %get-tuple-element.19), channel_id=1, source_target_pairs={{0,256},{128,384},{256,0},{384,128},{1,257},{129,385},{257,1},{385... | collective-permute-start | bytes 1572872 | tf_op jit(solution)/shard_map/ppermute | solution.py:45
  103.3 3.0 %all-to-all-done.2.parts_ref = bf16[8,72,640]{2,1,0:T(8,128)(2,1)S(1)} async-done(((bf16[8,72,640]{2,1,0:T(8,128)(2,1)}), bf16[8,72,640]{2,1,0:T(8,128)(2,1)S(1)}, u32[]{:S(2)}, u32[]{:S(2)}) %all-to-all-start.2) | async-done | bytes 737312 | tf_op jit(solution)/shard_map/all_to_all | solution.py:290
  106.5 2.5 %collective-permute-start.5 = (bf16[320,128]{1,0:T(8,128)(2,1)S(1)}, bf16[320,128]{1,0:T(8,128)(2,1)S(1)}, u32[]{:S(2)}, u32[]{:S(2)}) collective-permute-start(bf16[320,128]{1,0:T(8,128)(2,1)S(1)} %finish.1.own_ref), channel_id=1, source_target_pairs={{0,8},{2,10},{4,12},{6,14},{8,0},{10,2},{12,4},{14,6},{1,9},{3,11}... | collective-permute-start | bytes 245768 | tf_op jit(solution)/shard_map/ppermute | solution.py:37
  109.1 8.4 %collective-permute-done.5.other_ref = bf16[320,128]{1,0:T(8,128)(2,1)S(1)} collective-permute-done((bf16[320,128]{1,0:T(8,128)(2,1)S(1)}, bf16[320,128]{1,0:T(8,128)(2,1)S(1)}, u32[]{:S(2)}, u32[]{:S(2)}) %collective-permute-start.5) | collective-permute-done | bytes 81952 | tf_op jit(solution)/shard_map/ppermute | solution.py:37
  117.5 3.1 %collective-permute-done.6.refs_1_ = bf16[8,128,256]{2,1,0:T(8,128)(2,1)S(1)} collective-permute-done((bf16[8,128,256]{2,1,0:T(8,128)(2,1)}, bf16[8,128,256]{2,1,0:T(8,128)(2,1)S(1)}, u32[]{:S(2)}, u32[]{:S(2)}) %collective-permute-start.6) | collective-permute-done | bytes 524320 | tf_op jit(solution)/shard_map/ppermute | solution.py:45
  120.6 5.3 %collective-permute-done.7.refs_2_ = bf16[8,128,256]{2,1,0:T(8,128)(2,1)} collective-permute-done((bf16[8,128,256]{2,1,0:T(8,128)(2,1)}, bf16[8,128,256]{2,1,0:T(8,128)(2,1)}, u32[]{:S(2)}, u32[]{:S(2)}) %collective-permute-start.7) | collective-permute-done | bytes 524320 | tf_op jit(solution)/shard_map/ppermute | solution.py:45
  125.9 4.8 %attend_early.1 = (f32[128,512]{1,0:T(8,128)S(1)}, f32[8,512]{1,0:T(8,128)S(1)}) custom-call(s32[1]{0:T(128)} %bitcast.15.flag_ref, bf16[320,128]{1,0:T(8,128)(2,1)S(1)} %finish.1.own_ref, bf16[320,128]{1,0:T(8,128)(2,1)S(1)} %collective-permute-done.5.other_ref, s32[128,32]{1,0:T(8,128)S(1)} %or_select_fusion.eff_ref, ...), custom_call_target="tpu_custom_call" | custom-call | flops 805306368 | bytes 1572864 | tf_op jit(solution)/shard_map/attend_early/pallas_call | solution.py:357
  130.7 1.3 attend_late.1
  132.0 2.5 %collective-permute-start.9 = (bf16[144,256]{1,0:T(8,128)(2,1)S(1)}, bf16[144,256]{1,0:T(8,128)(2,1)S(1)}, u32[]{:S(2)}, u32[]{:S(2)}) collective-permute-start(bf16[144,256]{1,0:T(8,128)(2,1)S(1)} %get-tuple-element.22), channel_id=1, source_target_pairs={{0,8},{2,10},{4,12},{6,14},{8,0},{10,2},{12,4},{14,6},{1,9},{3,11}... | collective-permute-start | bytes 221192 | tf_op jit(solution)/shard_map/ppermute | solution.py:37
  134.5 7.8 %collective-permute-done.9.got_ref = bf16[144,256]{1,0:T(8,128)(2,1)S(1)} collective-permute-done((bf16[144,256]{1,0:T(8,128)(2,1)S(1)}, bf16[144,256]{1,0:T(8,128)(2,1)S(1)}, u32[]{:S(2)}, u32[]{:S(2)}) %collective-permute-start.9) | collective-permute-done | bytes 73760 | tf_op jit(solution)/shard_map/ppermute | solution.py:37
  142.3 0.8 merge.1
  (58 shorter events, 5.9 us)
Async XLA Ops:
  6.5 69.7 %copy-start.2 = (s32[1,64]{1,0:T(1,128)S(1)}, s32[1,64]{1,0:T(1,128)}, u32[]{:S(2)}) copy-start(s32[1,64]{1,0:T(1,128)} %param.15) | copy-start | bytes 772
  6.5 80.1 %all-gather.3.cloned.1.call-start = ((), (), s32[]{:S(2)}) async-start(), calls=%async_computation.3 | async-start | bytes 4718592 | tf_op jit(solution)/shard_map/all_gather | solution.py:249
  8.9 76.2 %copy-start.1 = (s32[256]{0:T(256)S(1)}, s32[256]{0:T(256)}, u32[]{:S(2)}) copy-start(s32[256]{0:T(256)} %param.13) | copy-start | bytes 3076
  9.0 67.6 %collective-permute-start.2 = (bf16[272,640]{1,0:T(8,128)(2,1)S(1)}, bf16[272,640]{1,0:T(8,128)(2,1)S(1)}, u32[]{:S(2)}, u32[]{:S(2)}) collective-permute-start(bf16[272,640]{1,0:T(8,128)(2,1)S(1)} %fusion.1.w0_ref), channel_id=1, source_target_pairs={{0,384},{128,0},{256,128},{384,256},{1,385},{129,1},{257,129},{385... | collective-permute-start | bytes 1044488 | tf_op jit(solution)/shard_map/ppermute | solution.py:45
  13.6 62.9 %collective-permute-start.3 = (bf16[272,640]{1,0:T(8,128)(2,1)S(1)}, bf16[272,640]{1,0:T(8,128)(2,1)S(1)}, u32[]{:S(2)}, u32[]{:S(2)}) collective-permute-start(bf16[272,640]{1,0:T(8,128)(2,1)S(1)} %fusion.1.w0_ref), channel_id=1, source_target_pairs={{0,256},{128,384},{256,0},{384,128},{1,257},{129,385},{257,1},{385... | collective-permute-start | bytes 1044488 | tf_op jit(solution)/shard_map/ppermute | solution.py:45
  16.3 60.2 %collective-permute-start.4 = (bf16[272,640]{1,0:T(8,128)(2,1)S(1)}, bf16[272,640]{1,0:T(8,128)(2,1)S(1)}, u32[]{:S(2)}, u32[]{:S(2)}) collective-permute-start(bf16[272,640]{1,0:T(8,128)(2,1)S(1)} %fusion.1.w0_ref), channel_id=1, source_target_pairs={{0,128},{128,256},{256,384},{384,0},{1,129},{129,257},{257,385},{3... | collective-permute-start | bytes 1044488 | tf_op jit(solution)/shard_map/ppermute | solution.py:45
  20.2 4.2 %collective-permute-start = (bf16[64,2,128]{2,0,1:T(8,128)(2,1)S(1)}, bf16[64,2,128]{2,0,1:T(8,128)(2,1)S(1)}, u32[]{:S(2)}, u32[]{:S(2)}) collective-permute-start(bf16[64,2,128]{2,0,1:T(8,128)(2,1)S(1)} %bitcast.42), channel_id=1, source_target_pairs={{0,1},{1,0},{2,3},{3,2},{4,5},{5,4},{6,7},{7,6},{8,9},{9,8},{10,11... | collective-permute-start | bytes 98312 | tf_op jit(solution)/shard_map/ppermute | solution.py:41
  25.1 28.1 %all-to-all-start = ((bf16[64,8,128]{2,1,0:T(8,128)(2,1)}), bf16[64,8,128]{2,1,0:T(8,128)(2,1)S(1)}, u32[]{:S(2)}, u32[]{:S(2)}) async-start(bf16[64,8,128]{2,1,0:T(8,128)(2,1)} %bitcast.5), calls=%async_computation | async-start | bytes 262144 | tf_op jit(solution)/shard_map/all_to_all | solution.py:259
  54.2 20.1 %all-to-all-start.1 = ((bf16[8,8,8,512]{3,2,1,0:T(8,128)(2,1)}), bf16[8,8,8,512]{3,2,1,0:T(8,128)(2,1)S(1)}, u32[]{:S(2)}, u32[]{:S(2)}) async-start(bf16[8,8,8,512]{3,2,1,0:T(8,128)(2,1)} %broadcast_in_dim.91), calls=%async_computation.1 | async-start | bytes 1048576 | tf_op jit(solution)/shard_map/all_to_all | solution.py:265
  74.3 3.8 %collective-permute-start.1 = (bf16[8,8,8,512]{3,2,1,0:T(8,128)(2,1)S(1)}, bf16[8,8,8,512]{3,2,1,0:T(8,128)(2,1)S(1)}, u32[]{:S(2)}, u32[]{:S(2)}) collective-permute-start(bf16[8,8,8,512]{3,2,1,0:T(8,128)(2,1)S(1)} %all-to-all-done.1.mine_ref), channel_id=1, source_target_pairs={{0,1},{1,0},{2,3},{3,2},{4,5},{5,4},{6,7},{7,6},{8,9},{9,8},{10,11... | collective-permute-start | bytes 1572872 | tf_op jit(solution)/shard_map/ppermute | solution.py:41
  80.0 26.3 %all-to-all-start.2 = ((bf16[8,72,640]{2,1,0:T(8,128)(2,1)}), bf16[8,72,640]{2,1,0:T(8,128)(2,1)S(1)}, u32[]{:S(2)}, u32[]{:S(2)}) async-start(bf16[8,72,640]{2,1,0:T(8,128)(2,1)} %project.1), calls=%async_computation.2 | async-start | bytes 1474560 | tf_op jit(solution)/shard_map/all_to_all | solution.py:290
  86.7 2.2 %copy-start = (bf16[64,1,128,256]{3,2,1,0:T(8,128)(2,1)S(1)}, bf16[64,1,128,256]{3,2,1,0:T(8,128)(2,1)}, u32[]{:S(2)}) copy-start(bf16[64,1,128,256]{3,2,1,0:T(8,128)(2,1)} %all-gather.3.cloned.1.call-done) | copy-start | bytes 12582916
  93.5 27.0 %collective-permute-start.6 = (bf16[8,128,256]{2,1,0:T(8,128)(2,1)}, bf16[8,128,256]{2,1,0:T(8,128)(2,1)S(1)}, u32[]{:S(2)}, u32[]{:S(2)}) collective-permute-start(bf16[8,128,256]{2,1,0:T(8,128)(2,1)} %get-tuple-element.15), channel_id=1, source_target_pairs={{0,384},{128,0},{256,128},{384,256},{1,385},{129,1},{257,129},{385... | collective-permute-start | bytes 1572872 | tf_op jit(solution)/shard_map/ppermute | solution.py:45
  97.8 28.1 %collective-permute-start.7 = (bf16[8,128,256]{2,1,0:T(8,128)(2,1)}, bf16[8,128,256]{2,1,0:T(8,128)(2,1)}, u32[]{:S(2)}, u32[]{:S(2)}) collective-permute-start(bf16[8,128,256]{2,1,0:T(8,128)(2,1)} %get-tuple-element.16), channel_id=1, source_target_pairs={{0,128},{128,256},{256,384},{384,0},{1,129},{129,257},{257,385},{3... | collective-permute-start | bytes 1572872 | tf_op jit(solution)/shard_map/ppermute | solution.py:45
  99.8 30.9 %collective-permute-start.8 = (bf16[8,128,256]{2,1,0:T(8,128)(2,1)S(1)}, bf16[8,128,256]{2,1,0:T(8,128)(2,1)S(1)}, u32[]{:S(2)}, u32[]{:S(2)}) collective-permute-start(bf16[8,128,256]{2,1,0:T(8,128)(2,1)S(1)} %get-tuple-element.19), channel_id=1, source_target_pairs={{0,256},{128,384},{256,0},{384,128},{1,257},{129,385},{257,1},{385... | collective-permute-start | bytes 1572872 | tf_op jit(solution)/shard_map/ppermute | solution.py:45
  106.5 11.0 %collective-permute-start.5 = (bf16[320,128]{1,0:T(8,128)(2,1)S(1)}, bf16[320,128]{1,0:T(8,128)(2,1)S(1)}, u32[]{:S(2)}, u32[]{:S(2)}) collective-permute-start(bf16[320,128]{1,0:T(8,128)(2,1)S(1)} %finish.1.own_ref), channel_id=1, source_target_pairs={{0,8},{2,10},{4,12},{6,14},{8,0},{10,2},{12,4},{14,6},{1,9},{3,11}... | collective-permute-start | bytes 245768 | tf_op jit(solution)/shard_map/ppermute | solution.py:37
  132.0 10.3 %collective-permute-start.9 = (bf16[144,256]{1,0:T(8,128)(2,1)S(1)}, bf16[144,256]{1,0:T(8,128)(2,1)S(1)}, u32[]{:S(2)}, u32[]{:S(2)}) collective-permute-start(bf16[144,256]{1,0:T(8,128)(2,1)S(1)} %get-tuple-element.22), channel_id=1, source_target_pairs={{0,8},{2,10},{4,12},{6,14},{8,0},{10,2},{12,4},{14,6},{1,9},{3,11}... | collective-permute-start | bytes 221192 | tf_op jit(solution)/shard_map/ppermute | solution.py:37
Sparse Core Ops, SparseCore 0:
  9.4 62.6 all-gather.2

commit v5 on v4

--- a/solution.py
+++ b/solution.py
@@ -113,13 +113,15 @@
 
 
 def pick_kernel(rows_ref, store_ref, *refs):
-    outs, sem = refs[:NX], refs[NX]
+    outs, sem = refs[: NX - 1], refs[NX - 1]
     copies = []
-    for k in (2, 1, 3, 0):
+    for k in (2, 1, 3):
         for i in range(NZ):
-            row = rows_ref[((NX - k) % NX) * NZ + i]
+            row = rows_ref[(NX - k) * NZ + i]
             copies.append(
-                pltpu.make_async_copy(store_ref.at[row], outs[k].at[i], sem.at[k * NZ + i])
+                pltpu.make_async_copy(
+                    store_ref.at[row], outs[k - 1].at[i], sem.at[(k - 1) * NZ + i]
+                )
             )
             copies[-1].start()
     for copy in copies:
@@ -151,8 +153,32 @@
     acc_ref[...] = acc
 
 
-def attend_early_kernel(which, flag_ref, own_ref, other_ref, eff_ref, fresh_eff_ref, pos_ref, *refs):
-    kv_refs, (acc_ref, run_ref) = refs[: len(which)], refs[len(which) :]
+def attend_slots(k, kv_ref, queries, eff_ref, pos, run_ref, acc_ref):
+    for half in range(0, NZ, 4):
+        slots = [(half + i, k * NZ + half + i) for i in range(4)]
+        attend_block(kv_ref, slots, queries, eff_ref, pos, run_ref, acc_ref)
+
+
+def attend_own_kernel(
+    flag_ref,
+    rows_ref,
+    own_ref,
+    other_ref,
+    eff_ref,
+    fresh_eff_ref,
+    pos_ref,
+    store_ref,
+    acc_ref,
+    run_ref,
+    kv_ref,
+    sem,
+):
+    copies = [
+        pltpu.make_async_copy(store_ref.at[rows_ref[i]], kv_ref.at[i], sem.at[i])
+        for i in range(NZ)
+    ]
+    for copy in copies:
+        copy.start()
     is_first = flag_ref[0] == 0
     queries = jnp.concatenate([own_ref[:QROWS, :], other_ref[:QROWS, :]], axis=0)
     own_piece = own_ref[QROWS:, :]
@@ -171,27 +197,39 @@
     acc_ref[...] = lax.dot_general(
         fresh_values, weights.astype(jnp.bfloat16), TN, preferred_element_type=jnp.float32
     )
-    for k, kv_ref in zip(which, kv_refs):
-        for half in range(0, NZ, 4):
-            slots = [(half + i, k * NZ + half + i) for i in range(4)]
-            attend_block(kv_ref, slots, queries, eff_ref, pos, run_ref, acc_ref)
-
-
-def attend_late_kernel(
-    which, own_ref, other_ref, eff_ref, pos_ref, acc_in_ref, run_in_ref, *refs
+    for copy in copies:
+        copy.wait()
+    attend_slots(0, kv_ref, queries, eff_ref, pos, run_ref, acc_ref)
+
+
+def attend_near_kernel(
+    own_ref, other_ref, eff_ref, pos_ref, acc_in_ref, run_in_ref, kv1_ref, kv3_ref, acc_ref, run_ref
 ):
-    kv_refs, (own_out_ref, stat_ref, sent_ref, acc_ref, run_ref) = (
-        refs[: len(which)],
-        refs[len(which) :],
-    )
     queries = jnp.concatenate([own_ref[:QROWS, :], other_ref[:QROWS, :]], axis=0)
-    pos = pos_ref[...]
     acc_ref[...] = acc_in_ref[...]
     run_ref[...] = run_in_ref[...]
-    for k, kv_ref in zip(which, kv_refs):
-        for half in range(0, NZ, 4):
-            slots = [(half + i, k * NZ + half + i) for i in range(4)]
-            attend_block(kv_ref, slots, queries, eff_ref, pos, run_ref, acc_ref)
+    attend_slots(1, kv1_ref, queries, eff_ref, pos_ref[...], run_ref, acc_ref)
+    attend_slots(3, kv3_ref, queries, eff_ref, pos_ref[...], run_ref, acc_ref)
+
+
+def attend_far_kernel(
+    own_ref,
+    other_ref,
+    eff_ref,
+    pos_ref,
+    acc_in_ref,
+    run_in_ref,
+    kv2_ref,
+    own_out_ref,
+    stat_ref,
+    sent_ref,
+    acc_ref,
+    run_ref,
+):
+    queries = jnp.concatenate([own_ref[:QROWS, :], other_ref[:QROWS, :]], axis=0)
+    acc_ref[...] = acc_in_ref[...]
+    run_ref[...] = run_in_ref[...]
+    attend_slots(2, kv2_ref, queries, eff_ref, pos_ref[...], run_ref, acc_ref)
     peak = run_ref[0:1, :]
     total = run_ref[1:2, :]
     mixed = acc_ref[...] / total
@@ -248,34 +286,32 @@
 
     store = lax.all_gather(cache_store[:, 0], "z", axis=0, tiled=True)
 
-    states = hidden[0].reshape(ROWS, 2, NC, HD)
-    keep = lax.dynamic_index_in_dim(states, c, 2, keepdims=False)
-    give = lax.dynamic_index_in_dim(states, 1 - c, 2, keepdims=False)
-    taken = swap_cores(give)
-    pairs = jnp.where(c == 0, jnp.stack([keep, taken]), jnp.stack([taken, keep]))
-    blocks = pairs.reshape(2, NY, 8, 2, HD).transpose(0, 3, 1, 2, 4)
-    blocks = jnp.broadcast_to(blocks[None], (2, 2, 2, NY, 8, HD)).reshape(NZ * NY, 8, HD)
-    weight = jnp.concatenate([q_weight[:, 0], kv_weight[:, 0]], axis=1)
-    blocks = lax.all_to_all(blocks, ("z", "y"), 0, 0, tiled=True)
-    blocks = blocks.reshape(NZ, NX, 2, 8, HD)
-    blocks = lax.dynamic_index_in_dim(blocks, z // 4, 2, keepdims=False)
+    blocks = hidden[0].reshape(NY, 8, 2, NC, HD).transpose(0, 3, 2, 1, 4)
+    blocks = lax.all_to_all(blocks.reshape(NY * NC, 2, 8, HD), TP, 0, 0, tiled=True)
+    blocks = blocks.reshape(NX, 2, 2, 2, 8, HD).transpose(1, 2, 3, 0, 4, 5)
+    blocks = blocks.reshape(NZ, NX, 8, HD)
+    first_blocks = blocks
+    blocks = lax.all_to_all(blocks, "z", 0, 0, tiled=True)
     blocks = jnp.concatenate([blocks, blocks], axis=1)
     blocks = lax.dynamic_slice_in_dim(blocks, x, NX, 1)
     blocks = blocks.transpose(0, 2, 1, 3).reshape(NZ, 8, NX * HD)
     tokens = lax.all_to_all(
         jnp.broadcast_to(blocks[None], (NY, NZ, 8, NX * HD)), "y", 0, 0, tiled=True
     )
+    listed = jnp.pad(own_list.astype(jnp.bfloat16)[None, :], ((0, 15), (0, COLS - MAXC)))
+    weight = jnp.concatenate([q_weight[:, 0], kv_weight[:, 0]], axis=1)
+    weight = jnp.concatenate([weight, listed], axis=0)
+    weight, blocks_seen = lax.optimization_barrier((weight, first_blocks))
+    weights = [weight] + [shifted(weight, "x", NX, -k) for k in range(1, NX)]
+    tokens, *weights = lax.optimization_barrier((tokens, *weights))
     mate_tokens = swap_cores(tokens)
-
-    listed = jnp.pad(own_list.astype(jnp.bfloat16)[None, :], ((0, 15), (0, COLS - MAXC)))
-    weight = jnp.concatenate([weight, listed], axis=0)
-    weights = [weight] + [shifted(weight, "x", NX, -k) for k in range(1, NX)]
     gain = lax.dynamic_index_in_dim(norm_gain.reshape(NX, NZ, NC * HD), z, 1, keepdims=False)
     gain = lax.dynamic_slice_in_dim(jnp.concatenate([gain, gain], axis=0), x, NX, 0)
     gain = gain.astype(jnp.float32).reshape(1, NX * NC * HD)
 
     smem = pl.BlockSpec(memory_space=pltpu.SMEM)
     vmem = pl.BlockSpec(memory_space=pltpu.VMEM)
+    hbm = pl.BlockSpec(memory_space=pltpu.MemorySpace.HBM)
     partial = pl.pallas_call(
         project_kernel,
         out_shape=jax.ShapeDtypeStruct((NZ, ROWS + 8, COLS), jnp.bfloat16),
@@ -299,15 +335,15 @@
     send_rows, _ = lax.optimization_barrier((send_rows, partial[0, ROWS:, :HD]))
     picked = pl.pallas_call(
         pick_kernel,
-        out_shape=[jax.ShapeDtypeStruct((NZ, HALF, 2 * HD), jnp.bfloat16)] * NX,
-        in_specs=[smem, pl.BlockSpec(memory_space=pl.ANY)],
-        out_specs=[vmem] * NX,
-        scratch_shapes=[pltpu.SemaphoreType.DMA((NX * NZ,))],
+        out_shape=[jax.ShapeDtypeStruct((NZ, HALF, 2 * HD), jnp.bfloat16)] * (NX - 1),
+        in_specs=[smem, hbm],
+        out_specs=[vmem] * (NX - 1),
+        scratch_shapes=[pltpu.SemaphoreType.DMA(((NX - 1) * NZ,))],
         name="pick",
         compiler_params=pltpu.CompilerParams(vmem_limit_bytes=32 * 1024 * 1024),
         cost_estimate=pl.CostEstimate(flops=0, bytes_accessed=1 << 22, transcendentals=0),
     )(send_rows.reshape(-1), store)
-    arrived = [picked[0]] + [shifted(picked[k], "x", NX, -k) for k in range(1, NX)]
+    arrived = [None] + [shifted(picked[k - 1], "x", NX, -k) for k in range(1, NX)]
 
     frequency = jnp.exp(
         -math.log(theta_base) * jnp.arange(HD // 2, dtype=jnp.float32) / (HD // 2)
@@ -343,7 +379,6 @@
     fresh_eff = jnp.broadcast_to(fresh_eff[:, None], (ROWS, HD))
     pos_row = jnp.tile(positions, 2 * QS).reshape(1, 2 * QROWS)
 
-    early, late = (0, 1, 3), (2,)
     params = pltpu.CompilerParams(vmem_limit_bytes=32 * 1024 * 1024)
     run_shapes = [
         jax.ShapeDtypeStruct((HD, 2 * QROWS), jnp.float32),
@@ -355,28 +390,41 @@
         return pl.CostEstimate(flops=4 * pairs * HD, bytes_accessed=count << 19, transcendentals=pairs)
 
     acc, run = pl.pallas_call(
-        functools.partial(attend_early_kernel, early),
+        attend_own_kernel,
         out_shape=run_shapes,
-        in_specs=[smem] + [vmem] * (5 + len(early)),
+        in_specs=[smem] * 2 + [vmem] * 5 + [hbm],
         out_specs=[vmem] * 2,
-        name="attend_early",
+        scratch_shapes=[
+            pltpu.VMEM((NZ, HALF, 2 * HD), jnp.bfloat16),
+            pltpu.SemaphoreType.DMA((NZ,)),
+        ],
+        name="attend_own",
         compiler_params=params,
-        cost_estimate=cost(len(early)),
-    )(which_half.reshape(1), own, other, eff, fresh_eff, pos_row, *[arrived[k] for k in early])
+        cost_estimate=cost(1),
+    )(which_half.reshape(1), send_rows[0], own, other, eff, fresh_eff, pos_row, store)
+    acc, run = pl.pallas_call(
+        attend_near_kernel,
+        out_shape=run_shapes,
+        in_specs=[vmem] * 8,
+        out_specs=[vmem] * 2,
+        name="attend_near",
+        compiler_params=params,
+        cost_estimate=cost(2),
+    )(own, other, eff, pos_row, acc, run, arrived[1], arrived[3])
     own_part, stats, sent = pl.pallas_call(
-        functools.partial(attend_late_kernel, late),
+        attend_far_kernel,
         out_shape=[
             jax.ShapeDtypeStruct((HD, QROWS), jnp.float32),
             jax.ShapeDtypeStruct((8, QROWS), jnp.float32),
             jax.ShapeDtypeStruct((HD + 16, QROWS), jnp.bfloat16),
         ],
-        in_specs=[vmem] * (6 + len(late)),
+        in_specs=[vmem] * 7,
         out_specs=[vmem] * 3,
         scratch_shapes=[pltpu.VMEM(r.shape, r.dtype) for r in run_shapes],
-        name="attend_late",
+        name="attend_far",
         compiler_params=params,
-        cost_estimate=cost(len(late)),
-    )(own, other, eff, pos_row, acc, run, *[arrived[k] for k in late])
+        cost_estimate=cost(1),
+    )(own, other, eff, pos_row, acc, run, arrived[2])
     got = exchange(sent)
     attended = call(merge_kernel, jax.ShapeDtypeStruct((ROWS, QW), jnp.bfloat16), "merge")(
         own_part, stats, got

time: 151 us -> 148 us (0.980)
  the two profiles are of different devices: /device:TPU:64 before, /device:TPU:16 now
where the time goes in v5:
time: 148 us; the launch traced here: 147 us
  starting transfers between devices  57 us (39%)
  waiting for transfers between devices  47.1 us (32%)
  Pallas kernels  14.3 us (10%)
  between operations  13.7 us (9%)
  local copies, waits for them, and re-layouts  8.54 us (6%)
  other arithmetic  6.85 us (5%)
    ppermute x6, starting transfers between devices, shifted(): lax.ppermute(block, axis, [(i, (i + by) % count) for i in range(count)])  18.7 us
    ppermute x2, waiting for transfers between devices, exchange(): lax.ppermute(block, 'y', [(i, (i + NY // 2) % NY) for i in range(NY)])  13.4 us
    ppermute x6, waiting for transfers between devices, shifted(): lax.ppermute(block, axis, [(i, (i + by) % count) for i in range(count)])  13 us
    ppermute x2, starting transfers between devices, exchange(): lax.ppermute(block, 'y', [(i, (i + NY // 2) % NY) for i in range(NY)])  9.41 us
    all_to_all x1, waiting for transfers between devices, body(): blocks = lax.all_to_all(blocks, 'z', 0, 0, tiled=True)  9.2 us
    all_to_all x1, starting transfers between devices, body(): lax.all_to_all(blocks.reshape(NY * NC, 2, 8, HD), TP, 0, 0, tiled=True)  9.02 us
    all_to_all x1, starting transfers between devices, body(): blocks = lax.all_to_all(blocks, 'z', 0, 0, tiled=True)  8.71 us
    all_to_all x1, waiting for transfers between devices, body(): parts = lax.all_to_all(partial, 'z', 0, 0, tiled=True)  6.37 us
  transfers between devices with their start and end apart: 14, of which 9 were waited for; matrix products, arithmetic and copies ran while one was open for 7% of the time, Pallas kernels for 8%

profile of v5, /device:TPU:16, one launch (start us, length us, event | category | flops | bytes accessed | tf_op | source)
XLA Modules:
  0.0 147.5 jit_solution(2713924536972434571)
XLA Ops:
  7.3 1.5 %copy.17 = bf16[8,2,2,8,128]{4,3,2,1,0:T(8,128)(2,1)} copy(bf16[8,2,2,8,128]{4,3,1,2,0:T(8,128)(2,1)} %bitcast.40) | data formatting | bytes 131072 | tf_op jit(solution)/shard_map/transpose | solution.py:289
  8.7 9.0 %all-to-all-start = ((bf16[16,2,8,128]{3,2,1,0:T(8,128)(2,1)}), bf16[16,2,8,128]{3,2,1,0:T(8,128)(2,1)S(1)}, u32[]{:S(2)}, u32[]{:S(2)}) async-start(bf16[16,2,8,128]{3,2,1,0:T(8,128)(2,1)} %bitcast.3), calls=%async_computation | async-start | bytes 131072 | tf_op jit(solution)/shard_map/all_to_all | solution.py:290
  19.2 0.9 select_reduce_fusion.1
  20.9 2.7 %all-to-all-done = bf16[16,2,8,128]{3,2,1,0:T(8,128)(2,1)S(1)} async-done(((bf16[16,2,8,128]{3,2,1,0:T(8,128)(2,1)}), bf16[16,2,8,128]{3,2,1,0:T(8,128)(2,1)S(1)}, u32[]{:S(2)}, u32[]{:S(2)}) %all-to-all-start) | async-done | bytes 65568 | tf_op jit(solution)/shard_map/all_to_all | solution.py:290
  24.2 8.7 %all-to-all-start.1 = ((bf16[8,4,8,128]{3,2,1,0:T(8,128)(2,1)}), bf16[8,4,8,128]{3,2,1,0:T(8,128)(2,1)S(1)}, u32[]{:S(2)}, u32[]{:S(2)}) async-start(bf16[8,4,8,128]{3,2,1,0:T(8,128)(2,1)} %copy.18), calls=%async_computation.1 | async-start | bytes 131072 | tf_op jit(solution)/shard_map/all_to_all | solution.py:294
  32.9 9.2 %all-to-all-done.1 = bf16[8,4,8,128]{3,2,1,0:T(8,128)(2,1)S(1)} async-done(((bf16[8,4,8,128]{3,2,1,0:T(8,128)(2,1)}), bf16[8,4,8,128]{3,2,1,0:T(8,128)(2,1)S(1)}, u32[]{:S(2)}, u32[]{:S(2)}) %all-to-all-start.1) | async-done | bytes 65568 | tf_op jit(solution)/shard_map/all_to_all | solution.py:294
  43.0 5.7 %all-to-all-start.2 = ((bf16[8,8,8,512]{3,2,1,0:T(8,128)(2,1)}), bf16[8,8,8,512]{3,2,1,0:T(8,128)(2,1)S(1)}, u32[]{:S(2)}, u32[]{:S(2)}) async-start(bf16[8,8,8,512]{3,2,1,0:T(8,128)(2,1)} %broadcast_in_dim.84), calls=%async_computation.2 | async-start | bytes 1048576 | tf_op jit(solution)/shard_map/all_to_all | solution.py:298
  49.0 1.0 fusion.1.w0_ref
  50.0 0.9 compare_reduce_fusion
  50.9 4.7 %collective-permute-start = (bf16[272,640]{1,0:T(8,128)(2,1)S(1)}, bf16[272,640]{1,0:T(8,128)(2,1)S(1)}, u32[]{:S(2)}, u32[]{:S(2)}) collective-permute-start(bf16[272,640]{1,0:T(8,128)(2,1)S(1)} %fusion.1.w0_ref), channel_id=1, source_target_pairs={{0,384},{128,0},{256,128},{384,256},{1,385},{129,1},{257,129},{385... | collective-permute-start | bytes 1044488 | tf_op jit(solution)/shard_map/ppermute | solution.py:45
  55.6 2.7 %collective-permute-start.1 = (bf16[272,640]{1,0:T(8,128)(2,1)S(1)}, bf16[272,640]{1,0:T(8,128)(2,1)S(1)}, u32[]{:S(2)}, u32[]{:S(2)}) collective-permute-start(bf16[272,640]{1,0:T(8,128)(2,1)S(1)} %fusion.1.w0_ref), channel_id=1, source_target_pairs={{0,256},{128,384},{256,0},{384,128},{1,257},{129,385},{257,1},{385... | collective-permute-start | bytes 1044488 | tf_op jit(solution)/shard_map/ppermute | solution.py:45
  58.3 2.8 %collective-permute-start.2 = (bf16[272,640]{1,0:T(8,128)(2,1)S(1)}, bf16[272,640]{1,0:T(8,128)(2,1)S(1)}, u32[]{:S(2)}, u32[]{:S(2)}) collective-permute-start(bf16[272,640]{1,0:T(8,128)(2,1)S(1)} %fusion.1.w0_ref), channel_id=1, source_target_pairs={{0,128},{128,256},{256,384},{384,0},{1,129},{129,257},{257,385},{3... | collective-permute-start | bytes 1044488 | tf_op jit(solution)/shard_map/ppermute | solution.py:45
  62.0 7.4 %collective-permute-done.w1_ref = bf16[272,640]{1,0:T(8,128)(2,1)S(1)} collective-permute-done((bf16[272,640]{1,0:T(8,128)(2,1)S(1)}, bf16[272,640]{1,0:T(8,128)(2,1)S(1)}, u32[]{:S(2)}, u32[]{:S(2)}) %collective-permute-start) | collective-permute-done | bytes 348192 | tf_op jit(solution)/shard_map/ppermute | solution.py:45
  70.1 4.8 %collective-permute-done.2.w3_ref = bf16[272,640]{1,0:T(8,128)(2,1)S(1)} collective-permute-done((bf16[272,640]{1,0:T(8,128)(2,1)S(1)}, bf16[272,640]{1,0:T(8,128)(2,1)S(1)}, u32[]{:S(2)}, u32[]{:S(2)}) %collective-permute-start.2) | collective-permute-done | bytes 348192 | tf_op jit(solution)/shard_map/ppermute | solution.py:45
  75.0 1.9 %collective-permute-start.3 = (bf16[8,8,8,512]{3,2,1,0:T(8,128)(2,1)S(1)}, bf16[8,8,8,512]{3,2,1,0:T(8,128)(2,1)S(1)}, u32[]{:S(2)}, u32[]{:S(2)}) collective-permute-start(bf16[8,8,8,512]{3,2,1,0:T(8,128)(2,1)S(1)} %all-to-all-done.2.mine_ref), channel_id=1, source_target_pairs={{0,1},{1,0},{2,3},{3,2},{4,5},{5,4},{6,7},{7,6},{8,9},{9,8},{10,11... | collective-permute-start | bytes 1572872 | tf_op jit(solution)/shard_map/ppermute | solution.py:41
  77.0 1.8 %collective-permute-done.3.mate_ref = bf16[8,8,8,512]{3,2,1,0:T(8,128)(2,1)S(1)} collective-permute-done((bf16[8,8,8,512]{3,2,1,0:T(8,128)(2,1)S(1)}, bf16[8,8,8,512]{3,2,1,0:T(8,128)(2,1)S(1)}, u32[]{:S(2)}, u32[]{:S(2)}) %collective-permute-start.3) | collective-permute-done | bytes 524320 | tf_op jit(solution)/shard_map/ppermute | solution.py:41
  78.8 1.9 %project.1 = bf16[8,72,640]{2,1,0:T(8,128)(2,1)} custom-call(s32[1]{0:T(128)} %bitcast.core_ref, bf16[8,8,8,512]{3,2,1,0:T(8,128)(2,1)S(1)} %all-to-all-done.2.mine_ref, bf16[8,8,8,512]{3,2,1,0:T(8,128)(2,1)S(1)} %collective-permute-done.3.mate_ref, f32[1,1024]{1,0:T(1,128)S(1)} %bitcast.36, bf16[272,640]{1,0:T(8,128)(2,1)S(1)} %fusion.1.w0_ref, ...), custom_call_target="tpu_custom_call" | custom-call | flops 671088640 | bytes 4194304 | tf_op jit(solution)/shard_map/project/pallas_call | solution.py:315
  80.7 3.5 %all-to-all-start.3 = ((bf16[8,72,640]{2,1,0:T(8,128)(2,1)}), bf16[8,72,640]{2,1,0:T(8,128)(2,1)S(1)}, u32[]{:S(2)}, u32[]{:S(2)}) async-start(bf16[8,72,640]{2,1,0:T(8,128)(2,1)} %project.1), calls=%async_computation.3 | async-start | bytes 1474560 | tf_op jit(solution)/shard_map/all_to_all | solution.py:326
  85.8 2.2 %copy-done = bf16[64,1,128,256]{3,2,1,0:T(8,128)(2,1)S(1)} copy-done((bf16[64,1,128,256]{3,2,1,0:T(8,128)(2,1)S(1)}, bf16[64,1,128,256]{3,2,1,0:T(8,128)(2,1)}, u32[]{:S(2)}) %copy-start) | copy-done | bytes 4194328
  88.0 3.7 %pick.1 = (bf16[8,128,256]{2,1,0:T(8,128)(2,1)}, bf16[8,128,256]{2,1,0:T(8,128)(2,1)S(1)}, bf16[8,128,256]{2,1,0:T(8,128)(2,1)S(1)}) custom-call(s32[32]{0:T(128)S(1)} %reshape.215.rows_ref, bf16[64,128,256]{2,1,0:T(8,128)(2,1)S(1)} %bitcast.34), custom_call_target="tpu_custom_call" | custom-call | bytes 4194304 | tf_op jit(solution)/shard_map/pick/pallas_call | solution.py:336
  91.7 2.5 %collective-permute-start.5 = (bf16[8,128,256]{2,1,0:T(8,128)(2,1)}, bf16[8,128,256]{2,1,0:T(8,128)(2,1)S(1)}, u32[]{:S(2)}, u32[]{:S(2)}) collective-permute-start(bf16[8,128,256]{2,1,0:T(8,128)(2,1)} %get-tuple-element.29), channel_id=1, source_target_pairs={{0,384},{128,0},{256,128},{384,256},{1,385},{129,1},{257,129},{385... | collective-permute-start | bytes 1572872 | tf_op jit(solution)/shard_map/ppermute | solution.py:45
  94.2 3.3 %collective-permute-start.6 = (bf16[8,128,256]{2,1,0:T(8,128)(2,1)S(1)}, bf16[8,128,256]{2,1,0:T(8,128)(2,1)}, u32[]{:S(2)}, u32[]{:S(2)}) collective-permute-start(bf16[8,128,256]{2,1,0:T(8,128)(2,1)S(1)} %get-tuple-element.30), channel_id=1, source_target_pairs={{0,128},{128,256},{256,384},{384,0},{1,129},{129,257},{257,385},{3... | collective-permute-start | bytes 1572872 | tf_op jit(solution)/shard_map/ppermute | solution.py:45
  97.7 2.7 %collective-permute-start.7 = (bf16[8,128,256]{2,1,0:T(8,128)(2,1)S(1)}, bf16[8,128,256]{2,1,0:T(8,128)(2,1)S(1)}, u32[]{:S(2)}, u32[]{:S(2)}) collective-permute-start(bf16[8,128,256]{2,1,0:T(8,128)(2,1)S(1)} %get-tuple-element.33), channel_id=1, source_target_pairs={{0,256},{128,384},{256,0},{384,128},{1,257},{129,385},{257,1},{385... | collective-permute-start | bytes 1572872 | tf_op jit(solution)/shard_map/ppermute | solution.py:45
  100.4 6.4 %all-to-all-done.3.parts_ref = bf16[8,72,640]{2,1,0:T(8,128)(2,1)S(1)} async-done(((bf16[8,72,640]{2,1,0:T(8,128)(2,1)}), bf16[8,72,640]{2,1,0:T(8,128)(2,1)S(1)}, u32[]{:S(2)}, u32[]{:S(2)}) %all-to-all-start.3) | async-done | bytes 737312 | tf_op jit(solution)/shard_map/all_to_all | solution.py:326
  107.0 5.5 %collective-permute-start.4 = (bf16[320,128]{1,0:T(8,128)(2,1)S(1)}, bf16[320,128]{1,0:T(8,128)(2,1)S(1)}, u32[]{:S(2)}, u32[]{:S(2)}) collective-permute-start(bf16[320,128]{1,0:T(8,128)(2,1)S(1)} %finish.1.own_ref), channel_id=1, source_target_pairs={{0,8},{2,10},{4,12},{6,14},{8,0},{10,2},{12,4},{14,6},{1,9},{3,11}... | collective-permute-start | bytes 245768 | tf_op jit(solution)/shard_map/ppermute | solution.py:37
  112.5 6.3 %collective-permute-done.4.other_ref = bf16[320,128]{1,0:T(8,128)(2,1)S(1)} collective-permute-done((bf16[320,128]{1,0:T(8,128)(2,1)S(1)}, bf16[320,128]{1,0:T(8,128)(2,1)S(1)}, u32[]{:S(2)}, u32[]{:S(2)}) %collective-permute-start.4) | collective-permute-done | bytes 81952 | tf_op jit(solution)/shard_map/ppermute | solution.py:37
  119.0 2.2 %copy-done.1 = bf16[64,1,128,256]{3,2,1,0:T(8,128)(2,1)S(1)} copy-done((bf16[64,1,128,256]{3,2,1,0:T(8,128)(2,1)S(1)}, bf16[64,1,128,256]{3,2,1,0:T(8,128)(2,1)}, u32[]{:S(2)}) %copy-start.1) | copy-done | bytes 4194328
  121.2 3.0 %attend_own.1 = (f32[128,512]{1,0:T(8,128)S(1)}, f32[8,512]{1,0:T(8,128)S(1)}) custom-call(s32[1]{0:T(128)} %bitcast.16.flag_ref, s32[8]{0:T(128)S(1)} %slice_bitcast_fusion.rows_ref, bf16[320,128]{1,0:T(8,128)(2,1)S(1)} %finish.1.own_ref, bf16[320,128]{1,0:T(8,128)(2,1)S(1)} %collective-permute-done.4.other_ref, s32[128,32]{1,0:T(8,128)S(1)} %or_select_fusion.eff_ref, ...), custom_call_target="tpu_custom_call" | custom-call | flops 268435456 | bytes 524288 | tf_op jit(solution)/shard_map/attend_own/pallas_call | solution.py:392
  124.1 3.5 %attend_near.1 = (f32[128,512]{1,0:T(8,128)S(1)}, f32[8,512]{1,0:T(8,128)S(1)}) custom-call(bf16[320,128]{1,0:T(8,128)(2,1)S(1)} %finish.1.own_ref, bf16[320,128]{1,0:T(8,128)(2,1)S(1)} %collective-permute-done.4.other_ref, s32[128,32]{1,0:T(8,128)S(1)} %or_select_fusion.eff_ref, s32[1,512]{1,0:T(1,128)S(1)} %reshape_tile.3.pos_ref, ...), custom_call_target="tpu_custom_call" | custom-call | flops 536870912 | bytes 1048576 | tf_op jit(solution)/shard_map/attend_near/pallas_call | solution.py:405
  127.6 1.3 attend_far.1
  128.9 3.9 %collective-permute-start.8 = (bf16[144,256]{1,0:T(8,128)(2,1)S(1)}, bf16[144,256]{1,0:T(8,128)(2,1)S(1)}, u32[]{:S(2)}, u32[]{:S(2)}) collective-permute-start(bf16[144,256]{1,0:T(8,128)(2,1)S(1)} %get-tuple-element.36), channel_id=1, source_target_pairs={{0,8},{2,10},{4,12},{6,14},{8,0},{10,2},{12,4},{14,6},{1,9},{3,11}... | collective-permute-start | bytes 221192 | tf_op jit(solution)/shard_map/ppermute | solution.py:37
  132.8 7.0 %collective-permute-done.8.got_ref = bf16[144,256]{1,0:T(8,128)(2,1)S(1)} collective-permute-done((bf16[144,256]{1,0:T(8,128)(2,1)S(1)}, bf16[144,256]{1,0:T(8,128)(2,1)S(1)}, u32[]{:S(2)}, u32[]{:S(2)}) %collective-permute-start.8) | collective-permute-done | bytes 73760 | tf_op jit(solution)/shard_map/ppermute | solution.py:37
  (58 shorter events, 9.2 us)
Async XLA Ops:
  6.5 77.7 %copy-start.2 = (s32[256]{0:T(256)S(1)}, s32[256]{0:T(256)}, u32[]{:S(2)}) copy-start(s32[256]{0:T(256)} %param.13) | copy-start | bytes 3076
  6.5 79.2 %all-gather.3.cloned.1.call-start = ((), (), s32[]{:S(2)}) async-start(), calls=%async_computation.4 | async-start | bytes 4718592 | tf_op jit(solution)/shard_map/all_gather | solution.py:287
  8.7 14.8 %all-to-all-start = ((bf16[16,2,8,128]{3,2,1,0:T(8,128)(2,1)}), bf16[16,2,8,128]{3,2,1,0:T(8,128)(2,1)S(1)}, u32[]{:S(2)}, u32[]{:S(2)}) async-start(bf16[16,2,8,128]{3,2,1,0:T(8,128)(2,1)} %bitcast.3), calls=%async_computation | async-start | bytes 131072 | tf_op jit(solution)/shard_map/all_to_all | solution.py:290
  24.2 17.9 %all-to-all-start.1 = ((bf16[8,4,8,128]{3,2,1,0:T(8,128)(2,1)}), bf16[8,4,8,128]{3,2,1,0:T(8,128)(2,1)S(1)}, u32[]{:S(2)}, u32[]{:S(2)}) async-start(bf16[8,4,8,128]{3,2,1,0:T(8,128)(2,1)} %copy.18), calls=%async_computation.1 | async-start | bytes 131072 | tf_op jit(solution)/shard_map/all_to_all | solution.py:294
  43.0 31.9 %all-to-all-start.2 = ((bf16[8,8,8,512]{3,2,1,0:T(8,128)(2,1)}), bf16[8,8,8,512]{3,2,1,0:T(8,128)(2,1)S(1)}, u32[]{:S(2)}, u32[]{:S(2)}) async-start(bf16[8,8,8,512]{3,2,1,0:T(8,128)(2,1)} %broadcast_in_dim.84), calls=%async_computation.2 | async-start | bytes 1048576 | tf_op jit(solution)/shard_map/all_to_all | solution.py:298
  50.9 18.5 %collective-permute-start = (bf16[272,640]{1,0:T(8,128)(2,1)S(1)}, bf16[272,640]{1,0:T(8,128)(2,1)S(1)}, u32[]{:S(2)}, u32[]{:S(2)}) collective-permute-start(bf16[272,640]{1,0:T(8,128)(2,1)S(1)} %fusion.1.w0_ref), channel_id=1, source_target_pairs={{0,384},{128,0},{256,128},{384,256},{1,385},{129,1},{257,129},{385... | collective-permute-start | bytes 1044488 | tf_op jit(solution)/shard_map/ppermute | solution.py:45
  55.6 14.5 %collective-permute-start.1 = (bf16[272,640]{1,0:T(8,128)(2,1)S(1)}, bf16[272,640]{1,0:T(8,128)(2,1)S(1)}, u32[]{:S(2)}, u32[]{:S(2)}) collective-permute-start(bf16[272,640]{1,0:T(8,128)(2,1)S(1)} %fusion.1.w0_ref), channel_id=1, source_target_pairs={{0,256},{128,384},{256,0},{384,128},{1,257},{129,385},{257,1},{385... | collective-permute-start | bytes 1044488 | tf_op jit(solution)/shard_map/ppermute | solution.py:45
  58.3 16.7 %collective-permute-start.2 = (bf16[272,640]{1,0:T(8,128)(2,1)S(1)}, bf16[272,640]{1,0:T(8,128)(2,1)S(1)}, u32[]{:S(2)}, u32[]{:S(2)}) collective-permute-start(bf16[272,640]{1,0:T(8,128)(2,1)S(1)} %fusion.1.w0_ref), channel_id=1, source_target_pairs={{0,128},{128,256},{256,384},{384,0},{1,129},{129,257},{257,385},{3... | collective-permute-start | bytes 1044488 | tf_op jit(solution)/shard_map/ppermute | solution.py:45
  75.0 3.8 %collective-permute-start.3 = (bf16[8,8,8,512]{3,2,1,0:T(8,128)(2,1)S(1)}, bf16[8,8,8,512]{3,2,1,0:T(8,128)(2,1)S(1)}, u32[]{:S(2)}, u32[]{:S(2)}) collective-permute-start(bf16[8,8,8,512]{3,2,1,0:T(8,128)(2,1)S(1)} %all-to-all-done.2.mine_ref), channel_id=1, source_target_pairs={{0,1},{1,0},{2,3},{3,2},{4,5},{5,4},{6,7},{7,6},{8,9},{9,8},{10,11... | collective-permute-start | bytes 1572872 | tf_op jit(solution)/shard_map/ppermute | solution.py:41
  78.8 18.8 %copy-start.3 = (s32[1,64]{1,0:T(1,128)S(1)}, s32[1,64]{1,0:T(1,128)}, u32[]{:S(2)}) copy-start(s32[1,64]{1,0:T(1,128)} %param.15) | copy-start | bytes 772
  80.7 26.1 %all-to-all-start.3 = ((bf16[8,72,640]{2,1,0:T(8,128)(2,1)}), bf16[8,72,640]{2,1,0:T(8,128)(2,1)S(1)}, u32[]{:S(2)}, u32[]{:S(2)}) async-start(bf16[8,72,640]{2,1,0:T(8,128)(2,1)} %project.1), calls=%async_computation.3 | async-start | bytes 1474560 | tf_op jit(solution)/shard_map/all_to_all | solution.py:326
  85.8 2.2 %copy-start = (bf16[64,1,128,256]{3,2,1,0:T(8,128)(2,1)S(1)}, bf16[64,1,128,256]{3,2,1,0:T(8,128)(2,1)}, u32[]{:S(2)}) copy-start(bf16[64,1,128,256]{3,2,1,0:T(8,128)(2,1)} %all-gather.3.cloned.1.call-done) | copy-start | bytes 12582916
  91.7 32.5 %collective-permute-start.5 = (bf16[8,128,256]{2,1,0:T(8,128)(2,1)}, bf16[8,128,256]{2,1,0:T(8,128)(2,1)S(1)}, u32[]{:S(2)}, u32[]{:S(2)}) collective-permute-start(bf16[8,128,256]{2,1,0:T(8,128)(2,1)} %get-tuple-element.29), channel_id=1, source_target_pairs={{0,384},{128,0},{256,128},{384,256},{1,385},{129,1},{257,129},{385... | collective-permute-start | bytes 1572872 | tf_op jit(solution)/shard_map/ppermute | solution.py:45
  94.2 29.9 %collective-permute-start.6 = (bf16[8,128,256]{2,1,0:T(8,128)(2,1)S(1)}, bf16[8,128,256]{2,1,0:T(8,128)(2,1)}, u32[]{:S(2)}, u32[]{:S(2)}) collective-permute-start(bf16[8,128,256]{2,1,0:T(8,128)(2,1)S(1)} %get-tuple-element.30), channel_id=1, source_target_pairs={{0,128},{128,256},{256,384},{384,0},{1,129},{129,257},{257,385},{3... | collective-permute-start | bytes 1572872 | tf_op jit(solution)/shard_map/ppermute | solution.py:45
  97.7 29.9 %collective-permute-start.7 = (bf16[8,128,256]{2,1,0:T(8,128)(2,1)S(1)}, bf16[8,128,256]{2,1,0:T(8,128)(2,1)S(1)}, u32[]{:S(2)}, u32[]{:S(2)}) collective-permute-start(bf16[8,128,256]{2,1,0:T(8,128)(2,1)S(1)} %get-tuple-element.33), channel_id=1, source_target_pairs={{0,256},{128,384},{256,0},{384,128},{1,257},{129,385},{257,1},{385... | collective-permute-start | bytes 1572872 | tf_op jit(solution)/shard_map/ppermute | solution.py:45
  107.0 11.9 %collective-permute-start.4 = (bf16[320,128]{1,0:T(8,128)(2,1)S(1)}, bf16[320,128]{1,0:T(8,128)(2,1)S(1)}, u32[]{:S(2)}, u32[]{:S(2)}) collective-permute-start(bf16[320,128]{1,0:T(8,128)(2,1)S(1)} %finish.1.own_ref), channel_id=1, source_target_pairs={{0,8},{2,10},{4,12},{6,14},{8,0},{10,2},{12,4},{14,6},{1,9},{3,11}... | collective-permute-start | bytes 245768 | tf_op jit(solution)/shard_map/ppermute | solution.py:37
  119.0 2.2 %copy-start.1 = (bf16[64,1,128,256]{3,2,1,0:T(8,128)(2,1)S(1)}, bf16[64,1,128,256]{3,2,1,0:T(8,128)(2,1)}, u32[]{:S(2)}) copy-start(bf16[64,1,128,256]{3,2,1,0:T(8,128)(2,1)} %all-gather.3.cloned.1.call-done) | copy-start | bytes 12582916
  128.9 10.9 %collective-permute-start.8 = (bf16[144,256]{1,0:T(8,128)(2,1)S(1)}, bf16[144,256]{1,0:T(8,128)(2,1)S(1)}, u32[]{:S(2)}, u32[]{:S(2)}) collective-permute-start(bf16[144,256]{1,0:T(8,128)(2,1)S(1)} %get-tuple-element.36), channel_id=1, source_target_pairs={{0,8},{2,10},{4,12},{6,14},{8,0},{10,2},{12,4},{14,6},{1,9},{3,11}... | collective-permute-start | bytes 221192 | tf_op jit(solution)/shard_map/ppermute | solution.py:37
Sparse Core Ops, SparseCore 0:
  9.4 64.1 all-gather.2

commit v6 on v5

--- a/solution.py
+++ b/solution.py
@@ -286,23 +286,25 @@
 
     store = lax.all_gather(cache_store[:, 0], "z", axis=0, tiled=True)
 
+    listed = jnp.pad(own_list.astype(jnp.bfloat16)[None, :], ((0, 15), (0, COLS - MAXC)))
+    weight = jnp.concatenate([q_weight[:, 0], kv_weight[:, 0]], axis=1)
+    weight = jnp.concatenate([weight, listed], axis=0)
+
     blocks = hidden[0].reshape(NY, 8, 2, NC, HD).transpose(0, 3, 2, 1, 4)
     blocks = lax.all_to_all(blocks.reshape(NY * NC, 2, 8, HD), TP, 0, 0, tiled=True)
     blocks = blocks.reshape(NX, 2, 2, 2, 8, HD).transpose(1, 2, 3, 0, 4, 5)
     blocks = blocks.reshape(NZ, NX, 8, HD)
-    first_blocks = blocks
+    blocks, weight = lax.optimization_barrier((blocks, weight))
+    weights = [weight] + [shifted(weight, "x", NX, -k) for k in range(1, NX)]
     blocks = lax.all_to_all(blocks, "z", 0, 0, tiled=True)
+    blocks, first_weight = lax.optimization_barrier((blocks, weights[2]))
+    weights[2] = first_weight
     blocks = jnp.concatenate([blocks, blocks], axis=1)
     blocks = lax.dynamic_slice_in_dim(blocks, x, NX, 1)
     blocks = blocks.transpose(0, 2, 1, 3).reshape(NZ, 8, NX * HD)
     tokens = lax.all_to_all(
         jnp.broadcast_to(blocks[None], (NY, NZ, 8, NX * HD)), "y", 0, 0, tiled=True
     )
-    listed = jnp.pad(own_list.astype(jnp.bfloat16)[None, :], ((0, 15), (0, COLS - MAXC)))
-    weight = jnp.concatenate([q_weight[:, 0], kv_weight[:, 0]], axis=1)
-    weight = jnp.concatenate([weight, listed], axis=0)
-    weight, blocks_seen = lax.optimization_barrier((weight, first_blocks))
-    weights = [weight] + [shifted(weight, "x", NX, -k) for k in range(1, NX)]
     tokens, *weights = lax.optimization_barrier((tokens, *weights))
     mate_tokens = swap_cores(tokens)
     gain = lax.dynamic_index_in_dim(norm_gain.reshape(NX, NZ, NC * HD), z, 1, keepdims=False)
@@ -340,7 +342,7 @@
         out_specs=[vmem] * (NX - 1),
         scratch_shapes=[pltpu.SemaphoreType.DMA(((NX - 1) * NZ,))],
         name="pick",
-        compiler_params=pltpu.CompilerParams(vmem_limit_bytes=32 * 1024 * 1024),
+        compiler_params=pltpu.CompilerParams(vmem_limit_bytes=60 * 1024 * 1024),
         cost_estimate=pl.CostEstimate(flops=0, bytes_accessed=1 << 22, transcendentals=0),
     )(send_rows.reshape(-1), store)
     arrived = [None] + [shifted(picked[k - 1], "x", NX, -k) for k in range(1, NX)]
@@ -399,7 +401,7 @@
             pltpu.SemaphoreType.DMA((NZ,)),
         ],
         name="attend_own",
-        compiler_params=params,
+        compiler_params=pltpu.CompilerParams(vmem_limit_bytes=60 * 1024 * 1024),
         cost_estimate=cost(1),
     )(which_half.reshape(1), send_rows[0], own, other, eff, fresh_eff, pos_row, store)
     acc, run = pl.pallas_call(

time: 148 us -> 146 us (0.986)
  the two profiles are of different devices: /device:TPU:16 before, /device:TPU:2 now
where the time goes in v6:
time: 146 us; the launch traced here: 144 us
  starting transfers between devices  58.2 us (40%)
  waiting for transfers between devices  40.5 us (28%)
  Pallas kernels  14.3 us (10%)
  between operations  13.8 us (9%)
  local copies, waits for them, and re-layouts  9.96 us (7%)
  other arithmetic  7.47 us (5%)
    ppermute x6, starting transfers between devices, shifted(): lax.ppermute(block, axis, [(i, (i + by) % count) for i in range(count)])  20.4 us
    ppermute x2, starting transfers between devices, exchange(): lax.ppermute(block, 'y', [(i, (i + NY // 2) % NY) for i in range(NY)])  11.4 us
    ppermute x2, waiting for transfers between devices, exchange(): lax.ppermute(block, 'y', [(i, (i + NY // 2) % NY) for i in range(NY)])  10.8 us
    all_to_all x1, starting transfers between devices, body(): blocks = lax.all_to_all(blocks, 'z', 0, 0, tiled=True)  10.3 us
    all_to_all x1, waiting for transfers between devices, body(): blocks = lax.all_to_all(blocks, 'z', 0, 0, tiled=True)  9.16 us
    all_to_all x1, starting transfers between devices, body(): lax.all_to_all(blocks.reshape(NY * NC, 2, 8, HD), TP, 0, 0, tiled=True)  7.21 us
    ppermute x6, waiting for transfers between devices, shifted(): lax.ppermute(block, axis, [(i, (i + by) % count) for i in range(count)])  6.91 us
    all_to_all x1, waiting for transfers between devices, body(): parts = lax.all_to_all(partial, 'z', 0, 0, tiled=True)  5.51 us
  transfers between devices with their start and end apart: 14, of which 9 were waited for; matrix products, arithmetic and copies ran while one was open for 10% of the time, Pallas kernels for 9%

profile of v6, /device:TPU:2, one launch (start us, length us, event | category | flops | bytes accessed | tf_op | source)
XLA Modules:
  0.0 144.3 jit_solution(7642301122230882411)
XLA Ops:
  7.3 1.5 %copy.17 = bf16[8,2,2,8,128]{4,3,2,1,0:T(8,128)(2,1)} copy(bf16[8,2,2,8,128]{4,3,1,2,0:T(8,128)(2,1)} %bitcast.40) | data formatting | bytes 131072 | tf_op jit(solution)/shard_map/transpose | solution.py:293
  8.7 7.2 %all-to-all-start = ((bf16[16,2,8,128]{3,2,1,0:T(8,128)(2,1)}), bf16[16,2,8,128]{3,2,1,0:T(8,128)(2,1)S(1)}, u32[]{:S(2)}, u32[]{:S(2)}) async-start(bf16[16,2,8,128]{3,2,1,0:T(8,128)(2,1)} %bitcast.3), calls=%async_computation | async-start | bytes 131072 | tf_op jit(solution)/shard_map/all_to_all | solution.py:294
  18.2 1.0 fusion.1.w0_ref
  19.2 4.6 %all-to-all-done = bf16[16,2,8,128]{3,2,1,0:T(8,128)(2,1)S(1)} async-done(((bf16[16,2,8,128]{3,2,1,0:T(8,128)(2,1)}), bf16[16,2,8,128]{3,2,1,0:T(8,128)(2,1)S(1)}, u32[]{:S(2)}, u32[]{:S(2)}) %all-to-all-start) | async-done | bytes 65568 | tf_op jit(solution)/shard_map/all_to_all | solution.py:294
  23.8 4.0 %collective-permute-start = (bf16[272,640]{1,0:T(8,128)(2,1)S(1)}, bf16[272,640]{1,0:T(8,128)(2,1)S(1)}, u32[]{:S(2)}, u32[]{:S(2)}) collective-permute-start(bf16[272,640]{1,0:T(8,128)(2,1)S(1)} %fusion.1.w0_ref), channel_id=1, source_target_pairs={{0,256},{128,384},{256,0},{384,128},{1,257},{129,385},{257,1},{385... | collective-permute-start | bytes 1044488 | tf_op jit(solution)/shard_map/ppermute | solution.py:45
  29.5 10.3 %all-to-all-start.1 = ((bf16[8,4,8,128]{3,2,1,0:T(8,128)(2,1)}), bf16[8,4,8,128]{3,2,1,0:T(8,128)(2,1)S(1)}, u32[]{:S(2)}, u32[]{:S(2)}) async-start(bf16[8,4,8,128]{3,2,1,0:T(8,128)(2,1)} %copy.18), calls=%async_computation.1 | async-start | bytes 131072 | tf_op jit(solution)/shard_map/all_to_all | solution.py:299
  39.8 9.2 %all-to-all-done.1 = bf16[8,4,8,128]{3,2,1,0:T(8,128)(2,1)S(1)} async-done(((bf16[8,4,8,128]{3,2,1,0:T(8,128)(2,1)}), bf16[8,4,8,128]{3,2,1,0:T(8,128)(2,1)S(1)}, u32[]{:S(2)}, u32[]{:S(2)}) %all-to-all-start.1) | async-done | bytes 65568 | tf_op jit(solution)/shard_map/all_to_all | solution.py:299
  49.8 3.5 %all-to-all-start.2 = ((bf16[8,8,8,512]{3,2,1,0:T(8,128)(2,1)}), bf16[8,8,8,512]{3,2,1,0:T(8,128)(2,1)S(1)}, u32[]{:S(2)}, u32[]{:S(2)}) async-start(bf16[8,8,8,512]{3,2,1,0:T(8,128)(2,1)} %broadcast_in_dim.84), calls=%async_computation.2 | async-start | bytes 1048576 | tf_op jit(solution)/shard_map/all_to_all | solution.py:305
  53.6 0.9 compare_reduce_fusion
  54.6 3.3 %collective-permute-start.1 = (bf16[272,640]{1,0:T(8,128)(2,1)S(1)}, bf16[272,640]{1,0:T(8,128)(2,1)S(1)}, u32[]{:S(2)}, u32[]{:S(2)}) collective-permute-start(bf16[272,640]{1,0:T(8,128)(2,1)S(1)} %fusion.1.w0_ref), channel_id=1, source_target_pairs={{0,384},{128,0},{256,128},{384,256},{1,385},{129,1},{257,129},{385... | collective-permute-start | bytes 1044488 | tf_op jit(solution)/shard_map/ppermute | solution.py:45
  57.9 2.5 %collective-permute-start.2 = (bf16[272,640]{1,0:T(8,128)(2,1)S(1)}, bf16[272,640]{1,0:T(8,128)(2,1)S(1)}, u32[]{:S(2)}, u32[]{:S(2)}) collective-permute-start(bf16[272,640]{1,0:T(8,128)(2,1)S(1)} %fusion.1.w0_ref), channel_id=1, source_target_pairs={{0,128},{128,256},{256,384},{384,0},{1,129},{129,257},{257,385},{3... | collective-permute-start | bytes 1044488 | tf_op jit(solution)/shard_map/ppermute | solution.py:45
  61.3 3.8 %collective-permute-done.1.w1_ref = bf16[272,640]{1,0:T(8,128)(2,1)S(1)} collective-permute-done((bf16[272,640]{1,0:T(8,128)(2,1)S(1)}, bf16[272,640]{1,0:T(8,128)(2,1)S(1)}, u32[]{:S(2)}, u32[]{:S(2)}) %collective-permute-start.1) | collective-permute-done | bytes 348192 | tf_op jit(solution)/shard_map/ppermute | solution.py:45
  65.1 3.1 %collective-permute-done.2.w3_ref = bf16[272,640]{1,0:T(8,128)(2,1)S(1)} collective-permute-done((bf16[272,640]{1,0:T(8,128)(2,1)S(1)}, bf16[272,640]{1,0:T(8,128)(2,1)S(1)}, u32[]{:S(2)}, u32[]{:S(2)}) %collective-permute-start.2) | collective-permute-done | bytes 348192 | tf_op jit(solution)/shard_map/ppermute | solution.py:45
  68.2 1.6 %all-to-all-done.2.mine_ref = bf16[8,8,8,512]{3,2,1,0:T(8,128)(2,1)S(1)} async-done(((bf16[8,8,8,512]{3,2,1,0:T(8,128)(2,1)}), bf16[8,8,8,512]{3,2,1,0:T(8,128)(2,1)S(1)}, u32[]{:S(2)}, u32[]{:S(2)}) %all-to-all-start.2) | async-done | bytes 524320 | tf_op jit(solution)/shard_map/all_to_all | solution.py:305
  69.8 1.9 %collective-permute-start.3 = (bf16[8,8,8,512]{3,2,1,0:T(8,128)(2,1)S(1)}, bf16[8,8,8,512]{3,2,1,0:T(8,128)(2,1)S(1)}, u32[]{:S(2)}, u32[]{:S(2)}) collective-permute-start(bf16[8,8,8,512]{3,2,1,0:T(8,128)(2,1)S(1)} %all-to-all-done.2.mine_ref), channel_id=1, source_target_pairs={{0,1},{1,0},{2,3},{3,2},{4,5},{5,4},{6,7},{7,6},{8,9},{9,8},{10,11... | collective-permute-start | bytes 1572872 | tf_op jit(solution)/shard_map/ppermute | solution.py:41
  72.4 1.1 collective-permute-done.3.mate_ref
  73.6 1.9 %project.1 = bf16[8,72,640]{2,1,0:T(8,128)(2,1)} custom-call(s32[1]{0:T(128)} %bitcast.core_ref, bf16[8,8,8,512]{3,2,1,0:T(8,128)(2,1)S(1)} %all-to-all-done.2.mine_ref, bf16[8,8,8,512]{3,2,1,0:T(8,128)(2,1)S(1)} %collective-permute-done.3.mate_ref, f32[1,1024]{1,0:T(1,128)S(1)} %bitcast.34, bf16[272,640]{1,0:T(8,128)(2,1)S(1)} %fusion.1.w0_ref, ...), custom_call_target="tpu_custom_call" | custom-call | flops 671088640 | bytes 4194304 | tf_op jit(solution)/shard_map/project/pallas_call | solution.py:317
  75.5 3.5 %all-to-all-start.3 = ((bf16[8,72,640]{2,1,0:T(8,128)(2,1)}), bf16[8,72,640]{2,1,0:T(8,128)(2,1)S(1)}, u32[]{:S(2)}, u32[]{:S(2)}) async-start(bf16[8,72,640]{2,1,0:T(8,128)(2,1)} %project.1), calls=%async_computation.3 | async-start | bytes 1474560 | tf_op jit(solution)/shard_map/all_to_all | solution.py:328
  81.2 3.6 %pick.1 = (bf16[8,128,256]{2,1,0:T(8,128)(2,1)}, bf16[8,128,256]{2,1,0:T(8,128)(2,1)}, bf16[8,128,256]{2,1,0:T(8,128)(2,1)}) custom-call(s32[32]{0:T(128)} %reshape.215.rows_ref, bf16[64,128,256]{2,1,0:T(8,128)(2,1)} %bitcast.35), custom_call_target="tpu_custom_call" | custom-call | bytes 4194304 | tf_op jit(solution)/shard_map/pick/pallas_call | solution.py:338
  84.8 3.3 %collective-permute-start.5 = (bf16[8,128,256]{2,1,0:T(8,128)(2,1)}, bf16[8,128,256]{2,1,0:T(8,128)(2,1)S(1)}, u32[]{:S(2)}, u32[]{:S(2)}) collective-permute-start(bf16[8,128,256]{2,1,0:T(8,128)(2,1)} %get-tuple-element.35), channel_id=1, source_target_pairs={{0,384},{128,0},{256,128},{384,256},{1,385},{129,1},{257,129},{385... | collective-permute-start | bytes 1572872 | tf_op jit(solution)/shard_map/ppermute | solution.py:45
  88.1 2.5 %collective-permute-start.6 = (bf16[8,128,256]{2,1,0:T(8,128)(2,1)}, bf16[8,128,256]{2,1,0:T(8,128)(2,1)S(1)}, u32[]{:S(2)}, u32[]{:S(2)}) collective-permute-start(bf16[8,128,256]{2,1,0:T(8,128)(2,1)} %get-tuple-element.36), channel_id=1, source_target_pairs={{0,128},{128,256},{256,384},{384,0},{1,129},{129,257},{257,385},{3... | collective-permute-start | bytes 1572872 | tf_op jit(solution)/shard_map/ppermute | solution.py:45
  91.4 4.7 %collective-permute-start.7 = (bf16[8,128,256]{2,1,0:T(8,128)(2,1)}, bf16[8,128,256]{2,1,0:T(8,128)(2,1)S(1)}, u32[]{:S(2)}, u32[]{:S(2)}) collective-permute-start(bf16[8,128,256]{2,1,0:T(8,128)(2,1)} %get-tuple-element.39), channel_id=1, source_target_pairs={{0,256},{128,384},{256,0},{384,128},{1,257},{129,385},{257,1},{385... | collective-permute-start | bytes 1572872 | tf_op jit(solution)/shard_map/ppermute | solution.py:45
  96.1 5.5 %all-to-all-done.3.parts_ref = bf16[8,72,640]{2,1,0:T(8,128)(2,1)S(1)} async-done(((bf16[8,72,640]{2,1,0:T(8,128)(2,1)}), bf16[8,72,640]{2,1,0:T(8,128)(2,1)S(1)}, u32[]{:S(2)}, u32[]{:S(2)}) %all-to-all-start.3) | async-done | bytes 737312 | tf_op jit(solution)/shard_map/all_to_all | solution.py:328
  101.8 5.9 %collective-permute-start.4 = (bf16[320,128]{1,0:T(8,128)(2,1)S(1)}, bf16[320,128]{1,0:T(8,128)(2,1)S(1)}, u32[]{:S(2)}, u32[]{:S(2)}) collective-permute-start(bf16[320,128]{1,0:T(8,128)(2,1)S(1)} %finish.1.own_ref), channel_id=1, source_target_pairs={{0,8},{2,10},{4,12},{6,14},{8,0},{10,2},{12,4},{14,6},{1,9},{3,11}... | collective-permute-start | bytes 245768 | tf_op jit(solution)/shard_map/ppermute | solution.py:37
  108.3 5.5 %collective-permute-done.4.other_ref = bf16[320,128]{1,0:T(8,128)(2,1)S(1)} collective-permute-done((bf16[320,128]{1,0:T(8,128)(2,1)S(1)}, bf16[320,128]{1,0:T(8,128)(2,1)S(1)}, u32[]{:S(2)}, u32[]{:S(2)}) %collective-permute-start.4) | collective-permute-done | bytes 81952 | tf_op jit(solution)/shard_map/ppermute | solution.py:37
  114.5 4.1 %attend_own.1 = (f32[128,512]{1,0:T(8,128)}, f32[8,512]{1,0:T(8,128)}) custom-call(s32[1]{0:T(128)} %bitcast.14.flag_ref, s32[8]{0:T(128)} %slice_bitcast_fusion.rows_ref, bf16[320,128]{1,0:T(8,128)(2,1)} %copy-done, bf16[320,128]{1,0:T(8,128)(2,1)} %copy-done.3, s32[128,32]{1,0:T(8,128)} %or_select_fusion.eff_ref, ...), custom_call_target="tpu_custom_call" | custom-call | flops 268435456 | bytes 524288 | tf_op jit(solution)/shard_map/attend_own/pallas_call | solution.py:394
  119.6 0.9 copy-done.4
  120.5 0.9 copy-done.6
  122.1 2.4 %attend_near.1 = (f32[128,512]{1,0:T(8,128)S(1)}, f32[8,512]{1,0:T(8,128)S(1)}) custom-call(bf16[320,128]{1,0:T(8,128)(2,1)S(1)} %copy-done.1, bf16[320,128]{1,0:T(8,128)(2,1)S(1)} %copy-done.4, s32[128,32]{1,0:T(8,128)S(1)} %copy-done.2, s32[1,512]{1,0:T(1,128)S(1)} %copy-done.5, f32[128,512]{1,0:T(8,128)S(1)} %copy-done.6, f32[8,512]{1,0:T(8,128)S(1)} %copy-done.7, ...), custom_call_target="tpu_custom_call" | custom-call | flops 536870912 | bytes 1048576 | tf_op jit(solution)/shard_map/attend_near/pallas_call | solution.py:407
  124.6 1.3 attend_far.1
  125.9 5.5 %collective-permute-start.8 = (bf16[144,256]{1,0:T(8,128)(2,1)S(1)}, bf16[144,256]{1,0:T(8,128)(2,1)S(1)}, u32[]{:S(2)}, u32[]{:S(2)}) collective-permute-start(bf16[144,256]{1,0:T(8,128)(2,1)S(1)} %get-tuple-element.42), channel_id=1, source_target_pairs={{0,8},{2,10},{4,12},{6,14},{8,0},{10,2},{12,4},{14,6},{1,9},{3,11}... | collective-permute-start | bytes 221192 | tf_op jit(solution)/shard_map/ppermute | solution.py:37
  131.4 5.3 %collective-permute-done.8.got_ref = bf16[144,256]{1,0:T(8,128)(2,1)S(1)} collective-permute-done((bf16[144,256]{1,0:T(8,128)(2,1)S(1)}, bf16[144,256]{1,0:T(8,128)(2,1)S(1)}, u32[]{:S(2)}, u32[]{:S(2)}) %collective-permute-start.8) | collective-permute-done | bytes 73760 | tf_op jit(solution)/shard_map/ppermute | solution.py:37
  (70 shorter events, 13.9 us)
Async XLA Ops:
  6.5 72.5 %copy-start.8 = (s32[256]{0:T(256)S(1)}, s32[256]{0:T(256)}, u32[]{:S(2)}) copy-start(s32[256]{0:T(256)} %param.13) | copy-start | bytes 3076
  6.5 74.6 %all-gather.3.cloned.1.call-start = ((), (), s32[]{:S(2)}) async-start(), calls=%async_computation.4 | async-start | bytes 4718592 | tf_op jit(solution)/shard_map/all_gather | solution.py:287
  8.7 15.1 %all-to-all-start = ((bf16[16,2,8,128]{3,2,1,0:T(8,128)(2,1)}), bf16[16,2,8,128]{3,2,1,0:T(8,128)(2,1)S(1)}, u32[]{:S(2)}, u32[]{:S(2)}) async-start(bf16[16,2,8,128]{3,2,1,0:T(8,128)(2,1)} %bitcast.3), calls=%async_computation | async-start | bytes 131072 | tf_op jit(solution)/shard_map/all_to_all | solution.py:294
  23.8 25.1 %collective-permute-start = (bf16[272,640]{1,0:T(8,128)(2,1)S(1)}, bf16[272,640]{1,0:T(8,128)(2,1)S(1)}, u32[]{:S(2)}, u32[]{:S(2)}) collective-permute-start(bf16[272,640]{1,0:T(8,128)(2,1)S(1)} %fusion.1.w0_ref), channel_id=1, source_target_pairs={{0,256},{128,384},{256,0},{384,128},{1,257},{129,385},{257,1},{385... | collective-permute-start | bytes 1044488 | tf_op jit(solution)/shard_map/ppermute | solution.py:45
  29.5 19.5 %all-to-all-start.1 = ((bf16[8,4,8,128]{3,2,1,0:T(8,128)(2,1)}), bf16[8,4,8,128]{3,2,1,0:T(8,128)(2,1)S(1)}, u32[]{:S(2)}, u32[]{:S(2)}) async-start(bf16[8,4,8,128]{3,2,1,0:T(8,128)(2,1)} %copy.18), calls=%async_computation.1 | async-start | bytes 131072 | tf_op jit(solution)/shard_map/all_to_all | solution.py:299
  49.8 20.0 %all-to-all-start.2 = ((bf16[8,8,8,512]{3,2,1,0:T(8,128)(2,1)}), bf16[8,8,8,512]{3,2,1,0:T(8,128)(2,1)S(1)}, u32[]{:S(2)}, u32[]{:S(2)}) async-start(bf16[8,8,8,512]{3,2,1,0:T(8,128)(2,1)} %broadcast_in_dim.84), calls=%async_computation.2 | async-start | bytes 1048576 | tf_op jit(solution)/shard_map/all_to_all | solution.py:305
  54.6 10.5 %collective-permute-start.1 = (bf16[272,640]{1,0:T(8,128)(2,1)S(1)}, bf16[272,640]{1,0:T(8,128)(2,1)S(1)}, u32[]{:S(2)}, u32[]{:S(2)}) collective-permute-start(bf16[272,640]{1,0:T(8,128)(2,1)S(1)} %fusion.1.w0_ref), channel_id=1, source_target_pairs={{0,384},{128,0},{256,128},{384,256},{1,385},{129,1},{257,129},{385... | collective-permute-start | bytes 1044488 | tf_op jit(solution)/shard_map/ppermute | solution.py:45
  57.9 10.3 %collective-permute-start.2 = (bf16[272,640]{1,0:T(8,128)(2,1)S(1)}, bf16[272,640]{1,0:T(8,128)(2,1)S(1)}, u32[]{:S(2)}, u32[]{:S(2)}) collective-permute-start(bf16[272,640]{1,0:T(8,128)(2,1)S(1)} %fusion.1.w0_ref), channel_id=1, source_target_pairs={{0,128},{128,256},{256,384},{384,0},{1,129},{129,257},{257,385},{3... | collective-permute-start | bytes 1044488 | tf_op jit(solution)/shard_map/ppermute | solution.py:45
  69.8 3.8 %collective-permute-start.3 = (bf16[8,8,8,512]{3,2,1,0:T(8,128)(2,1)S(1)}, bf16[8,8,8,512]{3,2,1,0:T(8,128)(2,1)S(1)}, u32[]{:S(2)}, u32[]{:S(2)}) collective-permute-start(bf16[8,8,8,512]{3,2,1,0:T(8,128)(2,1)S(1)} %all-to-all-done.2.mine_ref), channel_id=1, source_target_pairs={{0,1},{1,0},{2,3},{3,2},{4,5},{5,4},{6,7},{7,6},{8,9},{9,8},{10,11... | collective-permute-start | bytes 1572872 | tf_op jit(solution)/shard_map/ppermute | solution.py:41
  73.6 17.1 %copy-start.9 = (s32[1,64]{1,0:T(1,128)S(1)}, s32[1,64]{1,0:T(1,128)}, u32[]{:S(2)}) copy-start(s32[1,64]{1,0:T(1,128)} %param.15) | copy-start | bytes 772
  75.5 26.1 %all-to-all-start.3 = ((bf16[8,72,640]{2,1,0:T(8,128)(2,1)}), bf16[8,72,640]{2,1,0:T(8,128)(2,1)S(1)}, u32[]{:S(2)}, u32[]{:S(2)}) async-start(bf16[8,72,640]{2,1,0:T(8,128)(2,1)} %project.1), calls=%async_computation.3 | async-start | bytes 1474560 | tf_op jit(solution)/shard_map/all_to_all | solution.py:328
  81.2 37.5 %copy-start.2 = (s32[128,32]{1,0:T(8,128)S(1)}, s32[128,32]{1,0:T(8,128)}, u32[]{:S(2)}) copy-start(s32[128,32]{1,0:T(8,128)} %or_select_fusion.eff_ref) | copy-start | bytes 49156
  84.8 33.9 %collective-permute-start.5 = (bf16[8,128,256]{2,1,0:T(8,128)(2,1)}, bf16[8,128,256]{2,1,0:T(8,128)(2,1)S(1)}, u32[]{:S(2)}, u32[]{:S(2)}) collective-permute-start(bf16[8,128,256]{2,1,0:T(8,128)(2,1)} %get-tuple-element.35), channel_id=1, source_target_pairs={{0,384},{128,0},{256,128},{384,256},{1,385},{129,1},{257,129},{385... | collective-permute-start | bytes 1572872 | tf_op jit(solution)/shard_map/ppermute | solution.py:45
  88.1 30.5 %collective-permute-start.6 = (bf16[8,128,256]{2,1,0:T(8,128)(2,1)}, bf16[8,128,256]{2,1,0:T(8,128)(2,1)S(1)}, u32[]{:S(2)}, u32[]{:S(2)}) collective-permute-start(bf16[8,128,256]{2,1,0:T(8,128)(2,1)} %get-tuple-element.36), channel_id=1, source_target_pairs={{0,128},{128,256},{256,384},{384,0},{1,129},{129,257},{257,385},{3... | collective-permute-start | bytes 1572872 | tf_op jit(solution)/shard_map/ppermute | solution.py:45
  91.4 27.3 %copy-start.5 = (s32[1,512]{1,0:T(1,128)S(1)}, s32[1,512]{1,0:T(1,128)}, u32[]{:S(2)}) copy-start(s32[1,512]{1,0:T(1,128)} %reshape_tile.3.pos_ref) | copy-start | bytes 6148
  91.4 33.2 %collective-permute-start.7 = (bf16[8,128,256]{2,1,0:T(8,128)(2,1)}, bf16[8,128,256]{2,1,0:T(8,128)(2,1)S(1)}, u32[]{:S(2)}, u32[]{:S(2)}) collective-permute-start(bf16[8,128,256]{2,1,0:T(8,128)(2,1)} %get-tuple-element.39), channel_id=1, source_target_pairs={{0,256},{128,384},{256,0},{384,128},{1,257},{129,385},{257,1},{385... | collective-permute-start | bytes 1572872 | tf_op jit(solution)/shard_map/ppermute | solution.py:45
  101.8 12.7 %copy-start = (bf16[320,128]{1,0:T(8,128)(2,1)}, bf16[320,128]{1,0:T(8,128)(2,1)S(1)}, u32[]{:S(2)}) copy-start(bf16[320,128]{1,0:T(8,128)(2,1)S(1)} %finish.1.own_ref) | copy-start | bytes 245764
  101.8 12.0 %collective-permute-start.4 = (bf16[320,128]{1,0:T(8,128)(2,1)S(1)}, bf16[320,128]{1,0:T(8,128)(2,1)S(1)}, u32[]{:S(2)}, u32[]{:S(2)}) collective-permute-start(bf16[320,128]{1,0:T(8,128)(2,1)S(1)} %finish.1.own_ref), channel_id=1, source_target_pairs={{0,8},{2,10},{4,12},{6,14},{8,0},{10,2},{12,4},{14,6},{1,9},{3,11}... | collective-permute-start | bytes 245768 | tf_op jit(solution)/shard_map/ppermute | solution.py:37
  113.8 0.7 copy-start.3
  118.7 0.9 copy-start.1
  119.6 0.9 copy-start.4
  120.5 0.9 copy-start.6
  121.4 0.7 copy-start.7
  125.9 10.8 %collective-permute-start.8 = (bf16[144,256]{1,0:T(8,128)(2,1)S(1)}, bf16[144,256]{1,0:T(8,128)(2,1)S(1)}, u32[]{:S(2)}, u32[]{:S(2)}) collective-permute-start(bf16[144,256]{1,0:T(8,128)(2,1)S(1)} %get-tuple-element.42), channel_id=1, source_target_pairs={{0,8},{2,10},{4,12},{6,14},{8,0},{10,2},{12,4},{14,6},{1,9},{3,11}... | collective-permute-start | bytes 221192 | tf_op jit(solution)/shard_map/ppermute | solution.py:37
Sparse Core Ops, SparseCore 0:
  9.4 64.2 all-gather.2

commit v7 on v4

--- a/solution.py
+++ b/solution.py
@@ -151,16 +151,18 @@
     acc_ref[...] = acc
 
 
-def attend_early_kernel(which, flag_ref, own_ref, other_ref, eff_ref, fresh_eff_ref, pos_ref, *refs):
-    kv_refs, (acc_ref, run_ref) = refs[: len(which)], refs[len(which) :]
-    is_first = flag_ref[0] == 0
-    queries = jnp.concatenate([own_ref[:QROWS, :], other_ref[:QROWS, :]], axis=0)
+def attend_slots(k, kv_ref, queries, eff_ref, pos, run_ref, acc_ref):
+    for half in range(0, NZ, 4):
+        slots = [(half + i, k * NZ + half + i) for i in range(4)]
+        attend_block(kv_ref, slots, queries, eff_ref, pos, run_ref, acc_ref)
+
+
+def attend_fresh(queries, flag_ref, own_ref, other_ref, fresh_eff_ref, pos, run_ref, acc_ref):
     own_piece = own_ref[QROWS:, :]
     other_piece = other_ref[QROWS:, :]
-    first = jnp.broadcast_to(is_first, own_piece.shape)
+    first = jnp.broadcast_to(flag_ref[0] == 0, own_piece.shape)
     fresh_keys = jnp.where(first, own_piece, other_piece)
     fresh_values = jnp.where(first, other_piece, own_piece)
-    pos = pos_ref[...]
     scores = lax.dot_general(fresh_keys, queries, NT, preferred_element_type=jnp.float32)
     scores = jnp.where(fresh_eff_ref[:, 0:1] <= pos, scores, neg_large)
     peak = jnp.max(scores, axis=0, keepdims=True)
@@ -171,36 +173,36 @@
     acc_ref[...] = lax.dot_general(
         fresh_values, weights.astype(jnp.bfloat16), TN, preferred_element_type=jnp.float32
     )
-    for k, kv_ref in zip(which, kv_refs):
-        for half in range(0, NZ, 4):
-            slots = [(half + i, k * NZ + half + i) for i in range(4)]
-            attend_block(kv_ref, slots, queries, eff_ref, pos, run_ref, acc_ref)
-
-
-def attend_late_kernel(
-    which, own_ref, other_ref, eff_ref, pos_ref, acc_in_ref, run_in_ref, *refs
+
+
+def other_near_kernel(
+    flag_ref,
+    own_ref,
+    other_ref,
+    eff_ref,
+    fresh_eff_ref,
+    pos_ref,
+    kv0_ref,
+    kv1_ref,
+    kv3_ref,
+    acc_ref,
+    run_ref,
 ):
-    kv_refs, (own_out_ref, stat_ref, sent_ref, acc_ref, run_ref) = (
-        refs[: len(which)],
-        refs[len(which) :],
-    )
-    queries = jnp.concatenate([own_ref[:QROWS, :], other_ref[:QROWS, :]], axis=0)
+    queries = other_ref[:QROWS, :]
     pos = pos_ref[...]
+    attend_fresh(queries, flag_ref, own_ref, other_ref, fresh_eff_ref, pos, run_ref, acc_ref)
+    for k, kv_ref in ((0, kv0_ref), (1, kv1_ref), (3, kv3_ref)):
+        attend_slots(k, kv_ref, queries, eff_ref, pos, run_ref, acc_ref)
+
+
+def other_far_kernel(
+    other_ref, eff_ref, pos_ref, acc_in_ref, run_in_ref, kv2_ref, sent_ref, acc_ref, run_ref
+):
     acc_ref[...] = acc_in_ref[...]
     run_ref[...] = run_in_ref[...]
-    for k, kv_ref in zip(which, kv_refs):
-        for half in range(0, NZ, 4):
-            slots = [(half + i, k * NZ + half + i) for i in range(4)]
-            attend_block(kv_ref, slots, queries, eff_ref, pos, run_ref, acc_ref)
+    attend_slots(2, kv2_ref, other_ref[:QROWS, :], eff_ref, pos_ref[...], run_ref, acc_ref)
     peak = run_ref[0:1, :]
     total = run_ref[1:2, :]
-    mixed = acc_ref[...] / total
-    own_out_ref[...] = mixed[:, :QROWS]
-    stat_ref[0:1, :] = peak[:, :QROWS]
-    stat_ref[1:2, :] = total[:, :QROWS]
-    stat_ref[2:8, :] = jnp.zeros((6, QROWS), jnp.float32)
-    peak = peak[:, QROWS:]
-    total = total[:, QROWS:]
     peak_high = peak.astype(jnp.bfloat16).astype(jnp.float32)
     total_high = total.astype(jnp.bfloat16).astype(jnp.float32)
     stats = jnp.concatenate(
@@ -213,21 +215,42 @@
         ],
         axis=0,
     )
-    sent_ref[:HD, :] = mixed[:, QROWS:].astype(jnp.bfloat16)
+    sent_ref[:HD, :] = (acc_ref[...] / total).astype(jnp.bfloat16)
     sent_ref[HD:, :] = stats.astype(jnp.bfloat16)
 
 
-def merge_kernel(own_ref, stat_ref, got_ref, out_ref):
+def own_kernel(
+    flag_ref,
+    own_ref,
+    other_ref,
+    eff_ref,
+    fresh_eff_ref,
+    pos_ref,
+    kv0_ref,
+    kv1_ref,
+    kv2_ref,
+    kv3_ref,
+    acc_ref,
+    run_ref,
+):
+    queries = own_ref[:QROWS, :]
+    pos = pos_ref[...]
+    attend_fresh(queries, flag_ref, own_ref, other_ref, fresh_eff_ref, pos, run_ref, acc_ref)
+    for k, kv_ref in ((0, kv0_ref), (1, kv1_ref), (2, kv2_ref), (3, kv3_ref)):
+        attend_slots(k, kv_ref, queries, eff_ref, pos, run_ref, acc_ref)
+
+
+def merge_kernel(acc_ref, run_ref, got_ref, out_ref):
     stats = got_ref[HD:, :].astype(jnp.float32)
     got_peak = stats[0:1, :] + stats[1:2, :]
     got_total = stats[2:3, :] + stats[3:4, :]
-    peak = stat_ref[0:1, :]
-    total = stat_ref[1:2, :]
+    peak = run_ref[0:1, :]
+    total = run_ref[1:2, :]
     joint = jnp.maximum(peak, got_peak)
-    mine = jnp.exp2(peak - joint) * total
+    mine = jnp.exp2(peak - joint)
     theirs = jnp.exp2(got_peak - joint) * got_total
-    whole = mine + theirs
-    mixed = own_ref[...] * (mine / whole) + got_ref[:HD, :].astype(jnp.float32) * (theirs / whole)
+    whole = mine * total + theirs
+    mixed = acc_ref[...] * (mine / whole) + got_ref[:HD, :].astype(jnp.float32) * (theirs / whole)
     turned = mixed.T.astype(jnp.bfloat16)
     for head in range(QS):
         out_ref[:, pl.ds(head * HD, HD)] = turned[head * ROWS : (head + 1) * ROWS, :]
@@ -248,34 +271,35 @@
 
     store = lax.all_gather(cache_store[:, 0], "z", axis=0, tiled=True)
 
-    states = hidden[0].reshape(ROWS, 2, NC, HD)
-    keep = lax.dynamic_index_in_dim(states, c, 2, keepdims=False)
-    give = lax.dynamic_index_in_dim(states, 1 - c, 2, keepdims=False)
-    taken = swap_cores(give)
-    pairs = jnp.where(c == 0, jnp.stack([keep, taken]), jnp.stack([taken, keep]))
-    blocks = pairs.reshape(2, NY, 8, 2, HD).transpose(0, 3, 1, 2, 4)
-    blocks = jnp.broadcast_to(blocks[None], (2, 2, 2, NY, 8, HD)).reshape(NZ * NY, 8, HD)
+    listed = jnp.pad(own_list.astype(jnp.bfloat16)[None, :], ((0, 15), (0, COLS - MAXC)))
     weight = jnp.concatenate([q_weight[:, 0], kv_weight[:, 0]], axis=1)
-    blocks = lax.all_to_all(blocks, ("z", "y"), 0, 0, tiled=True)
-    blocks = blocks.reshape(NZ, NX, 2, 8, HD)
-    blocks = lax.dynamic_index_in_dim(blocks, z // 4, 2, keepdims=False)
+    weight = jnp.concatenate([weight, listed], axis=0)
+
+    far_weight = shifted(weight, "x", NX, -2)
+    blocks = hidden[0].reshape(NY, 8, 2, NC, HD).transpose(2, 0, 3, 1, 4)
+    blocks = jnp.broadcast_to(blocks[None], (4, 2, NY, NC, 8, HD))
+    blocks = lax.all_to_all(
+        blocks.reshape(NZ * NY * NC, 8, HD), ("z", "y", "c"), 0, 0, tiled=True
+    )
+    blocks, weight, far_weight = lax.optimization_barrier((blocks, weight, far_weight))
+    weights = [weight, shifted(weight, "x", NX, -1), far_weight, shifted(weight, "x", NX, -3)]
+    blocks = blocks.reshape(NZ, NX, 4, 8, HD)
+    blocks = lax.dynamic_index_in_dim(blocks, z // 2, 2, keepdims=False)
     blocks = jnp.concatenate([blocks, blocks], axis=1)
     blocks = lax.dynamic_slice_in_dim(blocks, x, NX, 1)
     blocks = blocks.transpose(0, 2, 1, 3).reshape(NZ, 8, NX * HD)
     tokens = lax.all_to_all(
         jnp.broadcast_to(blocks[None], (NY, NZ, 8, NX * HD)), "y", 0, 0, tiled=True
     )
+    tokens, *weights = lax.optimization_barrier((tokens, *weights))
     mate_tokens = swap_cores(tokens)
-
-    listed = jnp.pad(own_list.astype(jnp.bfloat16)[None, :], ((0, 15), (0, COLS - MAXC)))
-    weight = jnp.concatenate([weight, listed], axis=0)
-    weights = [weight] + [shifted(weight, "x", NX, -k) for k in range(1, NX)]
     gain = lax.dynamic_index_in_dim(norm_gain.reshape(NX, NZ, NC * HD), z, 1, keepdims=False)
     gain = lax.dynamic_slice_in_dim(jnp.concatenate([gain, gain], axis=0), x, NX, 0)
     gain = gain.astype(jnp.float32).reshape(1, NX * NC * HD)
 
     smem = pl.BlockSpec(memory_space=pltpu.SMEM)
     vmem = pl.BlockSpec(memory_space=pltpu.VMEM)
+    hbm = pl.BlockSpec(memory_space=pltpu.MemorySpace.HBM)
     partial = pl.pallas_call(
         project_kernel,
         out_shape=jax.ShapeDtypeStruct((NZ, ROWS + 8, COLS), jnp.bfloat16),
@@ -300,11 +324,11 @@
     picked = pl.pallas_call(
         pick_kernel,
         out_shape=[jax.ShapeDtypeStruct((NZ, HALF, 2 * HD), jnp.bfloat16)] * NX,
-        in_specs=[smem, pl.BlockSpec(memory_space=pl.ANY)],
+        in_specs=[smem, hbm],
         out_specs=[vmem] * NX,
         scratch_shapes=[pltpu.SemaphoreType.DMA((NX * NZ,))],
         name="pick",
-        compiler_params=pltpu.CompilerParams(vmem_limit_bytes=32 * 1024 * 1024),
+        compiler_params=pltpu.CompilerParams(vmem_limit_bytes=60 * 1024 * 1024),
         cost_estimate=pl.CostEstimate(flops=0, bytes_accessed=1 << 22, transcendentals=0),
     )(send_rows.reshape(-1), store)
     arrived = [picked[0]] + [shifted(picked[k], "x", NX, -k) for k in range(1, NX)]
@@ -341,45 +365,51 @@
     eff = jnp.where(replaced | ~slot_live[None, :], far_away, key_pos)
     fresh_eff = jnp.where(positions % STRETCH // HALF == which_half, positions, far_away)
     fresh_eff = jnp.broadcast_to(fresh_eff[:, None], (ROWS, HD))
-    pos_row = jnp.tile(positions, 2 * QS).reshape(1, 2 * QROWS)
-
-    early, late = (0, 1, 3), (2,)
+    pos_row = jnp.tile(positions, QS).reshape(1, QROWS)
+
     params = pltpu.CompilerParams(vmem_limit_bytes=32 * 1024 * 1024)
     run_shapes = [
-        jax.ShapeDtypeStruct((HD, 2 * QROWS), jnp.float32),
-        jax.ShapeDtypeStruct((8, 2 * QROWS), jnp.float32),
+        jax.ShapeDtypeStruct((HD, QROWS), jnp.float32),
+        jax.ShapeDtypeStruct((8, QROWS), jnp.float32),
     ]
 
     def cost(count):
-        pairs = count * NZ * HALF * 2 * QROWS
+        pairs = count * NZ * HALF * QROWS
         return pl.CostEstimate(flops=4 * pairs * HD, bytes_accessed=count << 19, transcendentals=pairs)
 
+    common = (which_half.reshape(1), own, other, eff, fresh_eff, pos_row)
     acc, run = pl.pallas_call(
-        functools.partial(attend_early_kernel, early),
+        other_near_kernel,
         out_shape=run_shapes,
-        in_specs=[smem] + [vmem] * (5 + len(early)),
+        in_specs=[smem] + [vmem] * 8,
         out_specs=[vmem] * 2,
-        name="attend_early",
+        name="other_near",
         compiler_params=params,
-        cost_estimate=cost(len(early)),
-    )(which_half.reshape(1), own, other, eff, fresh_eff, pos_row, *[arrived[k] for k in early])
-    own_part, stats, sent = pl.pallas_call(
-        functools.partial(attend_late_kernel, late),
-        out_shape=[
-            jax.ShapeDtypeStruct((HD, QROWS), jnp.float32),
-            jax.ShapeDtypeStruct((8, QROWS), jnp.float32),
-            jax.ShapeDtypeStruct((HD + 16, QROWS), jnp.bfloat16),
-        ],
-        in_specs=[vmem] * (6 + len(late)),
-        out_specs=[vmem] * 3,
+        cost_estimate=cost(3),
+    )(*common, arrived[0], arrived[1], arrived[3])
+    sent = pl.pallas_call(
+        other_far_kernel,
+        out_shape=jax.ShapeDtypeStruct((HD + 16, QROWS), jnp.bfloat16),
+        in_specs=[vmem] * 6,
+        out_specs=vmem,
         scratch_shapes=[pltpu.VMEM(r.shape, r.dtype) for r in run_shapes],
-        name="attend_late",
+        name="other_far",
         compiler_params=params,
-        cost_estimate=cost(len(late)),
-    )(own, other, eff, pos_row, acc, run, *[arrived[k] for k in late])
+        cost_estimate=cost(1),
+    )(other, eff, pos_row, acc, run, arrived[2])
     got = exchange(sent)
+    queries, allowed, sent = lax.optimization_barrier((own, eff, sent))
+    own_acc, own_run = pl.pallas_call(
+        own_kernel,
+        out_shape=run_shapes,
+        in_specs=[smem] + [vmem] * 9,
+        out_specs=[vmem] * 2,
+        name="own",
+        compiler_params=params,
+        cost_estimate=cost(4),
+    )(which_half.reshape(1), queries, other, allowed, fresh_eff, pos_row, *arrived)
     attended = call(merge_kernel, jax.ShapeDtypeStruct((ROWS, QW), jnp.bfloat16), "merge")(
-        own_part, stats, got
+        own_acc, own_run, got
     )
     return attended.reshape(1, ROWS, 1, QW)
 

time: 151 us -> 139 us (0.921)
  waiting for transfers between devices: 58.1 us -> 35.4 us
  starting transfers between devices: 52.9 us -> 67.3 us
  Pallas kernels: 13.6 us -> 11.3 us
    all_to_all x1, waiting for transfers between devices: 16.1 us -> 0.3 us  [body(): lax.all_to_all(jnp.broadcast_to(blocks[None], (NY, NZ, 8, NX * HD)), 'y',...]
    ppermute x6, waiting for transfers between devices: 8.42 us -> 22.4 us  [shifted(): lax.ppermute(block, axis, [(i, (i + by) % count) for i in range(count)])]
    all_to_all x1, waiting for transfers between devices: 12.3 us -> 0.01 us  [body(): lax.all_to_all(blocks.reshape(NZ * NY * NC, 8, HD), ('z', 'y', 'c'), 0, 0...]
    ppermute x2, waiting for transfers between devices: 16.2 us -> 7 us  [exchange(): lax.ppermute(block, 'y', [(i, (i + NY // 2) % NY) for i in range(NY)])]
    ppermute x2, starting transfers between devices: 4.94 us -> 12.1 us  [exchange(): lax.ppermute(block, 'y', [(i, (i + NY // 2) % NY) for i in range(NY)])]
    all_to_all x1, starting transfers between devices: 3.49 us -> 6.68 us  [body(): lax.all_to_all(jnp.broadcast_to(blocks[None], (NY, NZ, 8, NX * HD)), 'y',...]
    ppermute x6, starting transfers between devices: 19.8 us -> 22.5 us  [shifted(): lax.ppermute(block, axis, [(i, (i + by) % count) for i in range(count)])]
    all_to_all x1, starting transfers between devices: 5.05 us -> 7.53 us  [body(): parts = lax.all_to_all(partial, 'z', 0, 0, tiled=True)]
  transfers between devices with their start and end apart: 14 -> 13, of which waited for: 8 -> 10; matrix products, arithmetic and copies ran while one was open for 6% -> 7% of each run, Pallas kernels for 8% -> 7%
where the time goes in v7:
time: 139 us
  starting transfers between devices  67.3 us (48%)
  waiting for transfers between devices  35.4 us (25%)
  between operations  13.8 us (10%)
  Pallas kernels  11.3 us (8%)
  other arithmetic  5.56 us (4%)
  local copies, waits for them, and re-layouts  5.19 us (4%)
    ppermute x6, starting transfers between devices, shifted(): lax.ppermute(block, axis, [(i, (i + by) % count) for i in range(count)])  22.5 us
    ppermute x6, waiting for transfers between devices, shifted(): lax.ppermute(block, axis, [(i, (i + by) % count) for i in range(count)])  22.4 us
    all_to_all x1, starting transfers between devices, body(): lax.all_to_all(blocks.reshape(NZ * NY * NC, 8, HD), ('z', 'y', 'c'), 0, 0...  16.6 us
    ppermute x2, starting transfers between devices, exchange(): lax.ppermute(block, 'y', [(i, (i + NY // 2) % NY) for i in range(NY)])  12.1 us
    all_to_all x1, starting transfers between devices, body(): parts = lax.all_to_all(partial, 'z', 0, 0, tiled=True)  7.53 us
    ppermute x2, waiting for transfers between devices, exchange(): lax.ppermute(block, 'y', [(i, (i + NY // 2) % NY) for i in range(NY)])  7 us
    all_to_all x1, starting transfers between devices, body(): lax.all_to_all(jnp.broadcast_to(blocks[None], (NY, NZ, 8, NX * HD)), 'y',...  6.68 us
    pallas_call x1, Pallas kernels, body(): pl.pallas_call(pick_kernel, out_shape=[jax.ShapeDtypeStruct((NZ, HALF, 2...  3.89 us
  transfers between devices with their start and end apart: 13, of which 10 were waited for; matrix products, arithmetic and copies ran while one was open for 7% of the time, Pallas kernels for 7%

profile of v7, /device:TPU:64, one launch (start us, length us, event | category | flops | bytes accessed | tf_op | source)
XLA Modules:
  0.0 138.5 jit_solution(11894731592236465087)
XLA Ops:
  7.3 0.8 copy.16
  8.8 16.6 %all-to-all-start = ((bf16[128,8,128]{2,1,0:T(8,128)(2,1)}), bf16[128,8,128]{2,1,0:T(8,128)(2,1)S(1)}, u32[]{:S(2)}, u32[]{:S(2)}) async-start(bf16[128,8,128]{2,1,0:T(8,128)(2,1)} %bitcast.4), calls=%async_computation | async-start | bytes 524288 | tf_op jit(solution)/shard_map/all_to_all | solution.py:281
  26.1 1.0 fusion.1.w0_ref
  27.1 4.9 %collective-permute-start = (bf16[272,640]{1,0:T(8,128)(2,1)S(1)}, bf16[272,640]{1,0:T(8,128)(2,1)S(1)}, u32[]{:S(2)}, u32[]{:S(2)}) collective-permute-start(bf16[272,640]{1,0:T(8,128)(2,1)S(1)} %fusion.1.w0_ref), channel_id=1, source_target_pairs={{0,256},{128,384},{256,0},{384,128},{1,257},{129,385},{257,1},{385... | collective-permute-start | bytes 1044488 | tf_op jit(solution)/shard_map/ppermute | solution.py:45
  32.7 0.9 select_reduce_fusion.1
  34.6 6.2 %collective-permute-done.w2_ref = bf16[272,640]{1,0:T(8,128)(2,1)S(1)} collective-permute-done((bf16[272,640]{1,0:T(8,128)(2,1)S(1)}, bf16[272,640]{1,0:T(8,128)(2,1)S(1)}, u32[]{:S(2)}, u32[]{:S(2)}) %collective-permute-start) | collective-permute-done | bytes 348192 | tf_op jit(solution)/shard_map/ppermute | solution.py:45
  40.8 0.8 broadcast_in_dim.91
  41.6 6.7 %all-to-all-start.1 = ((bf16[8,8,8,512]{3,2,1,0:T(8,128)(2,1)}), bf16[8,8,8,512]{3,2,1,0:T(8,128)(2,1)S(1)}, u32[]{:S(2)}, u32[]{:S(2)}) async-start(bf16[8,8,8,512]{3,2,1,0:T(8,128)(2,1)} %broadcast_in_dim.91), calls=%async_computation.1 | async-start | bytes 1048576 | tf_op jit(solution)/shard_map/all_to_all | solution.py:291
  48.4 4.7 %collective-permute-start.1 = (bf16[272,640]{1,0:T(8,128)(2,1)S(1)}, bf16[272,640]{1,0:T(8,128)(2,1)S(1)}, u32[]{:S(2)}, u32[]{:S(2)}) collective-permute-start(bf16[272,640]{1,0:T(8,128)(2,1)S(1)} %fusion.1.w0_ref), channel_id=1, source_target_pairs={{0,384},{128,0},{256,128},{384,256},{1,385},{129,1},{257,129},{385... | collective-permute-start | bytes 1044488 | tf_op jit(solution)/shard_map/ppermute | solution.py:45
  53.1 1.9 %collective-permute-start.2 = (bf16[272,640]{1,0:T(8,128)(2,1)S(1)}, bf16[272,640]{1,0:T(8,128)(2,1)S(1)}, u32[]{:S(2)}, u32[]{:S(2)}) collective-permute-start(bf16[272,640]{1,0:T(8,128)(2,1)S(1)} %fusion.1.w0_ref), channel_id=1, source_target_pairs={{0,128},{128,256},{256,384},{384,0},{1,129},{129,257},{257,385},{3... | collective-permute-start | bytes 1044488 | tf_op jit(solution)/shard_map/ppermute | solution.py:45
  55.1 4.5 %collective-permute-done.1.w1_ref = bf16[272,640]{1,0:T(8,128)(2,1)S(1)} collective-permute-done((bf16[272,640]{1,0:T(8,128)(2,1)S(1)}, bf16[272,640]{1,0:T(8,128)(2,1)S(1)}, u32[]{:S(2)}, u32[]{:S(2)}) %collective-permute-start.1) | collective-permute-done | bytes 348192 | tf_op jit(solution)/shard_map/ppermute | solution.py:45
  59.7 5.3 %collective-permute-done.2.w3_ref = bf16[272,640]{1,0:T(8,128)(2,1)S(1)} collective-permute-done((bf16[272,640]{1,0:T(8,128)(2,1)S(1)}, bf16[272,640]{1,0:T(8,128)(2,1)S(1)}, u32[]{:S(2)}, u32[]{:S(2)}) %collective-permute-start.2) | collective-permute-done | bytes 348192 | tf_op jit(solution)/shard_map/ppermute | solution.py:45
  65.3 1.9 %collective-permute-start.3 = (bf16[8,8,8,512]{3,2,1,0:T(8,128)(2,1)S(1)}, bf16[8,8,8,512]{3,2,1,0:T(8,128)(2,1)S(1)}, u32[]{:S(2)}, u32[]{:S(2)}) collective-permute-start(bf16[8,8,8,512]{3,2,1,0:T(8,128)(2,1)S(1)} %all-to-all-done.1.mine_ref), channel_id=1, source_target_pairs={{0,1},{1,0},{2,3},{3,2},{4,5},{5,4},{6,7},{7,6},{8,9},{9,8},{10,11... | collective-permute-start | bytes 1572872 | tf_op jit(solution)/shard_map/ppermute | solution.py:41
  67.5 1.6 %collective-permute-done.3.mate_ref = bf16[8,8,8,512]{3,2,1,0:T(8,128)(2,1)S(1)} collective-permute-done((bf16[8,8,8,512]{3,2,1,0:T(8,128)(2,1)S(1)}, bf16[8,8,8,512]{3,2,1,0:T(8,128)(2,1)S(1)}, u32[]{:S(2)}, u32[]{:S(2)}) %collective-permute-start.3) | collective-permute-done | bytes 524320 | tf_op jit(solution)/shard_map/ppermute | solution.py:41
  69.1 1.9 %project.1 = bf16[8,72,640]{2,1,0:T(8,128)(2,1)} custom-call(s32[1]{0:T(128)} %bitcast.1.core_ref, bf16[8,8,8,512]{3,2,1,0:T(8,128)(2,1)S(1)} %all-to-all-done.1.mine_ref, bf16[8,8,8,512]{3,2,1,0:T(8,128)(2,1)S(1)} %collective-permute-done.3.mate_ref, f32[1,1024]{1,0:T(1,128)S(1)} %bitcast.30, bf16[272,640]{1,0:T(8,128)(2,1)S(1)} %fusion.1.w0_ref, ...), custom_call_target="tpu_custom_call" | custom-call | flops 671088640 | bytes 4194304 | tf_op jit(solution)/shard_map/project/pallas_call | solution.py:303
  71.0 7.5 %all-to-all-start.2 = ((bf16[8,72,640]{2,1,0:T(8,128)(2,1)}), bf16[8,72,640]{2,1,0:T(8,128)(2,1)S(1)}, u32[]{:S(2)}, u32[]{:S(2)}) async-start(bf16[8,72,640]{2,1,0:T(8,128)(2,1)} %project.1), calls=%async_computation.2 | async-start | bytes 1474560 | tf_op jit(solution)/shard_map/all_to_all | solution.py:314
  80.8 3.9 %pick.1 = (bf16[8,128,256]{2,1,0:T(8,128)(2,1)}, bf16[8,128,256]{2,1,0:T(8,128)(2,1)}, bf16[8,128,256]{2,1,0:T(8,128)(2,1)}, bf16[8,128,256]{2,1,0:T(8,128)(2,1)}) custom-call(s32[32]{0:T(128)} %reshape.213.rows_ref, bf16[64,128,256]{2,1,0:T(8,128)(2,1)} %bitcast.31), custom_call_target="tpu_custom_call" | custom-call | bytes 4194304 | tf_op jit(solution)/shard_map/pick/pallas_call | solution.py:324
  84.7 4.8 %collective-permute-start.5 = (bf16[8,128,256]{2,1,0:T(8,128)(2,1)}, bf16[8,128,256]{2,1,0:T(8,128)(2,1)S(1)}, u32[]{:S(2)}, u32[]{:S(2)}) collective-permute-start(bf16[8,128,256]{2,1,0:T(8,128)(2,1)} %get-tuple-element.32), channel_id=1, source_target_pairs={{0,384},{128,0},{256,128},{384,256},{1,385},{129,1},{257,129},{385... | collective-permute-start | bytes 1572872 | tf_op jit(solution)/shard_map/ppermute | solution.py:45
  89.5 1.9 %collective-permute-start.6 = (bf16[8,128,256]{2,1,0:T(8,128)(2,1)}, bf16[8,128,256]{2,1,0:T(8,128)(2,1)S(1)}, u32[]{:S(2)}, u32[]{:S(2)}) collective-permute-start(bf16[8,128,256]{2,1,0:T(8,128)(2,1)} %get-tuple-element.33), channel_id=1, source_target_pairs={{0,128},{128,256},{256,384},{384,0},{1,129},{129,257},{257,385},{3... | collective-permute-start | bytes 1572872 | tf_op jit(solution)/shard_map/ppermute | solution.py:45
  91.4 4.3 %collective-permute-start.7 = (bf16[8,128,256]{2,1,0:T(8,128)(2,1)}, bf16[8,128,256]{2,1,0:T(8,128)(2,1)S(1)}, u32[]{:S(2)}, u32[]{:S(2)}) collective-permute-start(bf16[8,128,256]{2,1,0:T(8,128)(2,1)} %get-tuple-element.36), channel_id=1, source_target_pairs={{0,256},{128,384},{256,0},{384,128},{1,257},{129,385},{257,1},{385... | collective-permute-start | bytes 1572872 | tf_op jit(solution)/shard_map/ppermute | solution.py:45
  96.1 3.3 %all-to-all-done.2.parts_ref = bf16[8,72,640]{2,1,0:T(8,128)(2,1)S(1)} async-done(((bf16[8,72,640]{2,1,0:T(8,128)(2,1)}), bf16[8,72,640]{2,1,0:T(8,128)(2,1)S(1)}, u32[]{:S(2)}, u32[]{:S(2)}) %all-to-all-start.2) | async-done | bytes 737312 | tf_op jit(solution)/shard_map/all_to_all | solution.py:314
  99.7 7.3 %collective-permute-start.4 = (bf16[320,128]{1,0:T(8,128)(2,1)S(1)}, bf16[320,128]{1,0:T(8,128)(2,1)S(1)}, u32[]{:S(2)}, u32[]{:S(2)}) collective-permute-start(bf16[320,128]{1,0:T(8,128)(2,1)S(1)} %finish.1.own_ref), channel_id=1, source_target_pairs={{0,8},{2,10},{4,12},{6,14},{8,0},{10,2},{12,4},{14,6},{1,9},{3,11}... | collective-permute-start | bytes 245768 | tf_op jit(solution)/shard_map/ppermute | solution.py:37
  107.1 3.7 %collective-permute-done.4.other_ref = bf16[320,128]{1,0:T(8,128)(2,1)S(1)} collective-permute-done((bf16[320,128]{1,0:T(8,128)(2,1)S(1)}, bf16[320,128]{1,0:T(8,128)(2,1)S(1)}, u32[]{:S(2)}, u32[]{:S(2)}) %collective-permute-start.4) | collective-permute-done | bytes 81952 | tf_op jit(solution)/shard_map/ppermute | solution.py:37
  110.8 1.2 collective-permute-done.5.kv1_ref
  112.0 5.2 %collective-permute-done.6.kv3_ref = bf16[8,128,256]{2,1,0:T(8,128)(2,1)S(1)} collective-permute-done((bf16[8,128,256]{2,1,0:T(8,128)(2,1)}, bf16[8,128,256]{2,1,0:T(8,128)(2,1)S(1)}, u32[]{:S(2)}, u32[]{:S(2)}) %collective-permute-start.6) | collective-permute-done | bytes 524320 | tf_op jit(solution)/shard_map/ppermute | solution.py:45
  117.2 1.0 copy-done
  118.3 1.7 %other_near.1 = (f32[128,256]{1,0:T(8,128)S(1)}, f32[8,256]{1,0:T(8,128)S(1)}) custom-call(s32[1]{0:T(128)} %bitcast.flag_ref, bf16[320,128]{1,0:T(8,128)(2,1)S(1)} %finish.1.own_ref, bf16[320,128]{1,0:T(8,128)(2,1)S(1)} %collective-permute-done.4.other_ref, s32[128,32]{1,0:T(8,128)S(1)} %or_select_fusion.eff_ref, ...), custom_call_target="tpu_custom_call" | custom-call | flops 402653184 | bytes 1572864 | tf_op jit(solution)/shard_map/other_near/pallas_call | solution.py:381
  119.9 0.8 other_far.1
  120.7 4.8 %collective-permute-start.8 = (bf16[144,256]{1,0:T(8,128)(2,1)S(1)}, bf16[144,256]{1,0:T(8,128)(2,1)S(1)}, u32[]{:S(2)}, u32[]{:S(2)}) collective-permute-start(bf16[144,256]{1,0:T(8,128)(2,1)S(1)} %other_far.1), channel_id=1, source_target_pairs={{0,8},{2,10},{4,12},{6,14},{8,0},{10,2},{12,4},{14,6},{1,9},{3,11}... | collective-permute-start | bytes 221192 | tf_op jit(solution)/shard_map/ppermute | solution.py:37
  125.6 2.0 %own.1 = (f32[128,256]{1,0:T(8,128)S(1)}, f32[8,256]{1,0:T(8,128)S(1)}) custom-call(s32[1]{0:T(128)} %bitcast.flag_ref, bf16[320,128]{1,0:T(8,128)(2,1)S(1)} %finish.1.own_ref, bf16[320,128]{1,0:T(8,128)(2,1)S(1)} %collective-permute-done.4.other_ref, s32[128,32]{1,0:T(8,128)S(1)} %or_select_fusion.eff_ref, s32[64,128]{1,0:T(8,128)S(1)} %broadcast_in_dim.100.fresh_eff_ref, ...), custom_call_target="tpu_custom_call" | custom-call | flops 536870912 | bytes 2097152 | tf_op jit(solution)/shard_map/own/pallas_call | solution.py:402
  127.6 3.3 %collective-permute-done.8.got_ref = bf16[144,256]{1,0:T(8,128)(2,1)S(1)} collective-permute-done((bf16[144,256]{1,0:T(8,128)(2,1)S(1)}, bf16[144,256]{1,0:T(8,128)(2,1)S(1)}, u32[]{:S(2)}, u32[]{:S(2)}) %collective-permute-start.8) | collective-permute-done | bytes 73760 | tf_op jit(solution)/shard_map/ppermute | solution.py:37
  130.9 0.8 merge.1
  (56 shorter events, 7.4 us)
Async XLA Ops:
  6.5 41.8 %copy-start.3 = (s32[1,64]{1,0:T(1,128)S(1)}, s32[1,64]{1,0:T(1,128)}, u32[]{:S(2)}) copy-start(s32[1,64]{1,0:T(1,128)} %param.15) | copy-start | bytes 772
  6.5 74.3 %all-gather.3.cloned.1.call-start = ((), (), s32[]{:S(2)}) async-start(), calls=%async_computation.3 | async-start | bytes 4718592 | tf_op jit(solution)/shard_map/all_gather | solution.py:272
  8.1 70.5 %copy-start.2 = (s32[256]{0:T(256)S(1)}, s32[256]{0:T(256)}, u32[]{:S(2)}) copy-start(s32[256]{0:T(256)} %param.13) | copy-start | bytes 3076
  8.8 31.9 %all-to-all-start = ((bf16[128,8,128]{2,1,0:T(8,128)(2,1)}), bf16[128,8,128]{2,1,0:T(8,128)(2,1)S(1)}, u32[]{:S(2)}, u32[]{:S(2)}) async-start(bf16[128,8,128]{2,1,0:T(8,128)(2,1)} %bitcast.4), calls=%async_computation | async-start | bytes 524288 | tf_op jit(solution)/shard_map/all_to_all | solution.py:281
  27.1 13.6 %collective-permute-start = (bf16[272,640]{1,0:T(8,128)(2,1)S(1)}, bf16[272,640]{1,0:T(8,128)(2,1)S(1)}, u32[]{:S(2)}, u32[]{:S(2)}) collective-permute-start(bf16[272,640]{1,0:T(8,128)(2,1)S(1)} %fusion.1.w0_ref), channel_id=1, source_target_pairs={{0,256},{128,384},{256,0},{384,128},{1,257},{129,385},{257,1},{385... | collective-permute-start | bytes 1044488 | tf_op jit(solution)/shard_map/ppermute | solution.py:45
  41.6 23.7 %all-to-all-start.1 = ((bf16[8,8,8,512]{3,2,1,0:T(8,128)(2,1)}), bf16[8,8,8,512]{3,2,1,0:T(8,128)(2,1)S(1)}, u32[]{:S(2)}, u32[]{:S(2)}) async-start(bf16[8,8,8,512]{3,2,1,0:T(8,128)(2,1)} %broadcast_in_dim.91), calls=%async_computation.1 | async-start | bytes 1048576 | tf_op jit(solution)/shard_map/all_to_all | solution.py:291
  48.4 11.3 %collective-permute-start.1 = (bf16[272,640]{1,0:T(8,128)(2,1)S(1)}, bf16[272,640]{1,0:T(8,128)(2,1)S(1)}, u32[]{:S(2)}, u32[]{:S(2)}) collective-permute-start(bf16[272,640]{1,0:T(8,128)(2,1)S(1)} %fusion.1.w0_ref), channel_id=1, source_target_pairs={{0,384},{128,0},{256,128},{384,256},{1,385},{129,1},{257,129},{385... | collective-permute-start | bytes 1044488 | tf_op jit(solution)/shard_map/ppermute | solution.py:45
  53.1 11.9 %collective-permute-start.2 = (bf16[272,640]{1,0:T(8,128)(2,1)S(1)}, bf16[272,640]{1,0:T(8,128)(2,1)S(1)}, u32[]{:S(2)}, u32[]{:S(2)}) collective-permute-start(bf16[272,640]{1,0:T(8,128)(2,1)S(1)} %fusion.1.w0_ref), channel_id=1, source_target_pairs={{0,128},{128,256},{256,384},{384,0},{1,129},{129,257},{257,385},{3... | collective-permute-start | bytes 1044488 | tf_op jit(solution)/shard_map/ppermute | solution.py:45
  65.3 3.8 %collective-permute-start.3 = (bf16[8,8,8,512]{3,2,1,0:T(8,128)(2,1)S(1)}, bf16[8,8,8,512]{3,2,1,0:T(8,128)(2,1)S(1)}, u32[]{:S(2)}, u32[]{:S(2)}) collective-permute-start(bf16[8,8,8,512]{3,2,1,0:T(8,128)(2,1)S(1)} %all-to-all-done.1.mine_ref), channel_id=1, source_target_pairs={{0,1},{1,0},{2,3},{3,2},{4,5},{5,4},{6,7},{7,6},{8,9},{9,8},{10,11... | collective-permute-start | bytes 1572872 | tf_op jit(solution)/shard_map/ppermute | solution.py:41
  71.0 28.4 %all-to-all-start.2 = ((bf16[8,72,640]{2,1,0:T(8,128)(2,1)}), bf16[8,72,640]{2,1,0:T(8,128)(2,1)S(1)}, u32[]{:S(2)}, u32[]{:S(2)}) async-start(bf16[8,72,640]{2,1,0:T(8,128)(2,1)} %project.1), calls=%async_computation.2 | async-start | bytes 1474560 | tf_op jit(solution)/shard_map/all_to_all | solution.py:314
  84.7 40.9 %copy-start.1 = (bf16[8,128,256]{2,1,0:T(8,128)(2,1)S(1)}, bf16[8,128,256]{2,1,0:T(8,128)(2,1)}, u32[]{:S(2)}) copy-start(bf16[8,128,256]{2,1,0:T(8,128)(2,1)} %get-tuple-element.31.kv0_ref) | copy-start | bytes 1572868
  84.7 27.2 %collective-permute-start.5 = (bf16[8,128,256]{2,1,0:T(8,128)(2,1)}, bf16[8,128,256]{2,1,0:T(8,128)(2,1)S(1)}, u32[]{:S(2)}, u32[]{:S(2)}) collective-permute-start(bf16[8,128,256]{2,1,0:T(8,128)(2,1)} %get-tuple-element.32), channel_id=1, source_target_pairs={{0,384},{128,0},{256,128},{384,256},{1,385},{129,1},{257,129},{385... | collective-permute-start | bytes 1572872 | tf_op jit(solution)/shard_map/ppermute | solution.py:45
  89.5 27.7 %collective-permute-start.6 = (bf16[8,128,256]{2,1,0:T(8,128)(2,1)}, bf16[8,128,256]{2,1,0:T(8,128)(2,1)S(1)}, u32[]{:S(2)}, u32[]{:S(2)}) collective-permute-start(bf16[8,128,256]{2,1,0:T(8,128)(2,1)} %get-tuple-element.33), channel_id=1, source_target_pairs={{0,128},{128,256},{256,384},{384,0},{1,129},{129,257},{257,385},{3... | collective-permute-start | bytes 1572872 | tf_op jit(solution)/shard_map/ppermute | solution.py:45
  91.4 28.5 %collective-permute-start.7 = (bf16[8,128,256]{2,1,0:T(8,128)(2,1)}, bf16[8,128,256]{2,1,0:T(8,128)(2,1)S(1)}, u32[]{:S(2)}, u32[]{:S(2)}) collective-permute-start(bf16[8,128,256]{2,1,0:T(8,128)(2,1)} %get-tuple-element.36), channel_id=1, source_target_pairs={{0,256},{128,384},{256,0},{384,128},{1,257},{129,385},{257,1},{385... | collective-permute-start | bytes 1572872 | tf_op jit(solution)/shard_map/ppermute | solution.py:45
  99.7 11.1 %collective-permute-start.4 = (bf16[320,128]{1,0:T(8,128)(2,1)S(1)}, bf16[320,128]{1,0:T(8,128)(2,1)S(1)}, u32[]{:S(2)}, u32[]{:S(2)}) collective-permute-start(bf16[320,128]{1,0:T(8,128)(2,1)S(1)} %finish.1.own_ref), channel_id=1, source_target_pairs={{0,8},{2,10},{4,12},{6,14},{8,0},{10,2},{12,4},{14,6},{1,9},{3,11}... | collective-permute-start | bytes 245768 | tf_op jit(solution)/shard_map/ppermute | solution.py:37
  117.2 1.0 copy-start
  120.7 10.2 %collective-permute-start.8 = (bf16[144,256]{1,0:T(8,128)(2,1)S(1)}, bf16[144,256]{1,0:T(8,128)(2,1)S(1)}, u32[]{:S(2)}, u32[]{:S(2)}) collective-permute-start(bf16[144,256]{1,0:T(8,128)(2,1)S(1)} %other_far.1), channel_id=1, source_target_pairs={{0,8},{2,10},{4,12},{6,14},{8,0},{10,2},{12,4},{14,6},{1,9},{3,11}... | collective-permute-start | bytes 221192 | tf_op jit(solution)/shard_map/ppermute | solution.py:37
Sparse Core Ops, SparseCore 0:
  9.4 64.7 all-gather.2

commit v8 on v7

--- a/solution.py
+++ b/solution.py
@@ -57,7 +57,30 @@
     )
 
 
-def project_kernel(core_ref, mine_ref, mate_ref, gain_ref, w0_ref, w1_ref, w2_ref, w3_ref, out_ref):
+def project_kernel(
+    core_ref,
+    mine_ref,
+    mate_ref,
+    gain_ref,
+    held_ref,
+    w0_ref,
+    w1_ref,
+    w2_ref,
+    w3_ref,
+    out_ref,
+    rows_ref,
+):
+    lane = lax.broadcasted_iota(jnp.int32, (NZ * CH_DEV, HD), 1)
+    line = lax.broadcasted_iota(jnp.int32, (NZ * CH_DEV, HD), 0)
+    for k, w_ref in enumerate((w0_ref, w1_ref, w2_ref, w3_ref)):
+        listed = w_ref[2 * HD :, :HD].astype(jnp.float32)[0:1, :]
+        hit = (held_ref[...] == listed) & (lane < MAXC)
+        found = jnp.where(hit, (line % CH_DEV).astype(jnp.float32), 0.0)
+        found = jnp.sum(found.reshape(NZ, CH_DEV, HD), axis=1)
+        found = jnp.sum(found, axis=1, keepdims=True).astype(jnp.int32)
+        base = lax.broadcasted_iota(jnp.int32, (NZ, HD), 0) * CH_DEV
+        rows_ref[k] = base + found
+
     weights = jnp.concatenate([w[: 2 * HD, :] for w in (w0_ref, w1_ref, w2_ref, w3_ref)], axis=0)
     gain = gain_ref[...]
     is_zero = core_ref[0] == 0
@@ -112,14 +135,17 @@
         out_ref[pl.ds(group * ROWS, ROWS), :] = turned.astype(jnp.bfloat16)
 
 
-def pick_kernel(rows_ref, store_ref, *refs):
-    outs, sem = refs[:NX], refs[NX]
+def pick_kernel(which, rows_ref, store_ref, *refs):
+    outs, (table_ref, sem, table_sem) = refs[: len(which)], refs[len(which) :]
+    table = pltpu.make_async_copy(rows_ref, table_ref, table_sem)
+    table.start()
+    table.wait()
     copies = []
-    for k in (2, 1, 3, 0):
+    for at, k in enumerate(which):
         for i in range(NZ):
-            row = rows_ref[((NX - k) % NX) * NZ + i]
+            row = table_ref[(NX - k) % NX, i, 0]
             copies.append(
-                pltpu.make_async_copy(store_ref.at[row], outs[k].at[i], sem.at[k * NZ + i])
+                pltpu.make_async_copy(store_ref.at[row], outs[at].at[i], sem.at[at * NZ + i])
             )
             copies[-1].start()
     for copy in copies:
@@ -291,47 +317,11 @@
     tokens = lax.all_to_all(
         jnp.broadcast_to(blocks[None], (NY, NZ, 8, NX * HD)), "y", 0, 0, tiled=True
     )
-    tokens, *weights = lax.optimization_barrier((tokens, *weights))
-    mate_tokens = swap_cores(tokens)
-    gain = lax.dynamic_index_in_dim(norm_gain.reshape(NX, NZ, NC * HD), z, 1, keepdims=False)
-    gain = lax.dynamic_slice_in_dim(jnp.concatenate([gain, gain], axis=0), x, NX, 0)
-    gain = gain.astype(jnp.float32).reshape(1, NX * NC * HD)
-
-    smem = pl.BlockSpec(memory_space=pltpu.SMEM)
-    vmem = pl.BlockSpec(memory_space=pltpu.VMEM)
-    hbm = pl.BlockSpec(memory_space=pltpu.MemorySpace.HBM)
-    partial = pl.pallas_call(
-        project_kernel,
-        out_shape=jax.ShapeDtypeStruct((NZ, ROWS + 8, COLS), jnp.bfloat16),
-        in_specs=[smem] + [vmem] * 7,
-        out_specs=vmem,
-        name="project",
-        compiler_params=pltpu.CompilerParams(vmem_limit_bytes=32 * 1024 * 1024),
-        cost_estimate=pl.CostEstimate(
-            flops=2 * NZ * ROWS * 1024 * COLS, bytes_accessed=1 << 22, transcendentals=0
-        ),
-    )(c.reshape(1), tokens, mate_tokens, gain, *weights)
-    parts = lax.all_to_all(partial, "z", 0, 0, tiled=True)
-
-    lists = jnp.stack([w[NC * HD, :MAXC] for w in weights]).astype(jnp.int32)
     steps = jnp.arange(NZ, dtype=jnp.int32)
-    row_ids = (x * NZ + steps)[:, None] * CH_DEV + int_rows[None, :]
-    here = location[None, None, :] == row_ids[:, :, None]
-    held = jnp.sum(jnp.where(here, table, 0), axis=2)
-    wanted = jnp.any(lists[:, :, None, None] == held[None, None], axis=1)
-    send_rows = jnp.sum(jnp.where(wanted, int_rows, 0), axis=2) + steps[None, :] * CH_DEV
-    send_rows, _ = lax.optimization_barrier((send_rows, partial[0, ROWS:, :HD]))
-    picked = pl.pallas_call(
-        pick_kernel,
-        out_shape=[jax.ShapeDtypeStruct((NZ, HALF, 2 * HD), jnp.bfloat16)] * NX,
-        in_specs=[smem, hbm],
-        out_specs=[vmem] * NX,
-        scratch_shapes=[pltpu.SemaphoreType.DMA((NX * NZ,))],
-        name="pick",
-        compiler_params=pltpu.CompilerParams(vmem_limit_bytes=60 * 1024 * 1024),
-        cost_estimate=pl.CostEstimate(flops=0, bytes_accessed=1 << 22, transcendentals=0),
-    )(send_rows.reshape(-1), store)
-    arrived = [picked[0]] + [shifted(picked[k], "x", NX, -k) for k in range(1, NX)]
+    row_ids = ((x * NZ + steps)[:, None] * CH_DEV + int_rows[None, :]).reshape(-1)
+    here = location[None, :] == row_ids[:, None]
+    held = jnp.sum(jnp.where(here, table, 0), axis=1).astype(jnp.float32)
+    held = jnp.broadcast_to(held[:, None], (NZ * CH_DEV, HD))
 
     frequency = jnp.exp(
         -math.log(theta_base) * jnp.arange(HD // 2, dtype=jnp.float32) / (HD // 2)
@@ -344,11 +334,6 @@
     fresh_cos = jnp.where(is_first, cos, 1.0)
     fresh_sin = jnp.where(is_first, sin, 0.0)
     scale = math.log2(math.e) / math.sqrt(HD)
-
-    own = call(
-        finish_kernel, jax.ShapeDtypeStruct((QROWS + ROWS, HD), jnp.bfloat16), "finish"
-    )(parts, cos * scale, sin * scale, fresh_cos, fresh_sin)
-    other = exchange(own)
 
     own_row = jnp.sum(jnp.where(own_list[:, None] == table[None, :], location[None, :], 0), axis=1)
     own_shard = own_row // CH_DEV
@@ -366,6 +351,63 @@
     fresh_eff = jnp.where(positions % STRETCH // HALF == which_half, positions, far_away)
     fresh_eff = jnp.broadcast_to(fresh_eff[:, None], (ROWS, HD))
     pos_row = jnp.tile(positions, QS).reshape(1, QROWS)
+
+    gain = lax.dynamic_index_in_dim(norm_gain.reshape(NX, NZ, NC * HD), z, 1, keepdims=False)
+    gain = lax.dynamic_slice_in_dim(jnp.concatenate([gain, gain], axis=0), x, NX, 0)
+    gain = gain.astype(jnp.float32).reshape(1, NX * NC * HD)
+
+    turns = (cos * scale, sin * scale, fresh_cos, fresh_sin)
+    tokens, weights, turns, eff, fresh_eff, pos_row, gain, held = lax.optimization_barrier(
+        (tokens, weights, turns, eff, fresh_eff, pos_row, gain, held)
+    )
+    mate_tokens = swap_cores(tokens)
+
+    smem = pl.BlockSpec(memory_space=pltpu.SMEM)
+    vmem = pl.BlockSpec(memory_space=pltpu.VMEM)
+    hbm = pl.BlockSpec(memory_space=pltpu.MemorySpace.HBM)
+    partial, send_rows = pl.pallas_call(
+        project_kernel,
+        out_shape=[
+            jax.ShapeDtypeStruct((NZ, ROWS + 8, COLS), jnp.bfloat16),
+            jax.ShapeDtypeStruct((NX, NZ, HD), jnp.int32),
+        ],
+        in_specs=[smem] + [vmem] * 8,
+        out_specs=[vmem] * 2,
+        name="project",
+        compiler_params=pltpu.CompilerParams(vmem_limit_bytes=32 * 1024 * 1024),
+        cost_estimate=pl.CostEstimate(
+            flops=2 * NZ * ROWS * 1024 * COLS, bytes_accessed=1 << 22, transcendentals=0
+        ),
+    )(c.reshape(1), tokens, mate_tokens, gain, held, *weights)
+    parts = lax.all_to_all(partial, "z", 0, 0, tiled=True)
+
+    def pick(which, rows):
+        return pl.pallas_call(
+            functools.partial(pick_kernel, which),
+            out_shape=[jax.ShapeDtypeStruct((NZ, HALF, 2 * HD), jnp.bfloat16)] * len(which),
+            in_specs=[vmem, hbm],
+            out_specs=[vmem] * len(which),
+            scratch_shapes=[
+                pltpu.SMEM((NX, NZ, HD), jnp.int32),
+                pltpu.SemaphoreType.DMA((len(which) * NZ,)),
+                pltpu.SemaphoreType.DMA,
+            ],
+            name="pick",
+            compiler_params=pltpu.CompilerParams(vmem_limit_bytes=50 * 1024 * 1024),
+            cost_estimate=pl.CostEstimate(
+                flops=0, bytes_accessed=len(which) << 20, transcendentals=0
+            ),
+        )(rows, store)
+
+    picked = dict(zip((2, 1, 3), pick((2, 1, 3), send_rows)))
+    arrived = {k: shifted(picked[k], "x", NX, -k) for k in (2, 1, 3)}
+    own_rows, parts = lax.optimization_barrier((send_rows, parts))
+    arrived[0] = pick((0,), own_rows)[0]
+
+    own = call(
+        finish_kernel, jax.ShapeDtypeStruct((QROWS + ROWS, HD), jnp.bfloat16), "finish"
+    )(parts, *turns)
+    other = exchange(own)
 
     params = pltpu.CompilerParams(vmem_limit_bytes=32 * 1024 * 1024)
     run_shapes = [
@@ -407,7 +449,7 @@
         name="own",
         compiler_params=params,
         cost_estimate=cost(4),
-    )(which_half.reshape(1), queries, other, allowed, fresh_eff, pos_row, *arrived)
+    )(which_half.reshape(1), queries, other, allowed, fresh_eff, pos_row, *[arrived[k] for k in range(NX)])
     attended = call(merge_kernel, jax.ShapeDtypeStruct((ROWS, QW), jnp.bfloat16), "merge")(
         own_acc, own_run, got
     )

time: 139 us -> 136 us (0.978)
  the two profiles are of different devices: /device:TPU:64 before, /device:TPU:8 now
where the time goes in v8:
time: 136 us; the launch traced here: 135 us
  starting transfers between devices  66.3 us (49%)
  waiting for transfers between devices  32.1 us (24%)
  between operations  13.7 us (10%)
  Pallas kernels  12.7 us (9%)
  other arithmetic  6.55 us (5%)
  local copies, waits for them, and re-layouts  3.7 us (3%)
    ppermute x6, starting transfers between devices, shifted(): lax.ppermute(block, axis, [(i, (i + by) % count) for i in range(count)])  21.4 us
    all_to_all x1, starting transfers between devices, body(): lax.all_to_all(blocks.reshape(NZ * NY * NC, 8, HD), ('z', 'y', 'c'), 0, 0...  17.4 us
    ppermute x6, waiting for transfers between devices, shifted(): lax.ppermute(block, axis, [(i, (i + by) % count) for i in range(count)])  14.7 us
    ppermute x2, starting transfers between devices, exchange(): lax.ppermute(block, 'y', [(i, (i + NY // 2) % NY) for i in range(NY)])  11.5 us
    all_to_all x1, waiting for transfers between devices, body(): parts = lax.all_to_all(partial, 'z', 0, 0, tiled=True)  9.07 us
    all_to_all x1, starting transfers between devices, body(): lax.all_to_all(jnp.broadcast_to(blocks[None], (NY, NZ, 8, NX * HD)), 'y',...  7.21 us
    all_to_all x1, starting transfers between devices, body(): parts = lax.all_to_all(partial, 'z', 0, 0, tiled=True)  7.02 us
    ppermute x2, waiting for transfers between devices, exchange(): lax.ppermute(block, 'y', [(i, (i + NY // 2) % NY) for i in range(NY)])  5.71 us
  transfers between devices with their start and end apart: 13, of which 8 were waited for; matrix products, arithmetic and copies ran while one was open for 8% of the time, Pallas kernels for 8%

profile of v8, /device:TPU:8, one launch (start us, length us, event | category | flops | bytes accessed | tf_op | source)
XLA Modules:
  0.0 135.1 jit_solution(15763631926061121885)
XLA Ops:
  7.3 0.8 copy.16
  8.8 17.4 %all-to-all-start = ((bf16[128,8,128]{2,1,0:T(8,128)(2,1)}), bf16[128,8,128]{2,1,0:T(8,128)(2,1)S(1)}, u32[]{:S(2)}, u32[]{:S(2)}) async-start(bf16[128,8,128]{2,1,0:T(8,128)(2,1)} %bitcast.4), calls=%async_computation | async-start | bytes 524288 | tf_op jit(solution)/shard_map/all_to_all | solution.py:307
  26.9 1.0 fusion.1.w0_ref
  27.9 4.9 %collective-permute-start = (bf16[272,640]{1,0:T(8,128)(2,1)S(1)}, bf16[272,640]{1,0:T(8,128)(2,1)S(1)}, u32[]{:S(2)}, u32[]{:S(2)}) collective-permute-start(bf16[272,640]{1,0:T(8,128)(2,1)S(1)} %fusion.1.w0_ref), channel_id=1, source_target_pairs={{0,256},{128,384},{256,0},{384,128},{1,257},{129,385},{257,1},{385... | collective-permute-start | bytes 1044488 | tf_op jit(solution)/shard_map/ppermute | solution.py:45
  32.9 0.9 select_reduce_fusion.1
  35.8 0.9 select_reduce_fusion
  36.7 0.9 compare_reduce_fusion
  38.3 3.2 %collective-permute-done.w2_ref = bf16[272,640]{1,0:T(8,128)(2,1)S(1)} collective-permute-done((bf16[272,640]{1,0:T(8,128)(2,1)S(1)}, bf16[272,640]{1,0:T(8,128)(2,1)S(1)}, u32[]{:S(2)}, u32[]{:S(2)}) %collective-permute-start) | collective-permute-done | bytes 348192 | tf_op jit(solution)/shard_map/ppermute | solution.py:45
  41.6 0.8 broadcast_in_dim.85
  42.4 7.2 %all-to-all-start.1 = ((bf16[8,8,8,512]{3,2,1,0:T(8,128)(2,1)}), bf16[8,8,8,512]{3,2,1,0:T(8,128)(2,1)S(1)}, u32[]{:S(2)}, u32[]{:S(2)}) async-start(bf16[8,8,8,512]{3,2,1,0:T(8,128)(2,1)} %broadcast_in_dim.85), calls=%async_computation.1 | async-start | bytes 1048576 | tf_op jit(solution)/shard_map/all_to_all | solution.py:317
  49.9 4.7 %collective-permute-start.1 = (bf16[272,640]{1,0:T(8,128)(2,1)S(1)}, bf16[272,640]{1,0:T(8,128)(2,1)S(1)}, u32[]{:S(2)}, u32[]{:S(2)}) collective-permute-start(bf16[272,640]{1,0:T(8,128)(2,1)S(1)} %fusion.1.w0_ref), channel_id=1, source_target_pairs={{0,384},{128,0},{256,128},{384,256},{1,385},{129,1},{257,129},{385... | collective-permute-start | bytes 1044488 | tf_op jit(solution)/shard_map/ppermute | solution.py:45
  54.6 1.9 %collective-permute-start.2 = (bf16[272,640]{1,0:T(8,128)(2,1)S(1)}, bf16[272,640]{1,0:T(8,128)(2,1)S(1)}, u32[]{:S(2)}, u32[]{:S(2)}) collective-permute-start(bf16[272,640]{1,0:T(8,128)(2,1)S(1)} %fusion.1.w0_ref), channel_id=1, source_target_pairs={{0,128},{128,256},{256,384},{384,0},{1,129},{129,257},{257,385},{3... | collective-permute-start | bytes 1044488 | tf_op jit(solution)/shard_map/ppermute | solution.py:45
  56.9 4.0 %collective-permute-done.1.w1_ref = bf16[272,640]{1,0:T(8,128)(2,1)S(1)} collective-permute-done((bf16[272,640]{1,0:T(8,128)(2,1)S(1)}, bf16[272,640]{1,0:T(8,128)(2,1)S(1)}, u32[]{:S(2)}, u32[]{:S(2)}) %collective-permute-start.1) | collective-permute-done | bytes 348192 | tf_op jit(solution)/shard_map/ppermute | solution.py:45
  60.9 5.3 %collective-permute-done.2.w3_ref = bf16[272,640]{1,0:T(8,128)(2,1)S(1)} collective-permute-done((bf16[272,640]{1,0:T(8,128)(2,1)S(1)}, bf16[272,640]{1,0:T(8,128)(2,1)S(1)}, u32[]{:S(2)}, u32[]{:S(2)}) %collective-permute-start.2) | collective-permute-done | bytes 348192 | tf_op jit(solution)/shard_map/ppermute | solution.py:45
  66.3 1.9 %collective-permute-start.3 = (bf16[8,8,8,512]{3,2,1,0:T(8,128)(2,1)S(1)}, bf16[8,8,8,512]{3,2,1,0:T(8,128)(2,1)S(1)}, u32[]{:S(2)}, u32[]{:S(2)}) collective-permute-start(bf16[8,8,8,512]{3,2,1,0:T(8,128)(2,1)S(1)} %all-to-all-done.1.mine_ref), channel_id=1, source_target_pairs={{0,1},{1,0},{2,3},{3,2},{4,5},{5,4},{6,7},{7,6},{8,9},{9,8},{10,11... | collective-permute-start | bytes 1572872 | tf_op jit(solution)/shard_map/ppermute | solution.py:41
  68.3 1.9 %collective-permute-done.3.mate_ref = bf16[8,8,8,512]{3,2,1,0:T(8,128)(2,1)S(1)} collective-permute-done((bf16[8,8,8,512]{3,2,1,0:T(8,128)(2,1)S(1)}, bf16[8,8,8,512]{3,2,1,0:T(8,128)(2,1)S(1)}, u32[]{:S(2)}, u32[]{:S(2)}) %collective-permute-start.3) | collective-permute-done | bytes 524320 | tf_op jit(solution)/shard_map/ppermute | solution.py:41
  70.1 1.9 %project.1 = (bf16[8,72,640]{2,1,0:T(8,128)(2,1)}, s32[4,8,128]{2,1,0:T(8,128)S(1)}) custom-call(s32[1]{0:T(128)} %bitcast.1.core_ref, bf16[8,8,8,512]{3,2,1,0:T(8,128)(2,1)S(1)} %all-to-all-done.1.mine_ref, bf16[8,8,8,512]{3,2,1,0:T(8,128)(2,1)S(1)} %collective-permute-done.3.mate_ref, f32[1,1024]{1,0:T(1,128)S(1)} %bitcast.30, ...), custom_call_target="tpu_custom_call" | custom-call | flops 671088640 | bytes 4194304 | tf_op jit(solution)/shard_map/project/pallas_call | solution.py:368
  72.1 7.0 %all-to-all-start.2 = ((bf16[8,72,640]{2,1,0:T(8,128)(2,1)}), bf16[8,72,640]{2,1,0:T(8,128)(2,1)S(1)}, u32[]{:S(2)}, u32[]{:S(2)}) async-start(bf16[8,72,640]{2,1,0:T(8,128)(2,1)} %get-tuple-element.46), calls=%async_computation.2 | async-start | bytes 1474560 | tf_op jit(solution)/shard_map/all_to_all | solution.py:382
  79.1 3.4 %pick.3 = (bf16[8,128,256]{2,1,0:T(8,128)(2,1)S(1)}, bf16[8,128,256]{2,1,0:T(8,128)(2,1)}, bf16[8,128,256]{2,1,0:T(8,128)(2,1)}) custom-call(s32[4,8,128]{2,1,0:T(8,128)S(1)} %get-tuple-element.55.rows_ref, bf16[64,128,256]{2,1,0:T(8,128)(2,1)} %bitcast.31), custom_call_target="tpu_custom_call" | custom-call | bytes 3145728 | tf_op jit(solution)/shard_map/pick/pallas_call | solution.py:385
  82.5 3.6 %collective-permute-start.5 = (bf16[8,128,256]{2,1,0:T(8,128)(2,1)}, bf16[8,128,256]{2,1,0:T(8,128)(2,1)S(1)}, u32[]{:S(2)}, u32[]{:S(2)}) collective-permute-start(bf16[8,128,256]{2,1,0:T(8,128)(2,1)} %get-tuple-element.56), channel_id=1, source_target_pairs={{0,384},{128,0},{256,128},{384,256},{1,385},{129,1},{257,129},{385... | collective-permute-start | bytes 1572872 | tf_op jit(solution)/shard_map/ppermute | solution.py:45
  86.2 2.2 %collective-permute-start.6 = (bf16[8,128,256]{2,1,0:T(8,128)(2,1)}, bf16[8,128,256]{2,1,0:T(8,128)(2,1)S(1)}, u32[]{:S(2)}, u32[]{:S(2)}) collective-permute-start(bf16[8,128,256]{2,1,0:T(8,128)(2,1)} %get-tuple-element.57), channel_id=1, source_target_pairs={{0,128},{128,256},{256,384},{384,0},{1,129},{129,257},{257,385},{3... | collective-permute-start | bytes 1572872 | tf_op jit(solution)/shard_map/ppermute | solution.py:45
  88.4 4.0 %collective-permute-start.7 = (bf16[8,128,256]{2,1,0:T(8,128)(2,1)S(1)}, bf16[8,128,256]{2,1,0:T(8,128)(2,1)S(1)}, u32[]{:S(2)}, u32[]{:S(2)}) collective-permute-start(bf16[8,128,256]{2,1,0:T(8,128)(2,1)S(1)} %get-tuple-element.60), channel_id=1, source_target_pairs={{0,256},{128,384},{256,0},{384,128},{1,257},{129,385},{257,1},{385... | collective-permute-start | bytes 1572872 | tf_op jit(solution)/shard_map/ppermute | solution.py:45
  92.4 9.1 %all-to-all-done.2.parts_ref = bf16[8,72,640]{2,1,0:T(8,128)(2,1)S(1)} async-done(((bf16[8,72,640]{2,1,0:T(8,128)(2,1)}), bf16[8,72,640]{2,1,0:T(8,128)(2,1)S(1)}, u32[]{:S(2)}, u32[]{:S(2)}) %all-to-all-start.2) | async-done | bytes 737312 | tf_op jit(solution)/shard_map/all_to_all | solution.py:382
  101.7 6.4 %collective-permute-start.4 = (bf16[320,128]{1,0:T(8,128)(2,1)S(1)}, bf16[320,128]{1,0:T(8,128)(2,1)S(1)}, u32[]{:S(2)}, u32[]{:S(2)}) collective-permute-start(bf16[320,128]{1,0:T(8,128)(2,1)S(1)} %finish.1.own_ref), channel_id=1, source_target_pairs={{0,8},{2,10},{4,12},{6,14},{8,0},{10,2},{12,4},{14,6},{1,9},{3,11}... | collective-permute-start | bytes 245768 | tf_op jit(solution)/shard_map/ppermute | solution.py:37
  108.1 1.9 %pick.2.kv0_ref = bf16[8,128,256]{2,1,0:T(8,128)(2,1)S(1)} custom-call(s32[4,8,128]{2,1,0:T(8,128)S(1)} %get-tuple-element.55.rows_ref, bf16[64,128,256]{2,1,0:T(8,128)(2,1)} %bitcast.32), custom_call_target="tpu_custom_call" | custom-call | bytes 1048576 | tf_op jit(solution)/shard_map/pick/pallas_call | solution.py:385
  110.0 1.9 %collective-permute-done.4.other_ref = bf16[320,128]{1,0:T(8,128)(2,1)S(1)} collective-permute-done((bf16[320,128]{1,0:T(8,128)(2,1)S(1)}, bf16[320,128]{1,0:T(8,128)(2,1)S(1)}, u32[]{:S(2)}, u32[]{:S(2)}) %collective-permute-start.4) | collective-permute-done | bytes 81952 | tf_op jit(solution)/shard_map/ppermute | solution.py:37
  112.0 2.2 %collective-permute-done.6.kv3_ref = bf16[8,128,256]{2,1,0:T(8,128)(2,1)S(1)} collective-permute-done((bf16[8,128,256]{2,1,0:T(8,128)(2,1)}, bf16[8,128,256]{2,1,0:T(8,128)(2,1)S(1)}, u32[]{:S(2)}, u32[]{:S(2)}) %collective-permute-start.6) | collective-permute-done | bytes 524320 | tf_op jit(solution)/shard_map/ppermute | solution.py:45
  114.1 1.6 %other_near.1 = (f32[128,256]{1,0:T(8,128)S(1)}, f32[8,256]{1,0:T(8,128)S(1)}) custom-call(s32[1]{0:T(128)} %bitcast.flag_ref, bf16[320,128]{1,0:T(8,128)(2,1)S(1)} %finish.1.own_ref, bf16[320,128]{1,0:T(8,128)(2,1)S(1)} %collective-permute-done.4.other_ref, s32[128,32]{1,0:T(8,128)S(1)} %or_select_fusion.eff_ref, ...), custom_call_target="tpu_custom_call" | custom-call | flops 402653184 | bytes 1572864 | tf_op jit(solution)/shard_map/other_near/pallas_call | solution.py:423
  116.5 5.1 %collective-permute-start.8 = (bf16[144,256]{1,0:T(8,128)(2,1)S(1)}, bf16[144,256]{1,0:T(8,128)(2,1)S(1)}, u32[]{:S(2)}, u32[]{:S(2)}) collective-permute-start(bf16[144,256]{1,0:T(8,128)(2,1)S(1)} %other_far.1), channel_id=1, source_target_pairs={{0,8},{2,10},{4,12},{6,14},{8,0},{10,2},{12,4},{14,6},{1,9},{3,11}... | collective-permute-start | bytes 221192 | tf_op jit(solution)/shard_map/ppermute | solution.py:37
  121.7 2.0 %own.1 = (f32[128,256]{1,0:T(8,128)S(1)}, f32[8,256]{1,0:T(8,128)S(1)}) custom-call(s32[1]{0:T(128)} %bitcast.flag_ref, bf16[320,128]{1,0:T(8,128)(2,1)S(1)} %finish.1.own_ref, bf16[320,128]{1,0:T(8,128)(2,1)S(1)} %collective-permute-done.4.other_ref, s32[128,32]{1,0:T(8,128)S(1)} %or_select_fusion.eff_ref, s32[64,128]{1,0:T(8,128)S(1)} %broadcast_in_dim.94.fresh_eff_ref, ...), custom_call_target="tpu_custom_call" | custom-call | flops 536870912 | bytes 2097152 | tf_op jit(solution)/shard_map/own/pallas_call | solution.py:444
  123.7 3.8 %collective-permute-done.8.got_ref = bf16[144,256]{1,0:T(8,128)(2,1)S(1)} collective-permute-done((bf16[144,256]{1,0:T(8,128)(2,1)S(1)}, bf16[144,256]{1,0:T(8,128)(2,1)S(1)}, u32[]{:S(2)}, u32[]{:S(2)}) %collective-permute-start.8) | collective-permute-done | bytes 73760 | tf_op jit(solution)/shard_map/ppermute | solution.py:37
  127.5 0.8 merge.1
  (44 shorter events, 6.6 us)
Async XLA Ops:
  6.5 43.1 %copy-start = (s32[1,64]{1,0:T(1,128)S(1)}, s32[1,64]{1,0:T(1,128)}, u32[]{:S(2)}) copy-start(s32[1,64]{1,0:T(1,128)} %param.15) | copy-start | bytes 772
  6.5 72.6 %all-gather.3.cloned.1.call-start = ((), (), s32[]{:S(2)}) async-start(), calls=%async_computation.3 | async-start | bytes 4718592 | tf_op jit(solution)/shard_map/all_gather | solution.py:298
  8.8 32.7 %all-to-all-start = ((bf16[128,8,128]{2,1,0:T(8,128)(2,1)}), bf16[128,8,128]{2,1,0:T(8,128)(2,1)S(1)}, u32[]{:S(2)}, u32[]{:S(2)}) async-start(bf16[128,8,128]{2,1,0:T(8,128)(2,1)} %bitcast.4), calls=%async_computation | async-start | bytes 524288 | tf_op jit(solution)/shard_map/all_to_all | solution.py:307
  27.9 13.6 %collective-permute-start = (bf16[272,640]{1,0:T(8,128)(2,1)S(1)}, bf16[272,640]{1,0:T(8,128)(2,1)S(1)}, u32[]{:S(2)}, u32[]{:S(2)}) collective-permute-start(bf16[272,640]{1,0:T(8,128)(2,1)S(1)} %fusion.1.w0_ref), channel_id=1, source_target_pairs={{0,256},{128,384},{256,0},{384,128},{1,257},{129,385},{257,1},{385... | collective-permute-start | bytes 1044488 | tf_op jit(solution)/shard_map/ppermute | solution.py:45
  42.4 23.8 %all-to-all-start.1 = ((bf16[8,8,8,512]{3,2,1,0:T(8,128)(2,1)}), bf16[8,8,8,512]{3,2,1,0:T(8,128)(2,1)S(1)}, u32[]{:S(2)}, u32[]{:S(2)}) async-start(bf16[8,8,8,512]{3,2,1,0:T(8,128)(2,1)} %broadcast_in_dim.85), calls=%async_computation.1 | async-start | bytes 1048576 | tf_op jit(solution)/shard_map/all_to_all | solution.py:317
  49.9 11.0 %collective-permute-start.1 = (bf16[272,640]{1,0:T(8,128)(2,1)S(1)}, bf16[272,640]{1,0:T(8,128)(2,1)S(1)}, u32[]{:S(2)}, u32[]{:S(2)}) collective-permute-start(bf16[272,640]{1,0:T(8,128)(2,1)S(1)} %fusion.1.w0_ref), channel_id=1, source_target_pairs={{0,384},{128,0},{256,128},{384,256},{1,385},{129,1},{257,129},{385... | collective-permute-start | bytes 1044488 | tf_op jit(solution)/shard_map/ppermute | solution.py:45
  54.6 11.6 %collective-permute-start.2 = (bf16[272,640]{1,0:T(8,128)(2,1)S(1)}, bf16[272,640]{1,0:T(8,128)(2,1)S(1)}, u32[]{:S(2)}, u32[]{:S(2)}) collective-permute-start(bf16[272,640]{1,0:T(8,128)(2,1)S(1)} %fusion.1.w0_ref), channel_id=1, source_target_pairs={{0,128},{128,256},{256,384},{384,0},{1,129},{129,257},{257,385},{3... | collective-permute-start | bytes 1044488 | tf_op jit(solution)/shard_map/ppermute | solution.py:45
  66.3 3.8 %collective-permute-start.3 = (bf16[8,8,8,512]{3,2,1,0:T(8,128)(2,1)S(1)}, bf16[8,8,8,512]{3,2,1,0:T(8,128)(2,1)S(1)}, u32[]{:S(2)}, u32[]{:S(2)}) collective-permute-start(bf16[8,8,8,512]{3,2,1,0:T(8,128)(2,1)S(1)} %all-to-all-done.1.mine_ref), channel_id=1, source_target_pairs={{0,1},{1,0},{2,3},{3,2},{4,5},{5,4},{6,7},{7,6},{8,9},{9,8},{10,11... | collective-permute-start | bytes 1572872 | tf_op jit(solution)/shard_map/ppermute | solution.py:41
  72.1 29.4 %all-to-all-start.2 = ((bf16[8,72,640]{2,1,0:T(8,128)(2,1)}), bf16[8,72,640]{2,1,0:T(8,128)(2,1)S(1)}, u32[]{:S(2)}, u32[]{:S(2)}) async-start(bf16[8,72,640]{2,1,0:T(8,128)(2,1)} %get-tuple-element.46), calls=%async_computation.2 | async-start | bytes 1474560 | tf_op jit(solution)/shard_map/all_to_all | solution.py:382
  82.5 29.4 %collective-permute-start.5 = (bf16[8,128,256]{2,1,0:T(8,128)(2,1)}, bf16[8,128,256]{2,1,0:T(8,128)(2,1)S(1)}, u32[]{:S(2)}, u32[]{:S(2)}) collective-permute-start(bf16[8,128,256]{2,1,0:T(8,128)(2,1)} %get-tuple-element.56), channel_id=1, source_target_pairs={{0,384},{128,0},{256,128},{384,256},{1,385},{129,1},{257,129},{385... | collective-permute-start | bytes 1572872 | tf_op jit(solution)/shard_map/ppermute | solution.py:45
  86.2 28.0 %collective-permute-start.6 = (bf16[8,128,256]{2,1,0:T(8,128)(2,1)}, bf16[8,128,256]{2,1,0:T(8,128)(2,1)S(1)}, u32[]{:S(2)}, u32[]{:S(2)}) collective-permute-start(bf16[8,128,256]{2,1,0:T(8,128)(2,1)} %get-tuple-element.57), channel_id=1, source_target_pairs={{0,128},{128,256},{256,384},{384,0},{1,129},{129,257},{257,385},{3... | collective-permute-start | bytes 1572872 | tf_op jit(solution)/shard_map/ppermute | solution.py:45
  88.4 27.4 %collective-permute-start.7 = (bf16[8,128,256]{2,1,0:T(8,128)(2,1)S(1)}, bf16[8,128,256]{2,1,0:T(8,128)(2,1)S(1)}, u32[]{:S(2)}, u32[]{:S(2)}) collective-permute-start(bf16[8,128,256]{2,1,0:T(8,128)(2,1)S(1)} %get-tuple-element.60), channel_id=1, source_target_pairs={{0,256},{128,384},{256,0},{384,128},{1,257},{129,385},{257,1},{385... | collective-permute-start | bytes 1572872 | tf_op jit(solution)/shard_map/ppermute | solution.py:45
  101.7 10.3 %collective-permute-start.4 = (bf16[320,128]{1,0:T(8,128)(2,1)S(1)}, bf16[320,128]{1,0:T(8,128)(2,1)S(1)}, u32[]{:S(2)}, u32[]{:S(2)}) collective-permute-start(bf16[320,128]{1,0:T(8,128)(2,1)S(1)} %finish.1.own_ref), channel_id=1, source_target_pairs={{0,8},{2,10},{4,12},{6,14},{8,0},{10,2},{12,4},{14,6},{1,9},{3,11}... | collective-permute-start | bytes 245768 | tf_op jit(solution)/shard_map/ppermute | solution.py:37
  116.5 10.9 %collective-permute-start.8 = (bf16[144,256]{1,0:T(8,128)(2,1)S(1)}, bf16[144,256]{1,0:T(8,128)(2,1)S(1)}, u32[]{:S(2)}, u32[]{:S(2)}) collective-permute-start(bf16[144,256]{1,0:T(8,128)(2,1)S(1)} %other_far.1), channel_id=1, source_target_pairs={{0,8},{2,10},{4,12},{6,14},{8,0},{10,2},{12,4},{14,6},{1,9},{3,11}... | collective-permute-start | bytes 221192 | tf_op jit(solution)/shard_map/ppermute | solution.py:37
Sparse Core Ops, SparseCore 0:
  9.4 67.1 all-gather.2

commit v9 on v8

--- a/solution.py
+++ b/solution.py
@@ -55,6 +55,28 @@
             flops=flops, bytes_accessed=bytes_accessed, transcendentals=0
         ),
     )
+
+
+def spread_kernel(hidden_ref, out_ref):
+    states = hidden_ref[...].astype(jnp.float32)
+    for b in range(2):
+        for y in range(NY):
+            for c in range(NC):
+                lanes = (b * NC + c) * HD
+                block = states[y * 8 : (y + 1) * 8, lanes : lanes + HD].astype(jnp.bfloat16)
+                for pair in range(4):
+                    out_ref[((pair * 2 + b) * NY + y) * NC + c] = block
+
+
+def gather_kernel(place_ref, blocks_ref, out_ref):
+    x = place_ref[0]
+    pair = place_ref[1]
+    for request in range(NZ):
+        block = jnp.concatenate(
+            [blocks_ref[request, lax.rem(x + i, NX), pair] for i in range(NX)], axis=1
+        )
+        for y in range(NY):
+            out_ref[y, request] = block
 
 
 def project_kernel(
@@ -302,21 +324,28 @@
     weight = jnp.concatenate([weight, listed], axis=0)
 
     far_weight = shifted(weight, "x", NX, -2)
-    blocks = hidden[0].reshape(NY, 8, 2, NC, HD).transpose(2, 0, 3, 1, 4)
-    blocks = jnp.broadcast_to(blocks[None], (4, 2, NY, NC, 8, HD))
-    blocks = lax.all_to_all(
-        blocks.reshape(NZ * NY * NC, 8, HD), ("z", "y", "c"), 0, 0, tiled=True
-    )
+    place = jnp.stack([x, z // 2])
+    blocks = call(
+        spread_kernel, jax.ShapeDtypeStruct((NZ * NY * NC, 8, HD), jnp.bfloat16), "spread"
+    )(hidden[0])
+    blocks = lax.all_to_all(blocks, ("z", "y", "c"), 0, 0, tiled=True)
     blocks, weight, far_weight = lax.optimization_barrier((blocks, weight, far_weight))
     weights = [weight, shifted(weight, "x", NX, -1), far_weight, shifted(weight, "x", NX, -3)]
     blocks = blocks.reshape(NZ, NX, 4, 8, HD)
-    blocks = lax.dynamic_index_in_dim(blocks, z // 2, 2, keepdims=False)
-    blocks = jnp.concatenate([blocks, blocks], axis=1)
-    blocks = lax.dynamic_slice_in_dim(blocks, x, NX, 1)
-    blocks = blocks.transpose(0, 2, 1, 3).reshape(NZ, 8, NX * HD)
-    tokens = lax.all_to_all(
-        jnp.broadcast_to(blocks[None], (NY, NZ, 8, NX * HD)), "y", 0, 0, tiled=True
-    )
+    smem = pl.BlockSpec(memory_space=pltpu.SMEM)
+    vmem = pl.BlockSpec(memory_space=pltpu.VMEM)
+    hbm = pl.BlockSpec(memory_space=pltpu.MemorySpace.HBM)
+    blocks = pl.pallas_call(
+        gather_kernel,
+        out_shape=jax.ShapeDtypeStruct((NY, NZ, 8, NX * HD), jnp.bfloat16),
+        in_specs=[smem, vmem],
+        out_specs=vmem,
+        name="gather",
+        compiler_params=pltpu.CompilerParams(vmem_limit_bytes=32 * 1024 * 1024),
+        cost_estimate=pl.CostEstimate(flops=0, bytes_accessed=1 << 20, transcendentals=0),
+    )(place, blocks)
+    tokens = lax.all_to_all(blocks, "y", 0, 0, tiled=True)
+
     steps = jnp.arange(NZ, dtype=jnp.int32)
     row_ids = ((x * NZ + steps)[:, None] * CH_DEV + int_rows[None, :]).reshape(-1)
     here = location[None, :] == row_ids[:, None]
@@ -362,9 +391,6 @@
     )
     mate_tokens = swap_cores(tokens)
 
-    smem = pl.BlockSpec(memory_space=pltpu.SMEM)
-    vmem = pl.BlockSpec(memory_space=pltpu.VMEM)
-    hbm = pl.BlockSpec(memory_space=pltpu.MemorySpace.HBM)
     partial, send_rows = pl.pallas_call(
         project_kernel,
         out_shape=[

time: 136 us -> 136 us (level)
  Pallas kernels: 12.7 us -> 14.9 us
  local copies, waits for them, and re-layouts: 3.7 us -> 2.09 us
    pallas_call x0 -> x2, Pallas kernels: none -> 2.14 us  [the longest x1 1.4 us: body(): pl.pallas_call(gather_kernel, out_shape=jax.ShapeDtypeStruct((NY, NZ, 8,...]
    broadcast_in_dim x2 -> x0, local copies, waits for them, and re-layouts: 1.58 us -> none  [the longest x1 0.85 us: body(): jnp.broadcast_to(blocks[None], (NY, NZ, 8, NX * HD))]
  transfers between devices with their start and end apart: 13 -> 13, of which waited for: 8 -> 8; matrix products, arithmetic and copies ran while one was open for 8% -> 6% of each run, Pallas kernels for 8% -> 10%
where the time goes in v9:
time: 136 us
  starting transfers between devices  66.3 us (49%)
  waiting for transfers between devices  32 us (24%)
  Pallas kernels  14.9 us (11%)
  between operations  13.7 us (10%)
  other arithmetic  6.58 us (5%)
  local copies, waits for them, and re-layouts  2.09 us (2%)
    ppermute x6, starting transfers between devices, shifted(): lax.ppermute(block, axis, [(i, (i + by) % count) for i in range(count)])  21.3 us
    all_to_all x1, starting transfers between devices, body(): blocks = lax.all_to_all(blocks, ('z', 'y', 'c'), 0, 0, tiled=True)  17.4 us
    ppermute x6, waiting for transfers between devices, shifted(): lax.ppermute(block, axis, [(i, (i + by) % count) for i in range(count)])  14.6 us
    ppermute x2, starting transfers between devices, exchange(): lax.ppermute(block, 'y', [(i, (i + NY // 2) % NY) for i in range(NY)])  11.5 us
    all_to_all x1, waiting for transfers between devices, body(): parts = lax.all_to_all(partial, 'z', 0, 0, tiled=True)  9.06 us
    all_to_all x1, starting transfers between devices, body(): tokens = lax.all_to_all(blocks, 'y', 0, 0, tiled=True)  7.21 us
    all_to_all x1, starting transfers between devices, body(): parts = lax.all_to_all(partial, 'z', 0, 0, tiled=True)  7.02 us
    ppermute x2, waiting for transfers between devices, exchange(): lax.ppermute(block, 'y', [(i, (i + NY // 2) % NY) for i in range(NY)])  5.72 us
  transfers between devices with their start and end apart: 13, of which 8 were waited for; matrix products, arithmetic and copies ran while one was open for 6% of the time, Pallas kernels for 10%

profile of v9, /device:TPU:8, one launch (start us, length us, event | category | flops | bytes accessed | tf_op | source)
XLA Modules:
  0.0 135.6 jit_solution(4621518012957523347)
XLA Ops:
  7.3 0.8 copy-done
  8.8 17.4 %all-to-all-start = ((bf16[128,8,128]{2,1,0:T(8,128)(2,1)}), bf16[128,8,128]{2,1,0:T(8,128)(2,1)S(1)}, u32[]{:S(2)}, u32[]{:S(2)}) async-start(bf16[128,8,128]{2,1,0:T(8,128)(2,1)} %spread.1), calls=%async_computation | async-start | bytes 524288 | tf_op jit(solution)/shard_map/all_to_all | solution.py:331
  26.9 1.0 fusion.1.w0_ref
  27.9 4.9 %collective-permute-start = (bf16[272,640]{1,0:T(8,128)(2,1)S(1)}, bf16[272,640]{1,0:T(8,128)(2,1)S(1)}, u32[]{:S(2)}, u32[]{:S(2)}) collective-permute-start(bf16[272,640]{1,0:T(8,128)(2,1)S(1)} %fusion.1.w0_ref), channel_id=1, source_target_pairs={{0,256},{128,384},{256,0},{384,128},{1,257},{129,385},{257,1},{385... | collective-permute-start | bytes 1044488 | tf_op jit(solution)/shard_map/ppermute | solution.py:45
  32.9 0.9 select_reduce_fusion.1
  35.9 0.9 select_reduce_fusion
  36.7 0.9 compare_reduce_fusion
  38.3 3.2 %collective-permute-done.w2_ref = bf16[272,640]{1,0:T(8,128)(2,1)S(1)} collective-permute-done((bf16[272,640]{1,0:T(8,128)(2,1)S(1)}, bf16[272,640]{1,0:T(8,128)(2,1)S(1)}, u32[]{:S(2)}, u32[]{:S(2)}) %collective-permute-start) | collective-permute-done | bytes 348192 | tf_op jit(solution)/shard_map/ppermute | solution.py:45
  41.5 1.4 %gather.1 = bf16[8,8,8,512]{3,2,1,0:T(8,128)(2,1)} custom-call(s32[2]{0:T(128)S(1)} %pad_add_fusion.place_ref, bf16[8,4,4,8,128]{4,3,2,1,0:T(8,128)(2,1)S(1)} %bitcast.23), custom_call_target="tpu_custom_call" | custom-call | bytes 1048576 | tf_op jit(solution)/shard_map/gather/pallas_call | solution.py:338
  42.9 7.2 %all-to-all-start.1 = ((bf16[8,8,8,512]{3,2,1,0:T(8,128)(2,1)}), bf16[8,8,8,512]{3,2,1,0:T(8,128)(2,1)S(1)}, u32[]{:S(2)}, u32[]{:S(2)}) async-start(bf16[8,8,8,512]{3,2,1,0:T(8,128)(2,1)} %gather.1), calls=%async_computation.1 | async-start | bytes 1048576 | tf_op jit(solution)/shard_map/all_to_all | solution.py:347
  50.4 4.7 %collective-permute-start.1 = (bf16[272,640]{1,0:T(8,128)(2,1)S(1)}, bf16[272,640]{1,0:T(8,128)(2,1)S(1)}, u32[]{:S(2)}, u32[]{:S(2)}) collective-permute-start(bf16[272,640]{1,0:T(8,128)(2,1)S(1)} %fusion.1.w0_ref), channel_id=1, source_target_pairs={{0,384},{128,0},{256,128},{384,256},{1,385},{129,1},{257,129},{385... | collective-permute-start | bytes 1044488 | tf_op jit(solution)/shard_map/ppermute | solution.py:45
  55.0 1.9 %collective-permute-start.2 = (bf16[272,640]{1,0:T(8,128)(2,1)S(1)}, bf16[272,640]{1,0:T(8,128)(2,1)S(1)}, u32[]{:S(2)}, u32[]{:S(2)}) collective-permute-start(bf16[272,640]{1,0:T(8,128)(2,1)S(1)} %fusion.1.w0_ref), channel_id=1, source_target_pairs={{0,128},{128,256},{256,384},{384,0},{1,129},{129,257},{257,385},{3... | collective-permute-start | bytes 1044488 | tf_op jit(solution)/shard_map/ppermute | solution.py:45
  57.3 4.0 %collective-permute-done.1.w1_ref = bf16[272,640]{1,0:T(8,128)(2,1)S(1)} collective-permute-done((bf16[272,640]{1,0:T(8,128)(2,1)S(1)}, bf16[272,640]{1,0:T(8,128)(2,1)S(1)}, u32[]{:S(2)}, u32[]{:S(2)}) %collective-permute-start.1) | collective-permute-done | bytes 348192 | tf_op jit(solution)/shard_map/ppermute | solution.py:45
  61.3 5.3 %collective-permute-done.2.w3_ref = bf16[272,640]{1,0:T(8,128)(2,1)S(1)} collective-permute-done((bf16[272,640]{1,0:T(8,128)(2,1)S(1)}, bf16[272,640]{1,0:T(8,128)(2,1)S(1)}, u32[]{:S(2)}, u32[]{:S(2)}) %collective-permute-start.2) | collective-permute-done | bytes 348192 | tf_op jit(solution)/shard_map/ppermute | solution.py:45
  66.8 1.9 %collective-permute-start.3 = (bf16[8,8,8,512]{3,2,1,0:T(8,128)(2,1)S(1)}, bf16[8,8,8,512]{3,2,1,0:T(8,128)(2,1)S(1)}, u32[]{:S(2)}, u32[]{:S(2)}) collective-permute-start(bf16[8,8,8,512]{3,2,1,0:T(8,128)(2,1)S(1)} %all-to-all-done.1.mine_ref), channel_id=1, source_target_pairs={{0,1},{1,0},{2,3},{3,2},{4,5},{5,4},{6,7},{7,6},{8,9},{9,8},{10,11... | collective-permute-start | bytes 1572872 | tf_op jit(solution)/shard_map/ppermute | solution.py:41
  68.7 1.9 %collective-permute-done.3.mate_ref = bf16[8,8,8,512]{3,2,1,0:T(8,128)(2,1)S(1)} collective-permute-done((bf16[8,8,8,512]{3,2,1,0:T(8,128)(2,1)S(1)}, bf16[8,8,8,512]{3,2,1,0:T(8,128)(2,1)S(1)}, u32[]{:S(2)}, u32[]{:S(2)}) %collective-permute-start.3) | collective-permute-done | bytes 524320 | tf_op jit(solution)/shard_map/ppermute | solution.py:41
  70.6 1.9 %project.1 = (bf16[8,72,640]{2,1,0:T(8,128)(2,1)}, s32[4,8,128]{2,1,0:T(8,128)S(1)}) custom-call(s32[1]{0:T(128)} %bitcast.1.core_ref, bf16[8,8,8,512]{3,2,1,0:T(8,128)(2,1)S(1)} %all-to-all-done.1.mine_ref, bf16[8,8,8,512]{3,2,1,0:T(8,128)(2,1)S(1)} %collective-permute-done.3.mate_ref, f32[1,1024]{1,0:T(1,128)S(1)} %bitcast.25, ...), custom_call_target="tpu_custom_call" | custom-call | flops 671088640 | bytes 4194304 | tf_op jit(solution)/shard_map/project/pallas_call | solution.py:394
  72.6 7.0 %all-to-all-start.2 = ((bf16[8,72,640]{2,1,0:T(8,128)(2,1)}), bf16[8,72,640]{2,1,0:T(8,128)(2,1)S(1)}, u32[]{:S(2)}, u32[]{:S(2)}) async-start(bf16[8,72,640]{2,1,0:T(8,128)(2,1)} %get-tuple-element.46), calls=%async_computation.2 | async-start | bytes 1474560 | tf_op jit(solution)/shard_map/all_to_all | solution.py:408
  79.6 3.4 %pick.3 = (bf16[8,128,256]{2,1,0:T(8,128)(2,1)S(1)}, bf16[8,128,256]{2,1,0:T(8,128)(2,1)}, bf16[8,128,256]{2,1,0:T(8,128)(2,1)}) custom-call(s32[4,8,128]{2,1,0:T(8,128)S(1)} %get-tuple-element.55.rows_ref, bf16[64,128,256]{2,1,0:T(8,128)(2,1)} %bitcast.26), custom_call_target="tpu_custom_call" | custom-call | bytes 3145728 | tf_op jit(solution)/shard_map/pick/pallas_call | solution.py:411
  83.0 3.6 %collective-permute-start.5 = (bf16[8,128,256]{2,1,0:T(8,128)(2,1)}, bf16[8,128,256]{2,1,0:T(8,128)(2,1)S(1)}, u32[]{:S(2)}, u32[]{:S(2)}) collective-permute-start(bf16[8,128,256]{2,1,0:T(8,128)(2,1)} %get-tuple-element.56), channel_id=1, source_target_pairs={{0,384},{128,0},{256,128},{384,256},{1,385},{129,1},{257,129},{385... | collective-permute-start | bytes 1572872 | tf_op jit(solution)/shard_map/ppermute | solution.py:45
  86.6 2.2 %collective-permute-start.6 = (bf16[8,128,256]{2,1,0:T(8,128)(2,1)}, bf16[8,128,256]{2,1,0:T(8,128)(2,1)S(1)}, u32[]{:S(2)}, u32[]{:S(2)}) collective-permute-start(bf16[8,128,256]{2,1,0:T(8,128)(2,1)} %get-tuple-element.57), channel_id=1, source_target_pairs={{0,128},{128,256},{256,384},{384,0},{1,129},{129,257},{257,385},{3... | collective-permute-start | bytes 1572872 | tf_op jit(solution)/shard_map/ppermute | solution.py:45
  88.9 4.0 %collective-permute-start.7 = (bf16[8,128,256]{2,1,0:T(8,128)(2,1)S(1)}, bf16[8,128,256]{2,1,0:T(8,128)(2,1)S(1)}, u32[]{:S(2)}, u32[]{:S(2)}) collective-permute-start(bf16[8,128,256]{2,1,0:T(8,128)(2,1)S(1)} %get-tuple-element.60), channel_id=1, source_target_pairs={{0,256},{128,384},{256,0},{384,128},{1,257},{129,385},{257,1},{385... | collective-permute-start | bytes 1572872 | tf_op jit(solution)/shard_map/ppermute | solution.py:45
  92.9 9.1 %all-to-all-done.2.parts_ref = bf16[8,72,640]{2,1,0:T(8,128)(2,1)S(1)} async-done(((bf16[8,72,640]{2,1,0:T(8,128)(2,1)}), bf16[8,72,640]{2,1,0:T(8,128)(2,1)S(1)}, u32[]{:S(2)}, u32[]{:S(2)}) %all-to-all-start.2) | async-done | bytes 737312 | tf_op jit(solution)/shard_map/all_to_all | solution.py:408
  102.2 6.4 %collective-permute-start.4 = (bf16[320,128]{1,0:T(8,128)(2,1)S(1)}, bf16[320,128]{1,0:T(8,128)(2,1)S(1)}, u32[]{:S(2)}, u32[]{:S(2)}) collective-permute-start(bf16[320,128]{1,0:T(8,128)(2,1)S(1)} %finish.1.own_ref), channel_id=1, source_target_pairs={{0,8},{2,10},{4,12},{6,14},{8,0},{10,2},{12,4},{14,6},{1,9},{3,11}... | collective-permute-start | bytes 245768 | tf_op jit(solution)/shard_map/ppermute | solution.py:37
  108.5 1.9 %pick.2.kv0_ref = bf16[8,128,256]{2,1,0:T(8,128)(2,1)S(1)} custom-call(s32[4,8,128]{2,1,0:T(8,128)S(1)} %get-tuple-element.55.rows_ref, bf16[64,128,256]{2,1,0:T(8,128)(2,1)} %bitcast.27), custom_call_target="tpu_custom_call" | custom-call | bytes 1048576 | tf_op jit(solution)/shard_map/pick/pallas_call | solution.py:411
  110.5 1.9 %collective-permute-done.4.other_ref = bf16[320,128]{1,0:T(8,128)(2,1)S(1)} collective-permute-done((bf16[320,128]{1,0:T(8,128)(2,1)S(1)}, bf16[320,128]{1,0:T(8,128)(2,1)S(1)}, u32[]{:S(2)}, u32[]{:S(2)}) %collective-permute-start.4) | collective-permute-done | bytes 81952 | tf_op jit(solution)/shard_map/ppermute | solution.py:37
  112.4 2.2 %collective-permute-done.6.kv3_ref = bf16[8,128,256]{2,1,0:T(8,128)(2,1)S(1)} collective-permute-done((bf16[8,128,256]{2,1,0:T(8,128)(2,1)}, bf16[8,128,256]{2,1,0:T(8,128)(2,1)S(1)}, u32[]{:S(2)}, u32[]{:S(2)}) %collective-permute-start.6) | collective-permute-done | bytes 524320 | tf_op jit(solution)/shard_map/ppermute | solution.py:45
  114.6 1.6 %other_near.1 = (f32[128,256]{1,0:T(8,128)S(1)}, f32[8,256]{1,0:T(8,128)S(1)}) custom-call(s32[1]{0:T(128)} %bitcast.flag_ref, bf16[320,128]{1,0:T(8,128)(2,1)S(1)} %finish.1.own_ref, bf16[320,128]{1,0:T(8,128)(2,1)S(1)} %collective-permute-done.4.other_ref, s32[128,32]{1,0:T(8,128)S(1)} %or_select_fusion.eff_ref, ...), custom_call_target="tpu_custom_call" | custom-call | flops 402653184 | bytes 1572864 | tf_op jit(solution)/shard_map/other_near/pallas_call | solution.py:449
  117.0 5.1 %collective-permute-start.8 = (bf16[144,256]{1,0:T(8,128)(2,1)S(1)}, bf16[144,256]{1,0:T(8,128)(2,1)S(1)}, u32[]{:S(2)}, u32[]{:S(2)}) collective-permute-start(bf16[144,256]{1,0:T(8,128)(2,1)S(1)} %other_far.1), channel_id=1, source_target_pairs={{0,8},{2,10},{4,12},{6,14},{8,0},{10,2},{12,4},{14,6},{1,9},{3,11}... | collective-permute-start | bytes 221192 | tf_op jit(solution)/shard_map/ppermute | solution.py:37
  122.1 2.0 %own.1 = (f32[128,256]{1,0:T(8,128)S(1)}, f32[8,256]{1,0:T(8,128)S(1)}) custom-call(s32[1]{0:T(128)} %bitcast.flag_ref, bf16[320,128]{1,0:T(8,128)(2,1)S(1)} %finish.1.own_ref, bf16[320,128]{1,0:T(8,128)(2,1)S(1)} %collective-permute-done.4.other_ref, s32[128,32]{1,0:T(8,128)S(1)} %or_select_fusion.eff_ref, s32[64,128]{1,0:T(8,128)S(1)} %broadcast_in_dim.78.fresh_eff_ref, ...), custom_call_target="tpu_custom_call" | custom-call | flops 536870912 | bytes 2097152 | tf_op jit(solution)/shard_map/own/pallas_call | solution.py:470
  124.2 3.8 %collective-permute-done.8.got_ref = bf16[144,256]{1,0:T(8,128)(2,1)S(1)} collective-permute-done((bf16[144,256]{1,0:T(8,128)(2,1)S(1)}, bf16[144,256]{1,0:T(8,128)(2,1)S(1)}, u32[]{:S(2)}, u32[]{:S(2)}) %collective-permute-start.8) | collective-permute-done | bytes 73760 | tf_op jit(solution)/shard_map/ppermute | solution.py:37
  128.0 0.8 merge.1
  (44 shorter events, 6.6 us)
Async XLA Ops:
  6.5 43.6 %copy-start.1 = (s32[1,64]{1,0:T(1,128)S(1)}, s32[1,64]{1,0:T(1,128)}, u32[]{:S(2)}) copy-start(s32[1,64]{1,0:T(1,128)} %param.15) | copy-start | bytes 772
  6.5 73.0 %all-gather.3.cloned.1.call-start = ((), (), s32[]{:S(2)}) async-start(), calls=%async_computation.3 | async-start | bytes 4718592 | tf_op jit(solution)/shard_map/all_gather | solution.py:320
  7.3 0.8 copy-start
  8.8 32.7 %all-to-all-start = ((bf16[128,8,128]{2,1,0:T(8,128)(2,1)}), bf16[128,8,128]{2,1,0:T(8,128)(2,1)S(1)}, u32[]{:S(2)}, u32[]{:S(2)}) async-start(bf16[128,8,128]{2,1,0:T(8,128)(2,1)} %spread.1), calls=%async_computation | async-start | bytes 524288 | tf_op jit(solution)/shard_map/all_to_all | solution.py:331
  27.9 13.6 %collective-permute-start = (bf16[272,640]{1,0:T(8,128)(2,1)S(1)}, bf16[272,640]{1,0:T(8,128)(2,1)S(1)}, u32[]{:S(2)}, u32[]{:S(2)}) collective-permute-start(bf16[272,640]{1,0:T(8,128)(2,1)S(1)} %fusion.1.w0_ref), channel_id=1, source_target_pairs={{0,256},{128,384},{256,0},{384,128},{1,257},{129,385},{257,1},{385... | collective-permute-start | bytes 1044488 | tf_op jit(solution)/shard_map/ppermute | solution.py:45
  42.9 23.8 %all-to-all-start.1 = ((bf16[8,8,8,512]{3,2,1,0:T(8,128)(2,1)}), bf16[8,8,8,512]{3,2,1,0:T(8,128)(2,1)S(1)}, u32[]{:S(2)}, u32[]{:S(2)}) async-start(bf16[8,8,8,512]{3,2,1,0:T(8,128)(2,1)} %gather.1), calls=%async_computation.1 | async-start | bytes 1048576 | tf_op jit(solution)/shard_map/all_to_all | solution.py:347
  50.4 11.0 %collective-permute-start.1 = (bf16[272,640]{1,0:T(8,128)(2,1)S(1)}, bf16[272,640]{1,0:T(8,128)(2,1)S(1)}, u32[]{:S(2)}, u32[]{:S(2)}) collective-permute-start(bf16[272,640]{1,0:T(8,128)(2,1)S(1)} %fusion.1.w0_ref), channel_id=1, source_target_pairs={{0,384},{128,0},{256,128},{384,256},{1,385},{129,1},{257,129},{385... | collective-permute-start | bytes 1044488 | tf_op jit(solution)/shard_map/ppermute | solution.py:45
  55.0 11.6 %collective-permute-start.2 = (bf16[272,640]{1,0:T(8,128)(2,1)S(1)}, bf16[272,640]{1,0:T(8,128)(2,1)S(1)}, u32[]{:S(2)}, u32[]{:S(2)}) collective-permute-start(bf16[272,640]{1,0:T(8,128)(2,1)S(1)} %fusion.1.w0_ref), channel_id=1, source_target_pairs={{0,128},{128,256},{256,384},{384,0},{1,129},{129,257},{257,385},{3... | collective-permute-start | bytes 1044488 | tf_op jit(solution)/shard_map/ppermute | solution.py:45
  66.8 3.8 %collective-permute-start.3 = (bf16[8,8,8,512]{3,2,1,0:T(8,128)(2,1)S(1)}, bf16[8,8,8,512]{3,2,1,0:T(8,128)(2,1)S(1)}, u32[]{:S(2)}, u32[]{:S(2)}) collective-permute-start(bf16[8,8,8,512]{3,2,1,0:T(8,128)(2,1)S(1)} %all-to-all-done.1.mine_ref), channel_id=1, source_target_pairs={{0,1},{1,0},{2,3},{3,2},{4,5},{5,4},{6,7},{7,6},{8,9},{9,8},{10,11... | collective-permute-start | bytes 1572872 | tf_op jit(solution)/shard_map/ppermute | solution.py:41
  72.6 29.4 %all-to-all-start.2 = ((bf16[8,72,640]{2,1,0:T(8,128)(2,1)}), bf16[8,72,640]{2,1,0:T(8,128)(2,1)S(1)}, u32[]{:S(2)}, u32[]{:S(2)}) async-start(bf16[8,72,640]{2,1,0:T(8,128)(2,1)} %get-tuple-element.46), calls=%async_computation.2 | async-start | bytes 1474560 | tf_op jit(solution)/shard_map/all_to_all | solution.py:408
  83.0 29.4 %collective-permute-start.5 = (bf16[8,128,256]{2,1,0:T(8,128)(2,1)}, bf16[8,128,256]{2,1,0:T(8,128)(2,1)S(1)}, u32[]{:S(2)}, u32[]{:S(2)}) collective-permute-start(bf16[8,128,256]{2,1,0:T(8,128)(2,1)} %get-tuple-element.56), channel_id=1, source_target_pairs={{0,384},{128,0},{256,128},{384,256},{1,385},{129,1},{257,129},{385... | collective-permute-start | bytes 1572872 | tf_op jit(solution)/shard_map/ppermute | solution.py:45
  86.6 28.0 %collective-permute-start.6 = (bf16[8,128,256]{2,1,0:T(8,128)(2,1)}, bf16[8,128,256]{2,1,0:T(8,128)(2,1)S(1)}, u32[]{:S(2)}, u32[]{:S(2)}) collective-permute-start(bf16[8,128,256]{2,1,0:T(8,128)(2,1)} %get-tuple-element.57), channel_id=1, source_target_pairs={{0,128},{128,256},{256,384},{384,0},{1,129},{129,257},{257,385},{3... | collective-permute-start | bytes 1572872 | tf_op jit(solution)/shard_map/ppermute | solution.py:45
  88.9 27.4 %collective-permute-start.7 = (bf16[8,128,256]{2,1,0:T(8,128)(2,1)S(1)}, bf16[8,128,256]{2,1,0:T(8,128)(2,1)S(1)}, u32[]{:S(2)}, u32[]{:S(2)}) collective-permute-start(bf16[8,128,256]{2,1,0:T(8,128)(2,1)S(1)} %get-tuple-element.60), channel_id=1, source_target_pairs={{0,256},{128,384},{256,0},{384,128},{1,257},{129,385},{257,1},{385... | collective-permute-start | bytes 1572872 | tf_op jit(solution)/shard_map/ppermute | solution.py:45
  102.2 10.3 %collective-permute-start.4 = (bf16[320,128]{1,0:T(8,128)(2,1)S(1)}, bf16[320,128]{1,0:T(8,128)(2,1)S(1)}, u32[]{:S(2)}, u32[]{:S(2)}) collective-permute-start(bf16[320,128]{1,0:T(8,128)(2,1)S(1)} %finish.1.own_ref), channel_id=1, source_target_pairs={{0,8},{2,10},{4,12},{6,14},{8,0},{10,2},{12,4},{14,6},{1,9},{3,11}... | collective-permute-start | bytes 245768 | tf_op jit(solution)/shard_map/ppermute | solution.py:37
  117.0 10.9 %collective-permute-start.8 = (bf16[144,256]{1,0:T(8,128)(2,1)S(1)}, bf16[144,256]{1,0:T(8,128)(2,1)S(1)}, u32[]{:S(2)}, u32[]{:S(2)}) collective-permute-start(bf16[144,256]{1,0:T(8,128)(2,1)S(1)} %other_far.1), channel_id=1, source_target_pairs={{0,8},{2,10},{4,12},{6,14},{8,0},{10,2},{12,4},{14,6},{1,9},{3,11}... | collective-permute-start | bytes 221192 | tf_op jit(solution)/shard_map/ppermute | solution.py:37
Sparse Core Ops, SparseCore 0:
  9.4 67.1 all-gather.2

commit v10 on v8

--- a/solution.py
+++ b/solution.py
@@ -79,7 +79,7 @@
         found = jnp.sum(found.reshape(NZ, CH_DEV, HD), axis=1)
         found = jnp.sum(found, axis=1, keepdims=True).astype(jnp.int32)
         base = lax.broadcasted_iota(jnp.int32, (NZ, HD), 0) * CH_DEV
-        rows_ref[k] = base + found
+        rows_ref[k] = base + jnp.minimum(found, CH_DEV - 1)
 
     weights = jnp.concatenate([w[: 2 * HD, :] for w in (w0_ref, w1_ref, w2_ref, w3_ref)], axis=0)
     gain = gain_ref[...]
@@ -302,13 +302,16 @@
     weight = jnp.concatenate([weight, listed], axis=0)
 
     far_weight = shifted(weight, "x", NX, -2)
+    back_weight = shifted(weight, "x", NX, -3)
     blocks = hidden[0].reshape(NY, 8, 2, NC, HD).transpose(2, 0, 3, 1, 4)
     blocks = jnp.broadcast_to(blocks[None], (4, 2, NY, NC, 8, HD))
     blocks = lax.all_to_all(
         blocks.reshape(NZ * NY * NC, 8, HD), ("z", "y", "c"), 0, 0, tiled=True
     )
-    blocks, weight, far_weight = lax.optimization_barrier((blocks, weight, far_weight))
-    weights = [weight, shifted(weight, "x", NX, -1), far_weight, shifted(weight, "x", NX, -3)]
+    blocks, weight, far_weight, back_weight = lax.optimization_barrier(
+        (blocks, weight, far_weight, back_weight)
+    )
+    weights = [weight, shifted(weight, "x", NX, -1), far_weight, back_weight]
     blocks = blocks.reshape(NZ, NX, 4, 8, HD)
     blocks = lax.dynamic_index_in_dim(blocks, z // 2, 2, keepdims=False)
     blocks = jnp.concatenate([blocks, blocks], axis=1)

time: 136 us -> 140 us (1.029)
  the two profiles are of different devices: /device:TPU:8 before, /device:TPU:64 now
where the time goes in v10:
time: 140 us; the launch traced here: 139 us
  starting transfers between devices  54.1 us (39%)
  waiting for transfers between devices  48 us (34%)
  between operations  13.7 us (10%)
  Pallas kernels  12.7 us (9%)
  other arithmetic  6.55 us (5%)
  local copies, waits for them, and re-layouts  3.7 us (3%)
    ppermute x6, starting transfers between devices, shifted(): lax.ppermute(block, axis, [(i, (i + by) % count) for i in range(count)])  21.8 us
    all_to_all x1, starting transfers between devices, body(): lax.all_to_all(blocks.reshape(NZ * NY * NC, 8, HD), ('z', 'y', 'c'), 0, 0...  16.6 us
    ppermute x2, waiting for transfers between devices, exchange(): lax.ppermute(block, 'y', [(i, (i + NY // 2) % NY) for i in range(NY)])  12.4 us
    ppermute x6, waiting for transfers between devices, shifted(): lax.ppermute(block, axis, [(i, (i + by) % count) for i in range(count)])  10.7 us
    all_to_all x1, waiting for transfers between devices, body(): lax.all_to_all(blocks.reshape(NZ * NY * NC, 8, HD), ('z', 'y', 'c'), 0, 0...  8.83 us
    all_to_all x1, waiting for transfers between devices, body(): parts = lax.all_to_all(partial, 'z', 0, 0, tiled=True)  7.93 us
    all_to_all x1, waiting for transfers between devices, body(): lax.all_to_all(jnp.broadcast_to(blocks[None], (NY, NZ, 8, NX * HD)), 'y',...  5.52 us
    ppermute x2, starting transfers between devices, exchange(): lax.ppermute(block, 'y', [(i, (i + NY // 2) % NY) for i in range(NY)])  5.42 us
  transfers between devices with their start and end apart: 13, of which 8 were waited for; matrix products, arithmetic and copies ran while one was open for 7% of the time, Pallas kernels for 8%

profile of v10, /device:TPU:64, one launch (start us, length us, event | category | flops | bytes accessed | tf_op | source)
XLA Modules:
  0.0 138.7 jit_solution(6442811692558708274)
XLA Ops:
  7.9 1.0 fusion.1.w0_ref
  8.9 4.9 %collective-permute-start = (bf16[272,640]{1,0:T(8,128)(2,1)S(1)}, bf16[272,640]{1,0:T(8,128)(2,1)S(1)}, u32[]{:S(2)}, u32[]{:S(2)}) collective-permute-start(bf16[272,640]{1,0:T(8,128)(2,1)S(1)} %fusion.1.w0_ref), channel_id=1, source_target_pairs={{0,256},{128,384},{256,0},{384,128},{1,257},{129,385},{257,1},{385... | collective-permute-start | bytes 1044488 | tf_op jit(solution)/shard_map/ppermute | solution.py:45
  13.9 2.5 %collective-permute-start.1 = (bf16[272,640]{1,0:T(8,128)(2,1)S(1)}, bf16[272,640]{1,0:T(8,128)(2,1)S(1)}, u32[]{:S(2)}, u32[]{:S(2)}) collective-permute-start(bf16[272,640]{1,0:T(8,128)(2,1)S(1)} %fusion.1.w0_ref), channel_id=1, source_target_pairs={{0,128},{128,256},{256,384},{384,0},{1,129},{129,257},{257,385},{3... | collective-permute-start | bytes 1044488 | tf_op jit(solution)/shard_map/ppermute | solution.py:45
  16.4 0.8 copy.16
  18.0 16.6 %all-to-all-start = ((bf16[128,8,128]{2,1,0:T(8,128)(2,1)}), bf16[128,8,128]{2,1,0:T(8,128)(2,1)S(1)}, u32[]{:S(2)}, u32[]{:S(2)}) async-start(bf16[128,8,128]{2,1,0:T(8,128)(2,1)} %bitcast.4), calls=%async_computation | async-start | bytes 524288 | tf_op jit(solution)/shard_map/all_to_all | solution.py:308
  34.6 0.9 select_reduce_fusion.1
  37.5 0.9 select_reduce_fusion
  38.4 0.9 compare_reduce_fusion
  40.0 8.8 %all-to-all-done = bf16[128,8,128]{2,1,0:T(8,128)(2,1)S(1)} async-done(((bf16[128,8,128]{2,1,0:T(8,128)(2,1)}), bf16[128,8,128]{2,1,0:T(8,128)(2,1)S(1)}, u32[]{:S(2)}, u32[]{:S(2)}) %all-to-all-start) | async-done | bytes 262176 | tf_op jit(solution)/shard_map/all_to_all | solution.py:308
  48.9 0.8 broadcast_in_dim.85
  49.8 3.5 %all-to-all-start.1 = ((bf16[8,8,8,512]{3,2,1,0:T(8,128)(2,1)}), bf16[8,8,8,512]{3,2,1,0:T(8,128)(2,1)S(1)}, u32[]{:S(2)}, u32[]{:S(2)}) async-start(bf16[8,8,8,512]{3,2,1,0:T(8,128)(2,1)} %broadcast_in_dim.85), calls=%async_computation.1 | async-start | bytes 1048576 | tf_op jit(solution)/shard_map/all_to_all | solution.py:320
  53.5 4.6 %collective-permute-start.2 = (bf16[272,640]{1,0:T(8,128)(2,1)S(1)}, bf16[272,640]{1,0:T(8,128)(2,1)S(1)}, u32[]{:S(2)}, u32[]{:S(2)}) collective-permute-start(bf16[272,640]{1,0:T(8,128)(2,1)S(1)} %fusion.1.w0_ref), channel_id=1, source_target_pairs={{0,384},{128,0},{256,128},{384,256},{1,385},{129,1},{257,129},{385... | collective-permute-start | bytes 1044488 | tf_op jit(solution)/shard_map/ppermute | solution.py:45
  58.5 7.3 %collective-permute-done.2.w1_ref = bf16[272,640]{1,0:T(8,128)(2,1)S(1)} collective-permute-done((bf16[272,640]{1,0:T(8,128)(2,1)S(1)}, bf16[272,640]{1,0:T(8,128)(2,1)S(1)}, u32[]{:S(2)}, u32[]{:S(2)}) %collective-permute-start.2) | collective-permute-done | bytes 348192 | tf_op jit(solution)/shard_map/ppermute | solution.py:45
  65.8 5.5 %all-to-all-done.1.mine_ref = bf16[8,8,8,512]{3,2,1,0:T(8,128)(2,1)S(1)} async-done(((bf16[8,8,8,512]{3,2,1,0:T(8,128)(2,1)}), bf16[8,8,8,512]{3,2,1,0:T(8,128)(2,1)S(1)}, u32[]{:S(2)}, u32[]{:S(2)}) %all-to-all-start.1) | async-done | bytes 524320 | tf_op jit(solution)/shard_map/all_to_all | solution.py:320
  71.4 1.9 %collective-permute-start.3 = (bf16[8,8,8,512]{3,2,1,0:T(8,128)(2,1)S(1)}, bf16[8,8,8,512]{3,2,1,0:T(8,128)(2,1)S(1)}, u32[]{:S(2)}, u32[]{:S(2)}) collective-permute-start(bf16[8,8,8,512]{3,2,1,0:T(8,128)(2,1)S(1)} %all-to-all-done.1.mine_ref), channel_id=1, source_target_pairs={{0,1},{1,0},{2,3},{3,2},{4,5},{5,4},{6,7},{7,6},{8,9},{9,8},{10,11... | collective-permute-start | bytes 1572872 | tf_op jit(solution)/shard_map/ppermute | solution.py:41
  73.4 1.9 %collective-permute-done.3.mate_ref = bf16[8,8,8,512]{3,2,1,0:T(8,128)(2,1)S(1)} collective-permute-done((bf16[8,8,8,512]{3,2,1,0:T(8,128)(2,1)S(1)}, bf16[8,8,8,512]{3,2,1,0:T(8,128)(2,1)S(1)}, u32[]{:S(2)}, u32[]{:S(2)}) %collective-permute-start.3) | collective-permute-done | bytes 524320 | tf_op jit(solution)/shard_map/ppermute | solution.py:41
  75.2 1.9 %project.1 = (bf16[8,72,640]{2,1,0:T(8,128)(2,1)}, s32[4,8,128]{2,1,0:T(8,128)S(1)}) custom-call(s32[1]{0:T(128)} %bitcast.1.core_ref, bf16[8,8,8,512]{3,2,1,0:T(8,128)(2,1)S(1)} %all-to-all-done.1.mine_ref, bf16[8,8,8,512]{3,2,1,0:T(8,128)(2,1)S(1)} %collective-permute-done.3.mate_ref, f32[1,1024]{1,0:T(1,128)S(1)} %bitcast.30, ...), custom_call_target="tpu_custom_call" | custom-call | flops 671088640 | bytes 4194304 | tf_op jit(solution)/shard_map/project/pallas_call | solution.py:371
  77.2 4.8 %all-to-all-start.2 = ((bf16[8,72,640]{2,1,0:T(8,128)(2,1)}), bf16[8,72,640]{2,1,0:T(8,128)(2,1)S(1)}, u32[]{:S(2)}, u32[]{:S(2)}) async-start(bf16[8,72,640]{2,1,0:T(8,128)(2,1)} %get-tuple-element.48), calls=%async_computation.2 | async-start | bytes 1474560 | tf_op jit(solution)/shard_map/all_to_all | solution.py:385
  82.0 3.4 %pick.3 = (bf16[8,128,256]{2,1,0:T(8,128)(2,1)S(1)}, bf16[8,128,256]{2,1,0:T(8,128)(2,1)}, bf16[8,128,256]{2,1,0:T(8,128)(2,1)}) custom-call(s32[4,8,128]{2,1,0:T(8,128)S(1)} %get-tuple-element.57.rows_ref, bf16[64,128,256]{2,1,0:T(8,128)(2,1)} %bitcast.31), custom_call_target="tpu_custom_call" | custom-call | bytes 3145728 | tf_op jit(solution)/shard_map/pick/pallas_call | solution.py:388
  85.4 4.5 %collective-permute-start.5 = (bf16[8,128,256]{2,1,0:T(8,128)(2,1)}, bf16[8,128,256]{2,1,0:T(8,128)(2,1)S(1)}, u32[]{:S(2)}, u32[]{:S(2)}) collective-permute-start(bf16[8,128,256]{2,1,0:T(8,128)(2,1)} %get-tuple-element.58), channel_id=1, source_target_pairs={{0,384},{128,0},{256,128},{384,256},{1,385},{129,1},{257,129},{385... | collective-permute-start | bytes 1572872 | tf_op jit(solution)/shard_map/ppermute | solution.py:45
  89.9 1.9 %collective-permute-start.6 = (bf16[8,128,256]{2,1,0:T(8,128)(2,1)}, bf16[8,128,256]{2,1,0:T(8,128)(2,1)S(1)}, u32[]{:S(2)}, u32[]{:S(2)}) collective-permute-start(bf16[8,128,256]{2,1,0:T(8,128)(2,1)} %get-tuple-element.59), channel_id=1, source_target_pairs={{0,128},{128,256},{256,384},{384,0},{1,129},{129,257},{257,385},{3... | collective-permute-start | bytes 1572872 | tf_op jit(solution)/shard_map/ppermute | solution.py:45
  91.9 3.4 %collective-permute-start.7 = (bf16[8,128,256]{2,1,0:T(8,128)(2,1)S(1)}, bf16[8,128,256]{2,1,0:T(8,128)(2,1)S(1)}, u32[]{:S(2)}, u32[]{:S(2)}) collective-permute-start(bf16[8,128,256]{2,1,0:T(8,128)(2,1)S(1)} %get-tuple-element.62), channel_id=1, source_target_pairs={{0,256},{128,384},{256,0},{384,128},{1,257},{129,385},{257,1},{385... | collective-permute-start | bytes 1572872 | tf_op jit(solution)/shard_map/ppermute | solution.py:45
  95.2 7.9 %all-to-all-done.2.parts_ref = bf16[8,72,640]{2,1,0:T(8,128)(2,1)S(1)} async-done(((bf16[8,72,640]{2,1,0:T(8,128)(2,1)}), bf16[8,72,640]{2,1,0:T(8,128)(2,1)S(1)}, u32[]{:S(2)}, u32[]{:S(2)}) %all-to-all-start.2) | async-done | bytes 737312 | tf_op jit(solution)/shard_map/all_to_all | solution.py:385
  103.4 2.4 %collective-permute-start.4 = (bf16[320,128]{1,0:T(8,128)(2,1)S(1)}, bf16[320,128]{1,0:T(8,128)(2,1)S(1)}, u32[]{:S(2)}, u32[]{:S(2)}) collective-permute-start(bf16[320,128]{1,0:T(8,128)(2,1)S(1)} %finish.1.own_ref), channel_id=1, source_target_pairs={{0,8},{2,10},{4,12},{6,14},{8,0},{10,2},{12,4},{14,6},{1,9},{3,11}... | collective-permute-start | bytes 245768 | tf_op jit(solution)/shard_map/ppermute | solution.py:37
  105.8 1.9 %pick.2.kv0_ref = bf16[8,128,256]{2,1,0:T(8,128)(2,1)S(1)} custom-call(s32[4,8,128]{2,1,0:T(8,128)S(1)} %get-tuple-element.57.rows_ref, bf16[64,128,256]{2,1,0:T(8,128)(2,1)} %bitcast.32), custom_call_target="tpu_custom_call" | custom-call | bytes 1048576 | tf_op jit(solution)/shard_map/pick/pallas_call | solution.py:388
  107.8 6.7 %collective-permute-done.4.other_ref = bf16[320,128]{1,0:T(8,128)(2,1)S(1)} collective-permute-done((bf16[320,128]{1,0:T(8,128)(2,1)S(1)}, bf16[320,128]{1,0:T(8,128)(2,1)S(1)}, u32[]{:S(2)}, u32[]{:S(2)}) %collective-permute-start.4) | collective-permute-done | bytes 81952 | tf_op jit(solution)/shard_map/ppermute | solution.py:37
  114.5 3.4 %collective-permute-done.6.kv3_ref = bf16[8,128,256]{2,1,0:T(8,128)(2,1)S(1)} collective-permute-done((bf16[8,128,256]{2,1,0:T(8,128)(2,1)}, bf16[8,128,256]{2,1,0:T(8,128)(2,1)S(1)}, u32[]{:S(2)}, u32[]{:S(2)}) %collective-permute-start.6) | collective-permute-done | bytes 524320 | tf_op jit(solution)/shard_map/ppermute | solution.py:45
  117.9 1.6 %other_near.1 = (f32[128,256]{1,0:T(8,128)S(1)}, f32[8,256]{1,0:T(8,128)S(1)}) custom-call(s32[1]{0:T(128)} %bitcast.flag_ref, bf16[320,128]{1,0:T(8,128)(2,1)S(1)} %finish.1.own_ref, bf16[320,128]{1,0:T(8,128)(2,1)S(1)} %collective-permute-done.4.other_ref, s32[128,32]{1,0:T(8,128)S(1)} %or_select_fusion.eff_ref, ...), custom_call_target="tpu_custom_call" | custom-call | flops 402653184 | bytes 1572864 | tf_op jit(solution)/shard_map/other_near/pallas_call | solution.py:426
  120.3 3.0 %collective-permute-start.8 = (bf16[144,256]{1,0:T(8,128)(2,1)S(1)}, bf16[144,256]{1,0:T(8,128)(2,1)S(1)}, u32[]{:S(2)}, u32[]{:S(2)}) collective-permute-start(bf16[144,256]{1,0:T(8,128)(2,1)S(1)} %other_far.1), channel_id=1, source_target_pairs={{0,8},{2,10},{4,12},{6,14},{8,0},{10,2},{12,4},{14,6},{1,9},{3,11}... | collective-permute-start | bytes 221192 | tf_op jit(solution)/shard_map/ppermute | solution.py:37
  123.3 2.0 %own.1 = (f32[128,256]{1,0:T(8,128)S(1)}, f32[8,256]{1,0:T(8,128)S(1)}) custom-call(s32[1]{0:T(128)} %bitcast.flag_ref, bf16[320,128]{1,0:T(8,128)(2,1)S(1)} %finish.1.own_ref, bf16[320,128]{1,0:T(8,128)(2,1)S(1)} %collective-permute-done.4.other_ref, s32[128,32]{1,0:T(8,128)S(1)} %or_select_fusion.eff_ref, s32[64,128]{1,0:T(8,128)S(1)} %broadcast_in_dim.94.fresh_eff_ref, ...), custom_call_target="tpu_custom_call" | custom-call | flops 536870912 | bytes 2097152 | tf_op jit(solution)/shard_map/own/pallas_call | solution.py:447
  125.4 5.7 %collective-permute-done.8.got_ref = bf16[144,256]{1,0:T(8,128)(2,1)S(1)} collective-permute-done((bf16[144,256]{1,0:T(8,128)(2,1)S(1)}, bf16[144,256]{1,0:T(8,128)(2,1)S(1)}, u32[]{:S(2)}, u32[]{:S(2)}) %collective-permute-start.8) | collective-permute-done | bytes 73760 | tf_op jit(solution)/shard_map/ppermute | solution.py:37
  131.1 0.8 merge.1
  (44 shorter events, 6.6 us)
Async XLA Ops:
  6.5 46.7 %copy-start = (s32[1,64]{1,0:T(1,128)S(1)}, s32[1,64]{1,0:T(1,128)}, u32[]{:S(2)}) copy-start(s32[1,64]{1,0:T(1,128)} %param.15) | copy-start | bytes 772
  6.5 75.4 %all-gather.3.cloned.1.call-start = ((), (), s32[]{:S(2)}) async-start(), calls=%async_computation.3 | async-start | bytes 4718592 | tf_op jit(solution)/shard_map/all_gather | solution.py:298
  8.9 31.1 %collective-permute-start = (bf16[272,640]{1,0:T(8,128)(2,1)S(1)}, bf16[272,640]{1,0:T(8,128)(2,1)S(1)}, u32[]{:S(2)}, u32[]{:S(2)}) collective-permute-start(bf16[272,640]{1,0:T(8,128)(2,1)S(1)} %fusion.1.w0_ref), channel_id=1, source_target_pairs={{0,256},{128,384},{256,0},{384,128},{1,257},{129,385},{257,1},{385... | collective-permute-start | bytes 1044488 | tf_op jit(solution)/shard_map/ppermute | solution.py:45
  13.9 26.1 %collective-permute-start.1 = (bf16[272,640]{1,0:T(8,128)(2,1)S(1)}, bf16[272,640]{1,0:T(8,128)(2,1)S(1)}, u32[]{:S(2)}, u32[]{:S(2)}) collective-permute-start(bf16[272,640]{1,0:T(8,128)(2,1)S(1)} %fusion.1.w0_ref), channel_id=1, source_target_pairs={{0,128},{128,256},{256,384},{384,0},{1,129},{129,257},{257,385},{3... | collective-permute-start | bytes 1044488 | tf_op jit(solution)/shard_map/ppermute | solution.py:45
  18.0 30.9 %all-to-all-start = ((bf16[128,8,128]{2,1,0:T(8,128)(2,1)}), bf16[128,8,128]{2,1,0:T(8,128)(2,1)S(1)}, u32[]{:S(2)}, u32[]{:S(2)}) async-start(bf16[128,8,128]{2,1,0:T(8,128)(2,1)} %bitcast.4), calls=%async_computation | async-start | bytes 524288 | tf_op jit(solution)/shard_map/all_to_all | solution.py:308
  49.8 21.5 %all-to-all-start.1 = ((bf16[8,8,8,512]{3,2,1,0:T(8,128)(2,1)}), bf16[8,8,8,512]{3,2,1,0:T(8,128)(2,1)S(1)}, u32[]{:S(2)}, u32[]{:S(2)}) async-start(bf16[8,8,8,512]{3,2,1,0:T(8,128)(2,1)} %broadcast_in_dim.85), calls=%async_computation.1 | async-start | bytes 1048576 | tf_op jit(solution)/shard_map/all_to_all | solution.py:320
  53.5 12.3 %collective-permute-start.2 = (bf16[272,640]{1,0:T(8,128)(2,1)S(1)}, bf16[272,640]{1,0:T(8,128)(2,1)S(1)}, u32[]{:S(2)}, u32[]{:S(2)}) collective-permute-start(bf16[272,640]{1,0:T(8,128)(2,1)S(1)} %fusion.1.w0_ref), channel_id=1, source_target_pairs={{0,384},{128,0},{256,128},{384,256},{1,385},{129,1},{257,129},{385... | collective-permute-start | bytes 1044488 | tf_op jit(solution)/shard_map/ppermute | solution.py:45
  71.4 3.8 %collective-permute-start.3 = (bf16[8,8,8,512]{3,2,1,0:T(8,128)(2,1)S(1)}, bf16[8,8,8,512]{3,2,1,0:T(8,128)(2,1)S(1)}, u32[]{:S(2)}, u32[]{:S(2)}) collective-permute-start(bf16[8,8,8,512]{3,2,1,0:T(8,128)(2,1)S(1)} %all-to-all-done.1.mine_ref), channel_id=1, source_target_pairs={{0,1},{1,0},{2,3},{3,2},{4,5},{5,4},{6,7},{7,6},{8,9},{9,8},{10,11... | collective-permute-start | bytes 1572872 | tf_op jit(solution)/shard_map/ppermute | solution.py:41
  77.2 26.0 %all-to-all-start.2 = ((bf16[8,72,640]{2,1,0:T(8,128)(2,1)}), bf16[8,72,640]{2,1,0:T(8,128)(2,1)S(1)}, u32[]{:S(2)}, u32[]{:S(2)}) async-start(bf16[8,72,640]{2,1,0:T(8,128)(2,1)} %get-tuple-element.48), calls=%async_computation.2 | async-start | bytes 1474560 | tf_op jit(solution)/shard_map/all_to_all | solution.py:385
  85.4 29.1 %collective-permute-start.5 = (bf16[8,128,256]{2,1,0:T(8,128)(2,1)}, bf16[8,128,256]{2,1,0:T(8,128)(2,1)S(1)}, u32[]{:S(2)}, u32[]{:S(2)}) collective-permute-start(bf16[8,128,256]{2,1,0:T(8,128)(2,1)} %get-tuple-element.58), channel_id=1, source_target_pairs={{0,384},{128,0},{256,128},{384,256},{1,385},{129,1},{257,129},{385... | collective-permute-start | bytes 1572872 | tf_op jit(solution)/shard_map/ppermute | solution.py:45
  89.9 28.0 %collective-permute-start.6 = (bf16[8,128,256]{2,1,0:T(8,128)(2,1)}, bf16[8,128,256]{2,1,0:T(8,128)(2,1)S(1)}, u32[]{:S(2)}, u32[]{:S(2)}) collective-permute-start(bf16[8,128,256]{2,1,0:T(8,128)(2,1)} %get-tuple-element.59), channel_id=1, source_target_pairs={{0,128},{128,256},{256,384},{384,0},{1,129},{129,257},{257,385},{3... | collective-permute-start | bytes 1572872 | tf_op jit(solution)/shard_map/ppermute | solution.py:45
  91.9 27.7 %collective-permute-start.7 = (bf16[8,128,256]{2,1,0:T(8,128)(2,1)S(1)}, bf16[8,128,256]{2,1,0:T(8,128)(2,1)S(1)}, u32[]{:S(2)}, u32[]{:S(2)}) collective-permute-start(bf16[8,128,256]{2,1,0:T(8,128)(2,1)S(1)} %get-tuple-element.62), channel_id=1, source_target_pairs={{0,256},{128,384},{256,0},{384,128},{1,257},{129,385},{257,1},{385... | collective-permute-start | bytes 1572872 | tf_op jit(solution)/shard_map/ppermute | solution.py:45
  103.4 11.1 %collective-permute-start.4 = (bf16[320,128]{1,0:T(8,128)(2,1)S(1)}, bf16[320,128]{1,0:T(8,128)(2,1)S(1)}, u32[]{:S(2)}, u32[]{:S(2)}) collective-permute-start(bf16[320,128]{1,0:T(8,128)(2,1)S(1)} %finish.1.own_ref), channel_id=1, source_target_pairs={{0,8},{2,10},{4,12},{6,14},{8,0},{10,2},{12,4},{14,6},{1,9},{3,11}... | collective-permute-start | bytes 245768 | tf_op jit(solution)/shard_map/ppermute | solution.py:37
  120.3 10.8 %collective-permute-start.8 = (bf16[144,256]{1,0:T(8,128)(2,1)S(1)}, bf16[144,256]{1,0:T(8,128)(2,1)S(1)}, u32[]{:S(2)}, u32[]{:S(2)}) collective-permute-start(bf16[144,256]{1,0:T(8,128)(2,1)S(1)} %other_far.1), channel_id=1, source_target_pairs={{0,8},{2,10},{4,12},{6,14},{8,0},{10,2},{12,4},{14,6},{1,9},{3,11}... | collective-permute-start | bytes 221192 | tf_op jit(solution)/shard_map/ppermute | solution.py:37
Sparse Core Ops, SparseCore 0:
  9.4 65.4 all-gather.2

commit v11 on v8

--- a/solution.py
+++ b/solution.py
@@ -79,7 +79,7 @@
         found = jnp.sum(found.reshape(NZ, CH_DEV, HD), axis=1)
         found = jnp.sum(found, axis=1, keepdims=True).astype(jnp.int32)
         base = lax.broadcasted_iota(jnp.int32, (NZ, HD), 0) * CH_DEV
-        rows_ref[k] = base + found
+        rows_ref[k] = base + jnp.minimum(found, CH_DEV - 1)
 
     weights = jnp.concatenate([w[: 2 * HD, :] for w in (w0_ref, w1_ref, w2_ref, w3_ref)], axis=0)
     gain = gain_ref[...]
@@ -209,24 +209,24 @@
     fresh_eff_ref,
     pos_ref,
     kv0_ref,
+    kv2_ref,
     kv1_ref,
-    kv3_ref,
     acc_ref,
     run_ref,
 ):
     queries = other_ref[:QROWS, :]
     pos = pos_ref[...]
     attend_fresh(queries, flag_ref, own_ref, other_ref, fresh_eff_ref, pos, run_ref, acc_ref)
-    for k, kv_ref in ((0, kv0_ref), (1, kv1_ref), (3, kv3_ref)):
+    for k, kv_ref in ((0, kv0_ref), (2, kv2_ref), (1, kv1_ref)):
         attend_slots(k, kv_ref, queries, eff_ref, pos, run_ref, acc_ref)
 
 
 def other_far_kernel(
-    other_ref, eff_ref, pos_ref, acc_in_ref, run_in_ref, kv2_ref, sent_ref, acc_ref, run_ref
+    other_ref, eff_ref, pos_ref, acc_in_ref, run_in_ref, kv3_ref, sent_ref, acc_ref, run_ref
 ):
     acc_ref[...] = acc_in_ref[...]
     run_ref[...] = run_in_ref[...]
-    attend_slots(2, kv2_ref, other_ref[:QROWS, :], eff_ref, pos_ref[...], run_ref, acc_ref)
+    attend_slots(3, kv3_ref, other_ref[:QROWS, :], eff_ref, pos_ref[...], run_ref, acc_ref)
     peak = run_ref[0:1, :]
     total = run_ref[1:2, :]
     peak_high = peak.astype(jnp.bfloat16).astype(jnp.float32)
@@ -428,7 +428,7 @@
         name="other_near",
         compiler_params=params,
         cost_estimate=cost(3),
-    )(*common, arrived[0], arrived[1], arrived[3])
+    )(*common, arrived[0], arrived[2], arrived[1])
     sent = pl.pallas_call(
         other_far_kernel,
         out_shape=jax.ShapeDtypeStruct((HD + 16, QROWS), jnp.bfloat16),
@@ -438,7 +438,7 @@
         name="other_far",
         compiler_params=params,
         cost_estimate=cost(1),
-    )(other, eff, pos_row, acc, run, arrived[2])
+    )(other, eff, pos_row, acc, run, arrived[3])
     got = exchange(sent)
     queries, allowed, sent = lax.optimization_barrier((own, eff, sent))
     own_acc, own_run = pl.pallas_call(

time: 136 us -> 135 us (level)
  the two profiles are of different devices: /device:TPU:8 before, /device:TPU:16 now
where the time goes in v11:
time: 135 us; the launch traced here: 134 us
  starting transfers between devices  62.5 us (46%)
  waiting for transfers between devices  35.3 us (26%)
  between operations  13.7 us (10%)
  Pallas kernels  12.7 us (9%)
  other arithmetic  6.55 us (5%)
  local copies, waits for them, and re-layouts  3.7 us (3%)
    ppermute x6, starting transfers between devices, shifted(): lax.ppermute(block, axis, [(i, (i + by) % count) for i in range(count)])  19.7 us
    all_to_all x1, starting transfers between devices, body(): lax.all_to_all(blocks.reshape(NZ * NY * NC, 8, HD), ('z', 'y', 'c'), 0, 0...  17.3 us
    ppermute x6, waiting for transfers between devices, shifted(): lax.ppermute(block, axis, [(i, (i + by) % count) for i in range(count)])  12.6 us
    all_to_all x1, waiting for transfers between devices, body(): parts = lax.all_to_all(partial, 'z', 0, 0, tiled=True)  10.7 us
    ppermute x2, waiting for transfers between devices, exchange(): lax.ppermute(block, 'y', [(i, (i + NY // 2) % NY) for i in range(NY)])  9.47 us
    ppermute x2, starting transfers between devices, exchange(): lax.ppermute(block, 'y', [(i, (i + NY // 2) % NY) for i in range(NY)])  9.34 us
    all_to_all x1, starting transfers between devices, body(): lax.all_to_all(jnp.broadcast_to(blocks[None], (NY, NZ, 8, NX * HD)), 'y',...  7.21 us
    all_to_all x1, starting transfers between devices, body(): parts = lax.all_to_all(partial, 'z', 0, 0, tiled=True)  7.01 us
  transfers between devices with their start and end apart: 13, of which 7 were waited for; matrix products, arithmetic and copies ran while one was open for 8% of the time, Pallas kernels for 8%

profile of v11, /device:TPU:16, one launch (start us, length us, event | category | flops | bytes accessed | tf_op | source)
XLA Modules:
  0.0 134.4 jit_solution(13774758624873431654)
XLA Ops:
  7.3 0.8 copy.16
  8.8 17.3 %all-to-all-start = ((bf16[128,8,128]{2,1,0:T(8,128)(2,1)}), bf16[128,8,128]{2,1,0:T(8,128)(2,1)S(1)}, u32[]{:S(2)}, u32[]{:S(2)}) async-start(bf16[128,8,128]{2,1,0:T(8,128)(2,1)} %bitcast.4), calls=%async_computation | async-start | bytes 524288 | tf_op jit(solution)/shard_map/all_to_all | solution.py:307
  26.8 1.0 fusion.1.w0_ref
  27.8 4.9 %collective-permute-start = (bf16[272,640]{1,0:T(8,128)(2,1)S(1)}, bf16[272,640]{1,0:T(8,128)(2,1)S(1)}, u32[]{:S(2)}, u32[]{:S(2)}) collective-permute-start(bf16[272,640]{1,0:T(8,128)(2,1)S(1)} %fusion.1.w0_ref), channel_id=1, source_target_pairs={{0,256},{128,384},{256,0},{384,128},{1,257},{129,385},{257,1},{385... | collective-permute-start | bytes 1044488 | tf_op jit(solution)/shard_map/ppermute | solution.py:45
  32.8 0.9 select_reduce_fusion.1
  35.7 0.9 select_reduce_fusion
  36.6 0.9 compare_reduce_fusion
  38.2 3.2 %collective-permute-done.w2_ref = bf16[272,640]{1,0:T(8,128)(2,1)S(1)} collective-permute-done((bf16[272,640]{1,0:T(8,128)(2,1)S(1)}, bf16[272,640]{1,0:T(8,128)(2,1)S(1)}, u32[]{:S(2)}, u32[]{:S(2)}) %collective-permute-start) | collective-permute-done | bytes 348192 | tf_op jit(solution)/shard_map/ppermute | solution.py:45
  41.5 0.8 broadcast_in_dim.85
  42.3 7.2 %all-to-all-start.1 = ((bf16[8,8,8,512]{3,2,1,0:T(8,128)(2,1)}), bf16[8,8,8,512]{3,2,1,0:T(8,128)(2,1)S(1)}, u32[]{:S(2)}, u32[]{:S(2)}) async-start(bf16[8,8,8,512]{3,2,1,0:T(8,128)(2,1)} %broadcast_in_dim.85), calls=%async_computation.1 | async-start | bytes 1048576 | tf_op jit(solution)/shard_map/all_to_all | solution.py:317
  49.8 4.7 %collective-permute-start.1 = (bf16[272,640]{1,0:T(8,128)(2,1)S(1)}, bf16[272,640]{1,0:T(8,128)(2,1)S(1)}, u32[]{:S(2)}, u32[]{:S(2)}) collective-permute-start(bf16[272,640]{1,0:T(8,128)(2,1)S(1)} %fusion.1.w0_ref), channel_id=1, source_target_pairs={{0,384},{128,0},{256,128},{384,256},{1,385},{129,1},{257,129},{385... | collective-permute-start | bytes 1044488 | tf_op jit(solution)/shard_map/ppermute | solution.py:45
  54.4 1.9 %collective-permute-start.2 = (bf16[272,640]{1,0:T(8,128)(2,1)S(1)}, bf16[272,640]{1,0:T(8,128)(2,1)S(1)}, u32[]{:S(2)}, u32[]{:S(2)}) collective-permute-start(bf16[272,640]{1,0:T(8,128)(2,1)S(1)} %fusion.1.w0_ref), channel_id=1, source_target_pairs={{0,128},{128,256},{256,384},{384,0},{1,129},{129,257},{257,385},{3... | collective-permute-start | bytes 1044488 | tf_op jit(solution)/shard_map/ppermute | solution.py:45
  56.8 4.0 %collective-permute-done.1.w1_ref = bf16[272,640]{1,0:T(8,128)(2,1)S(1)} collective-permute-done((bf16[272,640]{1,0:T(8,128)(2,1)S(1)}, bf16[272,640]{1,0:T(8,128)(2,1)S(1)}, u32[]{:S(2)}, u32[]{:S(2)}) %collective-permute-start.1) | collective-permute-done | bytes 348192 | tf_op jit(solution)/shard_map/ppermute | solution.py:45
  60.8 5.3 %collective-permute-done.2.w3_ref = bf16[272,640]{1,0:T(8,128)(2,1)S(1)} collective-permute-done((bf16[272,640]{1,0:T(8,128)(2,1)S(1)}, bf16[272,640]{1,0:T(8,128)(2,1)S(1)}, u32[]{:S(2)}, u32[]{:S(2)}) %collective-permute-start.2) | collective-permute-done | bytes 348192 | tf_op jit(solution)/shard_map/ppermute | solution.py:45
  66.2 1.9 %collective-permute-start.3 = (bf16[8,8,8,512]{3,2,1,0:T(8,128)(2,1)S(1)}, bf16[8,8,8,512]{3,2,1,0:T(8,128)(2,1)S(1)}, u32[]{:S(2)}, u32[]{:S(2)}) collective-permute-start(bf16[8,8,8,512]{3,2,1,0:T(8,128)(2,1)S(1)} %all-to-all-done.1.mine_ref), channel_id=1, source_target_pairs={{0,1},{1,0},{2,3},{3,2},{4,5},{5,4},{6,7},{7,6},{8,9},{9,8},{10,11... | collective-permute-start | bytes 1572872 | tf_op jit(solution)/shard_map/ppermute | solution.py:41
  68.2 1.9 %collective-permute-done.3.mate_ref = bf16[8,8,8,512]{3,2,1,0:T(8,128)(2,1)S(1)} collective-permute-done((bf16[8,8,8,512]{3,2,1,0:T(8,128)(2,1)S(1)}, bf16[8,8,8,512]{3,2,1,0:T(8,128)(2,1)S(1)}, u32[]{:S(2)}, u32[]{:S(2)}) %collective-permute-start.3) | collective-permute-done | bytes 524320 | tf_op jit(solution)/shard_map/ppermute | solution.py:41
  70.0 1.9 %project.1 = (bf16[8,72,640]{2,1,0:T(8,128)(2,1)}, s32[4,8,128]{2,1,0:T(8,128)S(1)}) custom-call(s32[1]{0:T(128)} %bitcast.1.core_ref, bf16[8,8,8,512]{3,2,1,0:T(8,128)(2,1)S(1)} %all-to-all-done.1.mine_ref, bf16[8,8,8,512]{3,2,1,0:T(8,128)(2,1)S(1)} %collective-permute-done.3.mate_ref, f32[1,1024]{1,0:T(1,128)S(1)} %bitcast.30, ...), custom_call_target="tpu_custom_call" | custom-call | flops 671088640 | bytes 4194304 | tf_op jit(solution)/shard_map/project/pallas_call | solution.py:368
  72.0 7.0 %all-to-all-start.2 = ((bf16[8,72,640]{2,1,0:T(8,128)(2,1)}), bf16[8,72,640]{2,1,0:T(8,128)(2,1)S(1)}, u32[]{:S(2)}, u32[]{:S(2)}) async-start(bf16[8,72,640]{2,1,0:T(8,128)(2,1)} %get-tuple-element.46), calls=%async_computation.2 | async-start | bytes 1474560 | tf_op jit(solution)/shard_map/all_to_all | solution.py:382
  79.0 3.4 %pick.3 = (bf16[8,128,256]{2,1,0:T(8,128)(2,1)}, bf16[8,128,256]{2,1,0:T(8,128)(2,1)}, bf16[8,128,256]{2,1,0:T(8,128)(2,1)S(1)}) custom-call(s32[4,8,128]{2,1,0:T(8,128)S(1)} %get-tuple-element.55.rows_ref, bf16[64,128,256]{2,1,0:T(8,128)(2,1)} %bitcast.31), custom_call_target="tpu_custom_call" | custom-call | bytes 3145728 | tf_op jit(solution)/shard_map/pick/pallas_call | solution.py:385
  82.4 2.4 %collective-permute-start.5 = (bf16[8,128,256]{2,1,0:T(8,128)(2,1)}, bf16[8,128,256]{2,1,0:T(8,128)(2,1)S(1)}, u32[]{:S(2)}, u32[]{:S(2)}) collective-permute-start(bf16[8,128,256]{2,1,0:T(8,128)(2,1)} %get-tuple-element.56), channel_id=1, source_target_pairs={{0,256},{128,384},{256,0},{384,128},{1,257},{129,385},{257,1},{385... | collective-permute-start | bytes 1572872 | tf_op jit(solution)/shard_map/ppermute | solution.py:45
  84.8 3.2 %collective-permute-start.6 = (bf16[8,128,256]{2,1,0:T(8,128)(2,1)}, bf16[8,128,256]{2,1,0:T(8,128)(2,1)S(1)}, u32[]{:S(2)}, u32[]{:S(2)}) collective-permute-start(bf16[8,128,256]{2,1,0:T(8,128)(2,1)} %get-tuple-element.57), channel_id=1, source_target_pairs={{0,384},{128,0},{256,128},{384,256},{1,385},{129,1},{257,129},{385... | collective-permute-start | bytes 1572872 | tf_op jit(solution)/shard_map/ppermute | solution.py:45
  88.0 2.6 %collective-permute-start.7 = (bf16[8,128,256]{2,1,0:T(8,128)(2,1)S(1)}, bf16[8,128,256]{2,1,0:T(8,128)(2,1)S(1)}, u32[]{:S(2)}, u32[]{:S(2)}) collective-permute-start(bf16[8,128,256]{2,1,0:T(8,128)(2,1)S(1)} %get-tuple-element.60), channel_id=1, source_target_pairs={{0,128},{128,256},{256,384},{384,0},{1,129},{129,257},{257,385},{3... | collective-permute-start | bytes 1572872 | tf_op jit(solution)/shard_map/ppermute | solution.py:45
  90.6 10.7 %all-to-all-done.2.parts_ref = bf16[8,72,640]{2,1,0:T(8,128)(2,1)S(1)} async-done(((bf16[8,72,640]{2,1,0:T(8,128)(2,1)}), bf16[8,72,640]{2,1,0:T(8,128)(2,1)S(1)}, u32[]{:S(2)}, u32[]{:S(2)}) %all-to-all-start.2) | async-done | bytes 737312 | tf_op jit(solution)/shard_map/all_to_all | solution.py:382
  101.6 5.5 %collective-permute-start.4 = (bf16[320,128]{1,0:T(8,128)(2,1)S(1)}, bf16[320,128]{1,0:T(8,128)(2,1)S(1)}, u32[]{:S(2)}, u32[]{:S(2)}) collective-permute-start(bf16[320,128]{1,0:T(8,128)(2,1)S(1)} %finish.1.own_ref), channel_id=1, source_target_pairs={{0,8},{2,10},{4,12},{6,14},{8,0},{10,2},{12,4},{14,6},{1,9},{3,11}... | collective-permute-start | bytes 245768 | tf_op jit(solution)/shard_map/ppermute | solution.py:37
  107.1 1.9 %pick.2.kv0_ref = bf16[8,128,256]{2,1,0:T(8,128)(2,1)S(1)} custom-call(s32[4,8,128]{2,1,0:T(8,128)S(1)} %get-tuple-element.55.rows_ref, bf16[64,128,256]{2,1,0:T(8,128)(2,1)} %bitcast.32), custom_call_target="tpu_custom_call" | custom-call | bytes 1048576 | tf_op jit(solution)/shard_map/pick/pallas_call | solution.py:385
  109.0 4.4 %collective-permute-done.4.other_ref = bf16[320,128]{1,0:T(8,128)(2,1)S(1)} collective-permute-done((bf16[320,128]{1,0:T(8,128)(2,1)S(1)}, bf16[320,128]{1,0:T(8,128)(2,1)S(1)}, u32[]{:S(2)}, u32[]{:S(2)}) %collective-permute-start.4) | collective-permute-done | bytes 81952 | tf_op jit(solution)/shard_map/ppermute | solution.py:37
  113.5 1.6 %other_near.1 = (f32[128,256]{1,0:T(8,128)S(1)}, f32[8,256]{1,0:T(8,128)S(1)}) custom-call(s32[1]{0:T(128)} %bitcast.flag_ref, bf16[320,128]{1,0:T(8,128)(2,1)S(1)} %finish.1.own_ref, bf16[320,128]{1,0:T(8,128)(2,1)S(1)} %collective-permute-done.4.other_ref, s32[128,32]{1,0:T(8,128)S(1)} %or_select_fusion.eff_ref, ...), custom_call_target="tpu_custom_call" | custom-call | flops 402653184 | bytes 1572864 | tf_op jit(solution)/shard_map/other_near/pallas_call | solution.py:423
  115.1 0.8 other_far.1
  115.9 3.9 %collective-permute-start.8 = (bf16[144,256]{1,0:T(8,128)(2,1)S(1)}, bf16[144,256]{1,0:T(8,128)(2,1)S(1)}, u32[]{:S(2)}, u32[]{:S(2)}) collective-permute-start(bf16[144,256]{1,0:T(8,128)(2,1)S(1)} %other_far.1), channel_id=1, source_target_pairs={{0,8},{2,10},{4,12},{6,14},{8,0},{10,2},{12,4},{14,6},{1,9},{3,11}... | collective-permute-start | bytes 221192 | tf_op jit(solution)/shard_map/ppermute | solution.py:37
  119.8 2.0 %own.1 = (f32[128,256]{1,0:T(8,128)S(1)}, f32[8,256]{1,0:T(8,128)S(1)}) custom-call(s32[1]{0:T(128)} %bitcast.flag_ref, bf16[320,128]{1,0:T(8,128)(2,1)S(1)} %finish.1.own_ref, bf16[320,128]{1,0:T(8,128)(2,1)S(1)} %collective-permute-done.4.other_ref, s32[128,32]{1,0:T(8,128)S(1)} %or_select_fusion.eff_ref, s32[64,128]{1,0:T(8,128)S(1)} %broadcast_in_dim.94.fresh_eff_ref, ...), custom_call_target="tpu_custom_call" | custom-call | flops 536870912 | bytes 2097152 | tf_op jit(solution)/shard_map/own/pallas_call | solution.py:444
  121.8 5.0 %collective-permute-done.8.got_ref = bf16[144,256]{1,0:T(8,128)(2,1)S(1)} collective-permute-done((bf16[144,256]{1,0:T(8,128)(2,1)S(1)}, bf16[144,256]{1,0:T(8,128)(2,1)S(1)}, u32[]{:S(2)}, u32[]{:S(2)}) %collective-permute-start.8) | collective-permute-done | bytes 73760 | tf_op jit(solution)/shard_map/ppermute | solution.py:37
  126.8 0.8 merge.1
  (44 shorter events, 5.8 us)
Async XLA Ops:
  6.5 43.0 %copy-start = (s32[1,64]{1,0:T(1,128)S(1)}, s32[1,64]{1,0:T(1,128)}, u32[]{:S(2)}) copy-start(s32[1,64]{1,0:T(1,128)} %param.15) | copy-start | bytes 772
  6.5 72.5 %all-gather.3.cloned.1.call-start = ((), (), s32[]{:S(2)}) async-start(), calls=%async_computation.3 | async-start | bytes 4718592 | tf_op jit(solution)/shard_map/all_gather | solution.py:298
  8.8 32.5 %all-to-all-start = ((bf16[128,8,128]{2,1,0:T(8,128)(2,1)}), bf16[128,8,128]{2,1,0:T(8,128)(2,1)S(1)}, u32[]{:S(2)}, u32[]{:S(2)}) async-start(bf16[128,8,128]{2,1,0:T(8,128)(2,1)} %bitcast.4), calls=%async_computation | async-start | bytes 524288 | tf_op jit(solution)/shard_map/all_to_all | solution.py:307
  27.8 13.6 %collective-permute-start = (bf16[272,640]{1,0:T(8,128)(2,1)S(1)}, bf16[272,640]{1,0:T(8,128)(2,1)S(1)}, u32[]{:S(2)}, u32[]{:S(2)}) collective-permute-start(bf16[272,640]{1,0:T(8,128)(2,1)S(1)} %fusion.1.w0_ref), channel_id=1, source_target_pairs={{0,256},{128,384},{256,0},{384,128},{1,257},{129,385},{257,1},{385... | collective-permute-start | bytes 1044488 | tf_op jit(solution)/shard_map/ppermute | solution.py:45
  42.3 23.8 %all-to-all-start.1 = ((bf16[8,8,8,512]{3,2,1,0:T(8,128)(2,1)}), bf16[8,8,8,512]{3,2,1,0:T(8,128)(2,1)S(1)}, u32[]{:S(2)}, u32[]{:S(2)}) async-start(bf16[8,8,8,512]{3,2,1,0:T(8,128)(2,1)} %broadcast_in_dim.85), calls=%async_computation.1 | async-start | bytes 1048576 | tf_op jit(solution)/shard_map/all_to_all | solution.py:317
  49.8 11.0 %collective-permute-start.1 = (bf16[272,640]{1,0:T(8,128)(2,1)S(1)}, bf16[272,640]{1,0:T(8,128)(2,1)S(1)}, u32[]{:S(2)}, u32[]{:S(2)}) collective-permute-start(bf16[272,640]{1,0:T(8,128)(2,1)S(1)} %fusion.1.w0_ref), channel_id=1, source_target_pairs={{0,384},{128,0},{256,128},{384,256},{1,385},{129,1},{257,129},{385... | collective-permute-start | bytes 1044488 | tf_op jit(solution)/shard_map/ppermute | solution.py:45
  54.4 11.6 %collective-permute-start.2 = (bf16[272,640]{1,0:T(8,128)(2,1)S(1)}, bf16[272,640]{1,0:T(8,128)(2,1)S(1)}, u32[]{:S(2)}, u32[]{:S(2)}) collective-permute-start(bf16[272,640]{1,0:T(8,128)(2,1)S(1)} %fusion.1.w0_ref), channel_id=1, source_target_pairs={{0,128},{128,256},{256,384},{384,0},{1,129},{129,257},{257,385},{3... | collective-permute-start | bytes 1044488 | tf_op jit(solution)/shard_map/ppermute | solution.py:45
  66.2 3.8 %collective-permute-start.3 = (bf16[8,8,8,512]{3,2,1,0:T(8,128)(2,1)S(1)}, bf16[8,8,8,512]{3,2,1,0:T(8,128)(2,1)S(1)}, u32[]{:S(2)}, u32[]{:S(2)}) collective-permute-start(bf16[8,8,8,512]{3,2,1,0:T(8,128)(2,1)S(1)} %all-to-all-done.1.mine_ref), channel_id=1, source_target_pairs={{0,1},{1,0},{2,3},{3,2},{4,5},{5,4},{6,7},{7,6},{8,9},{9,8},{10,11... | collective-permute-start | bytes 1572872 | tf_op jit(solution)/shard_map/ppermute | solution.py:41
  72.0 29.4 %all-to-all-start.2 = ((bf16[8,72,640]{2,1,0:T(8,128)(2,1)}), bf16[8,72,640]{2,1,0:T(8,128)(2,1)S(1)}, u32[]{:S(2)}, u32[]{:S(2)}) async-start(bf16[8,72,640]{2,1,0:T(8,128)(2,1)} %get-tuple-element.46), calls=%async_computation.2 | async-start | bytes 1474560 | tf_op jit(solution)/shard_map/all_to_all | solution.py:382
  82.4 31.0 %collective-permute-start.5 = (bf16[8,128,256]{2,1,0:T(8,128)(2,1)}, bf16[8,128,256]{2,1,0:T(8,128)(2,1)S(1)}, u32[]{:S(2)}, u32[]{:S(2)}) collective-permute-start(bf16[8,128,256]{2,1,0:T(8,128)(2,1)} %get-tuple-element.56), channel_id=1, source_target_pairs={{0,256},{128,384},{256,0},{384,128},{1,257},{129,385},{257,1},{385... | collective-permute-start | bytes 1572872 | tf_op jit(solution)/shard_map/ppermute | solution.py:45
  84.8 28.7 %collective-permute-start.6 = (bf16[8,128,256]{2,1,0:T(8,128)(2,1)}, bf16[8,128,256]{2,1,0:T(8,128)(2,1)S(1)}, u32[]{:S(2)}, u32[]{:S(2)}) collective-permute-start(bf16[8,128,256]{2,1,0:T(8,128)(2,1)} %get-tuple-element.57), channel_id=1, source_target_pairs={{0,384},{128,0},{256,128},{384,256},{1,385},{129,1},{257,129},{385... | collective-permute-start | bytes 1572872 | tf_op jit(solution)/shard_map/ppermute | solution.py:45
  88.0 27.1 %collective-permute-start.7 = (bf16[8,128,256]{2,1,0:T(8,128)(2,1)S(1)}, bf16[8,128,256]{2,1,0:T(8,128)(2,1)S(1)}, u32[]{:S(2)}, u32[]{:S(2)}) collective-permute-start(bf16[8,128,256]{2,1,0:T(8,128)(2,1)S(1)} %get-tuple-element.60), channel_id=1, source_target_pairs={{0,128},{128,256},{256,384},{384,0},{1,129},{129,257},{257,385},{3... | collective-permute-start | bytes 1572872 | tf_op jit(solution)/shard_map/ppermute | solution.py:45
  101.6 11.9 %collective-permute-start.4 = (bf16[320,128]{1,0:T(8,128)(2,1)S(1)}, bf16[320,128]{1,0:T(8,128)(2,1)S(1)}, u32[]{:S(2)}, u32[]{:S(2)}) collective-permute-start(bf16[320,128]{1,0:T(8,128)(2,1)S(1)} %finish.1.own_ref), channel_id=1, source_target_pairs={{0,8},{2,10},{4,12},{6,14},{8,0},{10,2},{12,4},{14,6},{1,9},{3,11}... | collective-permute-start | bytes 245768 | tf_op jit(solution)/shard_map/ppermute | solution.py:37
  115.9 10.9 %collective-permute-start.8 = (bf16[144,256]{1,0:T(8,128)(2,1)S(1)}, bf16[144,256]{1,0:T(8,128)(2,1)S(1)}, u32[]{:S(2)}, u32[]{:S(2)}) collective-permute-start(bf16[144,256]{1,0:T(8,128)(2,1)S(1)} %other_far.1), channel_id=1, source_target_pairs={{0,8},{2,10},{4,12},{6,14},{8,0},{10,2},{12,4},{14,6},{1,9},{3,11}... | collective-permute-start | bytes 221192 | tf_op jit(solution)/shard_map/ppermute | solution.py:37
Sparse Core Ops, SparseCore 0:
  9.4 66.9 all-gather.2

commit v12 on v11

--- a/solution.py
+++ b/solution.py
@@ -201,7 +201,7 @@
     )
 
 
-def other_near_kernel(
+def other_kernel(
     flag_ref,
     own_ref,
     other_ref,
@@ -211,22 +211,16 @@
     kv0_ref,
     kv2_ref,
     kv1_ref,
+    kv3_ref,
+    sent_ref,
     acc_ref,
     run_ref,
 ):
     queries = other_ref[:QROWS, :]
     pos = pos_ref[...]
     attend_fresh(queries, flag_ref, own_ref, other_ref, fresh_eff_ref, pos, run_ref, acc_ref)
-    for k, kv_ref in ((0, kv0_ref), (2, kv2_ref), (1, kv1_ref)):
+    for k, kv_ref in ((0, kv0_ref), (2, kv2_ref), (1, kv1_ref), (3, kv3_ref)):
         attend_slots(k, kv_ref, queries, eff_ref, pos, run_ref, acc_ref)
-
-
-def other_far_kernel(
-    other_ref, eff_ref, pos_ref, acc_in_ref, run_in_ref, kv3_ref, sent_ref, acc_ref, run_ref
-):
-    acc_ref[...] = acc_in_ref[...]
-    run_ref[...] = run_in_ref[...]
-    attend_slots(3, kv3_ref, other_ref[:QROWS, :], eff_ref, pos_ref[...], run_ref, acc_ref)
     peak = run_ref[0:1, :]
     total = run_ref[1:2, :]
     peak_high = peak.astype(jnp.bfloat16).astype(jnp.float32)
@@ -420,25 +414,16 @@
         return pl.CostEstimate(flops=4 * pairs * HD, bytes_accessed=count << 19, transcendentals=pairs)
 
     common = (which_half.reshape(1), own, other, eff, fresh_eff, pos_row)
-    acc, run = pl.pallas_call(
-        other_near_kernel,
-        out_shape=run_shapes,
-        in_specs=[smem] + [vmem] * 8,
-        out_specs=[vmem] * 2,
-        name="other_near",
-        compiler_params=params,
-        cost_estimate=cost(3),
-    )(*common, arrived[0], arrived[2], arrived[1])
     sent = pl.pallas_call(
-        other_far_kernel,
+        other_kernel,
         out_shape=jax.ShapeDtypeStruct((HD + 16, QROWS), jnp.bfloat16),
-        in_specs=[vmem] * 6,
+        in_specs=[smem] + [vmem] * 9,
         out_specs=vmem,
         scratch_shapes=[pltpu.VMEM(r.shape, r.dtype) for r in run_shapes],
-        name="other_far",
+        name="other",
         compiler_params=params,
-        cost_estimate=cost(1),
-    )(other, eff, pos_row, acc, run, arrived[3])
+        cost_estimate=cost(4),
+    )(*common, *[arrived[k] for k in (0, 2, 1, 3)])
     got = exchange(sent)
     queries, allowed, sent = lax.optimization_barrier((own, eff, sent))
     own_acc, own_run = pl.pallas_call(

time: 135 us -> 135 us (level)
  transfers between devices with their start and end apart: 13 -> 13, of which waited for: 7 -> 7; matrix products, arithmetic and copies ran while one was open for 8% -> 8% of each run, Pallas kernels for 8% -> 7%
where the time goes in v12:
time: 135 us; the launch traced here: 134 us
  starting transfers between devices  62.5 us (46%)
  waiting for transfers between devices  35.3 us (26%)
  between operations  13.7 us (10%)
  Pallas kernels  12.4 us (9%)
  other arithmetic  6.55 us (5%)
  local copies, waits for them, and re-layouts  3.7 us (3%)
    ppermute x6, starting transfers between devices, shifted(): lax.ppermute(block, axis, [(i, (i + by) % count) for i in range(count)])  19.7 us
    all_to_all x1, starting transfers between devices, body(): lax.all_to_all(blocks.reshape(NZ * NY * NC, 8, HD), ('z', 'y', 'c'), 0, 0...  17.3 us
    ppermute x6, waiting for transfers between devices, shifted(): lax.ppermute(block, axis, [(i, (i + by) % count) for i in range(count)])  12.6 us
    all_to_all x1, waiting for transfers between devices, body(): parts = lax.all_to_all(partial, 'z', 0, 0, tiled=True)  10.7 us
    ppermute x2, waiting for transfers between devices, exchange(): lax.ppermute(block, 'y', [(i, (i + NY // 2) % NY) for i in range(NY)])  9.41 us
    ppermute x2, starting transfers between devices, exchange(): lax.ppermute(block, 'y', [(i, (i + NY // 2) % NY) for i in range(NY)])  9.34 us
    all_to_all x1, starting transfers between devices, body(): lax.all_to_all(jnp.broadcast_to(blocks[None], (NY, NZ, 8, NX * HD)), 'y',...  7.21 us
    all_to_all x1, starting transfers between devices, body(): parts = lax.all_to_all(partial, 'z', 0, 0, tiled=True)  7.02 us
  transfers between devices with their start and end apart: 13, of which 7 were waited for; matrix products, arithmetic and copies ran while one was open for 8% of the time, Pallas kernels for 7%

profile of v12, /device:TPU:16, one launch (start us, length us, event | category | flops | bytes accessed | tf_op | source)
XLA Modules:
  0.0 134.0 jit_solution(9648036220180958806)
XLA Ops:
  7.3 0.8 copy.16
  8.8 17.3 %all-to-all-start = ((bf16[128,8,128]{2,1,0:T(8,128)(2,1)}), bf16[128,8,128]{2,1,0:T(8,128)(2,1)S(1)}, u32[]{:S(2)}, u32[]{:S(2)}) async-start(bf16[128,8,128]{2,1,0:T(8,128)(2,1)} %bitcast.4), calls=%async_computation | async-start | bytes 524288 | tf_op jit(solution)/shard_map/all_to_all | solution.py:301
  26.8 1.0 fusion.1.w0_ref
  27.8 4.9 %collective-permute-start = (bf16[272,640]{1,0:T(8,128)(2,1)S(1)}, bf16[272,640]{1,0:T(8,128)(2,1)S(1)}, u32[]{:S(2)}, u32[]{:S(2)}) collective-permute-start(bf16[272,640]{1,0:T(8,128)(2,1)S(1)} %fusion.1.w0_ref), channel_id=1, source_target_pairs={{0,256},{128,384},{256,0},{384,128},{1,257},{129,385},{257,1},{385... | collective-permute-start | bytes 1044488 | tf_op jit(solution)/shard_map/ppermute | solution.py:45
  32.8 0.9 select_reduce_fusion.1
  34.6 0.7 reshape.169
  35.7 0.9 select_reduce_fusion
  36.6 0.9 compare_reduce_fusion
  38.2 3.2 %collective-permute-done.w2_ref = bf16[272,640]{1,0:T(8,128)(2,1)S(1)} collective-permute-done((bf16[272,640]{1,0:T(8,128)(2,1)S(1)}, bf16[272,640]{1,0:T(8,128)(2,1)S(1)}, u32[]{:S(2)}, u32[]{:S(2)}) %collective-permute-start) | collective-permute-done | bytes 348192 | tf_op jit(solution)/shard_map/ppermute | solution.py:45
  41.5 0.9 broadcast_in_dim.85
  42.3 7.2 %all-to-all-start.1 = ((bf16[8,8,8,512]{3,2,1,0:T(8,128)(2,1)}), bf16[8,8,8,512]{3,2,1,0:T(8,128)(2,1)S(1)}, u32[]{:S(2)}, u32[]{:S(2)}) async-start(bf16[8,8,8,512]{3,2,1,0:T(8,128)(2,1)} %broadcast_in_dim.85), calls=%async_computation.1 | async-start | bytes 1048576 | tf_op jit(solution)/shard_map/all_to_all | solution.py:311
  49.8 4.7 %collective-permute-start.1 = (bf16[272,640]{1,0:T(8,128)(2,1)S(1)}, bf16[272,640]{1,0:T(8,128)(2,1)S(1)}, u32[]{:S(2)}, u32[]{:S(2)}) collective-permute-start(bf16[272,640]{1,0:T(8,128)(2,1)S(1)} %fusion.1.w0_ref), channel_id=1, source_target_pairs={{0,384},{128,0},{256,128},{384,256},{1,385},{129,1},{257,129},{385... | collective-permute-start | bytes 1044488 | tf_op jit(solution)/shard_map/ppermute | solution.py:45
  54.4 1.9 %collective-permute-start.2 = (bf16[272,640]{1,0:T(8,128)(2,1)S(1)}, bf16[272,640]{1,0:T(8,128)(2,1)S(1)}, u32[]{:S(2)}, u32[]{:S(2)}) collective-permute-start(bf16[272,640]{1,0:T(8,128)(2,1)S(1)} %fusion.1.w0_ref), channel_id=1, source_target_pairs={{0,128},{128,256},{256,384},{384,0},{1,129},{129,257},{257,385},{3... | collective-permute-start | bytes 1044488 | tf_op jit(solution)/shard_map/ppermute | solution.py:45
  56.8 4.0 %collective-permute-done.1.w1_ref = bf16[272,640]{1,0:T(8,128)(2,1)S(1)} collective-permute-done((bf16[272,640]{1,0:T(8,128)(2,1)S(1)}, bf16[272,640]{1,0:T(8,128)(2,1)S(1)}, u32[]{:S(2)}, u32[]{:S(2)}) %collective-permute-start.1) | collective-permute-done | bytes 348192 | tf_op jit(solution)/shard_map/ppermute | solution.py:45
  60.8 5.3 %collective-permute-done.2.w3_ref = bf16[272,640]{1,0:T(8,128)(2,1)S(1)} collective-permute-done((bf16[272,640]{1,0:T(8,128)(2,1)S(1)}, bf16[272,640]{1,0:T(8,128)(2,1)S(1)}, u32[]{:S(2)}, u32[]{:S(2)}) %collective-permute-start.2) | collective-permute-done | bytes 348192 | tf_op jit(solution)/shard_map/ppermute | solution.py:45
  66.2 1.9 %collective-permute-start.3 = (bf16[8,8,8,512]{3,2,1,0:T(8,128)(2,1)S(1)}, bf16[8,8,8,512]{3,2,1,0:T(8,128)(2,1)S(1)}, u32[]{:S(2)}, u32[]{:S(2)}) collective-permute-start(bf16[8,8,8,512]{3,2,1,0:T(8,128)(2,1)S(1)} %all-to-all-done.1.mine_ref), channel_id=1, source_target_pairs={{0,1},{1,0},{2,3},{3,2},{4,5},{5,4},{6,7},{7,6},{8,9},{9,8},{10,11... | collective-permute-start | bytes 1572872 | tf_op jit(solution)/shard_map/ppermute | solution.py:41
  68.2 1.9 %collective-permute-done.3.mate_ref = bf16[8,8,8,512]{3,2,1,0:T(8,128)(2,1)S(1)} collective-permute-done((bf16[8,8,8,512]{3,2,1,0:T(8,128)(2,1)S(1)}, bf16[8,8,8,512]{3,2,1,0:T(8,128)(2,1)S(1)}, u32[]{:S(2)}, u32[]{:S(2)}) %collective-permute-start.3) | collective-permute-done | bytes 524320 | tf_op jit(solution)/shard_map/ppermute | solution.py:41
  70.0 1.9 %project.1 = (bf16[8,72,640]{2,1,0:T(8,128)(2,1)}, s32[4,8,128]{2,1,0:T(8,128)S(1)}) custom-call(s32[1]{0:T(128)} %bitcast.1.core_ref, bf16[8,8,8,512]{3,2,1,0:T(8,128)(2,1)S(1)} %all-to-all-done.1.mine_ref, bf16[8,8,8,512]{3,2,1,0:T(8,128)(2,1)S(1)} %collective-permute-done.3.mate_ref, f32[1,1024]{1,0:T(1,128)S(1)} %bitcast.30, ...), custom_call_target="tpu_custom_call" | custom-call | flops 671088640 | bytes 4194304 | tf_op jit(solution)/shard_map/project/pallas_call | solution.py:362
  72.0 7.0 %all-to-all-start.2 = ((bf16[8,72,640]{2,1,0:T(8,128)(2,1)}), bf16[8,72,640]{2,1,0:T(8,128)(2,1)S(1)}, u32[]{:S(2)}, u32[]{:S(2)}) async-start(bf16[8,72,640]{2,1,0:T(8,128)(2,1)} %get-tuple-element.44), calls=%async_computation.2 | async-start | bytes 1474560 | tf_op jit(solution)/shard_map/all_to_all | solution.py:376
  79.0 3.4 %pick.3 = (bf16[8,128,256]{2,1,0:T(8,128)(2,1)}, bf16[8,128,256]{2,1,0:T(8,128)(2,1)}, bf16[8,128,256]{2,1,0:T(8,128)(2,1)S(1)}) custom-call(s32[4,8,128]{2,1,0:T(8,128)S(1)} %get-tuple-element.53.rows_ref, bf16[64,128,256]{2,1,0:T(8,128)(2,1)} %bitcast.31), custom_call_target="tpu_custom_call" | custom-call | bytes 3145728 | tf_op jit(solution)/shard_map/pick/pallas_call | solution.py:379
  82.4 2.4 %collective-permute-start.5 = (bf16[8,128,256]{2,1,0:T(8,128)(2,1)}, bf16[8,128,256]{2,1,0:T(8,128)(2,1)S(1)}, u32[]{:S(2)}, u32[]{:S(2)}) collective-permute-start(bf16[8,128,256]{2,1,0:T(8,128)(2,1)} %get-tuple-element.54), channel_id=1, source_target_pairs={{0,256},{128,384},{256,0},{384,128},{1,257},{129,385},{257,1},{385... | collective-permute-start | bytes 1572872 | tf_op jit(solution)/shard_map/ppermute | solution.py:45
  84.8 3.2 %collective-permute-start.6 = (bf16[8,128,256]{2,1,0:T(8,128)(2,1)}, bf16[8,128,256]{2,1,0:T(8,128)(2,1)S(1)}, u32[]{:S(2)}, u32[]{:S(2)}) collective-permute-start(bf16[8,128,256]{2,1,0:T(8,128)(2,1)} %get-tuple-element.55), channel_id=1, source_target_pairs={{0,384},{128,0},{256,128},{384,256},{1,385},{129,1},{257,129},{385... | collective-permute-start | bytes 1572872 | tf_op jit(solution)/shard_map/ppermute | solution.py:45
  88.0 2.6 %collective-permute-start.7 = (bf16[8,128,256]{2,1,0:T(8,128)(2,1)S(1)}, bf16[8,128,256]{2,1,0:T(8,128)(2,1)S(1)}, u32[]{:S(2)}, u32[]{:S(2)}) collective-permute-start(bf16[8,128,256]{2,1,0:T(8,128)(2,1)S(1)} %get-tuple-element.56), channel_id=1, source_target_pairs={{0,128},{128,256},{256,384},{384,0},{1,129},{129,257},{257,385},{3... | collective-permute-start | bytes 1572872 | tf_op jit(solution)/shard_map/ppermute | solution.py:45
  90.6 10.7 %all-to-all-done.2.parts_ref = bf16[8,72,640]{2,1,0:T(8,128)(2,1)S(1)} async-done(((bf16[8,72,640]{2,1,0:T(8,128)(2,1)}), bf16[8,72,640]{2,1,0:T(8,128)(2,1)S(1)}, u32[]{:S(2)}, u32[]{:S(2)}) %all-to-all-start.2) | async-done | bytes 737312 | tf_op jit(solution)/shard_map/all_to_all | solution.py:376
  101.6 5.5 %collective-permute-start.4 = (bf16[320,128]{1,0:T(8,128)(2,1)S(1)}, bf16[320,128]{1,0:T(8,128)(2,1)S(1)}, u32[]{:S(2)}, u32[]{:S(2)}) collective-permute-start(bf16[320,128]{1,0:T(8,128)(2,1)S(1)} %finish.1.own_ref), channel_id=1, source_target_pairs={{0,8},{2,10},{4,12},{6,14},{8,0},{10,2},{12,4},{14,6},{1,9},{3,11}... | collective-permute-start | bytes 245768 | tf_op jit(solution)/shard_map/ppermute | solution.py:37
  107.1 1.9 %pick.2.kv0_ref = bf16[8,128,256]{2,1,0:T(8,128)(2,1)S(1)} custom-call(s32[4,8,128]{2,1,0:T(8,128)S(1)} %get-tuple-element.53.rows_ref, bf16[64,128,256]{2,1,0:T(8,128)(2,1)} %bitcast.32), custom_call_target="tpu_custom_call" | custom-call | bytes 1048576 | tf_op jit(solution)/shard_map/pick/pallas_call | solution.py:379
  109.0 4.4 %collective-permute-done.4.other_ref = bf16[320,128]{1,0:T(8,128)(2,1)S(1)} collective-permute-done((bf16[320,128]{1,0:T(8,128)(2,1)S(1)}, bf16[320,128]{1,0:T(8,128)(2,1)S(1)}, u32[]{:S(2)}, u32[]{:S(2)}) %collective-permute-start.4) | collective-permute-done | bytes 81952 | tf_op jit(solution)/shard_map/ppermute | solution.py:37
  113.5 2.1 %other.1 = bf16[144,256]{1,0:T(8,128)(2,1)S(1)} custom-call(s32[1]{0:T(128)} %bitcast.flag_ref, bf16[320,128]{1,0:T(8,128)(2,1)S(1)} %finish.1.own_ref, bf16[320,128]{1,0:T(8,128)(2,1)S(1)} %collective-permute-done.4.other_ref, s32[128,32]{1,0:T(8,128)S(1)} %or_select_fusion.eff_ref, s32[64,128]{1,0:T(8,128)S(1)} %broadcast_in_dim.94.fresh_eff_ref, ...), custom_call_target="tpu_custom_call" | custom-call | flops 536870912 | bytes 2097152 | tf_op jit(solution)/shard_map/other/pallas_call | solution.py:417
  115.5 3.9 %collective-permute-start.8 = (bf16[144,256]{1,0:T(8,128)(2,1)S(1)}, bf16[144,256]{1,0:T(8,128)(2,1)S(1)}, u32[]{:S(2)}, u32[]{:S(2)}) collective-permute-start(bf16[144,256]{1,0:T(8,128)(2,1)S(1)} %other.1), channel_id=1, source_target_pairs={{0,8},{2,10},{4,12},{6,14},{8,0},{10,2},{12,4},{14,6},{1,9},{3,11}... | collective-permute-start | bytes 221192 | tf_op jit(solution)/shard_map/ppermute | solution.py:37
  119.4 2.0 %own.1 = (f32[128,256]{1,0:T(8,128)S(1)}, f32[8,256]{1,0:T(8,128)S(1)}) custom-call(s32[1]{0:T(128)} %bitcast.flag_ref, bf16[320,128]{1,0:T(8,128)(2,1)S(1)} %finish.1.own_ref, bf16[320,128]{1,0:T(8,128)(2,1)S(1)} %collective-permute-done.4.other_ref, s32[128,32]{1,0:T(8,128)S(1)} %or_select_fusion.eff_ref, s32[64,128]{1,0:T(8,128)S(1)} %broadcast_in_dim.94.fresh_eff_ref, ...), custom_call_target="tpu_custom_call" | custom-call | flops 536870912 | bytes 2097152 | tf_op jit(solution)/shard_map/own/pallas_call | solution.py:429
  121.4 5.0 %collective-permute-done.8.got_ref = bf16[144,256]{1,0:T(8,128)(2,1)S(1)} collective-permute-done((bf16[144,256]{1,0:T(8,128)(2,1)S(1)}, bf16[144,256]{1,0:T(8,128)(2,1)S(1)}, u32[]{:S(2)}, u32[]{:S(2)}) %collective-permute-start.8) | collective-permute-done | bytes 73760 | tf_op jit(solution)/shard_map/ppermute | solution.py:37
  126.4 0.8 merge.1
  (43 shorter events, 5.1 us)
Async XLA Ops:
  6.5 43.0 %copy-start = (s32[1,64]{1,0:T(1,128)S(1)}, s32[1,64]{1,0:T(1,128)}, u32[]{:S(2)}) copy-start(s32[1,64]{1,0:T(1,128)} %param.15) | copy-start | bytes 772
  6.5 72.5 %all-gather.3.cloned.1.call-start = ((), (), s32[]{:S(2)}) async-start(), calls=%async_computation.3 | async-start | bytes 4718592 | tf_op jit(solution)/shard_map/all_gather | solution.py:292
  8.8 32.5 %all-to-all-start = ((bf16[128,8,128]{2,1,0:T(8,128)(2,1)}), bf16[128,8,128]{2,1,0:T(8,128)(2,1)S(1)}, u32[]{:S(2)}, u32[]{:S(2)}) async-start(bf16[128,8,128]{2,1,0:T(8,128)(2,1)} %bitcast.4), calls=%async_computation | async-start | bytes 524288 | tf_op jit(solution)/shard_map/all_to_all | solution.py:301
  27.8 13.6 %collective-permute-start = (bf16[272,640]{1,0:T(8,128)(2,1)S(1)}, bf16[272,640]{1,0:T(8,128)(2,1)S(1)}, u32[]{:S(2)}, u32[]{:S(2)}) collective-permute-start(bf16[272,640]{1,0:T(8,128)(2,1)S(1)} %fusion.1.w0_ref), channel_id=1, source_target_pairs={{0,256},{128,384},{256,0},{384,128},{1,257},{129,385},{257,1},{385... | collective-permute-start | bytes 1044488 | tf_op jit(solution)/shard_map/ppermute | solution.py:45
  42.3 23.8 %all-to-all-start.1 = ((bf16[8,8,8,512]{3,2,1,0:T(8,128)(2,1)}), bf16[8,8,8,512]{3,2,1,0:T(8,128)(2,1)S(1)}, u32[]{:S(2)}, u32[]{:S(2)}) async-start(bf16[8,8,8,512]{3,2,1,0:T(8,128)(2,1)} %broadcast_in_dim.85), calls=%async_computation.1 | async-start | bytes 1048576 | tf_op jit(solution)/shard_map/all_to_all | solution.py:311
  49.8 11.0 %collective-permute-start.1 = (bf16[272,640]{1,0:T(8,128)(2,1)S(1)}, bf16[272,640]{1,0:T(8,128)(2,1)S(1)}, u32[]{:S(2)}, u32[]{:S(2)}) collective-permute-start(bf16[272,640]{1,0:T(8,128)(2,1)S(1)} %fusion.1.w0_ref), channel_id=1, source_target_pairs={{0,384},{128,0},{256,128},{384,256},{1,385},{129,1},{257,129},{385... | collective-permute-start | bytes 1044488 | tf_op jit(solution)/shard_map/ppermute | solution.py:45
  54.4 11.6 %collective-permute-start.2 = (bf16[272,640]{1,0:T(8,128)(2,1)S(1)}, bf16[272,640]{1,0:T(8,128)(2,1)S(1)}, u32[]{:S(2)}, u32[]{:S(2)}) collective-permute-start(bf16[272,640]{1,0:T(8,128)(2,1)S(1)} %fusion.1.w0_ref), channel_id=1, source_target_pairs={{0,128},{128,256},{256,384},{384,0},{1,129},{129,257},{257,385},{3... | collective-permute-start | bytes 1044488 | tf_op jit(solution)/shard_map/ppermute | solution.py:45
  66.2 3.8 %collective-permute-start.3 = (bf16[8,8,8,512]{3,2,1,0:T(8,128)(2,1)S(1)}, bf16[8,8,8,512]{3,2,1,0:T(8,128)(2,1)S(1)}, u32[]{:S(2)}, u32[]{:S(2)}) collective-permute-start(bf16[8,8,8,512]{3,2,1,0:T(8,128)(2,1)S(1)} %all-to-all-done.1.mine_ref), channel_id=1, source_target_pairs={{0,1},{1,0},{2,3},{3,2},{4,5},{5,4},{6,7},{7,6},{8,9},{9,8},{10,11... | collective-permute-start | bytes 1572872 | tf_op jit(solution)/shard_map/ppermute | solution.py:41
  72.0 29.4 %all-to-all-start.2 = ((bf16[8,72,640]{2,1,0:T(8,128)(2,1)}), bf16[8,72,640]{2,1,0:T(8,128)(2,1)S(1)}, u32[]{:S(2)}, u32[]{:S(2)}) async-start(bf16[8,72,640]{2,1,0:T(8,128)(2,1)} %get-tuple-element.44), calls=%async_computation.2 | async-start | bytes 1474560 | tf_op jit(solution)/shard_map/all_to_all | solution.py:376
  82.4 31.0 %collective-permute-start.5 = (bf16[8,128,256]{2,1,0:T(8,128)(2,1)}, bf16[8,128,256]{2,1,0:T(8,128)(2,1)S(1)}, u32[]{:S(2)}, u32[]{:S(2)}) collective-permute-start(bf16[8,128,256]{2,1,0:T(8,128)(2,1)} %get-tuple-element.54), channel_id=1, source_target_pairs={{0,256},{128,384},{256,0},{384,128},{1,257},{129,385},{257,1},{385... | collective-permute-start | bytes 1572872 | tf_op jit(solution)/shard_map/ppermute | solution.py:45
  84.8 28.7 %collective-permute-start.6 = (bf16[8,128,256]{2,1,0:T(8,128)(2,1)}, bf16[8,128,256]{2,1,0:T(8,128)(2,1)S(1)}, u32[]{:S(2)}, u32[]{:S(2)}) collective-permute-start(bf16[8,128,256]{2,1,0:T(8,128)(2,1)} %get-tuple-element.55), channel_id=1, source_target_pairs={{0,384},{128,0},{256,128},{384,256},{1,385},{129,1},{257,129},{385... | collective-permute-start | bytes 1572872 | tf_op jit(solution)/shard_map/ppermute | solution.py:45
  88.0 25.4 %collective-permute-start.7 = (bf16[8,128,256]{2,1,0:T(8,128)(2,1)S(1)}, bf16[8,128,256]{2,1,0:T(8,128)(2,1)S(1)}, u32[]{:S(2)}, u32[]{:S(2)}) collective-permute-start(bf16[8,128,256]{2,1,0:T(8,128)(2,1)S(1)} %get-tuple-element.56), channel_id=1, source_target_pairs={{0,128},{128,256},{256,384},{384,0},{1,129},{129,257},{257,385},{3... | collective-permute-start | bytes 1572872 | tf_op jit(solution)/shard_map/ppermute | solution.py:45
  101.6 11.9 %collective-permute-start.4 = (bf16[320,128]{1,0:T(8,128)(2,1)S(1)}, bf16[320,128]{1,0:T(8,128)(2,1)S(1)}, u32[]{:S(2)}, u32[]{:S(2)}) collective-permute-start(bf16[320,128]{1,0:T(8,128)(2,1)S(1)} %finish.1.own_ref), channel_id=1, source_target_pairs={{0,8},{2,10},{4,12},{6,14},{8,0},{10,2},{12,4},{14,6},{1,9},{3,11}... | collective-permute-start | bytes 245768 | tf_op jit(solution)/shard_map/ppermute | solution.py:37
  115.5 10.9 %collective-permute-start.8 = (bf16[144,256]{1,0:T(8,128)(2,1)S(1)}, bf16[144,256]{1,0:T(8,128)(2,1)S(1)}, u32[]{:S(2)}, u32[]{:S(2)}) collective-permute-start(bf16[144,256]{1,0:T(8,128)(2,1)S(1)} %other.1), channel_id=1, source_target_pairs={{0,8},{2,10},{4,12},{6,14},{8,0},{10,2},{12,4},{14,6},{1,9},{3,11}... | collective-permute-start | bytes 221192 | tf_op jit(solution)/shard_map/ppermute | solution.py:37
Sparse Core Ops, SparseCore 0:
  9.4 66.9 all-gather.2
